TPU v7x, 32 devices: a whole 2x2x4 slice. The times are simulated.
32 devices in a mesh: rep: 2 (over y), ep: 4 (over z), tp: 2 (over x), sub: 2 (over core).
Axes of the slice: x: 2, y: 2, z: 4, core: 2. Of those that a mesh axis runs over, the one named last changes fastest.
Arguments:
- grad_values: bfloat16 [2048, 3584], P(('rep', 'ep', 'tp'), 'sub'), parts along dimension 0, may hold values from -6 to 6
- grad_scales: float32 [2048, 28], P(('rep', 'ep', 'tp'), 'sub'), parts along dimension 0, may hold values from 0.2 to 2
- expert_ids: int32 [2048, 1], P(('rep', 'ep', 'tp')), parts along dimension 0, may hold values from 0 to 3; in each aligned block of 128 rows (0 to 127, 128 to 255, ...) at most 36 rows name the same one
- route_weights: float32 [2048, 1], P(('rep', 'ep', 'tp')), parts along dimension 0, may hold values from 0.2 to 1
- w_gate: bfloat16 [4, 3584, 1024], P('ep', 'sub', 'tp'), may hold values from -0.1875 to 0.1875
- w_up: bfloat16 [4, 3584, 1024], P('ep', 'sub', 'tp'), may hold values from -0.1875 to 0.1875
- w_down: bfloat16 [4, 1024, 3584], P('ep', 'tp', 'sub'), may hold values from -0.09375 to 0.09375
- pre_acts: bfloat16 [8, 2, 288, 1024], P(('rep', 'ep'), None, None, 'tp'), parts along dimension 0, may hold values from -6 to 6
- latent_partials: bfloat16 [2, 2048, 512], P('tp', ('rep', 'ep'), 'sub'), parts along dimension 1, may hold values from -6 to 6
- latent: bfloat16 [2048, 512], P(('rep', 'ep', 'tp'), 'sub'), parts along dimension 0, may hold values from -120 to 120
- latent_gain: float32 [512], P('sub'), may hold values from 0.25 to 1.75
Outputs:
- grad_input: bfloat16 [2048, 3584], P(('rep', 'ep', 'tp'), 'sub'), parts along dimension 0
- d_latent: bfloat16 [2048, 512], P(('rep', 'ep', 'tp'), 'sub'), parts along dimension 0
There are 2 independent parts, one for each index of `rep`. A program takes and returns all parts, laid end to end along the dimension named above; an argument that names none is the same for every part. Nothing has to cross between parts.
Inputs may be any that keep to these rules, and one draw needn't show every extreme that they name: `expert_ids`: among the routes of the tokens of one index pair of ep and tp, no expert is named more than 36 times.
All inputs are finite; a program needn't handle non-finite values.
Results may differ from a plain program's by a relative error of at most 0.0066.
Values may be sent and summed in bfloat16 or wider, within the bound.
No kernel may reach another device: no remote copies, remote signals or barrier semaphores. Data moves between devices by JAX's collectives and lax.ppermute only.
A program may use at most 64 MiB of HBM per device.

v0:
```python
import jax
import jax.numpy as jnp
from jax import lax
from jax.sharding import PartitionSpec as P

LAT = 512


def local(
    grad_values,
    grad_scales,
    expert_ids,
    route_weights,
    w_gate,
    w_up,
    w_down,
    pre_acts,
    latent_partials,
    latent,
    latent_gain,
):
    wide_count = lax.axis_size("ep")
    narrow_count = lax.axis_size("tp")
    tok_rows, half_width = grad_values.shape
    route_count = expert_ids.shape[1]
    slot_total = pre_acts.shape[2]
    most_rows = slot_total // (wide_count * narrow_count)
    arrived_latent = lax.all_to_all(latent_partials, "tp", split_axis=1, concat_axis=0, tiled=True)
    own_grad = jnp.sum(arrived_latent.astype(jnp.float32), axis=0)
    values = latent.astype(jnp.float32)
    gained = own_grad * latent_gain[None, :]
    scaled = (
        grad_values.astype(jnp.float32).reshape(tok_rows, half_width // 128, 128)
        * grad_scales[:, :, None]
    ).reshape(tok_rows, half_width)
    weighted = (
        (scaled[:, None, :] * route_weights[:, :, None])
        .astype(jnp.bfloat16)
        .reshape(tok_rows * route_count, half_width)
    )
    flat_ids = expert_ids.reshape(-1)
    onehot = (flat_ids[:, None] == jnp.arange(wide_count, dtype=jnp.int32)[None, :]).astype(
        jnp.int32
    )
    earlier = jnp.cumsum(onehot, axis=0) - onehot
    position = jnp.sum(earlier * onehot, axis=1)
    target = flat_ids * most_rows + position
    placing = (
        jnp.arange(wide_count * most_rows, dtype=jnp.int32)[:, None] == target[None, :]
    ).astype(jnp.bfloat16)
    packed = jnp.dot(placing, weighted, preferred_element_type=jnp.float32).astype(jnp.bfloat16)
    grouped = lax.all_gather(
        packed.reshape(wide_count, 1, most_rows, half_width), "tp", axis=1, tiled=True
    )
    arrived = lax.all_to_all(grouped, "ep", split_axis=0, concat_axis=0, tiled=True)
    received = arrived.reshape(slot_total, half_width)
    hidden_part = jnp.einsum("sd,fd->sf", received, w_down[0], preferred_element_type=jnp.float32)
    hidden_grad, squares, cross_terms = lax.psum(
        (hidden_part, jnp.sum(values * values, axis=1), jnp.sum(gained * values, axis=1)), "sub"
    )
    inverse_rms = lax.rsqrt(squares / LAT + 1e-06)[:, None]
    d_latent = (
        inverse_rms * gained - values * inverse_rms**3 * cross_terms[:, None] / LAT
    ).astype(jnp.bfloat16)
    gate_pre = pre_acts[0, 0].astype(jnp.float32)
    up_pre = pre_acts[0, 1].astype(jnp.float32)
    sigmoid_gate = jax.nn.sigmoid(gate_pre)
    up_grad = (hidden_grad * gate_pre * sigmoid_gate).astype(jnp.bfloat16)
    gate_grad = (
        hidden_grad * up_pre * sigmoid_gate * (1.0 + gate_pre * (1.0 - sigmoid_gate))
    ).astype(jnp.bfloat16)
    back_rows = jnp.einsum("sf,df->sd", gate_grad, w_gate[0], preferred_element_type=jnp.float32)
    back_rows = back_rows + jnp.einsum(
        "sf,df->sd", up_grad, w_up[0], preferred_element_type=jnp.float32
    )
    partial_rows = back_rows.astype(jnp.bfloat16).reshape(
        wide_count, narrow_count, most_rows, half_width
    )
    summed = lax.psum_scatter(
        partial_rows.astype(jnp.float32).astype(jnp.bfloat16), "tp", scatter_dimension=1, tiled=True
    )
    returned_rows = lax.all_to_all(summed, "ep", split_axis=0, concat_axis=0, tiled=True)
    home_rows = returned_rows.reshape(wide_count * most_rows, half_width)
    picked = jnp.take(home_rows, target, axis=0)
    grad_input = jnp.sum(
        picked.astype(jnp.float32).reshape(tok_rows, route_count, half_width), axis=1
    ).astype(jnp.bfloat16)
    return (grad_input, d_latent)


def solution(mesh):
    placed = (
        P(("rep", "ep", "tp"), "sub"),
        P(("rep", "ep", "tp"), "sub"),
        P(("rep", "ep", "tp"), None),
        P(("rep", "ep", "tp"), None),
        P("ep", "sub", "tp"),
        P("ep", "sub", "tp"),
        P("ep", "tp", "sub"),
        P(("rep", "ep"), None, None, "tp"),
        P("tp", ("rep", "ep"), "sub"),
        P(("rep", "ep", "tp"), "sub"),
        P("sub"),
    )
    return jax.shard_map(
        local,
        mesh=mesh,
        in_specs=placed,
        out_specs=(P(("rep", "ep", "tp"), "sub"), P(("rep", "ep", "tp"), "sub")),
        check_vma=False,
    )
```

profile of v0, /device:TPU:0, one launch (start us, length us, event | category | flops | bytes accessed | tf_op | source)
XLA Modules:
  0.0 161.9 jit_solution(5155437167518231375)
XLA Ops:
  7.2 1.4 copy.31
  9.6 0.8 select_reduce_fusion
  11.1 0.8 fusion.7
  12.5 15.4 %all_gather.3 = bf16[4,2,36,1792]{3,0,2,1:T(4,128)(2,1)S(1)} all-gather(bf16[4,1,36,1792]{3,0,2,1:T(4,128)(2,1)S(1)} %copy.32), channel_id=1, replica_groups=mesh['rep'=2,'ep'=4,'tp'=2,'sub'=2] {'tp'}, dimensions={1}, use_global_device_ids=true | all-gather | bytes 1548288 | tf_op jit(solution)/shard_map/all_gather | solution.py:52
  27.9 0.8 copy.33
  28.7 29.4 %all_to_all.19 = bf16[4,2,36,1792]{3,1,2,0:T(2,128)(2,1)S(1)} all-to-all(bf16[4,2,36,1792]{3,1,2,0:T(2,128)(2,1)S(1)} %copy.33), channel_id=1, replica_groups=mesh['rep'=2,'ep'=4,'tp'=2,'sub'=2] {'ep'}, dimensions={0} | all-to-all | bytes 2064384 | tf_op jit(solution)/shard_map/all_to_all | solution.py:55
  58.2 1.1 reshape.67
  59.4 3.4 %fusion.4 = f32[288,512]{1,0:T(8,128)} fusion(bf16[288,1792]{1,0:T(8,128)(2,1)} %reshape.67, bf16[1,512,1792]{2,1,0:T(8,128)(2,1)} %param.17), kind=kOutput, calls=%fused_computation.7 | convolution fusion | flops 528482304 | bytes 3457024 | tf_op jit(solution)/shard_map/sd,fd->sf/dot_general | solution.py:57
  62.9 18.1 %all-reduce.5.cloned.1.call-done = f32[288,512]{1,0:T(8,128)} async-done(((f32[288,512]{1,0:T(8,128)}), f32[288,512]{1,0:T(8,128)}) %all-reduce.5.cloned.1.call-update) | async-done | bytes 589840 | tf_op jit(solution)/shard_map/psum | solution.py:58
  80.9 2.1 %fusion.2 = f32[288,1792]{1,0:T(8,128)S(1)} fusion(bf16[1,1792,512]{2,1,0:T(8,128)(2,1)S(1)} %copy-done, f32[288,512]{1,0:T(8,128)} %all-reduce.5.cloned.1.call-done, bf16[1,2,288,512]{3,2,1,0:T(8,128)(2,1)S(1)} %copy-done.6), kind=kOutput, calls=%fused_computation.5 | convolution fusion | flops 530251776 | bytes 5079040 | tf_op jit(solution)/shard_map/sf,df->sd/dot_general | solution.py:72
  83.1 1.8 %fusion = bf16[288,1792]{1,0:T(8,128)(2,1)} fusion(f32[288,1792]{1,0:T(8,128)S(1)} %fusion.2, bf16[1,1792,512]{2,1,0:T(8,128)(2,1)S(1)} %copy-done.5, f32[288,512]{1,0:T(8,128)S(1)} %copy-done.7, bf16[1,2,288,512]{3,2,1,0:T(8,128)(2,1)S(1)} %copy-done.6), kind=kOutput, calls=%fused_computation.2 | convolution fusion | flops 530546688 | bytes 5816320 | tf_op jit(solution)/shard_map/sf,df->sd/dot_general | solution.py:73
  84.9 1.3 reshape.68
  86.3 1.6 copy.35
  88.6 1.4 reduce
  90.7 3.4 %all-to-all-start.2 = ((bf16[2,2,16384]{2,1,0:T(2,128)(2,1)}), bf16[2,2,16384]{2,1,0:T(2,128)(2,1)S(1)}, u32[]{:S(2)}, u32[]{:S(2)}) async-start(bf16[2,2,16384]{2,1,0:T(2,128)(2,1)} %reshape.82), calls=%async_computation.2 | async-start | bytes 262144 | tf_op jit(solution)/shard_map/all_to_all | solution.py:28
  94.7 35.6 %all-reduce.7.cloned.1.call-done = bf16[4,2,36,1792]{3,0,2,1:T(4,128)(2,1)} async-done(((bf16[4,2,36,1792]{3,0,2,1:T(4,128)(2,1)}), bf16[4,2,36,1792]{3,0,2,1:T(4,128)(2,1)}) %all-reduce.7.cloned.1.call-update) | async-done | bytes 1032208
  130.3 1.9 %constant_dynamic-slice_fusion = bf16[4,1,36,1792]{3,0,2,1:T(4,128)(2,1)S(1)} fusion(bf16[4,2,36,1792]{3,0,2,1:T(4,128)(2,1)} %all-reduce.7.cloned.1.call-done, u32[]{:T(128)} %bitcast.14), kind=kLoop, calls=%fused_computation.53 | loop fusion | bytes 1032196
  132.1 0.9 copy.36
  133.0 4.6 %all-to-all-start.1 = ((bf16[4,1,36,1792]{3,2,1,0:T(8,128)(2,1)}), bf16[4,1,36,1792]{3,2,1,0:T(8,128)(2,1)S(1)}, u32[]{:S(2)}, u32[]{:S(2)}) async-start(bf16[4,1,36,1792]{3,2,1,0:T(8,128)(2,1)} %copy.36), calls=%async_computation.1 | async-start | bytes 1146880 | tf_op jit(solution)/shard_map/all_to_all | solution.py:82
  137.9 2.5 %all-reduce.1 = (f32[128]{0:T(128)S(1)}, f32[128]{0:T(128)S(1)}) all-reduce(f32[128]{0:T(128)S(1)} %get-tuple-element.3, f32[128]{0:T(128)S(1)} %get-tuple-element.2), channel_id=1, replica_groups=mesh['rep'=2,'ep'=4,'tp'=2,'sub'=2] {'sub'}, use_global_device_ids=true, to_apply=%region_8.9 | all-reduce | flops 256 | bytes 2048 | tf_op jit(solution)/shard_map/psum | solution.py:58
  140.4 0.8 fusion.31
  141.2 12.0 %all-to-all-done.1 = bf16[4,1,36,1792]{3,2,1,0:T(8,128)(2,1)S(1)} async-done(((bf16[4,1,36,1792]{3,2,1,0:T(8,128)(2,1)}), bf16[4,1,36,1792]{3,2,1,0:T(8,128)(2,1)S(1)}, u32[]{:S(2)}, u32[]{:S(2)}) %all-to-all-start.1) | async-done | bytes 516128 | tf_op jit(solution)/shard_map/all_to_all | solution.py:82
  153.3 0.9 gather_fusion
  154.2 0.9 broadcast_select_fusion
  (42 shorter events, 4.9 us)
Async XLA Ops:
  7.2 73.8 %copy-start = (bf16[1,1792,512]{2,1,0:T(8,128)(2,1)S(1)}, bf16[1,1792,512]{2,1,0:T(8,128)(2,1)}, u32[]{:S(2)}) copy-start(bf16[1,1792,512]{2,1,0:T(8,128)(2,1)} %param.15) | copy-start | bytes 5505028
  7.2 73.8 %all-reduce.5.cloned.1.call-start = ((), (), s32[]{:S(2)}) async-start(), calls=%async_computation.3 | async-start | bytes 1179648 | tf_op jit(solution)/shard_map/psum | solution.py:58
  59.4 21.6 %copy-start.6 = (bf16[1,2,288,512]{3,2,1,0:T(8,128)(2,1)S(1)}, bf16[1,2,288,512]{3,2,1,0:T(8,128)(2,1)}, u32[]{:S(2)}) copy-start(bf16[1,2,288,512]{3,2,1,0:T(8,128)(2,1)} %param.18) | copy-start | bytes 1769476
  62.8 67.4 %all-reduce.7.cloned.1.call-start = ((), (), s32[]{:S(2)}) async-start(), calls=%async_computation.4 | async-start | bytes 2064384
  80.9 2.1 %copy-start.5 = (bf16[1,1792,512]{2,1,0:T(8,128)(2,1)S(1)}, bf16[1,1792,512]{2,1,0:T(8,128)(2,1)}, u32[]{:S(2)}) copy-start(bf16[1,1792,512]{2,1,0:T(8,128)(2,1)} %param.16) | copy-start | bytes 5505028
  80.9 2.1 %copy-start.7 = (f32[288,512]{1,0:T(8,128)S(1)}, f32[288,512]{1,0:T(8,128)}, u32[]{:S(2)}) copy-start(f32[288,512]{1,0:T(8,128)} %all-reduce.5.cloned.1.call-done) | copy-start | bytes 1769476
  86.2 1.6 copy-start.2
  86.2 7.9 %copy-start.8 = (u32[32]{0:T(128)S(1)}, u32[32]{0:T(128)}, u32[]{:S(2)}) copy-start(u32[32]{0:T(128)} %constant.41) | copy-start | bytes 388
  86.2 8.4 %copy-start.3 = (s32[128,1]{0,1:T(1,128)S(1)}, s32[128,1]{0,1:T(1,128)}, u32[]{:S(2)}) copy-start(s32[128,1]{0,1:T(1,128)} %param.13) | copy-start | bytes 1540
  90.7 42.3 %all-to-all-start.2 = ((bf16[2,2,16384]{2,1,0:T(2,128)(2,1)}), bf16[2,2,16384]{2,1,0:T(2,128)(2,1)S(1)}, u32[]{:S(2)}, u32[]{:S(2)}) async-start(bf16[2,2,16384]{2,1,0:T(2,128)(2,1)} %reshape.82), calls=%async_computation.2 | async-start | bytes 262144 | tf_op jit(solution)/shard_map/all_to_all | solution.py:28
  132.1 5.7 %copy-start.1 = (bf16[128,256]{1,0:T(8,128)(2,1)S(1)}, bf16[128,256]{1,0:T(8,128)(2,1)}, u32[]{:S(2)}) copy-start(bf16[128,256]{1,0:T(8,128)(2,1)} %param.20) | copy-start | bytes 196612
  132.1 5.7 %copy-start.4 = (f32[256]{0:T(256)S(1)}, f32[256]{0:T(256)}, u32[]{:S(2)}) copy-start(f32[256]{0:T(256)} %param.21) | copy-start | bytes 3076
  133.0 20.1 %all-to-all-start.1 = ((bf16[4,1,36,1792]{3,2,1,0:T(8,128)(2,1)}), bf16[4,1,36,1792]{3,2,1,0:T(8,128)(2,1)S(1)}, u32[]{:S(2)}, u32[]{:S(2)}) async-start(bf16[4,1,36,1792]{3,2,1,0:T(8,128)(2,1)} %copy.36), calls=%async_computation.1 | async-start | bytes 1146880 | tf_op jit(solution)/shard_map/all_to_all | solution.py:82
Sparse Core Ops, SparseCore 0:
  62.9 17.9 all-reduce.4
  88.0 42.2 all-reduce.6
where the time goes:
time: 162 us
  waiting for transfers between devices  65.7 us (41%)
  blocking collectives  47.3 us (29%)
  between operations  14.3 us (9%)
  local copies, waits for them, and re-layouts  12.6 us (8%)
  starting transfers between devices  8.06 us (5%)
  matrix products  7.66 us (5%)
  other arithmetic  6.47 us (4%)
    unnamed x3, waiting for transfers between devices  35.6 us
    all_to_all x1, blocking collectives, local(): lax.all_to_all(grouped, 'ep', split_axis=0, concat_axis=0, tiled=True)  29.4 us
    psum x1, waiting for transfers between devices, local(): lax.psum((hidden_part, jnp.sum(values * values, axis=1), jnp.sum(gained *...  18.1 us
    all_gather x1, blocking collectives, local(): lax.all_gather(packed.reshape(wide_count, 1, most_rows, half_width), 'tp'...  15.4 us
    all_to_all x1, waiting for transfers between devices, local(): lax.all_to_all(summed, 'ep', split_axis=0, concat_axis=0, tiled=True)  12 us
    unnamed x25, local copies, waits for them, and re-layouts  5.45 us
    all_to_all x1, starting transfers between devices, local(): lax.all_to_all(summed, 'ep', split_axis=0, concat_axis=0, tiled=True)  4.6 us
    dot_general x1, matrix products, local(): jnp.einsum('sd,fd->sf', received, w_down[0], preferred_element_type=jnp.f...  3.43 us
  transfers between devices with their start and end apart: 4, of which 3 were waited for; matrix products, arithmetic and copies ran while one was open for 4% of the time, Pallas kernels for 0%

commit v1 on v0

v1 whole, which is shorter than its diff:
```python
import functools

import jax
import jax.numpy as jnp
from jax import lax
from jax.experimental import pallas as pl
from jax.experimental.pallas import tpu as pltpu
from jax.sharding import PartitionSpec as P

LAT = 512
NT = (((1,), (1,)), ((), ()))
TN = (((0,), (0,)), ((), ()))
VMEM = pl.BlockSpec(memory_space=pltpu.VMEM)
VMEM_LIMIT = 32 * 1024 * 1024


def dot(a, b, dims, precision=None):
    return lax.dot_general(a, b, dims, precision=precision, preferred_element_type=jnp.float32)


def swap(value, axis, step):
    count = lax.axis_size(axis)
    return lax.ppermute(value, axis, [(i, i ^ step) for i in range(count)])


def call(kernel, outs, *args, flops=0, name=None):
    read = sum(a.size * a.dtype.itemsize for a in args)
    written = sum(o.size * o.dtype.itemsize for o in outs)
    return pl.pallas_call(
        kernel,
        out_shape=outs,
        in_specs=[VMEM] * len(args),
        out_specs=[VMEM] * len(outs),
        compiler_params=pltpu.CompilerParams(vmem_limit_bytes=VMEM_LIMIT),
        cost_estimate=pl.CostEstimate(flops=flops, bytes_accessed=read + written, transcendentals=0),
        name=name,
    )(*args)


def pack_kernel(wide, most, ids_ref, weights_ref, scales_ref, grad_ref, *outs):
    blocks, place_ref = outs[:-1], outs[-1]
    tokens, width = grad_ref.shape
    half, scale_half = width // 2, scales_ref.shape[0] // 2
    rows = blocks[0].shape[0]
    me = lax.axis_index("ep")
    ids = ids_ref[...]
    expert = lax.broadcasted_iota(jnp.int32, (max(8, wide), tokens), 0)
    named = expert == ids
    before = lax.broadcasted_iota(jnp.int32, (tokens, tokens), 0) < lax.broadcasted_iota(
        jnp.int32, (tokens, tokens), 1
    )
    earlier = jnp.dot(
        named.astype(jnp.bfloat16), before.astype(jnp.bfloat16), preferred_element_type=jnp.float32
    )
    position = jnp.sum(jnp.where(named, earlier, 0.0), axis=0, keepdims=True).astype(jnp.int32)
    row = lax.broadcasted_iota(jnp.int32, (rows, tokens), 0)
    for k in range(wide):
        local = jnp.where(ids == (me ^ k), position, -2 * rows)
        low, high = row == local, row - most == local
        low_place, high_place = low.astype(jnp.bfloat16), high.astype(jnp.bfloat16)
        place_ref[0, k] = low_place
        place_ref[1, k] = high_place
        placed = jnp.dot(low_place, grad_ref[:, :half], preferred_element_type=jnp.float32)
        placed += jnp.dot(high_place, grad_ref[:, half:], preferred_element_type=jnp.float32)
        scale = dot(low.astype(jnp.float32), scales_ref[:scale_half], NT, lax.Precision.HIGHEST)
        scale += dot(high.astype(jnp.float32), scales_ref[scale_half:], NT, lax.Precision.HIGHEST)
        weight = jnp.sum(jnp.where(low | high, weights_ref[...], 0.0), axis=1, keepdims=True)
        for b in range(scale_half):
            part = slice(b * 128, (b + 1) * 128)
            blocks[k][:, part] = (placed[:, part] * scale[:, b : b + 1] * weight).astype(
                jnp.bfloat16
            )


def hidden_kernel(most, narrow, *refs):
    blocks, (down_ref, sum_ref, sent_ref) = refs[:-3], refs[-3:]
    half = down_ref.shape[1] // 2
    values = [b[...].astype(jnp.float32) for b in blocks]
    low = jnp.concatenate([v[:most] for v in values], axis=0).astype(jnp.bfloat16)
    high = jnp.concatenate([v[most : 2 * most] for v in values], axis=0).astype(jnp.bfloat16)
    total = dot(low, down_ref[:, :half], NT) + dot(high, down_ref[:, half:], NT)
    sum_ref[...] = total
    sent_ref[...] = total.astype(jnp.bfloat16)


def back_kernel(most, sum_ref, other_ref, pre_ref, gate_ref, up_ref, *outs):
    half = gate_ref.shape[0] // 2
    hidden = sum_ref[...] + other_ref[...].astype(jnp.float32)
    gate_pre = pre_ref[0].astype(jnp.float32)
    up_pre = pre_ref[1].astype(jnp.float32)
    sig = 1.0 / (1.0 + jnp.exp(-gate_pre))
    up_grad = (hidden * gate_pre * sig).astype(jnp.bfloat16)
    gate_grad = (hidden * up_pre * sig * (1.0 + gate_pre * (1.0 - sig))).astype(jnp.bfloat16)
    low = dot(gate_grad, gate_ref[:half], NT) + dot(up_grad, up_ref[:half], NT)
    high = dot(gate_grad, gate_ref[half:], NT) + dot(up_grad, up_ref[half:], NT)
    for i, out in enumerate(outs):
        part = slice(i * most, (i + 1) * most)
        pieces = [low[part], high[part]]
        spare = out.shape[0] - 2 * most
        if spare:
            pieces.append(jnp.zeros((spare, half), jnp.float32))
        out[...] = jnp.concatenate(pieces, axis=0).astype(jnp.bfloat16)


def unpack_kernel(wide, place_ref, *refs):
    blocks, out_ref = refs[:-1], refs[-1]
    half = out_ref.shape[1] // 2
    for side in range(2):
        total = None
        for k in range(wide):
            if k == 0:
                rows = blocks[0][...].astype(jnp.float32)
                for other in blocks[wide:]:
                    rows += other[...].astype(jnp.float32)
                rows = rows.astype(jnp.bfloat16)
            else:
                rows = blocks[k][...]
            term = dot(place_ref[side, k], rows, TN)
            total = term if total is None else total + term
        out_ref[:, side * half : (side + 1) * half] = total.astype(jnp.bfloat16)


def local(
    grad_values,
    grad_scales,
    expert_ids,
    route_weights,
    w_gate,
    w_up,
    w_down,
    pre_acts,
    latent_partials,
    latent,
    latent_gain,
):
    wide, narrow = lax.axis_size("ep"), lax.axis_size("tp")
    me, lane = lax.axis_index("ep"), lax.axis_index("tp")
    tokens, width = grad_values.shape
    half = width // 2
    slots, hidden_width = pre_acts.shape[2:]
    most = slots // (wide * narrow)
    rows = -(-2 * most // 8) * 8
    f32, bf16 = jnp.float32, jnp.bfloat16
    block = jax.ShapeDtypeStruct((rows, half), bf16)

    packed = call(
        functools.partial(pack_kernel, wide, most),
        [block] * wide + [jax.ShapeDtypeStruct((2, wide, rows, tokens), bf16)],
        expert_ids.reshape(1, tokens),
        route_weights.reshape(1, tokens),
        grad_scales.T,
        grad_values,
        name="pack",
    )
    place = packed[wide]
    order = list(range(wide - 1, 0, -1))
    arrived = {0: packed[0]}
    for k in order:
        arrived[k] = swap(packed[k], "ep", k)

    share = tokens
    partials = latent_partials.reshape(narrow, share, latent_partials.shape[2])
    own_grad = lax.dynamic_index_in_dim(partials, lane, 0, keepdims=False).astype(f32)
    for j in range(1, narrow):
        own_grad += swap(
            lax.dynamic_index_in_dim(partials, lane ^ j, 0, keepdims=False), "tp", j
        ).astype(f32)

    values = latent.astype(f32)
    gained = own_grad * latent_gain[None, :]
    sums = jnp.stack([jnp.sum(values * values, axis=1), jnp.sum(gained * values, axis=1)])
    for step in range(1, lax.axis_size("sub")):
        sums = sums + swap(sums, "sub", step)
    inverse_rms = lax.rsqrt(sums[0] / LAT + 1e-06)[:, None]
    d_latent = (inverse_rms * gained - values * inverse_rms**3 * sums[1][:, None] / LAT).astype(
        bf16
    )

    groups = [list(range(i, min(i + 4, wide))) for i in range(0, wide, 4)]
    returned = {}
    own = []
    for group in groups:
        taken = []
        for k in group:
            taken += [arrived[k]] + [swap(arrived[k], "tp", j) for j in range(1, narrow)]
        count = len(group) * narrow * most
        summed, sent = call(
            functools.partial(hidden_kernel, most, narrow),
            [
                jax.ShapeDtypeStruct((count, hidden_width), f32),
                jax.ShapeDtypeStruct((count, hidden_width), bf16),
            ],
            *taken,
            w_down[0],
            flops=2 * count * width * hidden_width,
            name="hidden",
        )
        received = swap(sent, "sub", 1)
        pre = jnp.concatenate(
            [
                lax.dynamic_slice_in_dim(
                    pre_acts[0], ((me ^ k) * narrow + (lane ^ j)) * most, most, axis=1
                )
                for k in group
                for j in range(narrow)
            ],
            axis=1,
        )
        products = call(
            functools.partial(back_kernel, most),
            [block] * (len(group) * narrow),
            summed,
            received,
            pre,
            w_gate[0],
            w_up[0],
            flops=4 * count * width * hidden_width,
            name="back",
        )
        for at, k in enumerate(group):
            mine = products[at * narrow]
            others = [swap(products[at * narrow + j], "tp", j) for j in range(1, narrow)]
            if k == 0:
                returned[0] = mine
                own = others
            else:
                total = mine.astype(f32)
                for other in others:
                    total += other.astype(f32)
                returned[k] = swap(total.astype(bf16), "ep", k)
    (grad_input,) = call(
        functools.partial(unpack_kernel, wide),
        [jax.ShapeDtypeStruct((tokens, width), bf16)],
        place,
        *[returned[k] for k in range(wide)],
        *own,
        name="unpack",
    )
    return (grad_input, d_latent)


def solution(mesh):
    placed = (
        P(("rep", "ep", "tp"), "sub"),
        P(("rep", "ep", "tp"), "sub"),
        P(("rep", "ep", "tp"), None),
        P(("rep", "ep", "tp"), None),
        P("ep", "sub", "tp"),
        P("ep", "sub", "tp"),
        P("ep", "tp", "sub"),
        P(("rep", "ep"), None, None, "tp"),
        P("tp", ("rep", "ep"), "sub"),
        P(("rep", "ep", "tp"), "sub"),
        P("sub"),
    )
    return jax.shard_map(
        local,
        mesh=mesh,
        in_specs=placed,
        out_specs=(P(("rep", "ep", "tp"), "sub"), P(("rep", "ep", "tp"), "sub")),
        check_vma=False,
    )
```

time: 162 us -> 62.5 us (0.39)
  waiting for transfers between devices: 65.7 us -> 15.7 us
  blocking collectives: 47.3 us -> 0 us
  starting transfers between devices: 8.06 us -> 21.7 us
  between operations: 14.3 us -> 0.77 us
  matrix products: 7.66 us -> 0 us
  Pallas kernels: 0 us -> 5.31 us
  other arithmetic: 6.47 us -> 2.72 us
  local copies, waits for them, and re-layouts: 12.6 us -> 15.6 us
    unnamed x3 -> x0, waiting for transfers between devices: 35.6 us -> none
    all_to_all x1 -> x0, blocking collectives: 29.4 us -> none  [local(): lax.all_to_all(grouped, 'ep', split_axis=0, concat_axis=0, tiled=True)]
    ppermute x0 -> x17, starting transfers between devices: none -> 21.7 us  [swap(): return lax.ppermute(value, axis, [(i, i ^ step) for i in range(count)])]
    psum x1 -> x0, waiting for transfers between devices: 18.1 us -> none  [local(): lax.psum((hidden_part, jnp.sum(values * values, axis=1), jnp.sum(gained *...]
    ppermute x0 -> x17, waiting for transfers between devices: none -> 15.7 us  [swap(): return lax.ppermute(value, axis, [(i, i ^ step) for i in range(count)])]
    all_gather x1 -> x0, blocking collectives: 15.4 us -> none  [local(): lax.all_gather(packed.reshape(wide_count, 1, most_rows, half_width), 'tp'...]
    all_to_all x2 -> x0, waiting for transfers between devices: 12 us -> none  [the longest x1 12 us: local(): lax.all_to_all(summed, 'ep', split_axis=0, concat_axis=0, tiled=True)]
    all_to_all x2 -> x0, starting transfers between devices: 7.98 us -> none  [the longest x1 4.6 us: local(): lax.all_to_all(summed, 'ep', split_axis=0, concat_axis=0, tiled=True)]
  transfers between devices with their start and end apart: 4 -> 17, of which waited for: 3 -> 8; matrix products, arithmetic and copies ran while one was open for 4% -> 22% of each run, Pallas kernels for 0% -> 1%
where the time goes in v1:
time: 62.5 us; the launch traced here: 61.7 us
  starting transfers between devices  21.7 us (35%)
  waiting for transfers between devices  15.7 us (25%)
  local copies, waits for them, and re-layouts  15.6 us (25%)
  Pallas kernels  5.31 us (8%)
  other arithmetic  2.72 us (4%)
  between operations  0.77 us (1%)
    ppermute x17, starting transfers between devices, swap(): return lax.ppermute(value, axis, [(i, i ^ step) for i in range(count)])  21.7 us
    ppermute x17, waiting for transfers between devices, swap(): return lax.ppermute(value, axis, [(i, i ^ step) for i in range(count)])  15.7 us
    concatenate x1, local copies, waits for them, and re-layouts, local(): jnp.concatenate([lax.dynamic_slice_in_dim(pre_acts[0], ((me ^ k) * narrow...  7.31 us
    pallas_call x4, Pallas kernels, call(): pl.pallas_call(kernel, out_shape=outs, in_specs=[VMEM] * len(args), out_s...  5.31 us
    unnamed x20, local copies, waits for them, and re-layouts  4.67 us
    dynamic_slice x1, local copies, waits for them, and re-layouts, local(): lax.dynamic_slice_in_dim(pre_acts[0], ((me ^ k) * narrow + (lane ^ j)) *...  2.14 us
    convert_element_type x1, other arithmetic, local(): (inverse_rms * gained - values * inverse_rms ** 3 * sums[1][:, None] / LA...  1.59 us
    squeeze x1, local copies, waits for them, and re-layouts, local(): lax.dynamic_index_in_dim(partials, lane ^ j, 0, keepdims=False)  1.47 us
  transfers between devices with their start and end apart: 17, of which 8 were waited for; matrix products, arithmetic and copies ran while one was open for 22% of the time, Pallas kernels for 1%

profile of v1, /device:TPU:0, one launch (start us, length us, event | category | flops | bytes accessed | tf_op | source)
XLA Modules:
  0.0 61.7 jit_solution(971575874752081457)
XLA Ops:
  3.8 1.6 %pack.1 = (bf16[72,896]{1,0:T(8,128)(2,1)S(1)}, bf16[72,896]{1,0:T(8,128)(2,1)}, bf16[72,896]{1,0:T(8,128)(2,1)S(1)}, bf16[72,896]{1,0:T(8,128)(2,1)S(1)}, bf16[2,4,72,128]{3,2,1,0:T(8,128)(2,1)S(1)}) custom-call(s32[1,128]{1,0:T(1,128)S(1)} %bitcast.40, f32[1,128]{1,0:T(1,128)S(1)} %bitcast.41, f32[14,128]{1,0:T(8,128)S(1)} %bitcast.39, ...), custom_call_target="tpu_custom_call" | custom-call | bytes 1130496 | tf_op jit(solution)/shard_map/pack/pallas_call | solution.py:29
  5.4 2.9 %collective-permute-start = (bf16[72,896]{1,0:T(8,128)(2,1)S(1)}, bf16[72,896]{1,0:T(8,128)(2,1)S(1)}, u32[]{:S(2)}, u32[]{:S(2)}) collective-permute-start(bf16[72,896]{1,0:T(8,128)(2,1)S(1)} %get-tuple-element.18.refs_0_), channel_id=1, source_target_pairs={{0,2},{2,0},{1,3},{3,1},{4,6},{6,4},{5,7},{7,5},{8,10},{10,8},{9,1... | collective-permute-start | bytes 387080 | tf_op jit(solution)/shard_map/ppermute | solution.py:23
  8.4 1.6 %collective-permute-start.1 = (bf16[72,896]{1,0:T(8,128)(2,1)}, bf16[72,896]{1,0:T(8,128)(2,1)S(1)}, u32[]{:S(2)}, u32[]{:S(2)}) collective-permute-start(bf16[72,896]{1,0:T(8,128)(2,1)} %get-tuple-element.19), channel_id=1, source_target_pairs={{0,4},{4,0},{8,12},{12,8},{1,5},{5,1},{9,13},{13,9},{2,6},{6,2},{1... | collective-permute-start | bytes 387080 | tf_op jit(solution)/shard_map/ppermute | solution.py:23
  9.9 2.6 %collective-permute-start.3 = (bf16[72,896]{1,0:T(8,128)(2,1)S(1)}, bf16[72,896]{1,0:T(8,128)(2,1)S(1)}, u32[]{:S(2)}, u32[]{:S(2)}) collective-permute-start(bf16[72,896]{1,0:T(8,128)(2,1)S(1)} %get-tuple-element.20), channel_id=1, source_target_pairs={{0,8},{4,12},{8,0},{12,4},{1,9},{5,13},{9,1},{13,5},{2,10},{6,14},... | collective-permute-start | bytes 387080 | tf_op jit(solution)/shard_map/ppermute | solution.py:23
  12.7 1.5 %dynamic-slice_bitcast_fusion.8 = bf16[128,256]{1,0:T(8,128)(2,1)} fusion(bf16[2,128,256]{2,1,0:T(8,128)(2,1)} %bitcast.42, s32[]{:T(128)S(6)} %select_n.40), kind=kLoop, calls=%fused_computation.22 | loop fusion | bytes 131076 | tf_op jit(solution)/shard_map/jit(dynamic_index_in_dim)/squeeze | solution.py:166
  14.5 2.1 %dynamic-slice_bitcast_fusion = (bf16[2,36,512]{2,1,0:T(8,128)(2,1)}, bf16[2,36,512]{2,1,0:T(8,128)(2,1)}, bf16[2,36,512]{2,1,0:T(8,128)(2,1)}, bf16[2,36,512]{2...) fusion(bf16[1,2,288,512]{3,2,1,0:T(8,128)(2,1)} %param.18, ...), kind=kLoop, calls=%fused_computation.14 | loop fusion | bytes 1179680 | tf_op jit(solution)/shard_map/dynamic_slice | solution.py:201
  16.7 7.3 %concatenate.3.pre_ref = bf16[2,288,512]{2,1,0:T(8,128)(2,1)S(1)} concatenate(bf16[2,36,512]{2,1,0:T(8,128)(2,1)} %get-tuple-element.42, bf16[2,36,512]{2,1,0:T(8,128)(2,1)} %get-tuple-element.41, bf16[2,36,512]{2,1,0:T(8,128)(2,1)} %get-tuple-element.40, bf16[2,36,512]{2,1,0:T(8,128)(2,1)} %get-tuple-element.39, bf16[2,36,512]{2,1,0:T(8,128)(2,1)} %get-tuple-element.38, ...), dimensions={1} | concatenate | bytes 1179648 | tf_op jit(solution)/shard_map/concatenate | solution.py:199
  24.0 1.8 %collective-permute-start.2 = (bf16[72,896]{1,0:T(8,128)(2,1)S(1)}, bf16[72,896]{1,0:T(8,128)(2,1)S(1)}, u32[]{:S(2)}, u32[]{:S(2)}) collective-permute-start(bf16[72,896]{1,0:T(8,128)(2,1)S(1)} %collective-permute-done.1.refs_2_), channel_id=1, source_target_pairs={{0,2},{2,0},{1,3},{3,1},{4,6},{6,4},{5,7},{7,5},{8,10},{10,8},{9,1... | collective-permute-start | bytes 387080 | tf_op jit(solution)/shard_map/ppermute | solution.py:23
  26.1 1.7 %collective-permute-start.6 = (bf16[72,896]{1,0:T(8,128)(2,1)S(1)}, bf16[72,896]{1,0:T(8,128)(2,1)S(1)}, u32[]{:S(2)}, u32[]{:S(2)}) collective-permute-start(bf16[72,896]{1,0:T(8,128)(2,1)S(1)} %collective-permute-done.5.refs_6_), channel_id=1, source_target_pairs={{0,2},{2,0},{1,3},{3,1},{4,6},{6,4},{5,7},{7,5},{8,10},{10,8},{9,1... | collective-permute-start | bytes 387080 | tf_op jit(solution)/shard_map/ppermute | solution.py:23
  29.0 1.5 %collective-permute-done.2.refs_3_ = bf16[72,896]{1,0:T(8,128)(2,1)S(1)} collective-permute-done((bf16[72,896]{1,0:T(8,128)(2,1)S(1)}, bf16[72,896]{1,0:T(8,128)(2,1)S(1)}, u32[]{:S(2)}, u32[]{:S(2)}) %collective-permute-start.2) | collective-permute-done | bytes 129056 | tf_op jit(solution)/shard_map/ppermute | solution.py:23
  30.5 1.8 %collective-permute-done.4.refs_5_ = bf16[72,896]{1,0:T(8,128)(2,1)S(1)} collective-permute-done((bf16[72,896]{1,0:T(8,128)(2,1)S(1)}, bf16[72,896]{1,0:T(8,128)(2,1)S(1)}, u32[]{:S(2)}, u32[]{:S(2)}) %collective-permute-start.4) | collective-permute-done | bytes 129056 | tf_op jit(solution)/shard_map/ppermute | solution.py:23
  32.3 1.4 %collective-permute-done.6.refs_7_ = bf16[72,896]{1,0:T(8,128)(2,1)S(1)} collective-permute-done((bf16[72,896]{1,0:T(8,128)(2,1)S(1)}, bf16[72,896]{1,0:T(8,128)(2,1)S(1)}, u32[]{:S(2)}, u32[]{:S(2)}) %collective-permute-start.6) | collective-permute-done | bytes 129056 | tf_op jit(solution)/shard_map/ppermute | solution.py:23
  34.6 1.5 %collective-permute-done.7.other_ref = bf16[288,512]{1,0:T(8,128)(2,1)S(1)} collective-permute-done((bf16[288,512]{1,0:T(8,128)(2,1)S(1)}, bf16[288,512]{1,0:T(8,128)(2,1)S(1)}, u32[]{:S(2)}, u32[]{:S(2)}) %collective-permute-start.7) | collective-permute-done | bytes 294944 | tf_op jit(solution)/shard_map/ppermute | solution.py:23
  36.2 1.5 %copy-done.2 = bf16[1,1792,512]{2,1,0:T(8,128)(2,1)S(1)} copy-done((bf16[1,1792,512]{2,1,0:T(8,128)(2,1)S(1)}, bf16[1,1792,512]{2,1,0:T(8,128)(2,1)}, u32[]{:S(2)}) %copy-start.2) | copy-done | bytes 1835032
  37.7 1.4 %back.1 = (bf16[72,896]{1,0:T(8,128)(2,1)S(1)}, bf16[72,896]{1,0:T(8,128)(2,1)S(1)}, bf16[72,896]{1,0:T(8,128)(2,1)S(1)}, bf16[72,896]{1,0:T(8,128)(2,1)S(1)}, b...) custom-call(f32[288,512]{1,0:T(8,128)S(1)} %get-tuple-element.22.sum, ...), custom_call_target="tpu_custom_call" | custom-call | flops 1056964608 | bytes 6176768 | tf_op jit(solution)/shard_map/back/pallas_call | solution.py:29
  39.1 1.6 %collective-permute-start.8 = (bf16[72,896]{1,0:T(8,128)(2,1)S(1)}, bf16[72,896]{1,0:T(8,128)(2,1)S(1)}, u32[]{:S(2)}, u32[]{:S(2)}) collective-permute-start(bf16[72,896]{1,0:T(8,128)(2,1)S(1)} %get-tuple-element.26), channel_id=1, source_target_pairs={{0,2},{2,0},{1,3},{3,1},{4,6},{6,4},{5,7},{7,5},{8,10},{10,8},{9,1... | collective-permute-start | bytes 387080 | tf_op jit(solution)/shard_map/ppermute | solution.py:23
  41.2 1.5 %collective-permute-start.12 = (bf16[72,896]{1,0:T(8,128)(2,1)S(1)}, bf16[72,896]{1,0:T(8,128)(2,1)S(1)}, u32[]{:S(2)}, u32[]{:S(2)}) collective-permute-start(bf16[72,896]{1,0:T(8,128)(2,1)S(1)} %get-tuple-element.30), channel_id=1, source_target_pairs={{0,2},{2,0},{1,3},{3,1},{4,6},{6,4},{5,7},{7,5},{8,10},{10,8},{9,1... | collective-permute-start | bytes 387080 | tf_op jit(solution)/shard_map/ppermute | solution.py:23
  43.2 2.2 %collective-permute-done.8 = bf16[72,896]{1,0:T(8,128)(2,1)S(1)} collective-permute-done((bf16[72,896]{1,0:T(8,128)(2,1)S(1)}, bf16[72,896]{1,0:T(8,128)(2,1)S(1)}, u32[]{:S(2)}, u32[]{:S(2)}) %collective-permute-start.8) | collective-permute-done | bytes 129056 | tf_op jit(solution)/shard_map/ppermute | solution.py:23
  46.2 2.1 %collective-permute-done.10 = bf16[72,896]{1,0:T(8,128)(2,1)S(1)} collective-permute-done((bf16[72,896]{1,0:T(8,128)(2,1)S(1)}, bf16[72,896]{1,0:T(8,128)(2,1)S(1)}, u32[]{:S(2)}, u32[]{:S(2)}) %collective-permute-start.10) | collective-permute-done | bytes 129056 | tf_op jit(solution)/shard_map/ppermute | solution.py:23
  48.3 1.7 %collective-permute-start.11 = (bf16[72,896]{1,0:T(8,128)(2,1)S(1)}, bf16[72,896]{1,0:T(8,128)(2,1)S(1)}, u32[]{:S(2)}, u32[]{:S(2)}) collective-permute-start(bf16[72,896]{1,0:T(8,128)(2,1)S(1)} %add_convert_fusion.1), channel_id=1, source_target_pairs={{0,8},{4,12},{8,0},{12,4},{1,9},{5,13},{9,1},{13,5},{2,10},{6,14},... | collective-permute-start | bytes 387080 | tf_op jit(solution)/shard_map/ppermute | solution.py:23
  51.1 3.6 %collective-permute-start.13 = (bf16[72,896]{1,0:T(8,128)(2,1)S(1)}, bf16[72,896]{1,0:T(8,128)(2,1)S(1)}, u32[]{:S(2)}, u32[]{:S(2)}) collective-permute-start(bf16[72,896]{1,0:T(8,128)(2,1)S(1)} %add_convert_fusion), channel_id=1, source_target_pairs={{0,12},{4,8},{8,4},{12,0},{1,13},{5,9},{9,5},{13,1},{2,14},{6,10},... | collective-permute-start | bytes 387080 | tf_op jit(solution)/shard_map/ppermute | solution.py:23
  54.7 1.6 %fusion.5 = bf16[128,256]{1,0:T(8,128)(2,1)} fusion(bf16[128,256]{1,0:T(8,128)(2,1)S(1)} %copy-done.8, bf16[128,256]{1,0:T(8,128)(2,1)} %collective-permute-done.15, f32[128]{0:T(128)S(1)} %slice_bitcast_fusion, f32[128]{0:T(128)S(1)} %get-tuple-element.34, f32[128]{0:T(128)S(1)} %get-tuple-element.35, f32[256]{0:T(256)S(1)} %copy-done.9, ...), kind=kLoop, calls=%fused_computation.11 | loop fusion | flops 360448 | bytes 264708 | tf_op jit(solution)/shard_map/convert_element_type | solution.py:175
  56.3 4.0 %collective-permute-done.11.refs_2_ = bf16[72,896]{1,0:T(8,128)(2,1)S(1)} collective-permute-done((bf16[72,896]{1,0:T(8,128)(2,1)S(1)}, bf16[72,896]{1,0:T(8,128)(2,1)S(1)}, u32[]{:S(2)}, u32[]{:S(2)}) %collective-permute-start.11) | collective-permute-done | bytes 129056 | tf_op jit(solution)/shard_map/ppermute | solution.py:23
  60.3 1.4 %unpack.1 = bf16[128,1792]{1,0:T(8,128)(2,1)} custom-call(bf16[2,4,72,128]{3,2,1,0:T(8,128)(2,1)S(1)} %get-tuple-element.17.place_ref, bf16[72,896]{1,0:T(8,128)(2,1)S(1)} %get-tuple-element.24.refs_0_, bf16[72,896]{1,0:T(8,128)(2,1)S(1)} %collective-permute-done.9.refs_1_, bf16[72,896]{1,0:T(8,128)(2,1)S(1)} %collective-permute-done.11.refs_2_, ...), custom_call_target="tpu_custom_call" | custom-call | bytes 1251328 | tf_op jit(solution)/shard_map/unpack/pallas_call | solution.py:29
  (46 shorter events, 8.9 us)
Async XLA Ops:
  0.6 33.1 %copy-start = (bf16[1,512,1792]{2,1,0:T(8,128)(2,1)S(1)}, bf16[1,512,1792]{2,1,0:T(8,128)(2,1)}, u32[]{:S(2)}) copy-start(bf16[1,512,1792]{2,1,0:T(8,128)(2,1)} %param.17) | copy-start | bytes 5505028
  0.6 1.2 %copy-start.3 = (bf16[128,1792]{1,0:T(8,128)(2,1)S(1)}, bf16[128,1792]{1,0:T(8,128)(2,1)}, u32[]{:S(2)}) copy-start(bf16[128,1792]{1,0:T(8,128)(2,1)} %grad_ref.1) | copy-start | bytes 1376260
  3.8 24.0 %copy-start.8 = (bf16[128,256]{1,0:T(8,128)(2,1)S(1)}, bf16[128,256]{1,0:T(8,128)(2,1)}, u32[]{:S(2)}) copy-start(bf16[128,256]{1,0:T(8,128)(2,1)} %param.20) | copy-start | bytes 196612
  5.4 23.5 %collective-permute-start = (bf16[72,896]{1,0:T(8,128)(2,1)S(1)}, bf16[72,896]{1,0:T(8,128)(2,1)S(1)}, u32[]{:S(2)}, u32[]{:S(2)}) collective-permute-start(bf16[72,896]{1,0:T(8,128)(2,1)S(1)} %get-tuple-element.18.refs_0_), channel_id=1, source_target_pairs={{0,2},{2,0},{1,3},{3,1},{4,6},{6,4},{5,7},{7,5},{8,10},{10,8},{9,1... | collective-permute-start | bytes 387080 | tf_op jit(solution)/shard_map/ppermute | solution.py:23
  8.4 15.7 %collective-permute-start.1 = (bf16[72,896]{1,0:T(8,128)(2,1)}, bf16[72,896]{1,0:T(8,128)(2,1)S(1)}, u32[]{:S(2)}, u32[]{:S(2)}) collective-permute-start(bf16[72,896]{1,0:T(8,128)(2,1)} %get-tuple-element.19), channel_id=1, source_target_pairs={{0,4},{4,0},{8,12},{12,8},{1,5},{5,1},{9,13},{13,9},{2,6},{6,2},{1... | collective-permute-start | bytes 387080 | tf_op jit(solution)/shard_map/ppermute | solution.py:23
  9.9 15.9 %collective-permute-start.3 = (bf16[72,896]{1,0:T(8,128)(2,1)S(1)}, bf16[72,896]{1,0:T(8,128)(2,1)S(1)}, u32[]{:S(2)}, u32[]{:S(2)}) collective-permute-start(bf16[72,896]{1,0:T(8,128)(2,1)S(1)} %get-tuple-element.20), channel_id=1, source_target_pairs={{0,8},{4,12},{8,0},{12,4},{1,9},{5,13},{9,1},{13,5},{2,10},{6,14},... | collective-permute-start | bytes 387080 | tf_op jit(solution)/shard_map/ppermute | solution.py:23
  12.5 13.6 %collective-permute-start.5 = (bf16[72,896]{1,0:T(8,128)(2,1)S(1)}, bf16[72,896]{1,0:T(8,128)(2,1)S(1)}, u32[]{:S(2)}, u32[]{:S(2)}) collective-permute-start(bf16[72,896]{1,0:T(8,128)(2,1)S(1)} %get-tuple-element.21), channel_id=1, source_target_pairs={{0,12},{4,8},{8,4},{12,0},{1,13},{5,9},{9,5},{13,1},{2,14},{6,10},... | collective-permute-start | bytes 387080 | tf_op jit(solution)/shard_map/ppermute | solution.py:23
  14.2 13.6 %collective-permute-start.15 = (bf16[128,256]{1,0:T(8,128)(2,1)}, bf16[128,256]{1,0:T(8,128)(2,1)}, u32[]{:S(2)}, u32[]{:S(2)}) collective-permute-start(bf16[128,256]{1,0:T(8,128)(2,1)} %dynamic-slice_bitcast_fusion.8), channel_id=1, source_target_pairs={{0,2},{2,0},{1,3},{3,1},{4,6},{6,4},{5,7},{7,5},{8,10},{10,8},{9,1... | collective-permute-start | bytes 196616 | tf_op jit(solution)/shard_map/ppermute | solution.py:23
  24.0 12.2 %copy-start.1 = (bf16[1,1792,512]{2,1,0:T(8,128)(2,1)S(1)}, bf16[1,1792,512]{2,1,0:T(8,128)(2,1)}, u32[]{:S(2)}) copy-start(bf16[1,1792,512]{2,1,0:T(8,128)(2,1)} %param.15) | copy-start | bytes 5505028
  24.0 6.5 %collective-permute-start.2 = (bf16[72,896]{1,0:T(8,128)(2,1)S(1)}, bf16[72,896]{1,0:T(8,128)(2,1)S(1)}, u32[]{:S(2)}, u32[]{:S(2)}) collective-permute-start(bf16[72,896]{1,0:T(8,128)(2,1)S(1)} %collective-permute-done.1.refs_2_), channel_id=1, source_target_pairs={{0,2},{2,0},{1,3},{3,1},{4,6},{6,4},{5,7},{7,5},{8,10},{10,8},{9,1... | collective-permute-start | bytes 387080 | tf_op jit(solution)/shard_map/ppermute | solution.py:23
  25.8 6.5 %collective-permute-start.4 = (bf16[72,896]{1,0:T(8,128)(2,1)S(1)}, bf16[72,896]{1,0:T(8,128)(2,1)S(1)}, u32[]{:S(2)}, u32[]{:S(2)}) collective-permute-start(bf16[72,896]{1,0:T(8,128)(2,1)S(1)} %collective-permute-done.3.refs_4_), channel_id=1, source_target_pairs={{0,2},{2,0},{1,3},{3,1},{4,6},{6,4},{5,7},{7,5},{8,10},{10,8},{9,1... | collective-permute-start | bytes 387080 | tf_op jit(solution)/shard_map/ppermute | solution.py:23
  26.1 7.6 %collective-permute-start.6 = (bf16[72,896]{1,0:T(8,128)(2,1)S(1)}, bf16[72,896]{1,0:T(8,128)(2,1)S(1)}, u32[]{:S(2)}, u32[]{:S(2)}) collective-permute-start(bf16[72,896]{1,0:T(8,128)(2,1)S(1)} %collective-permute-done.5.refs_6_), channel_id=1, source_target_pairs={{0,2},{2,0},{1,3},{3,1},{4,6},{6,4},{5,7},{7,5},{8,10},{10,8},{9,1... | collective-permute-start | bytes 387080 | tf_op jit(solution)/shard_map/ppermute | solution.py:23
  28.9 5.7 %collective-permute-start.16 = (f32[2,128]{1,0:T(2,128)S(1)}, f32[2,128]{1,0:T(2,128)S(1)}, u32[]{:S(2)}, u32[]{:S(2)}) collective-permute-start(f32[2,128]{1,0:T(2,128)S(1)} %pad_maximum_fusion), channel_id=1, source_target_pairs={{0,1},{1,0},{2,3},{3,2},{4,5},{5,4},{6,7},{7,6},{8,9},{9,8},{10,11... | collective-permute-start | bytes 3080 | tf_op jit(solution)/shard_map/ppermute | solution.py:23
  34.5 1.6 %collective-permute-start.7 = (bf16[288,512]{1,0:T(8,128)(2,1)S(1)}, bf16[288,512]{1,0:T(8,128)(2,1)S(1)}, u32[]{:S(2)}, u32[]{:S(2)}) collective-permute-start(bf16[288,512]{1,0:T(8,128)(2,1)S(1)} %get-tuple-element.23), channel_id=1, source_target_pairs={{0,1},{1,0},{2,3},{3,2},{4,5},{5,4},{6,7},{7,6},{8,9},{9,8},{10,11... | collective-permute-start | bytes 884744 | tf_op jit(solution)/shard_map/ppermute | solution.py:23
  36.2 1.5 %copy-start.2 = (bf16[1,1792,512]{2,1,0:T(8,128)(2,1)S(1)}, bf16[1,1792,512]{2,1,0:T(8,128)(2,1)}, u32[]{:S(2)}) copy-start(bf16[1,1792,512]{2,1,0:T(8,128)(2,1)} %param.16) | copy-start | bytes 5505028
  37.7 17.0 %copy-start.7 = (bf16[1,256,256]{2,1,0:T(8,128)(2,1)S(1)}, bf16[1,256,256]{2,1,0:T(8,128)(2,1)}, u32[]{:S(2)}) copy-start(bf16[1,256,256]{2,1,0:T(8,128)(2,1)} %param.19) | copy-start | bytes 393220
  37.7 17.0 %copy-start.9 = (f32[256]{0:T(256)S(1)}, f32[256]{0:T(256)}, u32[]{:S(2)}) copy-start(f32[256]{0:T(256)} %param.21) | copy-start | bytes 3076
  39.1 6.4 %collective-permute-start.8 = (bf16[72,896]{1,0:T(8,128)(2,1)S(1)}, bf16[72,896]{1,0:T(8,128)(2,1)S(1)}, u32[]{:S(2)}, u32[]{:S(2)}) collective-permute-start(bf16[72,896]{1,0:T(8,128)(2,1)S(1)} %get-tuple-element.26), channel_id=1, source_target_pairs={{0,2},{2,0},{1,3},{3,1},{4,6},{6,4},{5,7},{7,5},{8,10},{10,8},{9,1... | collective-permute-start | bytes 387080 | tf_op jit(solution)/shard_map/ppermute | solution.py:23
  40.7 7.6 %collective-permute-start.10 = (bf16[72,896]{1,0:T(8,128)(2,1)S(1)}, bf16[72,896]{1,0:T(8,128)(2,1)S(1)}, u32[]{:S(2)}, u32[]{:S(2)}) collective-permute-start(bf16[72,896]{1,0:T(8,128)(2,1)S(1)} %get-tuple-element.28), channel_id=1, source_target_pairs={{0,2},{2,0},{1,3},{3,1},{4,6},{6,4},{5,7},{7,5},{8,10},{10,8},{9,1... | collective-permute-start | bytes 387080 | tf_op jit(solution)/shard_map/ppermute | solution.py:23
  41.2 9.8 %collective-permute-start.12 = (bf16[72,896]{1,0:T(8,128)(2,1)S(1)}, bf16[72,896]{1,0:T(8,128)(2,1)S(1)}, u32[]{:S(2)}, u32[]{:S(2)}) collective-permute-start(bf16[72,896]{1,0:T(8,128)(2,1)S(1)} %get-tuple-element.30), channel_id=1, source_target_pairs={{0,2},{2,0},{1,3},{3,1},{4,6},{6,4},{5,7},{7,5},{8,10},{10,8},{9,1... | collective-permute-start | bytes 387080 | tf_op jit(solution)/shard_map/ppermute | solution.py:23
  42.7 13.5 %collective-permute-start.14 = (bf16[72,896]{1,0:T(8,128)(2,1)S(1)}, bf16[72,896]{1,0:T(8,128)(2,1)S(1)}, u32[]{:S(2)}, u32[]{:S(2)}) collective-permute-start(bf16[72,896]{1,0:T(8,128)(2,1)S(1)} %get-tuple-element.31), channel_id=1, source_target_pairs={{0,2},{2,0},{1,3},{3,1},{4,6},{6,4},{5,7},{7,5},{8,10},{10,8},{9,1... | collective-permute-start | bytes 387080 | tf_op jit(solution)/shard_map/ppermute | solution.py:23
  45.5 10.7 %collective-permute-start.9 = (bf16[72,896]{1,0:T(8,128)(2,1)S(1)}, bf16[72,896]{1,0:T(8,128)(2,1)S(1)}, u32[]{:S(2)}, u32[]{:S(2)}) collective-permute-start(bf16[72,896]{1,0:T(8,128)(2,1)S(1)} %add_convert_fusion.2), channel_id=1, source_target_pairs={{0,4},{4,0},{8,12},{12,8},{1,5},{5,1},{9,13},{13,9},{2,6},{6,2},{1... | collective-permute-start | bytes 387080 | tf_op jit(solution)/shard_map/ppermute | solution.py:23
  48.3 12.0 %collective-permute-start.11 = (bf16[72,896]{1,0:T(8,128)(2,1)S(1)}, bf16[72,896]{1,0:T(8,128)(2,1)S(1)}, u32[]{:S(2)}, u32[]{:S(2)}) collective-permute-start(bf16[72,896]{1,0:T(8,128)(2,1)S(1)} %add_convert_fusion.1), channel_id=1, source_target_pairs={{0,8},{4,12},{8,0},{12,4},{1,9},{5,13},{9,1},{13,5},{2,10},{6,14},... | collective-permute-start | bytes 387080 | tf_op jit(solution)/shard_map/ppermute | solution.py:23
  51.1 9.2 %collective-permute-start.13 = (bf16[72,896]{1,0:T(8,128)(2,1)S(1)}, bf16[72,896]{1,0:T(8,128)(2,1)S(1)}, u32[]{:S(2)}, u32[]{:S(2)}) collective-permute-start(bf16[72,896]{1,0:T(8,128)(2,1)S(1)} %add_convert_fusion), channel_id=1, source_target_pairs={{0,12},{4,8},{8,4},{12,0},{1,13},{5,9},{9,5},{13,1},{2,14},{6,10},... | collective-permute-start | bytes 387080 | tf_op jit(solution)/shard_map/ppermute | solution.py:23
  (3 other events, 2.0 us)

commit v2 on v1

v2 whole, which is shorter than its diff:
```python
import functools

import jax
import jax.numpy as jnp
from jax import lax
from jax.experimental import pallas as pl
from jax.experimental.pallas import tpu as pltpu
from jax.sharding import PartitionSpec as P

LAT = 512
NT = (((1,), (1,)), ((), ()))
TN = (((0,), (0,)), ((), ()))
VMEM = pl.BlockSpec(memory_space=pltpu.VMEM)
ANY = pl.BlockSpec(memory_space=pl.ANY)
HBM = pl.BlockSpec(memory_space=pltpu.HBM)
EXTRA = 16
VMEM_LIMIT = 20 * 1024 * 1024


def dot(a, b, dims, precision=None):
    return lax.dot_general(a, b, dims, precision=precision, preferred_element_type=jnp.float32)


def swap(value, axis, step):
    count = lax.axis_size(axis)
    return lax.ppermute(value, axis, [(i, i ^ step) for i in range(count)])


def call(kernel, outs, *args, cost=0, name=None, specs=None, scratch=(), limit=VMEM_LIMIT, earlier=()):
    specs = (specs or [VMEM] * len(args)) + [ANY] * len(earlier)
    if earlier:
        taken, body = len(args), kernel

        def kernel(*refs):
            body(*refs[:taken], *refs[taken + len(earlier) :])

    return pl.pallas_call(
        kernel,
        out_shape=outs,
        in_specs=specs,
        out_specs=[VMEM] * len(outs),
        scratch_shapes=scratch,
        compiler_params=pltpu.CompilerParams(vmem_limit_bytes=limit),
        cost_estimate=pl.CostEstimate(flops=0, bytes_accessed=cost, transcendentals=0),
        name=name,
    )(*args, *earlier)


def after(value, earlier, cost=0):
    return pl.pallas_call(
        lambda value_ref, earlier_ref, out_ref: None,
        out_shape=jax.ShapeDtypeStruct(value.shape, value.dtype),
        in_specs=[ANY, ANY],
        out_specs=ANY,
        input_output_aliases={0: 0},
        cost_estimate=pl.CostEstimate(flops=0, bytes_accessed=cost, transcendentals=0),
        name="after",
    )(value, earlier)


def fill(block_ref, most, low, high, weights_ref, scales_ref, grad_ref):
    half, scale_half = grad_ref.shape[1] // 2, scales_ref.shape[0] // 2
    placed = jnp.dot(
        low.astype(jnp.bfloat16), grad_ref[:, :half], preferred_element_type=jnp.float32
    )
    placed += jnp.dot(
        high.astype(jnp.bfloat16), grad_ref[:, half:], preferred_element_type=jnp.float32
    )
    scale = dot(low.astype(jnp.float32), scales_ref[:scale_half], NT, lax.Precision.HIGHEST)
    scale += dot(high.astype(jnp.float32), scales_ref[scale_half:], NT, lax.Precision.HIGHEST)
    weight = jnp.sum(jnp.where(low | high, weights_ref[...], 0.0), axis=1, keepdims=True)
    for b in range(scale_half):
        part = slice(b * 128, (b + 1) * 128)
        block_ref[:, part] = (placed[:, part] * scale[:, b : b + 1] * weight).astype(jnp.bfloat16)


def pack_kernel(wide, most, order, *refs):
    given, partial_ref, refs = refs[:4], refs[4], refs[5:]
    blocks, (place_ref, *held, share_ref) = refs[: len(order)], refs[len(order) : -3]
    ids_ref, sems, share_sems = refs[-3:]
    held = [ids_ref] + held
    lane = lax.axis_index("tp")
    shares = [
        pltpu.make_async_copy(partial_ref.at[lane ^ j], share_ref.at[j], share_sems.at[j])
        for j in range(partial_ref.shape[0])
    ]
    copies = [
        pltpu.make_async_copy(source, target, sems.at[i])
        for i, (source, target) in enumerate(zip(given, held))
    ]
    for copy in copies + shares:
        copy.start()
    copies[0].wait()
    weights_ref, scales_ref, grad_ref = held[1:]
    tokens, rows = grad_ref.shape[0], blocks[0].shape[0]
    me = lax.axis_index("ep")
    ids = ids_ref[...]
    expert = lax.broadcasted_iota(jnp.int32, (max(8, wide), tokens), 0)
    named = expert == ids
    before = lax.broadcasted_iota(jnp.int32, (tokens, tokens), 0) < lax.broadcasted_iota(
        jnp.int32, (tokens, tokens), 1
    )
    earlier = jnp.dot(
        named.astype(jnp.bfloat16), before.astype(jnp.bfloat16), preferred_element_type=jnp.float32
    )
    position = jnp.sum(jnp.where(named, earlier, 0.0), axis=0, keepdims=True).astype(jnp.int32)
    row = lax.broadcasted_iota(jnp.int32, (rows, tokens), 0)
    found = []
    for k in range(wide):
        local = jnp.where(ids == (me ^ k), position, -2 * rows)
        found.append((row == local, row - most == local))
        place_ref[0, k] = found[k][0].astype(jnp.bfloat16)
        place_ref[1, k] = found[k][1].astype(jnp.bfloat16)
    for copy in copies[1:]:
        copy.wait()
    for block_ref, k in zip(blocks, order):
        fill(block_ref, most, *found[k], weights_ref, scales_ref, grad_ref)
    for copy in shares:
        copy.wait()


def pack_more_kernel(most, order, place_ref, weights_ref, scales_ref, grad_ref, *blocks):
    for block_ref, k in zip(blocks, order):
        low, high = place_ref[0, k] != 0, place_ref[1, k] != 0
        fill(block_ref, most, low, high, weights_ref, scales_ref, grad_ref)


def hidden_kernel(most, extra, *refs):
    blocks, (down_ref, sum_ref, sent_ref) = refs[:-3], refs[-3:]
    half = down_ref.shape[1] // 2
    count = sum_ref.shape[0]
    if extra:
        blocks, row_sums = blocks[:-1], blocks[-1][...]
        high = row_sums.astype(jnp.bfloat16).astype(jnp.float32)
        spare = jnp.zeros((EXTRA - 4, row_sums.shape[1]), jnp.float32)
        tail = jnp.concatenate([high, row_sums - high, spare], axis=0)
        sent_ref[count:, :] = jnp.zeros((EXTRA, sent_ref.shape[1]), jnp.bfloat16)
        sent_ref[count:, : row_sums.shape[1]] = tail.astype(jnp.bfloat16)
    values = [b[...].astype(jnp.float32) for b in blocks]
    low = jnp.concatenate([v[:most] for v in values], axis=0).astype(jnp.bfloat16)
    high = jnp.concatenate([v[most : 2 * most] for v in values], axis=0).astype(jnp.bfloat16)
    total = dot(low, down_ref[:, :half], NT) + dot(high, down_ref[:, half:], NT)
    sum_ref[...] = total
    sent_ref[:count, :] = total.astype(jnp.bfloat16)


def by_xor(value, most, narrow, lane):
    step = 1
    while step < narrow:
        pieces = [value[i * most : (i + step) * most] for i in range(0, narrow, step)]
        turned = [pieces[i ^ 1] for i in range(len(pieces))]
        value = jnp.where((lane & step) != 0, jnp.concatenate(turned, axis=0), value)
        step *= 2
    return value


def back_kernel(most, narrow, group, sum_ref, other_ref, pre_ref, gate_ref, up_ref, *outs):
    half = gate_ref.shape[0] // 2
    me, lane = lax.axis_index("ep"), lax.axis_index("tp")
    hidden = sum_ref[...] + other_ref[: sum_ref.shape[0], :].astype(jnp.float32)
    gate_pre, up_pre = [
        jnp.concatenate(
            [by_xor(pre_ref[i, me ^ k].astype(jnp.float32), most, narrow, lane) for k in group],
            axis=0,
        )
        for i in range(2)
    ]
    sig = 1.0 / (1.0 + jnp.exp(-gate_pre))
    up_grad = (hidden * gate_pre * sig).astype(jnp.bfloat16)
    gate_grad = (hidden * up_pre * sig * (1.0 + gate_pre * (1.0 - sig))).astype(jnp.bfloat16)
    low = dot(gate_grad, gate_ref[:half], NT) + dot(up_grad, up_ref[:half], NT)
    high = dot(gate_grad, gate_ref[half:], NT) + dot(up_grad, up_ref[half:], NT)
    for i, out in enumerate(outs):
        part = slice(i * most, (i + 1) * most)
        pieces = [low[part], high[part]]
        spare = out.shape[0] - 2 * most
        if spare:
            pieces.append(jnp.zeros((spare, half), jnp.float32))
        out[...] = jnp.concatenate(pieces, axis=0).astype(jnp.bfloat16)


def unpack_kernel(wide, place_ref, *refs):
    blocks, out_ref = refs[:-1], refs[-1]
    half = out_ref.shape[1] // 2
    for side in range(2):
        total = None
        for k in range(wide):
            if k == 0:
                rows = blocks[0][...].astype(jnp.float32)
                for other in blocks[wide:]:
                    rows += other[...].astype(jnp.float32)
                rows = rows.astype(jnp.bfloat16)
            else:
                rows = blocks[k][...]
            term = dot(place_ref[side, k], rows, TN)
            total = term if total is None else total + term
        out_ref[:, side * half : (side + 1) * half] = total.astype(jnp.bfloat16)


def groups_of(wide):
    left = list(range(wide - 1, -1, -1))
    if wide < 4:
        return [left]
    return [[left[0], left[-1]]] + [left[i : min(i + 2, wide - 1)] for i in range(1, wide - 1, 2)]


def local(
    grad_values,
    grad_scales,
    expert_ids,
    route_weights,
    w_gate,
    w_up,
    w_down,
    pre_acts,
    latent_partials,
    latent,
    latent_gain,
):
    wide, narrow = lax.axis_size("ep"), lax.axis_size("tp")
    tokens, width = grad_values.shape
    half = width // 2
    slots, hidden_width = pre_acts.shape[2:]
    most = slots // (wide * narrow)
    rows = -(-2 * most // 8) * 8
    f32, bf16 = jnp.float32, jnp.bfloat16
    block = jax.ShapeDtypeStruct((rows, half), bf16)

    groups = groups_of(wide)
    order, more = groups[0], [k for group in groups[1:] for k in reversed(group)]
    packed = call(
        functools.partial(pack_kernel, wide, most, order),
        [block] * len(order)
        + [
            jax.ShapeDtypeStruct((2, wide, rows, tokens), bf16),
            jax.ShapeDtypeStruct((1, tokens), f32),
            jax.ShapeDtypeStruct((grad_scales.shape[1], tokens), f32),
            jax.ShapeDtypeStruct((tokens, width), bf16),
            jax.ShapeDtypeStruct((narrow, tokens, latent.shape[1]), bf16),
        ],
        expert_ids.reshape(1, tokens),
        route_weights.reshape(1, tokens),
        grad_scales.T,
        grad_values,
        latent_partials.reshape(narrow, tokens, latent.shape[1]),
        specs=[HBM] * 5,
        scratch=[
            pltpu.VMEM((1, tokens), jnp.int32),
            pltpu.SemaphoreType.DMA((4,)),
            pltpu.SemaphoreType.DMA((narrow,)),
        ],
        limit=None,
        name="pack",
    )
    place, *fillers, shares = packed[len(order) :]
    packed = dict(zip(order, packed))
    if more:
        blocks = call(
            functools.partial(pack_more_kernel, most, more),
            [block] * len(more),
            place,
            *fillers,
            cost=1 << 25,
            name="pack_more",
        )
        packed.update(zip(more, blocks))

    def across(k, rows_of_k):
        return [rows_of_k] + [swap(rows_of_k, "tp", j) for j in range(1, narrow)]

    taken = {0: across(0, packed[0])}
    first = groups[0][0]
    arrived = {}
    for k in order + more:
        if k:
            arrived[k] = swap(packed[k], "ep", k)
            if len(groups) > 1 and k == groups[1][0]:
                arrived[k] = after(arrived[k], place, 1 << 25)
    pre = pre_acts.reshape(2, wide, narrow * most, hidden_width)
    latent_parts = [shares[0]] + [
        swap(after(shares[j], taken[0][-1]), "tp", j) for j in range(1, narrow)
    ]

    returned = {}
    own = []
    values = latent.astype(f32)
    received, products, moved = None, None, None
    for group in groups:
        for k in group:
            if k == 0:
                continue
            taken[k] = across(k, arrived[k])
        count = len(group) * narrow * most
        extra = group is groups[-1]
        if extra:
            if received is not None:
                latent_parts[-1] = after(latent_parts[-1], summed)
            own_grad = sum(part.astype(f32) for part in latent_parts)
            gained = own_grad * latent_gain[None, :]
            row_sums = jnp.stack(
                [jnp.sum(values * values, axis=1), jnp.sum(gained * values, axis=1)]
            )
        summed, sent = call(
            functools.partial(hidden_kernel, most, extra),
            [
                jax.ShapeDtypeStruct((count, hidden_width), f32),
                jax.ShapeDtypeStruct((count + (EXTRA if extra else 0), hidden_width), bf16),
            ],
            *[rows_of_k for k in group for rows_of_k in taken[k]],
            *([row_sums] if extra else []),
            w_down[0],
            name="hidden",
            earlier=products[:1] if products else [arrived[g[0]] for g in groups[1:2]],
        )
        received = swap(sent, "sub", 1)
        products = call(
            functools.partial(back_kernel, most, narrow, group),
            [block] * (len(group) * narrow),
            summed,
            received,
            pre,
            w_gate[0],
            w_up[0],
            name="back",
            earlier=(moved,) if moved is not None else (),
        )
        for at, k in enumerate(group):
            mine = products[at * narrow]
            if k == 0:
                returned[0] = mine
                own = products[1 + at * narrow : (at + 1) * narrow]
            else:
                others = [swap(products[at * narrow + j], "tp", j) for j in range(1, narrow)]
                total = mine.astype(f32)
                for other in others:
                    total += other.astype(f32)
                moved = total.astype(bf16)
                returned[k] = swap(moved, "ep", k)
                last = moved if k == group[0] else last
    own = [swap(after(value, last), "tp", j + 1) for j, value in enumerate(own)]
    tail = received[count : count + 4, :tokens].astype(f32)
    row_sums = row_sums + tail[:2] + tail[2:]
    inverse_rms = lax.rsqrt(row_sums[0] / LAT + 1e-06)[:, None]
    d_latent = (
        inverse_rms * gained - values * inverse_rms**3 * row_sums[1][:, None] / LAT
    ).astype(bf16)
    (grad_input,) = call(
        functools.partial(unpack_kernel, wide),
        [jax.ShapeDtypeStruct((tokens, width), bf16)],
        place,
        *[returned[k] for k in range(wide)],
        *own,
        name="unpack",
    )
    return (grad_input, d_latent)


def solution(mesh):
    placed = (
        P(("rep", "ep", "tp"), "sub"),
        P(("rep", "ep", "tp"), "sub"),
        P(("rep", "ep", "tp"), None),
        P(("rep", "ep", "tp"), None),
        P("ep", "sub", "tp"),
        P("ep", "sub", "tp"),
        P("ep", "tp", "sub"),
        P(("rep", "ep"), None, None, "tp"),
        P("tp", ("rep", "ep"), "sub"),
        P(("rep", "ep", "tp"), "sub"),
        P("sub"),
    )
    return jax.shard_map(
        local,
        mesh=mesh,
        in_specs=placed,
        out_specs=(P(("rep", "ep", "tp"), "sub"), P(("rep", "ep", "tp"), "sub")),
        check_vma=False,
    )
```

time: 62.5 us -> 59.5 us (0.952)
  local copies, waits for them, and re-layouts: 15.6 us -> 11.8 us
  Pallas kernels: 5.31 us -> 9.1 us
  other arithmetic: 2.72 us -> 1 us
  waiting for transfers between devices: 15.7 us -> 14.4 us
    concatenate x1 -> x0, local copies, waits for them, and re-layouts: 7.31 us -> none  [local(): jnp.concatenate([lax.dynamic_slice_in_dim(pre_acts[0], ((me ^ k) * narrow...]
    unnamed x20 -> x52, local copies, waits for them, and re-layouts: 4.67 us -> 11.2 us
    pallas_call x4 -> x11, Pallas kernels: 5.31 us -> 9.1 us  [the longest x7 9.1 us: call(): pl.pallas_call(kernel, out_shape=outs, in_specs=specs, out_specs=[VMEM] *...]
    dynamic_slice x1 -> x0, local copies, waits for them, and re-layouts: 2.14 us -> none  [local(): lax.dynamic_slice_in_dim(pre_acts[0], ((me ^ k) * narrow + (lane ^ j)) *...]
    ppermute x17, waiting for transfers between devices: 15.7 us -> 14.4 us  [swap(): return lax.ppermute(value, axis, [(i, i ^ step) for i in range(count)])]
    reduce_sum x1, other arithmetic: 1.01 us -> 0.12 us  [local(): jnp.sum(values * values, axis=1)]
    squeeze x1, local copies, waits for them, and re-layouts: 1.47 us -> 0.63 us  [local(): shares[j]]
    convert_element_type x4 -> x5, other arithmetic: 1.69 us -> 0.85 us  [the longest x1 0.75 us: local(): d_latent = (inverse_rms * gained - values * inverse_rms ** 3 * row_sums[1...]
  transfers between devices with their start and end apart: 17 -> 17, of which waited for: 8 -> 7; matrix products, arithmetic and copies ran while one was open for 22% -> 3% of each run, Pallas kernels for 1% -> 8%
where the time goes in v2:
time: 59.5 us; the launch traced here: 59.1 us
  starting transfers between devices  21.9 us (37%)
  waiting for transfers between devices  14.4 us (24%)
  local copies, waits for them, and re-layouts  11.8 us (20%)
  Pallas kernels  9.1 us (15%)
  other arithmetic  1 us (2%)
  between operations  0.86 us (1%)
    ppermute x17, starting transfers between devices, swap(): return lax.ppermute(value, axis, [(i, i ^ step) for i in range(count)])  21.9 us
    ppermute x17, waiting for transfers between devices, swap(): return lax.ppermute(value, axis, [(i, i ^ step) for i in range(count)])  14.4 us
    unnamed x52, local copies, waits for them, and re-layouts  11.2 us
    pallas_call x7, Pallas kernels, call(): pl.pallas_call(kernel, out_shape=outs, in_specs=specs, out_specs=[VMEM] *...  9.1 us
  transfers between devices with their start and end apart: 17, of which 7 were waited for; matrix products, arithmetic and copies ran while one was open for 3% of the time, Pallas kernels for 8%

profile of v2, /device:TPU:0, one launch (start us, length us, event | category | flops | bytes accessed | tf_op | source)
XLA Modules:
  0.0 59.1 jit_solution(4711514907150153497)
XLA Ops:
  0.6 2.9 %pack.1 = (bf16[72,896]{1,0:T(8,128)(2,1)}, bf16[72,896]{1,0:T(8,128)(2,1)}, bf16[2,4,72,128]{3,2,1,0:T(8,128)(2,1)}, f32[1,128]{1,0:T(1,128)}, f32[14,128]{1,0:...) custom-call(s32[1,128]{1,0:T(1,128)} %bitcast.35, f32[1,128]{1,0:T(1,128)} %bitcast.36, ...), custom_call_target="tpu_custom_call" | custom-call | tf_op jit(solution)/shard_map/pack/pallas_call | solution.py:37
  3.5 5.1 %collective-permute-start = (bf16[72,896]{1,0:T(8,128)(2,1)}, bf16[72,896]{1,0:T(8,128)(2,1)S(1)}, u32[]{:S(2)}, u32[]{:S(2)}) collective-permute-start(bf16[72,896]{1,0:T(8,128)(2,1)} %get-tuple-element.24), channel_id=1, source_target_pairs={{0,12},{4,8},{8,4},{12,0},{1,13},{5,9},{9,5},{13,1},{2,14},{6,10},... | collective-permute-start | bytes 387080 | tf_op jit(solution)/shard_map/ppermute | solution.py:26
  9.5 1.0 %copy-done.14 = bf16[128,1792]{1,0:T(8,128)(2,1)S(1)} copy-done((bf16[128,1792]{1,0:T(8,128)(2,1)S(1)}, bf16[128,1792]{1,0:T(8,128)(2,1)}, u32[]{:S(2)}) %copy-start.14) | copy-done | bytes 458776
  12.8 1.6 %collective-permute-start.2 = (bf16[72,896]{1,0:T(8,128)(2,1)}, bf16[72,896]{1,0:T(8,128)(2,1)S(1)}, u32[]{:S(2)}, u32[]{:S(2)}) collective-permute-start(bf16[72,896]{1,0:T(8,128)(2,1)} %get-tuple-element.25.refs_2_), channel_id=1, source_target_pairs={{0,2},{2,0},{1,3},{3,1},{4,6},{6,4},{5,7},{7,5},{8,10},{10,8},{9,1... | collective-permute-start | bytes 387080 | tf_op jit(solution)/shard_map/ppermute | solution.py:26
  14.9 1.3 %collective-permute-start.6 = (bf16[72,896]{1,0:T(8,128)(2,1)S(1)}, bf16[72,896]{1,0:T(8,128)(2,1)S(1)}, u32[]{:S(2)}, u32[]{:S(2)}) collective-permute-start(bf16[72,896]{1,0:T(8,128)(2,1)S(1)} %get-tuple-element.33), channel_id=1, source_target_pairs={{0,4},{4,0},{8,12},{12,8},{1,5},{5,1},{9,13},{13,9},{2,6},{6,2},{1... | collective-permute-start | bytes 387080 | tf_op jit(solution)/shard_map/ppermute | solution.py:26
  16.3 4.2 %collective-permute-done.3.value_ref = bf16[72,896]{1,0:T(8,128)(2,1)S(1)} collective-permute-done((bf16[72,896]{1,0:T(8,128)(2,1)S(1)}, bf16[72,896]{1,0:T(8,128)(2,1)S(1)}, u32[]{:S(2)}, u32[]{:S(2)}) %collective-permute-start.3) | collective-permute-done | bytes 129056 | tf_op jit(solution)/shard_map/ppermute | solution.py:26
  21.2 1.5 %copy-done.3 = bf16[1,512,1792]{2,1,0:T(8,128)(2,1)S(1)} copy-done((bf16[1,512,1792]{2,1,0:T(8,128)(2,1)S(1)}, bf16[1,512,1792]{2,1,0:T(8,128)(2,1)}, u32[]{:S(2)}) %copy-start.3) | copy-done | bytes 1835032
  26.6 1.5 %collective-permute-start.8 = (bf16[128,256]{1,0:T(8,128)(2,1)}, bf16[128,256]{1,0:T(8,128)(2,1)S(1)}, u32[]{:S(2)}, u32[]{:S(2)}) collective-permute-start(bf16[128,256]{1,0:T(8,128)(2,1)} %after.5), channel_id=1, source_target_pairs={{0,2},{2,0},{1,3},{3,1},{4,6},{6,4},{5,7},{7,5},{8,10},{10,8},{9,1... | collective-permute-start | bytes 196616 | tf_op jit(solution)/shard_map/ppermute | solution.py:26
  28.7 1.5 %collective-permute-start.7 = (bf16[72,896]{1,0:T(8,128)(2,1)S(1)}, bf16[72,896]{1,0:T(8,128)(2,1)S(1)}, u32[]{:S(2)}, u32[]{:S(2)}) collective-permute-start(bf16[72,896]{1,0:T(8,128)(2,1)S(1)} %collective-permute-done.6.refs_2_), channel_id=1, source_target_pairs={{0,2},{2,0},{1,3},{3,1},{4,6},{6,4},{5,7},{7,5},{8,10},{10,8},{9,1... | collective-permute-start | bytes 387080 | tf_op jit(solution)/shard_map/ppermute | solution.py:26
  30.2 1.6 %collective-permute-done.8.value_ref = bf16[128,256]{1,0:T(8,128)(2,1)S(1)} collective-permute-done((bf16[128,256]{1,0:T(8,128)(2,1)}, bf16[128,256]{1,0:T(8,128)(2,1)S(1)}, u32[]{:S(2)}, u32[]{:S(2)}) %collective-permute-start.8) | collective-permute-done | bytes 65568 | tf_op jit(solution)/shard_map/ppermute | solution.py:26
  32.4 1.5 %copy-done.1 = bf16[1,1792,512]{2,1,0:T(8,128)(2,1)S(1)} copy-done((bf16[1,1792,512]{2,1,0:T(8,128)(2,1)S(1)}, bf16[1,1792,512]{2,1,0:T(8,128)(2,1)}, u32[]{:S(2)}) %copy-start.1) | copy-done | bytes 1835032
  34.9 1.2 %back.2 = (bf16[72,896]{1,0:T(8,128)(2,1)S(1)}, bf16[72,896]{1,0:T(8,128)(2,1)S(1)}, bf16[72,896]{1,0:T(8,128)(2,1)S(1)}, bf16[72,896]{1,0:T(8,128)(2,1)S(1)}) custom-call(f32[144,512]{1,0:T(8,128)S(1)} %copy-done.9, bf16[144,512]{1,0:T(8,128)(2,1)S(1)} %collective-permute-done.4.other_ref, bf16[2,4,72,512]{3,2,1,0:T(8,128)(2,1)S(1)} %bitcast.27, ...), custom_call_target="tpu_custom_call" | custom-call | tf_op jit(solution)/shard_map/back/pallas_call | solution.py:37
  36.1 1.5 %collective-permute-start.10 = (bf16[72,896]{1,0:T(8,128)(2,1)S(1)}, bf16[72,896]{1,0:T(8,128)(2,1)S(1)}, u32[]{:S(2)}, u32[]{:S(2)}) collective-permute-start(bf16[72,896]{1,0:T(8,128)(2,1)S(1)} %get-tuple-element.38), channel_id=1, source_target_pairs={{0,2},{2,0},{1,3},{3,1},{4,6},{6,4},{5,7},{7,5},{8,10},{10,8},{9,1... | collective-permute-start | bytes 387080 | tf_op jit(solution)/shard_map/ppermute | solution.py:26
  38.7 2.4 %collective-permute-done.10 = bf16[72,896]{1,0:T(8,128)(2,1)S(1)} collective-permute-done((bf16[72,896]{1,0:T(8,128)(2,1)S(1)}, bf16[72,896]{1,0:T(8,128)(2,1)S(1)}, u32[]{:S(2)}, u32[]{:S(2)}) %collective-permute-start.10) | collective-permute-done | bytes 129056 | tf_op jit(solution)/shard_map/ppermute | solution.py:26
  41.2 1.9 %collective-permute-start.15 = (bf16[72,896]{1,0:T(8,128)(2,1)S(1)}, bf16[72,896]{1,0:T(8,128)(2,1)S(1)}, u32[]{:S(2)}, u32[]{:S(2)}) collective-permute-start(bf16[72,896]{1,0:T(8,128)(2,1)S(1)} %add_convert_fusion.2.refs_5_), channel_id=1, source_target_pairs={{0,12},{4,8},{8,4},{12,0},{1,13},{5,9},{9,5},{13,1},{2,14},{6,10},... | collective-permute-start | bytes 387080 | tf_op jit(solution)/shard_map/ppermute | solution.py:26
  43.1 1.3 %back.3 = (bf16[72,896]{1,0:T(8,128)(2,1)S(1)}, bf16[72,896]{1,0:T(8,128)(2,1)S(1)}, bf16[72,896]{1,0:T(8,128)(2,1)S(1)}, bf16[72,896]{1,0:T(8,128)(2,1)S(1)}) custom-call(f32[144,512]{1,0:T(8,128)S(1)} %get-tuple-element.36.refs_0_, bf16[160,512]{1,0:T(8,128)(2,1)S(1)} %collective-permute-done.9.refs_1_, bf16[2,4,72,512]{3,2,1,0:T(8,128)(2,1)S(1)} %bitcast.28, ...), custom_call_target="tpu_custom_call" | custom-call | tf_op jit(solution)/shard_map/back/pallas_call | solution.py:37
  44.4 1.6 %collective-permute-start.13 = (bf16[72,896]{1,0:T(8,128)(2,1)S(1)}, bf16[72,896]{1,0:T(8,128)(2,1)S(1)}, u32[]{:S(2)}, u32[]{:S(2)}) collective-permute-start(bf16[72,896]{1,0:T(8,128)(2,1)S(1)} %get-tuple-element.42), channel_id=1, source_target_pairs={{0,2},{2,0},{1,3},{3,1},{4,6},{6,4},{5,7},{7,5},{8,10},{10,8},{9,1... | collective-permute-start | bytes 387080 | tf_op jit(solution)/shard_map/ppermute | solution.py:26
  46.5 2.9 %collective-permute-done.13 = bf16[72,896]{1,0:T(8,128)(2,1)S(1)} collective-permute-done((bf16[72,896]{1,0:T(8,128)(2,1)S(1)}, bf16[72,896]{1,0:T(8,128)(2,1)S(1)}, u32[]{:S(2)}, u32[]{:S(2)}) %collective-permute-start.13) | collective-permute-done | bytes 129056 | tf_op jit(solution)/shard_map/ppermute | solution.py:26
  49.5 1.1 %collective-permute-start.14 = (bf16[72,896]{1,0:T(8,128)(2,1)S(1)}, bf16[72,896]{1,0:T(8,128)(2,1)S(1)}, u32[]{:S(2)}, u32[]{:S(2)}) collective-permute-start(bf16[72,896]{1,0:T(8,128)(2,1)S(1)} %add_convert_fusion.earlier_ref), channel_id=1, source_target_pairs={{0,8},{4,12},{8,0},{12,4},{1,9},{5,13},{9,1},{13,5},{2,10},{6,14},... | collective-permute-start | bytes 387080 | tf_op jit(solution)/shard_map/ppermute | solution.py:26
  50.6 1.0 %collective-permute-start.16 = (bf16[72,896]{1,0:T(8,128)(2,1)}, bf16[72,896]{1,0:T(8,128)(2,1)S(1)}, u32[]{:S(2)}, u32[]{:S(2)}) collective-permute-start(bf16[72,896]{1,0:T(8,128)(2,1)} %after.7), channel_id=1, source_target_pairs={{0,2},{2,0},{1,3},{3,1},{4,6},{6,4},{5,7},{7,5},{8,10},{10,8},{9,1... | collective-permute-start | bytes 387080 | tf_op jit(solution)/shard_map/ppermute | solution.py:26
  51.6 2.0 %collective-permute-start.12 = (bf16[72,896]{1,0:T(8,128)(2,1)S(1)}, bf16[72,896]{1,0:T(8,128)(2,1)S(1)}, u32[]{:S(2)}, u32[]{:S(2)}) collective-permute-start(bf16[72,896]{1,0:T(8,128)(2,1)S(1)} %add_convert_fusion.1), channel_id=1, source_target_pairs={{0,4},{4,0},{8,12},{12,8},{1,5},{5,1},{9,13},{13,9},{2,6},{6,2},{1... | collective-permute-start | bytes 387080 | tf_op jit(solution)/shard_map/ppermute | solution.py:26
  54.4 1.3 %collective-permute-done.16.refs_4_ = bf16[72,896]{1,0:T(8,128)(2,1)S(1)} collective-permute-done((bf16[72,896]{1,0:T(8,128)(2,1)}, bf16[72,896]{1,0:T(8,128)(2,1)S(1)}, u32[]{:S(2)}, u32[]{:S(2)}) %collective-permute-start.16) | collective-permute-done | bytes 129056 | tf_op jit(solution)/shard_map/ppermute | solution.py:26
  55.8 1.1 %collective-permute-done.14.refs_2_ = bf16[72,896]{1,0:T(8,128)(2,1)S(1)} collective-permute-done((bf16[72,896]{1,0:T(8,128)(2,1)S(1)}, bf16[72,896]{1,0:T(8,128)(2,1)S(1)}, u32[]{:S(2)}, u32[]{:S(2)}) %collective-permute-start.14) | collective-permute-done | bytes 129056 | tf_op jit(solution)/shard_map/ppermute | solution.py:26
  57.6 1.4 %unpack.1 = bf16[128,1792]{1,0:T(8,128)(2,1)} custom-call(bf16[2,4,72,128]{3,2,1,0:T(8,128)(2,1)S(1)} %copy-done.7, bf16[72,896]{1,0:T(8,128)(2,1)S(1)} %get-tuple-element.32.refs_0_, bf16[72,896]{1,0:T(8,128)(2,1)S(1)} %collective-permute-done.12.refs_1_, bf16[72,896]{1,0:T(8,128)(2,1)S(1)} %collective-permute-done.14.refs_2_, ...), custom_call_target="tpu_custom_call" | custom-call | tf_op jit(solution)/shard_map/unpack/pallas_call | solution.py:37
  (84 shorter events, 13.6 us)
Async XLA Ops:
  3.5 10.9 %collective-permute-start = (bf16[72,896]{1,0:T(8,128)(2,1)}, bf16[72,896]{1,0:T(8,128)(2,1)S(1)}, u32[]{:S(2)}, u32[]{:S(2)}) collective-permute-start(bf16[72,896]{1,0:T(8,128)(2,1)} %get-tuple-element.24), channel_id=1, source_target_pairs={{0,12},{4,8},{8,4},{12,0},{1,13},{5,9},{9,5},{13,1},{2,14},{6,10},... | collective-permute-start | bytes 387080 | tf_op jit(solution)/shard_map/ppermute | solution.py:26
  11.9 14.1 %copy-start.22 = (bf16[2,128,256]{2,1,0:T(8,128)(2,1)S(1)}, bf16[2,128,256]{2,1,0:T(8,128)(2,1)}, u32[]{:S(2)}) copy-start(bf16[2,128,256]{2,1,0:T(8,128)(2,1)} %get-tuple-element.34) | copy-start | bytes 393220
  12.8 7.7 %collective-permute-start.3 = (bf16[72,896]{1,0:T(8,128)(2,1)S(1)}, bf16[72,896]{1,0:T(8,128)(2,1)S(1)}, u32[]{:S(2)}, u32[]{:S(2)}) collective-permute-start(bf16[72,896]{1,0:T(8,128)(2,1)S(1)} %get-tuple-element.29), channel_id=1, source_target_pairs={{0,8},{4,12},{8,0},{12,4},{1,9},{5,13},{9,1},{13,5},{2,10},{6,14},... | collective-permute-start | bytes 387080 | tf_op jit(solution)/shard_map/ppermute | solution.py:26
  12.8 8.3 %collective-permute-start.2 = (bf16[72,896]{1,0:T(8,128)(2,1)}, bf16[72,896]{1,0:T(8,128)(2,1)S(1)}, u32[]{:S(2)}, u32[]{:S(2)}) collective-permute-start(bf16[72,896]{1,0:T(8,128)(2,1)} %get-tuple-element.25.refs_2_), channel_id=1, source_target_pairs={{0,2},{2,0},{1,3},{3,1},{4,6},{6,4},{5,7},{7,5},{8,10},{10,8},{9,1... | collective-permute-start | bytes 387080 | tf_op jit(solution)/shard_map/ppermute | solution.py:26
  14.4 6.8 %collective-permute-start.1 = (bf16[72,896]{1,0:T(8,128)(2,1)S(1)}, bf16[72,896]{1,0:T(8,128)(2,1)S(1)}, u32[]{:S(2)}, u32[]{:S(2)}) collective-permute-start(bf16[72,896]{1,0:T(8,128)(2,1)S(1)} %collective-permute-done.refs_0_), channel_id=1, source_target_pairs={{0,2},{2,0},{1,3},{3,1},{4,6},{6,4},{5,7},{7,5},{8,10},{10,8},{9,1... | collective-permute-start | bytes 387080 | tf_op jit(solution)/shard_map/ppermute | solution.py:26
  14.9 17.4 %copy-start = (bf16[1,1792,512]{2,1,0:T(8,128)(2,1)S(1)}, bf16[1,1792,512]{2,1,0:T(8,128)(2,1)}, u32[]{:S(2)}) copy-start(bf16[1,1792,512]{2,1,0:T(8,128)(2,1)} %param.15) | copy-start | bytes 5505028
  14.9 13.7 %collective-permute-start.6 = (bf16[72,896]{1,0:T(8,128)(2,1)S(1)}, bf16[72,896]{1,0:T(8,128)(2,1)S(1)}, u32[]{:S(2)}, u32[]{:S(2)}) collective-permute-start(bf16[72,896]{1,0:T(8,128)(2,1)S(1)} %get-tuple-element.33), channel_id=1, source_target_pairs={{0,4},{4,0},{8,12},{12,8},{1,5},{5,1},{9,13},{13,9},{2,6},{6,2},{1... | collective-permute-start | bytes 387080 | tf_op jit(solution)/shard_map/ppermute | solution.py:26
  21.2 5.5 %copy-start.13 = (bf16[72,896]{1,0:T(8,128)(2,1)}, bf16[72,896]{1,0:T(8,128)(2,1)S(1)}, u32[]{:S(2)}) copy-start(bf16[72,896]{1,0:T(8,128)(2,1)S(1)} %collective-permute-done.2.refs_3_.earlier_ref) | copy-start | bytes 387076
  24.5 3.6 %copy-start.12 = (bf16[72,896]{1,0:T(8,128)(2,1)S(1)}, bf16[72,896]{1,0:T(8,128)(2,1)}, u32[]{:S(2)}) copy-start(bf16[72,896]{1,0:T(8,128)(2,1)} %after.4.refs_5_.refs_0_) | copy-start | bytes 387076
  24.5 7.9 %copy-start.5 = (bf16[1,2,288,512]{3,2,1,0:T(8,128)(2,1)S(1)}, bf16[1,2,288,512]{3,2,1,0:T(8,128)(2,1)}, u32[]{:S(2)}) copy-start(bf16[1,2,288,512]{3,2,1,0:T(8,128)(2,1)} %param.18) | copy-start | bytes 1769476
  26.0 6.4 %collective-permute-start.4 = (bf16[144,512]{1,0:T(8,128)(2,1)S(1)}, bf16[144,512]{1,0:T(8,128)(2,1)S(1)}, u32[]{:S(2)}, u32[]{:S(2)}) collective-permute-start(bf16[144,512]{1,0:T(8,128)(2,1)S(1)} %get-tuple-element.31), channel_id=1, source_target_pairs={{0,1},{1,0},{2,3},{3,2},{4,5},{5,4},{6,7},{7,6},{8,9},{9,8},{10,11... | collective-permute-start | bytes 442376 | tf_op jit(solution)/shard_map/ppermute | solution.py:26
  26.6 5.1 %collective-permute-start.8 = (bf16[128,256]{1,0:T(8,128)(2,1)}, bf16[128,256]{1,0:T(8,128)(2,1)S(1)}, u32[]{:S(2)}, u32[]{:S(2)}) collective-permute-start(bf16[128,256]{1,0:T(8,128)(2,1)} %after.5), channel_id=1, source_target_pairs={{0,2},{2,0},{1,3},{3,1},{4,6},{6,4},{5,7},{7,5},{8,10},{10,8},{9,1... | collective-permute-start | bytes 196616 | tf_op jit(solution)/shard_map/ppermute | solution.py:26
  28.1 9.7 %collective-permute-start.5 = (bf16[72,896]{1,0:T(8,128)(2,1)S(1)}, bf16[72,896]{1,0:T(8,128)(2,1)S(1)}, u32[]{:S(2)}, u32[]{:S(2)}) collective-permute-start(bf16[72,896]{1,0:T(8,128)(2,1)S(1)} %copy-done.12), channel_id=1, source_target_pairs={{0,2},{2,0},{1,3},{3,1},{4,6},{6,4},{5,7},{7,5},{8,10},{10,8},{9,1... | collective-permute-start | bytes 387080 | tf_op jit(solution)/shard_map/ppermute | solution.py:26
  28.7 9.2 %collective-permute-start.7 = (bf16[72,896]{1,0:T(8,128)(2,1)S(1)}, bf16[72,896]{1,0:T(8,128)(2,1)S(1)}, u32[]{:S(2)}, u32[]{:S(2)}) collective-permute-start(bf16[72,896]{1,0:T(8,128)(2,1)S(1)} %collective-permute-done.6.refs_2_), channel_id=1, source_target_pairs={{0,2},{2,0},{1,3},{3,1},{4,6},{6,4},{5,7},{7,5},{8,10},{10,8},{9,1... | collective-permute-start | bytes 387080 | tf_op jit(solution)/shard_map/ppermute | solution.py:26
  36.1 7.0 %copy-start.2 = (bf16[1,1792,512]{2,1,0:T(8,128)(2,1)S(1)}, bf16[1,1792,512]{2,1,0:T(8,128)(2,1)}, u32[]{:S(2)}) copy-start(bf16[1,1792,512]{2,1,0:T(8,128)(2,1)} %param.16) | copy-start | bytes 5505028
  36.1 5.0 %collective-permute-start.10 = (bf16[72,896]{1,0:T(8,128)(2,1)S(1)}, bf16[72,896]{1,0:T(8,128)(2,1)S(1)}, u32[]{:S(2)}, u32[]{:S(2)}) collective-permute-start(bf16[72,896]{1,0:T(8,128)(2,1)S(1)} %get-tuple-element.38), channel_id=1, source_target_pairs={{0,2},{2,0},{1,3},{3,1},{4,6},{6,4},{5,7},{7,5},{8,10},{10,8},{9,1... | collective-permute-start | bytes 387080 | tf_op jit(solution)/shard_map/ppermute | solution.py:26
  38.6 4.5 %collective-permute-start.9 = (bf16[160,512]{1,0:T(8,128)(2,1)S(1)}, bf16[160,512]{1,0:T(8,128)(2,1)S(1)}, u32[]{:S(2)}, u32[]{:S(2)}) collective-permute-start(bf16[160,512]{1,0:T(8,128)(2,1)S(1)} %get-tuple-element.37), channel_id=1, source_target_pairs={{0,1},{1,0},{2,3},{3,2},{4,5},{5,4},{6,7},{7,6},{8,9},{9,8},{10,11... | collective-permute-start | bytes 491528 | tf_op jit(solution)/shard_map/ppermute | solution.py:26
  41.2 13.2 %collective-permute-start.15 = (bf16[72,896]{1,0:T(8,128)(2,1)S(1)}, bf16[72,896]{1,0:T(8,128)(2,1)S(1)}, u32[]{:S(2)}, u32[]{:S(2)}) collective-permute-start(bf16[72,896]{1,0:T(8,128)(2,1)S(1)} %add_convert_fusion.2.refs_5_), channel_id=1, source_target_pairs={{0,12},{4,8},{8,4},{12,0},{1,13},{5,9},{9,5},{13,1},{2,14},{6,10},... | collective-permute-start | bytes 387080 | tf_op jit(solution)/shard_map/ppermute | solution.py:26
  43.1 14.5 %copy-start.7 = (bf16[2,4,72,128]{3,2,1,0:T(8,128)(2,1)S(1)}, bf16[2,4,72,128]{3,2,1,0:T(8,128)(2,1)}, u32[]{:S(2)}) copy-start(bf16[2,4,72,128]{3,2,1,0:T(8,128)(2,1)} %get-tuple-element.23.place_ref.earlier_ref) | copy-start | bytes 442372
  44.4 5.0 %collective-permute-start.13 = (bf16[72,896]{1,0:T(8,128)(2,1)S(1)}, bf16[72,896]{1,0:T(8,128)(2,1)S(1)}, u32[]{:S(2)}, u32[]{:S(2)}) collective-permute-start(bf16[72,896]{1,0:T(8,128)(2,1)S(1)} %get-tuple-element.42), channel_id=1, source_target_pairs={{0,2},{2,0},{1,3},{3,1},{4,6},{6,4},{5,7},{7,5},{8,10},{10,8},{9,1... | collective-permute-start | bytes 387080 | tf_op jit(solution)/shard_map/ppermute | solution.py:26
  45.9 5.6 %collective-permute-start.11 = (bf16[72,896]{1,0:T(8,128)(2,1)S(1)}, bf16[72,896]{1,0:T(8,128)(2,1)S(1)}, u32[]{:S(2)}, u32[]{:S(2)}) collective-permute-start(bf16[72,896]{1,0:T(8,128)(2,1)S(1)} %get-tuple-element.40), channel_id=1, source_target_pairs={{0,2},{2,0},{1,3},{3,1},{4,6},{6,4},{5,7},{7,5},{8,10},{10,8},{9,1... | collective-permute-start | bytes 387080 | tf_op jit(solution)/shard_map/ppermute | solution.py:26
  49.5 7.4 %collective-permute-start.14 = (bf16[72,896]{1,0:T(8,128)(2,1)S(1)}, bf16[72,896]{1,0:T(8,128)(2,1)S(1)}, u32[]{:S(2)}, u32[]{:S(2)}) collective-permute-start(bf16[72,896]{1,0:T(8,128)(2,1)S(1)} %add_convert_fusion.earlier_ref), channel_id=1, source_target_pairs={{0,8},{4,12},{8,0},{12,4},{1,9},{5,13},{9,1},{13,5},{2,10},{6,14},... | collective-permute-start | bytes 387080 | tf_op jit(solution)/shard_map/ppermute | solution.py:26
  50.6 5.2 %collective-permute-start.16 = (bf16[72,896]{1,0:T(8,128)(2,1)}, bf16[72,896]{1,0:T(8,128)(2,1)S(1)}, u32[]{:S(2)}, u32[]{:S(2)}) collective-permute-start(bf16[72,896]{1,0:T(8,128)(2,1)} %after.7), channel_id=1, source_target_pairs={{0,2},{2,0},{1,3},{3,1},{4,6},{6,4},{5,7},{7,5},{8,10},{10,8},{9,1... | collective-permute-start | bytes 387080 | tf_op jit(solution)/shard_map/ppermute | solution.py:26
  51.6 6.0 %collective-permute-start.12 = (bf16[72,896]{1,0:T(8,128)(2,1)S(1)}, bf16[72,896]{1,0:T(8,128)(2,1)S(1)}, u32[]{:S(2)}, u32[]{:S(2)}) collective-permute-start(bf16[72,896]{1,0:T(8,128)(2,1)S(1)} %add_convert_fusion.1), channel_id=1, source_target_pairs={{0,4},{4,0},{8,12},{12,8},{1,5},{5,1},{9,13},{13,9},{2,6},{6,2},{1... | collective-permute-start | bytes 387080 | tf_op jit(solution)/shard_map/ppermute | solution.py:26
  (19 other events, 28.4 us)

commit v3 on v2

--- a/solution.py
+++ b/solution.py
@@ -26,7 +26,15 @@
     return lax.ppermute(value, axis, [(i, i ^ step) for i in range(count)])
 
 
-def call(kernel, outs, *args, cost=0, name=None, specs=None, scratch=(), limit=VMEM_LIMIT, earlier=()):
+def pinned(*arrays):
+    return [pltpu.with_memory_space_constraint(array, pltpu.HBM) for array in arrays]
+
+
+def like(array):
+    return pltpu.VMEM(array.shape, array.dtype)
+
+
+def call(kernel, outs, *args, cost=0, name=None, specs=None, scratch=(), earlier=()):
     specs = (specs or [VMEM] * len(args)) + [ANY] * len(earlier)
     if earlier:
         taken, body = len(args), kernel
@@ -40,7 +48,7 @@
         in_specs=specs,
         out_specs=[VMEM] * len(outs),
         scratch_shapes=scratch,
-        compiler_params=pltpu.CompilerParams(vmem_limit_bytes=limit),
+        compiler_params=pltpu.CompilerParams(vmem_limit_bytes=VMEM_LIMIT),
         cost_estimate=pl.CostEstimate(flops=0, bytes_accessed=cost, transcendentals=0),
         name=name,
     )(*args, *earlier)
@@ -74,22 +82,22 @@
         block_ref[:, part] = (placed[:, part] * scale[:, b : b + 1] * weight).astype(jnp.bfloat16)
 
 
+def fetch(sources, targets, sems, first=0):
+    copies = [
+        pltpu.make_async_copy(source, target, sems.at[first + i])
+        for i, (source, target) in enumerate(zip(sources, targets))
+    ]
+    for copy in copies:
+        copy.start()
+    return copies
+
+
 def pack_kernel(wide, most, order, *refs):
-    given, partial_ref, refs = refs[:4], refs[4], refs[5:]
-    blocks, (place_ref, *held, share_ref) = refs[: len(order)], refs[len(order) : -3]
-    ids_ref, sems, share_sems = refs[-3:]
+    given, refs = refs[:4], refs[4:]
+    blocks, (place_ref, *held) = refs[: len(order)], refs[len(order) : -2]
+    ids_ref, sems = refs[-2:]
     held = [ids_ref] + held
-    lane = lax.axis_index("tp")
-    shares = [
-        pltpu.make_async_copy(partial_ref.at[lane ^ j], share_ref.at[j], share_sems.at[j])
-        for j in range(partial_ref.shape[0])
-    ]
-    copies = [
-        pltpu.make_async_copy(source, target, sems.at[i])
-        for i, (source, target) in enumerate(zip(given, held))
-    ]
-    for copy in copies + shares:
-        copy.start()
+    copies = fetch(given, held, sems)
     copies[0].wait()
     weights_ref, scales_ref, grad_ref = held[1:]
     tokens, rows = grad_ref.shape[0], blocks[0].shape[0]
@@ -115,14 +123,24 @@
         copy.wait()
     for block_ref, k in zip(blocks, order):
         fill(block_ref, most, *found[k], weights_ref, scales_ref, grad_ref)
-    for copy in shares:
-        copy.wait()
-
-
-def pack_more_kernel(most, order, place_ref, weights_ref, scales_ref, grad_ref, *blocks):
+
+
+def pack_more_kernel(most, order, place_ref, weights_ref, scales_ref, grad_ref, partial_ref, *refs):
+    taken = (len(refs) - 3 - len(order)) // 2
+    given, blocks, (share_ref, *held) = refs[:taken], refs[taken : -taken - 3], refs[-taken - 3 : -2]
+    sems, share_sems = refs[-2:]
+    lane, count = lax.axis_index("tp"), partial_ref.shape[0]
+    copies = fetch(
+        [partial_ref.at[lane ^ j] for j in range(count)],
+        [share_ref.at[j] for j in range(count)],
+        share_sems,
+    )
+    copies += fetch(given, held, sems)
     for block_ref, k in zip(blocks, order):
         low, high = place_ref[0, k] != 0, place_ref[1, k] != 0
         fill(block_ref, most, low, high, weights_ref, scales_ref, grad_ref)
+    for copy in copies:
+        copy.wait()
 
 
 def hidden_kernel(most, extra, *refs):
@@ -224,46 +242,55 @@
     most = slots // (wide * narrow)
     rows = -(-2 * most // 8) * 8
     f32, bf16 = jnp.float32, jnp.bfloat16
-    block = jax.ShapeDtypeStruct((rows, half), bf16)
-
+    block = pltpu.VMEM((rows, half), bf16)
     groups = groups_of(wide)
     order, more = groups[0], [k for group in groups[1:] for k in reversed(group)]
     packed = call(
         functools.partial(pack_kernel, wide, most, order),
         [block] * len(order)
         + [
-            jax.ShapeDtypeStruct((2, wide, rows, tokens), bf16),
-            jax.ShapeDtypeStruct((1, tokens), f32),
-            jax.ShapeDtypeStruct((grad_scales.shape[1], tokens), f32),
-            jax.ShapeDtypeStruct((tokens, width), bf16),
-            jax.ShapeDtypeStruct((narrow, tokens, latent.shape[1]), bf16),
+            pltpu.VMEM((2, wide, rows, tokens), bf16),
+            pltpu.VMEM((1, tokens), f32),
+            pltpu.VMEM((grad_scales.shape[1], tokens), f32),
+            pltpu.VMEM((tokens, width), bf16),
         ],
-        expert_ids.reshape(1, tokens),
-        route_weights.reshape(1, tokens),
-        grad_scales.T,
-        grad_values,
-        latent_partials.reshape(narrow, tokens, latent.shape[1]),
-        specs=[HBM] * 5,
+        *pinned(
+            expert_ids.reshape(1, tokens),
+            route_weights.reshape(1, tokens),
+            grad_scales.T,
+            grad_values,
+        ),
+        specs=[HBM] * 4,
+        scratch=[pltpu.VMEM((1, tokens), jnp.int32), pltpu.SemaphoreType.DMA((4,))],
+        name="pack",
+    )
+    place, *fillers = packed[len(order) :]
+    packed = dict(zip(order, packed))
+    partials = latent_partials.reshape(narrow, tokens, latent.shape[1])
+    fetched = [
+        w_down[0],
+        pre_acts.reshape(2, wide, narrow * most, hidden_width),
+        w_gate[0],
+        w_up[0],
+        latent,
+        latent_gain.reshape(1, -1),
+    ]
+    blocks = call(
+        functools.partial(pack_more_kernel, most, more),
+        [block] * len(more) + [like(partials)] + [like(array) for array in fetched],
+        place,
+        *fillers,
+        *pinned(partials, *fetched),
+        specs=[VMEM] * 4 + [HBM] * (1 + len(fetched)),
         scratch=[
-            pltpu.VMEM((1, tokens), jnp.int32),
-            pltpu.SemaphoreType.DMA((4,)),
+            pltpu.SemaphoreType.DMA((len(fetched),)),
             pltpu.SemaphoreType.DMA((narrow,)),
         ],
-        limit=None,
-        name="pack",
-    )
-    place, *fillers, shares = packed[len(order) :]
-    packed = dict(zip(order, packed))
-    if more:
-        blocks = call(
-            functools.partial(pack_more_kernel, most, more),
-            [block] * len(more),
-            place,
-            *fillers,
-            cost=1 << 25,
-            name="pack_more",
-        )
-        packed.update(zip(more, blocks))
+        cost=1 << 25,
+        name="pack_more",
+    )
+    packed.update(zip(more, blocks))
+    shares, down, pre, gate, up, latent, latent_gain = blocks[len(more) :]
 
     def across(k, rows_of_k):
         return [rows_of_k] + [swap(rows_of_k, "tp", j) for j in range(1, narrow)]
@@ -275,8 +302,7 @@
         if k:
             arrived[k] = swap(packed[k], "ep", k)
             if len(groups) > 1 and k == groups[1][0]:
-                arrived[k] = after(arrived[k], place, 1 << 25)
-    pre = pre_acts.reshape(2, wide, narrow * most, hidden_width)
+                arrived[k] = after(arrived[k], packed[first], 1 << 25)
     latent_parts = [shares[0]] + [
         swap(after(shares[j], taken[0][-1]), "tp", j) for j in range(1, narrow)
     ]
@@ -296,19 +322,19 @@
             if received is not None:
                 latent_parts[-1] = after(latent_parts[-1], summed)
             own_grad = sum(part.astype(f32) for part in latent_parts)
-            gained = own_grad * latent_gain[None, :]
+            gained = own_grad * latent_gain
             row_sums = jnp.stack(
                 [jnp.sum(values * values, axis=1), jnp.sum(gained * values, axis=1)]
             )
         summed, sent = call(
             functools.partial(hidden_kernel, most, extra),
             [
-                jax.ShapeDtypeStruct((count, hidden_width), f32),
-                jax.ShapeDtypeStruct((count + (EXTRA if extra else 0), hidden_width), bf16),
+                pltpu.VMEM((count, hidden_width), f32),
+                pltpu.VMEM((count + (EXTRA if extra else 0), hidden_width), bf16),
             ],
             *[rows_of_k for k in group for rows_of_k in taken[k]],
             *([row_sums] if extra else []),
-            w_down[0],
+            down,
             name="hidden",
             earlier=products[:1] if products else [arrived[g[0]] for g in groups[1:2]],
         )
@@ -319,8 +345,8 @@
             summed,
             received,
             pre,
-            w_gate[0],
-            w_up[0],
+            gate,
+            up,
             name="back",
             earlier=(moved,) if moved is not None else (),
         )
@@ -331,6 +357,8 @@
                 own = products[1 + at * narrow : (at + 1) * narrow]
             else:
                 others = [swap(products[at * narrow + j], "tp", j) for j in range(1, narrow)]
+                if k == group[0]:
+                    others[0] = after(others[0], mine, 1 << 24)
                 total = mine.astype(f32)
                 for other in others:
                     total += other.astype(f32)

time: 59.5 us -> 70 us (1.18)
  Pallas kernels: 9.1 us -> 14.1 us
  other arithmetic: 1 us -> 4.61 us
  starting transfers between devices: 21.9 us -> 19.3 us
  waiting for transfers between devices: 14.4 us -> 16.8 us
  local copies, waits for them, and re-layouts: 11.8 us -> 13.8 us
    pallas_call x7, Pallas kernels: 9.1 us -> 14.1 us  [call(): pl.pallas_call(kernel, out_shape=outs, in_specs=specs, out_specs=[VMEM] *...]
    ppermute x17, starting transfers between devices: 21.9 us -> 19.3 us  [swap(): return lax.ppermute(value, axis, [(i, i ^ step) for i in range(count)])]
    ppermute x17, waiting for transfers between devices: 14.4 us -> 16.8 us  [swap(): return lax.ppermute(value, axis, [(i, i ^ step) for i in range(count)])]
    unnamed x52 -> x44, local copies, waits for them, and re-layouts: 11.2 us -> 13.1 us
    convert_element_type x3, other arithmetic: 0.1 us -> 2.03 us  [local(): moved = total.astype(bf16)]
    convert_element_type x1, other arithmetic: 0.75 us -> 1.59 us  [local(): d_latent = (inverse_rms * gained - values * inverse_rms ** 3 * row_sums[1...]
    reduce_sum x1, other arithmetic: 0.12 us -> 0.96 us  [local(): jnp.sum(values * values, axis=1)]
  transfers between devices with their start and end apart: 17 -> 17, of which waited for: 7 -> 6; matrix products, arithmetic and copies ran while one was open for 3% -> 8% of each run, Pallas kernels for 8% -> 16%
where the time goes in v3:
time: 70 us; the launch traced here: 69.5 us
  starting transfers between devices  19.3 us (28%)
  waiting for transfers between devices  16.8 us (24%)
  Pallas kernels  14.1 us (20%)
  local copies, waits for them, and re-layouts  13.8 us (20%)
  other arithmetic  4.61 us (7%)
  between operations  0.84 us (1%)
    ppermute x17, starting transfers between devices, swap(): return lax.ppermute(value, axis, [(i, i ^ step) for i in range(count)])  19.3 us
    ppermute x17, waiting for transfers between devices, swap(): return lax.ppermute(value, axis, [(i, i ^ step) for i in range(count)])  16.8 us
    pallas_call x7, Pallas kernels, call(): pl.pallas_call(kernel, out_shape=outs, in_specs=specs, out_specs=[VMEM] *...  14.1 us
    unnamed x44, local copies, waits for them, and re-layouts  13.1 us
    convert_element_type x3, other arithmetic, local(): moved = total.astype(bf16)  2.03 us
    convert_element_type x1, other arithmetic, local(): d_latent = (inverse_rms * gained - values * inverse_rms ** 3 * row_sums[1...  1.59 us
  transfers between devices with their start and end apart: 17, of which 6 were waited for; matrix products, arithmetic and copies ran while one was open for 8% of the time, Pallas kernels for 16%

profile of v3, /device:TPU:0, one launch (start us, length us, event | category | flops | bytes accessed | tf_op | source)
XLA Modules:
  0.0 69.5 jit_solution(456403161792796825)
XLA Ops:
  0.6 1.9 %pack.1 = (bf16[72,896]{1,0:T(8,128)(2,1)S(1)}, bf16[72,896]{1,0:T(8,128)(2,1)S(1)}, bf16[2,4,72,128]{3,2,1,0:T(8,128)(2,1)S(1)}, f32[1,128]{1,0:T(1,128)S(1)}, ...) custom-call(s32[1,128]{1,0:T(1,128)} %bitcast.36, f32[1,128]{1,0:T(1,128)} %bitcast.37, f32[14,128]{1,0:T(8,128)} %bitcast.30, ...), custom_call_target="tpu_custom_call" | custom-call | tf_op jit(solution)/shard_map/pack/pallas_call | solution.py:45
  2.6 5.1 %collective-permute-start = (bf16[72,896]{1,0:T(8,128)(2,1)S(1)}, bf16[72,896]{1,0:T(8,128)(2,1)S(1)}, u32[]{:S(2)}, u32[]{:S(2)}) collective-permute-start(bf16[72,896]{1,0:T(8,128)(2,1)S(1)} %get-tuple-element.30.earlier_ref), channel_id=1, source_target_pairs={{0,12},{4,8},{8,4},{12,0},{1,13},{5,9},{9,5},{13,1},{2,14},{6,10},... | collective-permute-start | bytes 387080 | tf_op jit(solution)/shard_map/ppermute | solution.py:26
  7.7 3.6 %pack_more.1 = (bf16[72,896]{1,0:T(8,128)(2,1)}, bf16[72,896]{1,0:T(8,128)(2,1)S(1)}, bf16[2,128,256]{2,1,0:T(8,128)(2,1)S(1)}, bf16[512,1792]{1,0:T(8,128)(2,1)...) custom-call(bf16[2,4,72,128]{3,2,1,0:T(8,128)(2,1)S(1)} %get-tuple-e, ...), custom_call_target="tpu_custom_call" | custom-call | bytes 33554432 | tf_op jit(solution)/shard_map/pack_more/pallas_call | solution.py:45
  11.3 1.2 %copy-done = bf16[1792,512]{1,0:T(8,128)(2,1)} copy-done((bf16[1792,512]{1,0:T(8,128)(2,1)}, bf16[1792,512]{1,0:T(8,128)(2,1)S(1)}, u32[]{:S(2)}) %copy-start) | copy-done | bytes 1835032
  13.8 1.5 %collective-permute-start.2 = (bf16[72,896]{1,0:T(8,128)(2,1)S(1)}, bf16[72,896]{1,0:T(8,128)(2,1)S(1)}, u32[]{:S(2)}, u32[]{:S(2)}) collective-permute-start(bf16[72,896]{1,0:T(8,128)(2,1)S(1)} %get-tuple-element.31.refs_2_), channel_id=1, source_target_pairs={{0,2},{2,0},{1,3},{3,1},{4,6},{6,4},{5,7},{7,5},{8,10},{10,8},{9,1... | collective-permute-start | bytes 387080 | tf_op jit(solution)/shard_map/ppermute | solution.py:26
  16.4 5.1 %collective-permute-done.3.value_ref = bf16[72,896]{1,0:T(8,128)(2,1)S(1)} collective-permute-done((bf16[72,896]{1,0:T(8,128)(2,1)S(1)}, bf16[72,896]{1,0:T(8,128)(2,1)S(1)}, u32[]{:S(2)}, u32[]{:S(2)}) %collective-permute-start.3) | collective-permute-done | bytes 129056 | tf_op jit(solution)/shard_map/ppermute | solution.py:26
  22.2 1.5 %copy-done.4 = bf16[512,1792]{1,0:T(8,128)(2,1)S(1)} copy-done((bf16[512,1792]{1,0:T(8,128)(2,1)S(1)}, bf16[512,1792]{1,0:T(8,128)(2,1)}, u32[]{:S(2)}) %copy-start.4) | copy-done | bytes 1835032
  24.6 2.4 %hidden.2 = (f32[144,512]{1,0:T(8,128)S(1)}, bf16[144,512]{1,0:T(8,128)(2,1)}) custom-call(bf16[72,896]{1,0:T(8,128)(2,1)S(1)} %collective-permute-done.refs_0_, bf16[72,896]{1,0:T(8,128)(2,1)} %collective-permute-done.1.refs_1_, bf16[72,896]{1,0:T(8,128)(2,1)S(1)} %get-tuple-element.31.refs_2_, ...), custom_call_target="tpu_custom_call" | custom-call | tf_op jit(solution)/shard_map/hidden/pallas_call | solution.py:45
  28.3 1.5 %collective-permute-start.8 = (bf16[128,256]{1,0:T(8,128)(2,1)}, bf16[128,256]{1,0:T(8,128)(2,1)}, u32[]{:S(2)}, u32[]{:S(2)}) collective-permute-start(bf16[128,256]{1,0:T(8,128)(2,1)} %after.7), channel_id=1, source_target_pairs={{0,2},{2,0},{1,3},{3,1},{4,6},{6,4},{5,7},{7,5},{8,10},{10,8},{9,1... | collective-permute-start | bytes 196616 | tf_op jit(solution)/shard_map/ppermute | solution.py:26
  30.4 1.5 %collective-permute-start.7 = (bf16[72,896]{1,0:T(8,128)(2,1)S(1)}, bf16[72,896]{1,0:T(8,128)(2,1)}, u32[]{:S(2)}, u32[]{:S(2)}) collective-permute-start(bf16[72,896]{1,0:T(8,128)(2,1)S(1)} %collective-permute-done.6.refs_2_), channel_id=1, source_target_pairs={{0,2},{2,0},{1,3},{3,1},{4,6},{6,4},{5,7},{7,5},{8,10},{10,8},{9,1... | collective-permute-start | bytes 387080 | tf_op jit(solution)/shard_map/ppermute | solution.py:26
  31.8 1.7 %collective-permute-done.8.value_ref = bf16[128,256]{1,0:T(8,128)(2,1)} collective-permute-done((bf16[128,256]{1,0:T(8,128)(2,1)}, bf16[128,256]{1,0:T(8,128)(2,1)}, u32[]{:S(2)}, u32[]{:S(2)}) %collective-permute-start.8) | collective-permute-done | bytes 65568 | tf_op jit(solution)/shard_map/ppermute | solution.py:26
  33.5 1.5 %copy-done.1 = bf16[1792,512]{1,0:T(8,128)(2,1)S(1)} copy-done((bf16[1792,512]{1,0:T(8,128)(2,1)S(1)}, bf16[1792,512]{1,0:T(8,128)(2,1)}, u32[]{:S(2)}) %copy-start.1) | copy-done | bytes 1835032
  37.3 1.6 %collective-permute-start.10 = (bf16[72,896]{1,0:T(8,128)(2,1)S(1)}, bf16[72,896]{1,0:T(8,128)(2,1)}, u32[]{:S(2)}, u32[]{:S(2)}) collective-permute-start(bf16[72,896]{1,0:T(8,128)(2,1)S(1)} %get-tuple-element.50), channel_id=1, source_target_pairs={{0,2},{2,0},{1,3},{3,1},{4,6},{6,4},{5,7},{7,5},{8,10},{10,8},{9,1... | collective-permute-start | bytes 387080 | tf_op jit(solution)/shard_map/ppermute | solution.py:26
  41.4 2.3 %hidden.3 = (f32[144,512]{1,0:T(8,128)S(1)}, bf16[160,512]{1,0:T(8,128)(2,1)}) custom-call(bf16[72,896]{1,0:T(8,128)(2,1)S(1)} %copy-done.11, bf16[72,896]{1,0:T(8,128)(2,1)S(1)} %copy-done.18, bf16[72,896]{1,0:T(8,128)(2,1)S(1)} %collective-permute-done.6.refs_2_, bf16[72,896]{1,0:T(8,128)(2,1)} %collective-permute-done.7.refs_3_, ...), custom_call_target="tpu_custom_call" | custom-call | tf_op jit(solution)/shard_map/hidden/pallas_call | solution.py:45
  44.7 1.4 %collective-permute-start.15 = (bf16[72,896]{1,0:T(8,128)(2,1)S(1)}, bf16[72,896]{1,0:T(8,128)(2,1)S(1)}, u32[]{:S(2)}, u32[]{:S(2)}) collective-permute-start(bf16[72,896]{1,0:T(8,128)(2,1)S(1)} %add_convert_fusion.2.refs_5_), channel_id=1, source_target_pairs={{0,12},{4,8},{8,4},{12,0},{1,13},{5,9},{9,5},{13,1},{2,14},{6,10},... | collective-permute-start | bytes 387080 | tf_op jit(solution)/shard_map/ppermute | solution.py:26
  46.2 1.5 %copy-done.2 = bf16[1792,512]{1,0:T(8,128)(2,1)S(1)} copy-done((bf16[1792,512]{1,0:T(8,128)(2,1)S(1)}, bf16[1792,512]{1,0:T(8,128)(2,1)}, u32[]{:S(2)}) %copy-start.2) | copy-done | bytes 1835032
  47.7 1.2 %back.3 = (bf16[72,896]{1,0:T(8,128)(2,1)S(1)}, bf16[72,896]{1,0:T(8,128)(2,1)S(1)}, bf16[72,896]{1,0:T(8,128)(2,1)S(1)}, bf16[72,896]{1,0:T(8,128)(2,1)S(1)}) custom-call(f32[144,512]{1,0:T(8,128)S(1)} %get-tuple-element.48.refs_0_, bf16[160,512]{1,0:T(8,128)(2,1)S(1)} %collective-permute-done.9.refs_1_, ...), custom_call_target="tpu_custom_call" | custom-call | tf_op jit(solution)/shard_map/back/pallas_call | solution.py:45
  50.1 1.5 %collective-permute-start.13 = (bf16[72,896]{1,0:T(8,128)(2,1)S(1)}, bf16[72,896]{1,0:T(8,128)(2,1)S(1)}, u32[]{:S(2)}, u32[]{:S(2)}) collective-permute-start(bf16[72,896]{1,0:T(8,128)(2,1)S(1)} %get-tuple-element.54), channel_id=1, source_target_pairs={{0,2},{2,0},{1,3},{3,1},{4,6},{6,4},{5,7},{7,5},{8,10},{10,8},{9,1... | collective-permute-start | bytes 387080 | tf_op jit(solution)/shard_map/ppermute | solution.py:26
  51.6 4.3 %collective-permute-done.11 = bf16[72,896]{1,0:T(8,128)(2,1)S(1)} collective-permute-done((bf16[72,896]{1,0:T(8,128)(2,1)S(1)}, bf16[72,896]{1,0:T(8,128)(2,1)S(1)}, u32[]{:S(2)}, u32[]{:S(2)}) %collective-permute-start.11) | collective-permute-done | bytes 129056 | tf_op jit(solution)/shard_map/ppermute | solution.py:26
  55.9 1.4 %collective-permute-start.12 = (bf16[72,896]{1,0:T(8,128)(2,1)S(1)}, bf16[72,896]{1,0:T(8,128)(2,1)S(1)}, u32[]{:S(2)}, u32[]{:S(2)}) collective-permute-start(bf16[72,896]{1,0:T(8,128)(2,1)S(1)} %add_convert_fusion.1), channel_id=1, source_target_pairs={{0,4},{4,0},{8,12},{12,8},{1,5},{5,1},{9,13},{13,9},{2,6},{6,2},{1... | collective-permute-start | bytes 387080 | tf_op jit(solution)/shard_map/ppermute | solution.py:26
  61.3 1.6 %fusion.5 = bf16[128,256]{1,0:T(8,128)(2,1)} fusion(bf16[128,256]{1,0:T(8,128)(2,1)S(1)} %get-tuple-element.44, bf16[128,256]{1,0:T(8,128)(2,1)} %after.8, f32[128]{0:T(128)S(1)} %slice_bitcast_fusion.1, f32[128]{0:T(128)S(1)} %get-tuple-element.58, f32[128]{0:T(128)S(1)} %get-tuple-element.59, f32[256]{0:T(256)S(1)} %bitcast.24, ...), kind=kLoop, calls=%fused_computation.11 | loop fusion | flops 360448 | bytes 264704 | tf_op jit(solution)/shard_map/convert_element_type | solution.py:374
  62.9 3.1 %collective-permute-done.16.refs_4_ = bf16[72,896]{1,0:T(8,128)(2,1)S(1)} collective-permute-done((bf16[72,896]{1,0:T(8,128)(2,1)}, bf16[72,896]{1,0:T(8,128)(2,1)S(1)}, u32[]{:S(2)}, u32[]{:S(2)}) %collective-permute-start.16) | collective-permute-done | bytes 129056 | tf_op jit(solution)/shard_map/ppermute | solution.py:26
  65.9 2.1 %collective-permute-done.14.refs_2_ = bf16[72,896]{1,0:T(8,128)(2,1)S(1)} collective-permute-done((bf16[72,896]{1,0:T(8,128)(2,1)S(1)}, bf16[72,896]{1,0:T(8,128)(2,1)S(1)}, u32[]{:S(2)}, u32[]{:S(2)}) %collective-permute-start.14) | collective-permute-done | bytes 129056 | tf_op jit(solution)/shard_map/ppermute | solution.py:26
  68.0 1.4 %unpack.1 = bf16[128,1792]{1,0:T(8,128)(2,1)} custom-call(bf16[2,4,72,128]{3,2,1,0:T(8,128)(2,1)S(1)} %get-tuple-element.29.place_ref, bf16[72,896]{1,0:T(8,128)(2,1)S(1)} %copy-done.15, bf16[72,896]{1,0:T(8,128)(2,1)S(1)} %collective-permute-done.12.refs_1_, bf16[72,896]{1,0:T(8,128)(2,1)S(1)} %collective-permute-done.14.refs_2_, ...), custom_call_target="tpu_custom_call" | custom-call | tf_op jit(solution)/shard_map/unpack/pallas_call | solution.py:45
  (78 shorter events, 16.9 us)
Async XLA Ops:
  2.5 8.8 %copy-start.19 = (bf16[72,896]{1,0:T(8,128)(2,1)}, bf16[72,896]{1,0:T(8,128)(2,1)S(1)}, u32[]{:S(2)}) copy-start(bf16[72,896]{1,0:T(8,128)(2,1)S(1)} %get-tuple-element.30.earlier_ref) | copy-start | bytes 387076
  2.6 12.8 %collective-permute-start = (bf16[72,896]{1,0:T(8,128)(2,1)S(1)}, bf16[72,896]{1,0:T(8,128)(2,1)S(1)}, u32[]{:S(2)}, u32[]{:S(2)}) collective-permute-start(bf16[72,896]{1,0:T(8,128)(2,1)S(1)} %get-tuple-element.30.earlier_ref), channel_id=1, source_target_pairs={{0,12},{4,8},{8,4},{12,0},{1,13},{5,9},{9,5},{13,1},{2,14},{6,10},... | collective-permute-start | bytes 387080 | tf_op jit(solution)/shard_map/ppermute | solution.py:26
  13.8 7.7 %collective-permute-start.3 = (bf16[72,896]{1,0:T(8,128)(2,1)S(1)}, bf16[72,896]{1,0:T(8,128)(2,1)S(1)}, u32[]{:S(2)}, u32[]{:S(2)}) collective-permute-start(bf16[72,896]{1,0:T(8,128)(2,1)S(1)} %get-tuple-element.36), channel_id=1, source_target_pairs={{0,8},{4,12},{8,0},{12,4},{1,9},{5,13},{9,1},{13,5},{2,10},{6,14},... | collective-permute-start | bytes 387080 | tf_op jit(solution)/shard_map/ppermute | solution.py:26
  13.8 8.3 %collective-permute-start.2 = (bf16[72,896]{1,0:T(8,128)(2,1)S(1)}, bf16[72,896]{1,0:T(8,128)(2,1)S(1)}, u32[]{:S(2)}, u32[]{:S(2)}) collective-permute-start(bf16[72,896]{1,0:T(8,128)(2,1)S(1)} %get-tuple-element.31.refs_2_), channel_id=1, source_target_pairs={{0,2},{2,0},{1,3},{3,1},{4,6},{6,4},{5,7},{7,5},{8,10},{10,8},{9,1... | collective-permute-start | bytes 387080 | tf_op jit(solution)/shard_map/ppermute | solution.py:26
  15.3 6.8 %collective-permute-start.1 = (bf16[72,896]{1,0:T(8,128)(2,1)S(1)}, bf16[72,896]{1,0:T(8,128)(2,1)}, u32[]{:S(2)}, u32[]{:S(2)}) collective-permute-start(bf16[72,896]{1,0:T(8,128)(2,1)S(1)} %collective-permute-done.refs_0_), channel_id=1, source_target_pairs={{0,2},{2,0},{1,3},{3,1},{4,6},{6,4},{5,7},{7,5},{8,10},{10,8},{9,1... | collective-permute-start | bytes 387080 | tf_op jit(solution)/shard_map/ppermute | solution.py:26
  15.8 14.5 %collective-permute-start.6 = (bf16[72,896]{1,0:T(8,128)(2,1)}, bf16[72,896]{1,0:T(8,128)(2,1)S(1)}, u32[]{:S(2)}, u32[]{:S(2)}) collective-permute-start(bf16[72,896]{1,0:T(8,128)(2,1)} %get-tuple-element.43), channel_id=1, source_target_pairs={{0,4},{4,0},{8,12},{12,8},{1,5},{5,1},{9,13},{13,9},{2,6},{6,2},{1... | collective-permute-start | bytes 387080 | tf_op jit(solution)/shard_map/ppermute | solution.py:26
  22.2 6.2 %copy-start.13 = (bf16[72,896]{1,0:T(8,128)(2,1)}, bf16[72,896]{1,0:T(8,128)(2,1)S(1)}, u32[]{:S(2)}) copy-start(bf16[72,896]{1,0:T(8,128)(2,1)S(1)} %collective-permute-done.2.refs_3_.earlier_ref) | copy-start | bytes 387076
  24.6 5.2 %copy-start.11 = (bf16[72,896]{1,0:T(8,128)(2,1)S(1)}, bf16[72,896]{1,0:T(8,128)(2,1)}, u32[]{:S(2)}) copy-start(bf16[72,896]{1,0:T(8,128)(2,1)} %after.6.refs_5_.refs_0_) | copy-start | bytes 387076
  27.7 5.9 %collective-permute-start.4 = (bf16[144,512]{1,0:T(8,128)(2,1)}, bf16[144,512]{1,0:T(8,128)(2,1)S(1)}, u32[]{:S(2)}, u32[]{:S(2)}) collective-permute-start(bf16[144,512]{1,0:T(8,128)(2,1)} %get-tuple-element.38), channel_id=1, source_target_pairs={{0,1},{1,0},{2,3},{3,2},{4,5},{5,4},{6,7},{7,6},{8,9},{9,8},{10,11... | collective-permute-start | bytes 442376 | tf_op jit(solution)/shard_map/ppermute | solution.py:26
  28.3 5.2 %collective-permute-start.8 = (bf16[128,256]{1,0:T(8,128)(2,1)}, bf16[128,256]{1,0:T(8,128)(2,1)}, u32[]{:S(2)}, u32[]{:S(2)}) collective-permute-start(bf16[128,256]{1,0:T(8,128)(2,1)} %after.7), channel_id=1, source_target_pairs={{0,2},{2,0},{1,3},{3,1},{4,6},{6,4},{5,7},{7,5},{8,10},{10,8},{9,1... | collective-permute-start | bytes 196616 | tf_op jit(solution)/shard_map/ppermute | solution.py:26
  29.8 10.0 %collective-permute-start.5 = (bf16[72,896]{1,0:T(8,128)(2,1)S(1)}, bf16[72,896]{1,0:T(8,128)(2,1)S(1)}, u32[]{:S(2)}, u32[]{:S(2)}) collective-permute-start(bf16[72,896]{1,0:T(8,128)(2,1)S(1)} %copy-done.11), channel_id=1, source_target_pairs={{0,2},{2,0},{1,3},{3,1},{4,6},{6,4},{5,7},{7,5},{8,10},{10,8},{9,1... | collective-permute-start | bytes 387080 | tf_op jit(solution)/shard_map/ppermute | solution.py:26
  30.4 10.1 %collective-permute-start.7 = (bf16[72,896]{1,0:T(8,128)(2,1)S(1)}, bf16[72,896]{1,0:T(8,128)(2,1)}, u32[]{:S(2)}, u32[]{:S(2)}) collective-permute-start(bf16[72,896]{1,0:T(8,128)(2,1)S(1)} %collective-permute-done.6.refs_2_), channel_id=1, source_target_pairs={{0,2},{2,0},{1,3},{3,1},{4,6},{6,4},{5,7},{7,5},{8,10},{10,8},{9,1... | collective-permute-start | bytes 387080 | tf_op jit(solution)/shard_map/ppermute | solution.py:26
  37.2 6.5 %copy-start.14 = (bf16[72,896]{1,0:T(8,128)(2,1)}, bf16[72,896]{1,0:T(8,128)(2,1)S(1)}, u32[]{:S(2)}) copy-start(bf16[72,896]{1,0:T(8,128)(2,1)S(1)} %get-tuple-element.42.refs_0_) | copy-start | bytes 387076
  37.3 6.4 %copy-start.16 = (bf16[72,896]{1,0:T(8,128)(2,1)}, bf16[72,896]{1,0:T(8,128)(2,1)S(1)}, u32[]{:S(2)}) copy-start(bf16[72,896]{1,0:T(8,128)(2,1)S(1)} %get-tuple-element.55.value_ref) | copy-start | bytes 387076
  37.3 6.5 %copy-start.8 = (bf16[72,896]{1,0:T(8,128)(2,1)}, bf16[72,896]{1,0:T(8,128)(2,1)S(1)}, u32[]{:S(2)}) copy-start(bf16[72,896]{1,0:T(8,128)(2,1)S(1)} %get-tuple-element.47.refs_6_.earlier_ref) | copy-start | bytes 387076
  37.3 6.4 %collective-permute-start.10 = (bf16[72,896]{1,0:T(8,128)(2,1)S(1)}, bf16[72,896]{1,0:T(8,128)(2,1)}, u32[]{:S(2)}, u32[]{:S(2)}) collective-permute-start(bf16[72,896]{1,0:T(8,128)(2,1)S(1)} %get-tuple-element.50), channel_id=1, source_target_pairs={{0,2},{2,0},{1,3},{3,1},{4,6},{6,4},{5,7},{7,5},{8,10},{10,8},{9,1... | collective-permute-start | bytes 387080 | tf_op jit(solution)/shard_map/ppermute | solution.py:26
  43.7 2.4 %collective-permute-start.9 = (bf16[160,512]{1,0:T(8,128)(2,1)}, bf16[160,512]{1,0:T(8,128)(2,1)S(1)}, u32[]{:S(2)}, u32[]{:S(2)}) collective-permute-start(bf16[160,512]{1,0:T(8,128)(2,1)} %get-tuple-element.49), channel_id=1, source_target_pairs={{0,1},{1,0},{2,3},{3,2},{4,5},{5,4},{6,7},{7,6},{8,9},{9,8},{10,11... | collective-permute-start | bytes 491528 | tf_op jit(solution)/shard_map/ppermute | solution.py:26
  44.7 18.1 %collective-permute-start.15 = (bf16[72,896]{1,0:T(8,128)(2,1)S(1)}, bf16[72,896]{1,0:T(8,128)(2,1)S(1)}, u32[]{:S(2)}, u32[]{:S(2)}) collective-permute-start(bf16[72,896]{1,0:T(8,128)(2,1)S(1)} %add_convert_fusion.2.refs_5_), channel_id=1, source_target_pairs={{0,12},{4,8},{8,4},{12,0},{1,13},{5,9},{9,5},{13,1},{2,14},{6,10},... | collective-permute-start | bytes 387080 | tf_op jit(solution)/shard_map/ppermute | solution.py:26
  49.5 18.5 %copy-start.15 = (bf16[72,896]{1,0:T(8,128)(2,1)S(1)}, bf16[72,896]{1,0:T(8,128)(2,1)}, u32[]{:S(2)}) copy-start(bf16[72,896]{1,0:T(8,128)(2,1)} %copy-done.14) | copy-start | bytes 387076
  49.5 6.3 %collective-permute-start.11 = (bf16[72,896]{1,0:T(8,128)(2,1)S(1)}, bf16[72,896]{1,0:T(8,128)(2,1)S(1)}, u32[]{:S(2)}, u32[]{:S(2)}) collective-permute-start(bf16[72,896]{1,0:T(8,128)(2,1)S(1)} %get-tuple-element.52), channel_id=1, source_target_pairs={{0,2},{2,0},{1,3},{3,1},{4,6},{6,4},{5,7},{7,5},{8,10},{10,8},{9,1... | collective-permute-start | bytes 387080 | tf_op jit(solution)/shard_map/ppermute | solution.py:26
  50.1 7.8 %collective-permute-start.13 = (bf16[72,896]{1,0:T(8,128)(2,1)S(1)}, bf16[72,896]{1,0:T(8,128)(2,1)S(1)}, u32[]{:S(2)}, u32[]{:S(2)}) collective-permute-start(bf16[72,896]{1,0:T(8,128)(2,1)S(1)} %get-tuple-element.54), channel_id=1, source_target_pairs={{0,2},{2,0},{1,3},{3,1},{4,6},{6,4},{5,7},{7,5},{8,10},{10,8},{9,1... | collective-permute-start | bytes 387080 | tf_op jit(solution)/shard_map/ppermute | solution.py:26
  55.9 7.0 %collective-permute-start.12 = (bf16[72,896]{1,0:T(8,128)(2,1)S(1)}, bf16[72,896]{1,0:T(8,128)(2,1)S(1)}, u32[]{:S(2)}, u32[]{:S(2)}) collective-permute-start(bf16[72,896]{1,0:T(8,128)(2,1)S(1)} %add_convert_fusion.1), channel_id=1, source_target_pairs={{0,4},{4,0},{8,12},{12,8},{1,5},{5,1},{9,13},{13,9},{2,6},{6,2},{1... | collective-permute-start | bytes 387080 | tf_op jit(solution)/shard_map/ppermute | solution.py:26
  59.6 8.5 %collective-permute-start.14 = (bf16[72,896]{1,0:T(8,128)(2,1)S(1)}, bf16[72,896]{1,0:T(8,128)(2,1)S(1)}, u32[]{:S(2)}, u32[]{:S(2)}) collective-permute-start(bf16[72,896]{1,0:T(8,128)(2,1)S(1)} %add_convert_fusion.earlier_ref), channel_id=1, source_target_pairs={{0,8},{4,12},{8,0},{12,4},{1,9},{5,13},{9,1},{13,5},{2,10},{6,14},... | collective-permute-start | bytes 387080 | tf_op jit(solution)/shard_map/ppermute | solution.py:26
  60.8 5.2 %collective-permute-start.16 = (bf16[72,896]{1,0:T(8,128)(2,1)}, bf16[72,896]{1,0:T(8,128)(2,1)S(1)}, u32[]{:S(2)}, u32[]{:S(2)}) collective-permute-start(bf16[72,896]{1,0:T(8,128)(2,1)} %after.11), channel_id=1, source_target_pairs={{0,2},{2,0},{1,3},{3,1},{4,6},{6,4},{5,7},{7,5},{8,10},{10,8},{9,1... | collective-permute-start | bytes 387080 | tf_op jit(solution)/shard_map/ppermute | solution.py:26
  (15 other events, 18.8 us)

commit v4 on v3

--- a/solution.py
+++ b/solution.py
@@ -61,6 +61,7 @@
         in_specs=[ANY, ANY],
         out_specs=ANY,
         input_output_aliases={0: 0},
+        compiler_params=pltpu.CompilerParams(vmem_limit_bytes=1 << 17),
         cost_estimate=pl.CostEstimate(flops=0, bytes_accessed=cost, transcendentals=0),
         name="after",
     )(value, earlier)

time: 70 us -> 54 us (0.77)
  local copies, waits for them, and re-layouts: 13.8 us -> 0.01 us
  starting transfers between devices: 19.3 us -> 27.8 us
  Pallas kernels: 14.1 us -> 10.4 us
  other arithmetic: 4.61 us -> 1.01 us
  waiting for transfers between devices: 16.8 us -> 13.9 us
    unnamed x44 -> x0, local copies, waits for them, and re-layouts: 13.1 us -> none
    ppermute x17, starting transfers between devices: 19.3 us -> 27.8 us  [swap(): return lax.ppermute(value, axis, [(i, i ^ step) for i in range(count)])]
    pallas_call x7, Pallas kernels: 14.1 us -> 10.4 us  [call(): pl.pallas_call(kernel, out_shape=outs, in_specs=specs, out_specs=[VMEM] *...]
    ppermute x17, waiting for transfers between devices: 16.8 us -> 13.9 us  [swap(): return lax.ppermute(value, axis, [(i, i ^ step) for i in range(count)])]
    convert_element_type x3, other arithmetic: 2.03 us -> 0.1 us  [local(): moved = total.astype(bf16)]
    reduce_sum x1, other arithmetic: 0.96 us -> 0.12 us  [local(): jnp.sum(values * values, axis=1)]
    convert_element_type x1, other arithmetic: 1.59 us -> 0.75 us  [local(): d_latent = (inverse_rms * gained - values * inverse_rms ** 3 * row_sums[1...]
  transfers between devices with their start and end apart: 17 -> 17, of which waited for: 6 -> 8; matrix products, arithmetic and copies ran while one was open for 8% -> 2% of each run, Pallas kernels for 16% -> 13%
where the time goes in v4:
time: 54 us; the launch traced here: 53.9 us
  starting transfers between devices  27.8 us (51%)
  waiting for transfers between devices  13.9 us (26%)
  Pallas kernels  10.4 us (19%)
  other arithmetic  1.01 us (2%)
  between operations  0.76 us (1%)
    ppermute x17, starting transfers between devices, swap(): return lax.ppermute(value, axis, [(i, i ^ step) for i in range(count)])  27.8 us
    ppermute x17, waiting for transfers between devices, swap(): return lax.ppermute(value, axis, [(i, i ^ step) for i in range(count)])  13.9 us
    pallas_call x7, Pallas kernels, call(): pl.pallas_call(kernel, out_shape=outs, in_specs=specs, out_specs=[VMEM] *...  10.4 us
  transfers between devices with their start and end apart: 17, of which 8 were waited for; matrix products, arithmetic and copies ran while one was open for 2% of the time, Pallas kernels for 13%

profile of v4, /device:TPU:0, one launch (start us, length us, event | category | flops | bytes accessed | tf_op | source)
XLA Modules:
  0.0 53.9 jit_solution(13340812833124494565)
XLA Ops:
  0.6 1.9 %pack.1 = (bf16[72,896]{1,0:T(8,128)(2,1)S(1)}, bf16[72,896]{1,0:T(8,128)(2,1)S(1)}, bf16[2,4,72,128]{3,2,1,0:T(8,128)(2,1)S(1)}, f32[1,128]{1,0:T(1,128)S(1)}, ...) custom-call(s32[1,128]{1,0:T(1,128)} %bitcast.36, f32[1,128]{1,0:T(1,128)} %bitcast.37, f32[14,128]{1,0:T(8,128)} %bitcast.30, ...), custom_call_target="tpu_custom_call" | custom-call | tf_op jit(solution)/shard_map/pack/pallas_call | solution.py:45
  2.5 5.1 %collective-permute-start = (bf16[72,896]{1,0:T(8,128)(2,1)S(1)}, bf16[72,896]{1,0:T(8,128)(2,1)S(1)}, u32[]{:S(2)}, u32[]{:S(2)}) collective-permute-start(bf16[72,896]{1,0:T(8,128)(2,1)S(1)} %get-tuple-element.30.earlier_ref), channel_id=1, source_target_pairs={{0,12},{4,8},{8,4},{12,0},{1,13},{5,9},{9,5},{13,1},{2,14},{6,10},... | collective-permute-start | bytes 387080 | tf_op jit(solution)/shard_map/ppermute | solution.py:26
  7.7 3.0 %pack_more.1 = (bf16[72,896]{1,0:T(8,128)(2,1)S(1)}, bf16[72,896]{1,0:T(8,128)(2,1)S(1)}, bf16[2,128,256]{2,1,0:T(8,128)(2,1)S(1)}, bf16[512,1792]{1,0:T(8,128)(...) custom-call(bf16[2,4,72,128]{3,2,1,0:T(8,128)(2,1)S(1)} %get-tuple-e, ...), custom_call_target="tpu_custom_call" | custom-call | bytes 33554432 | tf_op jit(solution)/shard_map/pack_more/pallas_call | solution.py:45
  10.8 1.6 %collective-permute-start.2 = (bf16[72,896]{1,0:T(8,128)(2,1)S(1)}, bf16[72,896]{1,0:T(8,128)(2,1)S(1)}, u32[]{:S(2)}, u32[]{:S(2)}) collective-permute-start(bf16[72,896]{1,0:T(8,128)(2,1)S(1)} %get-tuple-element.31.refs_2_), channel_id=1, source_target_pairs={{0,2},{2,0},{1,3},{3,1},{4,6},{6,4},{5,7},{7,5},{8,10},{10,8},{9,1... | collective-permute-start | bytes 387080 | tf_op jit(solution)/shard_map/ppermute | solution.py:26
  12.9 5.0 %collective-permute-start.6 = (bf16[72,896]{1,0:T(8,128)(2,1)S(1)}, bf16[72,896]{1,0:T(8,128)(2,1)S(1)}, u32[]{:S(2)}, u32[]{:S(2)}) collective-permute-start(bf16[72,896]{1,0:T(8,128)(2,1)S(1)} %get-tuple-element.43), channel_id=1, source_target_pairs={{0,4},{4,0},{8,12},{12,8},{1,5},{5,1},{9,13},{13,9},{2,6},{6,2},{1... | collective-permute-start | bytes 387080 | tf_op jit(solution)/shard_map/ppermute | solution.py:26
  17.9 0.8 %collective-permute-done.3.value_ref = bf16[72,896]{1,0:T(8,128)(2,1)S(1)} collective-permute-done((bf16[72,896]{1,0:T(8,128)(2,1)S(1)}, bf16[72,896]{1,0:T(8,128)(2,1)S(1)}, u32[]{:S(2)}, u32[]{:S(2)}) %collective-permute-start.3) | collective-permute-done | bytes 129056 | tf_op jit(solution)/shard_map/ppermute | solution.py:26
  19.5 1.5 %collective-permute-start.8 = (bf16[128,256]{1,0:T(8,128)(2,1)S(1)}, bf16[128,256]{1,0:T(8,128)(2,1)S(1)}, u32[]{:S(2)}, u32[]{:S(2)}) collective-permute-start(bf16[128,256]{1,0:T(8,128)(2,1)S(1)} %after.7), channel_id=1, source_target_pairs={{0,2},{2,0},{1,3},{3,1},{4,6},{6,4},{5,7},{7,5},{8,10},{10,8},{9,1... | collective-permute-start | bytes 196616 | tf_op jit(solution)/shard_map/ppermute | solution.py:26
  21.6 1.5 %collective-permute-start.7 = (bf16[72,896]{1,0:T(8,128)(2,1)S(1)}, bf16[72,896]{1,0:T(8,128)(2,1)S(1)}, u32[]{:S(2)}, u32[]{:S(2)}) collective-permute-start(bf16[72,896]{1,0:T(8,128)(2,1)S(1)} %collective-permute-done.6.refs_2_), channel_id=1, source_target_pairs={{0,2},{2,0},{1,3},{3,1},{4,6},{6,4},{5,7},{7,5},{8,10},{10,8},{9,1... | collective-permute-start | bytes 387080 | tf_op jit(solution)/shard_map/ppermute | solution.py:26
  23.1 1.2 %collective-permute-done.8.value_ref = bf16[128,256]{1,0:T(8,128)(2,1)S(1)} collective-permute-done((bf16[128,256]{1,0:T(8,128)(2,1)S(1)}, bf16[128,256]{1,0:T(8,128)(2,1)S(1)}, u32[]{:S(2)}, u32[]{:S(2)}) %collective-permute-start.8) | collective-permute-done | bytes 65568 | tf_op jit(solution)/shard_map/ppermute | solution.py:26
  24.3 1.2 %back.2 = (bf16[72,896]{1,0:T(8,128)(2,1)S(1)}, bf16[72,896]{1,0:T(8,128)(2,1)S(1)}, bf16[72,896]{1,0:T(8,128)(2,1)S(1)}, bf16[72,896]{1,0:T(8,128)(2,1)S(1)}) custom-call(f32[144,512]{1,0:T(8,128)S(1)} %get-tuple-element.37.sum_ref.earlier_ref, bf16[144,512]{1,0:T(8,128)(2,1)S(1)} %collective-permute-done.4.other_ref, ...), custom_call_target="tpu_custom_call" | custom-call | tf_op jit(solution)/shard_map/back/pallas_call | solution.py:45
  25.5 1.8 %collective-permute-start.10 = (bf16[72,896]{1,0:T(8,128)(2,1)S(1)}, bf16[72,896]{1,0:T(8,128)(2,1)S(1)}, u32[]{:S(2)}, u32[]{:S(2)}) collective-permute-start(bf16[72,896]{1,0:T(8,128)(2,1)S(1)} %get-tuple-element.50), channel_id=1, source_target_pairs={{0,2},{2,0},{1,3},{3,1},{4,6},{6,4},{5,7},{7,5},{8,10},{10,8},{9,1... | collective-permute-start | bytes 387080 | tf_op jit(solution)/shard_map/ppermute | solution.py:26
  27.4 2.7 %collective-permute-done.7.refs_3_ = bf16[72,896]{1,0:T(8,128)(2,1)S(1)} collective-permute-done((bf16[72,896]{1,0:T(8,128)(2,1)S(1)}, bf16[72,896]{1,0:T(8,128)(2,1)S(1)}, u32[]{:S(2)}, u32[]{:S(2)}) %collective-permute-start.7) | collective-permute-done | bytes 129056 | tf_op jit(solution)/shard_map/ppermute | solution.py:26
  31.0 1.4 %collective-permute-done.10.value_ref = bf16[72,896]{1,0:T(8,128)(2,1)S(1)} collective-permute-done((bf16[72,896]{1,0:T(8,128)(2,1)S(1)}, bf16[72,896]{1,0:T(8,128)(2,1)S(1)}, u32[]{:S(2)}, u32[]{:S(2)}) %collective-permute-start.10) | collective-permute-done | bytes 129056 | tf_op jit(solution)/shard_map/ppermute | solution.py:26
  32.3 2.5 %collective-permute-start.15 = (bf16[72,896]{1,0:T(8,128)(2,1)S(1)}, bf16[72,896]{1,0:T(8,128)(2,1)S(1)}, u32[]{:S(2)}, u32[]{:S(2)}) collective-permute-start(bf16[72,896]{1,0:T(8,128)(2,1)S(1)} %add_convert_fusion.2.refs_5_), channel_id=1, source_target_pairs={{0,12},{4,8},{8,4},{12,0},{1,13},{5,9},{9,5},{13,1},{2,14},{6,10},... | collective-permute-start | bytes 387080 | tf_op jit(solution)/shard_map/ppermute | solution.py:26
  34.9 1.3 %back.3 = (bf16[72,896]{1,0:T(8,128)(2,1)S(1)}, bf16[72,896]{1,0:T(8,128)(2,1)S(1)}, bf16[72,896]{1,0:T(8,128)(2,1)S(1)}, bf16[72,896]{1,0:T(8,128)(2,1)S(1)}) custom-call(f32[144,512]{1,0:T(8,128)S(1)} %get-tuple-element.48.refs_0_, bf16[160,512]{1,0:T(8,128)(2,1)S(1)} %collective-permute-done.9.refs_1_, ...), custom_call_target="tpu_custom_call" | custom-call | tf_op jit(solution)/shard_map/back/pallas_call | solution.py:45
  36.2 1.4 %collective-permute-start.11 = (bf16[72,896]{1,0:T(8,128)(2,1)S(1)}, bf16[72,896]{1,0:T(8,128)(2,1)S(1)}, u32[]{:S(2)}, u32[]{:S(2)}) collective-permute-start(bf16[72,896]{1,0:T(8,128)(2,1)S(1)} %get-tuple-element.52), channel_id=1, source_target_pairs={{0,2},{2,0},{1,3},{3,1},{4,6},{6,4},{5,7},{7,5},{8,10},{10,8},{9,1... | collective-permute-start | bytes 387080 | tf_op jit(solution)/shard_map/ppermute | solution.py:26
  38.3 4.0 %collective-permute-done.11 = bf16[72,896]{1,0:T(8,128)(2,1)S(1)} collective-permute-done((bf16[72,896]{1,0:T(8,128)(2,1)S(1)}, bf16[72,896]{1,0:T(8,128)(2,1)S(1)}, u32[]{:S(2)}, u32[]{:S(2)}) %collective-permute-start.11) | collective-permute-done | bytes 129056 | tf_op jit(solution)/shard_map/ppermute | solution.py:26
  42.4 2.4 %collective-permute-start.12 = (bf16[72,896]{1,0:T(8,128)(2,1)S(1)}, bf16[72,896]{1,0:T(8,128)(2,1)S(1)}, u32[]{:S(2)}, u32[]{:S(2)}) collective-permute-start(bf16[72,896]{1,0:T(8,128)(2,1)S(1)} %add_convert_fusion.1), channel_id=1, source_target_pairs={{0,4},{4,0},{8,12},{12,8},{1,5},{5,1},{9,13},{13,9},{2,6},{6,2},{1... | collective-permute-start | bytes 387080 | tf_op jit(solution)/shard_map/ppermute | solution.py:26
  44.8 1.6 %collective-permute-start.14 = (bf16[72,896]{1,0:T(8,128)(2,1)S(1)}, bf16[72,896]{1,0:T(8,128)(2,1)S(1)}, u32[]{:S(2)}, u32[]{:S(2)}) collective-permute-start(bf16[72,896]{1,0:T(8,128)(2,1)S(1)} %add_convert_fusion.earlier_ref), channel_id=1, source_target_pairs={{0,8},{4,12},{8,0},{12,4},{1,9},{5,13},{9,1},{13,5},{2,10},{6,14},... | collective-permute-start | bytes 387080 | tf_op jit(solution)/shard_map/ppermute | solution.py:26
  46.4 1.4 %collective-permute-start.16 = (bf16[72,896]{1,0:T(8,128)(2,1)S(1)}, bf16[72,896]{1,0:T(8,128)(2,1)S(1)}, u32[]{:S(2)}, u32[]{:S(2)}) collective-permute-start(bf16[72,896]{1,0:T(8,128)(2,1)S(1)} %after.11), channel_id=1, source_target_pairs={{0,2},{2,0},{1,3},{3,1},{4,6},{6,4},{5,7},{7,5},{8,10},{10,8},{9,1... | collective-permute-start | bytes 387080 | tf_op jit(solution)/shard_map/ppermute | solution.py:26
  47.8 0.8 %fusion.5 = bf16[128,256]{1,0:T(8,128)(2,1)} fusion(bf16[128,256]{1,0:T(8,128)(2,1)S(1)} %get-tuple-element.44, bf16[128,256]{1,0:T(8,128)(2,1)S(1)} %after.8, f32[128]{0:T(128)S(1)} %slice_bitcast_fusion.1, f32[128]{0:T(128)S(1)} %get-tuple-element.58, f32[128]{0:T(128)S(1)} %get-tuple-element.59, f32[256]{0:T(256)S(1)} %bitcast.24, ...), kind=kLoop, calls=%fused_computation.11 | loop fusion | flops 360448 | bytes 264704 | tf_op jit(solution)/shard_map/convert_element_type | solution.py:375
  49.1 2.3 %collective-permute-done.16.refs_4_ = bf16[72,896]{1,0:T(8,128)(2,1)S(1)} collective-permute-done((bf16[72,896]{1,0:T(8,128)(2,1)S(1)}, bf16[72,896]{1,0:T(8,128)(2,1)S(1)}, u32[]{:S(2)}, u32[]{:S(2)}) %collective-permute-start.16) | collective-permute-done | bytes 129056 | tf_op jit(solution)/shard_map/ppermute | solution.py:26
  51.4 1.0 %collective-permute-done.14.refs_2_ = bf16[72,896]{1,0:T(8,128)(2,1)S(1)} collective-permute-done((bf16[72,896]{1,0:T(8,128)(2,1)S(1)}, bf16[72,896]{1,0:T(8,128)(2,1)S(1)}, u32[]{:S(2)}, u32[]{:S(2)}) %collective-permute-start.14) | collective-permute-done | bytes 129056 | tf_op jit(solution)/shard_map/ppermute | solution.py:26
  52.4 1.4 %unpack.1 = bf16[128,1792]{1,0:T(8,128)(2,1)} custom-call(bf16[2,4,72,128]{3,2,1,0:T(8,128)(2,1)S(1)} %get-tuple-element.29.place_ref, bf16[72,896]{1,0:T(8,128)(2,1)S(1)} %get-tuple-element.42.refs_0_, bf16[72,896]{1,0:T(8,128)(2,1)S(1)} %collective-permute-done.12.refs_1_, bf16[72,896]{1,0:T(8,128)(2,1)S(1)} %collective-permute-done.14.refs_2_, ...), custom_call_target="tpu_custom_call" | custom-call | tf_op jit(solution)/shard_map/unpack/pallas_call | solution.py:45
  (34 shorter events, 4.2 us)
Async XLA Ops:
  2.5 9.8 %collective-permute-start = (bf16[72,896]{1,0:T(8,128)(2,1)S(1)}, bf16[72,896]{1,0:T(8,128)(2,1)S(1)}, u32[]{:S(2)}, u32[]{:S(2)}) collective-permute-start(bf16[72,896]{1,0:T(8,128)(2,1)S(1)} %get-tuple-element.30.earlier_ref), channel_id=1, source_target_pairs={{0,12},{4,8},{8,4},{12,0},{1,13},{5,9},{9,5},{13,1},{2,14},{6,10},... | collective-permute-start | bytes 387080 | tf_op jit(solution)/shard_map/ppermute | solution.py:26
  10.7 8.0 %collective-permute-start.3 = (bf16[72,896]{1,0:T(8,128)(2,1)S(1)}, bf16[72,896]{1,0:T(8,128)(2,1)S(1)}, u32[]{:S(2)}, u32[]{:S(2)}) collective-permute-start(bf16[72,896]{1,0:T(8,128)(2,1)S(1)} %get-tuple-element.36), channel_id=1, source_target_pairs={{0,8},{4,12},{8,0},{12,4},{1,9},{5,13},{9,1},{13,5},{2,10},{6,14},... | collective-permute-start | bytes 387080 | tf_op jit(solution)/shard_map/ppermute | solution.py:26
  10.8 7.9 %collective-permute-start.2 = (bf16[72,896]{1,0:T(8,128)(2,1)S(1)}, bf16[72,896]{1,0:T(8,128)(2,1)S(1)}, u32[]{:S(2)}, u32[]{:S(2)}) collective-permute-start(bf16[72,896]{1,0:T(8,128)(2,1)S(1)} %get-tuple-element.31.refs_2_), channel_id=1, source_target_pairs={{0,2},{2,0},{1,3},{3,1},{4,6},{6,4},{5,7},{7,5},{8,10},{10,8},{9,1... | collective-permute-start | bytes 387080 | tf_op jit(solution)/shard_map/ppermute | solution.py:26
  12.4 6.3 %collective-permute-start.1 = (bf16[72,896]{1,0:T(8,128)(2,1)S(1)}, bf16[72,896]{1,0:T(8,128)(2,1)S(1)}, u32[]{:S(2)}, u32[]{:S(2)}) collective-permute-start(bf16[72,896]{1,0:T(8,128)(2,1)S(1)} %collective-permute-done.refs_0_), channel_id=1, source_target_pairs={{0,2},{2,0},{1,3},{3,1},{4,6},{6,4},{5,7},{7,5},{8,10},{10,8},{9,1... | collective-permute-start | bytes 387080 | tf_op jit(solution)/shard_map/ppermute | solution.py:26
  12.9 8.7 %collective-permute-start.6 = (bf16[72,896]{1,0:T(8,128)(2,1)S(1)}, bf16[72,896]{1,0:T(8,128)(2,1)S(1)}, u32[]{:S(2)}, u32[]{:S(2)}) collective-permute-start(bf16[72,896]{1,0:T(8,128)(2,1)S(1)} %get-tuple-element.43), channel_id=1, source_target_pairs={{0,4},{4,0},{8,12},{12,8},{1,5},{5,1},{9,13},{13,9},{2,6},{6,2},{1... | collective-permute-start | bytes 387080 | tf_op jit(solution)/shard_map/ppermute | solution.py:26
  19.4 4.9 %collective-permute-start.4 = (bf16[144,512]{1,0:T(8,128)(2,1)S(1)}, bf16[144,512]{1,0:T(8,128)(2,1)S(1)}, u32[]{:S(2)}, u32[]{:S(2)}) collective-permute-start(bf16[144,512]{1,0:T(8,128)(2,1)S(1)} %get-tuple-element.38), channel_id=1, source_target_pairs={{0,1},{1,0},{2,3},{3,2},{4,5},{5,4},{6,7},{7,6},{8,9},{9,8},{10,11... | collective-permute-start | bytes 442376 | tf_op jit(solution)/shard_map/ppermute | solution.py:26
  19.5 4.7 %collective-permute-start.8 = (bf16[128,256]{1,0:T(8,128)(2,1)S(1)}, bf16[128,256]{1,0:T(8,128)(2,1)S(1)}, u32[]{:S(2)}, u32[]{:S(2)}) collective-permute-start(bf16[128,256]{1,0:T(8,128)(2,1)S(1)} %after.7), channel_id=1, source_target_pairs={{0,2},{2,0},{1,3},{3,1},{4,6},{6,4},{5,7},{7,5},{8,10},{10,8},{9,1... | collective-permute-start | bytes 196616 | tf_op jit(solution)/shard_map/ppermute | solution.py:26
  21.1 6.4 %collective-permute-start.5 = (bf16[72,896]{1,0:T(8,128)(2,1)S(1)}, bf16[72,896]{1,0:T(8,128)(2,1)S(1)}, u32[]{:S(2)}, u32[]{:S(2)}) collective-permute-start(bf16[72,896]{1,0:T(8,128)(2,1)S(1)} %after.6.refs_5_.refs_0_), channel_id=1, source_target_pairs={{0,2},{2,0},{1,3},{3,1},{4,6},{6,4},{5,7},{7,5},{8,10},{10,8},{9,1... | collective-permute-start | bytes 387080 | tf_op jit(solution)/shard_map/ppermute | solution.py:26
  21.6 8.5 %collective-permute-start.7 = (bf16[72,896]{1,0:T(8,128)(2,1)S(1)}, bf16[72,896]{1,0:T(8,128)(2,1)S(1)}, u32[]{:S(2)}, u32[]{:S(2)}) collective-permute-start(bf16[72,896]{1,0:T(8,128)(2,1)S(1)} %collective-permute-done.6.refs_2_), channel_id=1, source_target_pairs={{0,2},{2,0},{1,3},{3,1},{4,6},{6,4},{5,7},{7,5},{8,10},{10,8},{9,1... | collective-permute-start | bytes 387080 | tf_op jit(solution)/shard_map/ppermute | solution.py:26
  25.5 6.8 %collective-permute-start.10 = (bf16[72,896]{1,0:T(8,128)(2,1)S(1)}, bf16[72,896]{1,0:T(8,128)(2,1)S(1)}, u32[]{:S(2)}, u32[]{:S(2)}) collective-permute-start(bf16[72,896]{1,0:T(8,128)(2,1)S(1)} %get-tuple-element.50), channel_id=1, source_target_pairs={{0,2},{2,0},{1,3},{3,1},{4,6},{6,4},{5,7},{7,5},{8,10},{10,8},{9,1... | collective-permute-start | bytes 387080 | tf_op jit(solution)/shard_map/ppermute | solution.py:26
  30.9 4.0 %collective-permute-start.9 = (bf16[160,512]{1,0:T(8,128)(2,1)S(1)}, bf16[160,512]{1,0:T(8,128)(2,1)S(1)}, u32[]{:S(2)}, u32[]{:S(2)}) collective-permute-start(bf16[160,512]{1,0:T(8,128)(2,1)S(1)} %get-tuple-element.49), channel_id=1, source_target_pairs={{0,1},{1,0},{2,3},{3,2},{4,5},{5,4},{6,7},{7,6},{8,9},{9,8},{10,11... | collective-permute-start | bytes 491528 | tf_op jit(solution)/shard_map/ppermute | solution.py:26
  32.3 16.2 %collective-permute-start.15 = (bf16[72,896]{1,0:T(8,128)(2,1)S(1)}, bf16[72,896]{1,0:T(8,128)(2,1)S(1)}, u32[]{:S(2)}, u32[]{:S(2)}) collective-permute-start(bf16[72,896]{1,0:T(8,128)(2,1)S(1)} %add_convert_fusion.2.refs_5_), channel_id=1, source_target_pairs={{0,12},{4,8},{8,4},{12,0},{1,13},{5,9},{9,5},{13,1},{2,14},{6,10},... | collective-permute-start | bytes 387080 | tf_op jit(solution)/shard_map/ppermute | solution.py:26
  36.2 6.1 %collective-permute-start.11 = (bf16[72,896]{1,0:T(8,128)(2,1)S(1)}, bf16[72,896]{1,0:T(8,128)(2,1)S(1)}, u32[]{:S(2)}, u32[]{:S(2)}) collective-permute-start(bf16[72,896]{1,0:T(8,128)(2,1)S(1)} %get-tuple-element.52), channel_id=1, source_target_pairs={{0,2},{2,0},{1,3},{3,1},{4,6},{6,4},{5,7},{7,5},{8,10},{10,8},{9,1... | collective-permute-start | bytes 387080 | tf_op jit(solution)/shard_map/ppermute | solution.py:26
  37.6 7.1 %collective-permute-start.13 = (bf16[72,896]{1,0:T(8,128)(2,1)S(1)}, bf16[72,896]{1,0:T(8,128)(2,1)S(1)}, u32[]{:S(2)}, u32[]{:S(2)}) collective-permute-start(bf16[72,896]{1,0:T(8,128)(2,1)S(1)} %get-tuple-element.54), channel_id=1, source_target_pairs={{0,2},{2,0},{1,3},{3,1},{4,6},{6,4},{5,7},{7,5},{8,10},{10,8},{9,1... | collective-permute-start | bytes 387080 | tf_op jit(solution)/shard_map/ppermute | solution.py:26
  42.4 6.7 %collective-permute-start.12 = (bf16[72,896]{1,0:T(8,128)(2,1)S(1)}, bf16[72,896]{1,0:T(8,128)(2,1)S(1)}, u32[]{:S(2)}, u32[]{:S(2)}) collective-permute-start(bf16[72,896]{1,0:T(8,128)(2,1)S(1)} %add_convert_fusion.1), channel_id=1, source_target_pairs={{0,4},{4,0},{8,12},{12,8},{1,5},{5,1},{9,13},{13,9},{2,6},{6,2},{1... | collective-permute-start | bytes 387080 | tf_op jit(solution)/shard_map/ppermute | solution.py:26
  44.8 7.6 %collective-permute-start.14 = (bf16[72,896]{1,0:T(8,128)(2,1)S(1)}, bf16[72,896]{1,0:T(8,128)(2,1)S(1)}, u32[]{:S(2)}, u32[]{:S(2)}) collective-permute-start(bf16[72,896]{1,0:T(8,128)(2,1)S(1)} %add_convert_fusion.earlier_ref), channel_id=1, source_target_pairs={{0,8},{4,12},{8,0},{12,4},{1,9},{5,13},{9,1},{13,5},{2,10},{6,14},... | collective-permute-start | bytes 387080 | tf_op jit(solution)/shard_map/ppermute | solution.py:26
  46.4 4.9 %collective-permute-start.16 = (bf16[72,896]{1,0:T(8,128)(2,1)S(1)}, bf16[72,896]{1,0:T(8,128)(2,1)S(1)}, u32[]{:S(2)}, u32[]{:S(2)}) collective-permute-start(bf16[72,896]{1,0:T(8,128)(2,1)S(1)} %after.11), channel_id=1, source_target_pairs={{0,2},{2,0},{1,3},{3,1},{4,6},{6,4},{5,7},{7,5},{8,10},{10,8},{9,1... | collective-permute-start | bytes 387080 | tf_op jit(solution)/shard_map/ppermute | solution.py:26

commit v5 on v4

--- a/solution.py
+++ b/solution.py
@@ -21,9 +21,10 @@
     return lax.dot_general(a, b, dims, precision=precision, preferred_element_type=jnp.float32)
 
 
-def swap(value, axis, step):
+def swap(value, axis, step, what):
     count = lax.axis_size(axis)
-    return lax.ppermute(value, axis, [(i, i ^ step) for i in range(count)])
+    with jax.named_scope(f"{what}_{axis}"):
+        return lax.ppermute(value, axis, [(i, i ^ step) for i in range(count)])
 
 
 def pinned(*arrays):
@@ -49,7 +50,7 @@
         out_specs=[VMEM] * len(outs),
         scratch_shapes=scratch,
         compiler_params=pltpu.CompilerParams(vmem_limit_bytes=VMEM_LIMIT),
-        cost_estimate=pl.CostEstimate(flops=0, bytes_accessed=cost, transcendentals=0),
+        cost_estimate=pl.CostEstimate(flops=cost, bytes_accessed=0, transcendentals=0),
         name=name,
     )(*args, *earlier)
 
@@ -62,7 +63,7 @@
         out_specs=ANY,
         input_output_aliases={0: 0},
         compiler_params=pltpu.CompilerParams(vmem_limit_bytes=1 << 17),
-        cost_estimate=pl.CostEstimate(flops=0, bytes_accessed=cost, transcendentals=0),
+        cost_estimate=pl.CostEstimate(flops=cost, bytes_accessed=0, transcendentals=0),
         name="after",
     )(value, earlier)
 
@@ -217,10 +218,10 @@
 
 
 def groups_of(wide):
-    left = list(range(wide - 1, -1, -1))
     if wide < 4:
-        return [left]
-    return [[left[0], left[-1]]] + [left[i : min(i + 2, wide - 1)] for i in range(1, wide - 1, 2)]
+        return [list(range(wide - 1, -1, -1))]
+    left = list(range(wide - 2, 1, -1))
+    return [[wide - 1, 1, 0]] + [left[i : i + 2] for i in range(0, len(left), 2)]
 
 
 def local(
@@ -245,7 +246,7 @@
     f32, bf16 = jnp.float32, jnp.bfloat16
     block = pltpu.VMEM((rows, half), bf16)
     groups = groups_of(wide)
-    order, more = groups[0], [k for group in groups[1:] for k in reversed(group)]
+    order, more = groups[0], [k for group in groups[1:] for k in group]
     packed = call(
         functools.partial(pack_kernel, wide, most, order),
         [block] * len(order)
@@ -294,18 +295,18 @@
     shares, down, pre, gate, up, latent, latent_gain = blocks[len(more) :]
 
     def across(k, rows_of_k):
-        return [rows_of_k] + [swap(rows_of_k, "tp", j) for j in range(1, narrow)]
+        return [rows_of_k] + [swap(rows_of_k, "tp", j, f"rows{k}") for j in range(1, narrow)]
 
     taken = {0: across(0, packed[0])}
     first = groups[0][0]
     arrived = {}
     for k in order + more:
         if k:
-            arrived[k] = swap(packed[k], "ep", k)
+            arrived[k] = swap(packed[k], "ep", k, f"rows{k}")
             if len(groups) > 1 and k == groups[1][0]:
-                arrived[k] = after(arrived[k], packed[first], 1 << 25)
+                arrived[k] = after(arrived[k], packed[first], 1 << 31)
     latent_parts = [shares[0]] + [
-        swap(after(shares[j], taken[0][-1]), "tp", j) for j in range(1, narrow)
+        swap(shares[j], "tp", j, "latent") for j in range(1, narrow)
     ]
 
     returned = {}
@@ -317,11 +318,15 @@
             if k == 0:
                 continue
             taken[k] = across(k, arrived[k])
+            if received is not None:
+                taken[k][-1] = after(taken[k][-1], products[0])
+            elif k != first and narrow > 1:
+                taken[k][-1] = after(taken[k][-1], packed[first], 1 << 31)
         count = len(group) * narrow * most
         extra = group is groups[-1]
         if extra:
             if received is not None:
-                latent_parts[-1] = after(latent_parts[-1], summed)
+                latent_parts[-1] = after(latent_parts[-1], summed, 1 << 30)
             own_grad = sum(part.astype(f32) for part in latent_parts)
             gained = own_grad * latent_gain
             row_sums = jnp.stack(
@@ -337,9 +342,11 @@
             *([row_sums] if extra else []),
             down,
             name="hidden",
-            earlier=products[:1] if products else [arrived[g[0]] for g in groups[1:2]],
+            earlier=products[:1] if products else (),
         )
-        received = swap(sent, "sub", 1)
+        received = swap(sent, "sub", 1, f"hidden{group[0]}")
+        if moved is not None:
+            received = after(received, moved)
         products = call(
             functools.partial(back_kernel, most, narrow, group),
             [block] * (len(group) * narrow),
@@ -349,24 +356,25 @@
             gate,
             up,
             name="back",
-            earlier=(moved,) if moved is not None else (),
         )
         for at, k in enumerate(group):
             mine = products[at * narrow]
             if k == 0:
                 returned[0] = mine
                 own = products[1 + at * narrow : (at + 1) * narrow]
-            else:
-                others = [swap(products[at * narrow + j], "tp", j) for j in range(1, narrow)]
-                if k == group[0]:
-                    others[0] = after(others[0], mine, 1 << 24)
-                total = mine.astype(f32)
-                for other in others:
-                    total += other.astype(f32)
-                moved = total.astype(bf16)
-                returned[k] = swap(moved, "ep", k)
-                last = moved if k == group[0] else last
-    own = [swap(after(value, last), "tp", j + 1) for j, value in enumerate(own)]
+                continue
+            others = products[at * narrow + 1 : (at + 1) * narrow]
+            if k != group[0]:
+                others = [after(other, moved) for other in others]
+            others = [swap(other, "tp", j + 1, f"back{k}") for j, other in enumerate(others)]
+            total = mine.astype(f32)
+            for other in others:
+                total += other.astype(f32)
+            total = total.astype(bf16)
+            returned[k] = swap(total, "ep", k, f"back{k}")
+            if k == group[0]:
+                moved = total
+    own = [swap(after(value, moved), "tp", j + 1, "back0") for j, value in enumerate(own)]
     tail = received[count : count + 4, :tokens].astype(f32)
     row_sums = row_sums + tail[:2] + tail[2:]
     inverse_rms = lax.rsqrt(row_sums[0] / LAT + 1e-06)[:, None]

time: 54 us -> 50.3 us (0.931)
  starting transfers between devices: 27.8 us -> 19.8 us
  waiting for transfers between devices: 13.9 us -> 18.1 us
    ppermute x17, starting transfers between devices: 27.8 us -> 19.8 us  [swap(): return lax.ppermute(value, axis, [(i, i ^ step) for i in range(count)])]
    ppermute x17, waiting for transfers between devices: 13.9 us -> 18.1 us  [swap(): return lax.ppermute(value, axis, [(i, i ^ step) for i in range(count)])]
  transfers between devices with their start and end apart: 17 -> 17, of which waited for: 8 -> 9; matrix products, arithmetic and copies ran while one was open for 2% -> 2% of each run, Pallas kernels for 13% -> 14%
where the time goes in v5:
time: 50.3 us; the launch traced here: 50.2 us
  starting transfers between devices  19.8 us (39%)
  waiting for transfers between devices  18.1 us (36%)
  Pallas kernels  10.4 us (21%)
  other arithmetic  1.01 us (2%)
  between operations  0.75 us (1%)
    ppermute x17, starting transfers between devices, swap(): return lax.ppermute(value, axis, [(i, i ^ step) for i in range(count)])  19.8 us
    ppermute x17, waiting for transfers between devices, swap(): return lax.ppermute(value, axis, [(i, i ^ step) for i in range(count)])  18.1 us
    pallas_call x7, Pallas kernels, call(): pl.pallas_call(kernel, out_shape=outs, in_specs=specs, out_specs=[VMEM] *...  10.4 us
  transfers between devices with their start and end apart: 17, of which 9 were waited for; matrix products, arithmetic and copies ran while one was open for 2% of the time, Pallas kernels for 14%

profile of v5, /device:TPU:0, one launch (start us, length us, event | category | flops | bytes accessed | tf_op | source)
XLA Modules:
  0.0 50.2 jit_solution(6535241849583846159)
XLA Ops:
  0.6 2.1 %pack.1 = (bf16[72,896]{1,0:T(8,128)(2,1)S(1)}, bf16[72,896]{1,0:T(8,128)(2,1)S(1)}, bf16[72,896]{1,0:T(8,128)(2,1)S(1)}, bf16[2,4,72,128]{3,2,1,0:T(8,128)(2,1)...) custom-call(s32[1,128]{1,0:T(1,128)} %bitcast.36, f32[1,128]{1,0:T(1,128)} %bitcast.37, ...), custom_call_target="tpu_custom_call" | custom-call | tf_op jit(solution)/shard_map/pack/pallas_call | solution.py:46
  2.7 3.1 %collective-permute-start.2 = (bf16[72,896]{1,0:T(8,128)(2,1)S(1)}, bf16[72,896]{1,0:T(8,128)(2,1)S(1)}, u32[]{:S(2)}, u32[]{:S(2)}) collective-permute-start(bf16[72,896]{1,0:T(8,128)(2,1)S(1)} %get-tuple-element.31), channel_id=1, source_target_pairs={{0,4},{4,0},{8,12},{12,8},{1,5},{5,1},{9,13},{13,9},{2,6},{6,2},{1... | collective-permute-start | bytes 387080 | tf_op jit(solution)/shard_map/rows1_ep/ppermute | solution.py:27
  5.8 2.5 %collective-permute-start = (bf16[72,896]{1,0:T(8,128)(2,1)S(1)}, bf16[72,896]{1,0:T(8,128)(2,1)S(1)}, u32[]{:S(2)}, u32[]{:S(2)}) collective-permute-start(bf16[72,896]{1,0:T(8,128)(2,1)S(1)} %get-tuple-element.30.earlier_ref), channel_id=1, source_target_pairs={{0,12},{4,8},{8,4},{12,0},{1,13},{5,9},{9,5},{13,1},{2,14},{6,10},... | collective-permute-start | bytes 387080 | tf_op jit(solution)/shard_map/rows3_ep/ppermute | solution.py:27
  8.3 1.5 %collective-permute-start.4 = (bf16[72,896]{1,0:T(8,128)(2,1)S(1)}, bf16[72,896]{1,0:T(8,128)(2,1)S(1)}, u32[]{:S(2)}, u32[]{:S(2)}) collective-permute-start(bf16[72,896]{1,0:T(8,128)(2,1)S(1)} %get-tuple-element.32.refs_4_), channel_id=1, source_target_pairs={{0,2},{2,0},{1,3},{3,1},{4,6},{6,4},{5,7},{7,5},{8,10},{10,8},{9,1... | collective-permute-start | bytes 387080 | tf_op jit(solution)/shard_map/rows0_tp/ppermute | solution.py:27
  9.8 2.9 %pack_more.1 = (bf16[72,896]{1,0:T(8,128)(2,1)S(1)}, bf16[2,128,256]{2,1,0:T(8,128)(2,1)S(1)}, bf16[512,1792]{1,0:T(8,128)(2,1)S(1)}, bf16[2,4,72,512]{3,2,1,0:T...) custom-call(bf16[2,4,72,128]{3,2,1,0:T(8,128)(2,1)S(1)} %get-tuple-e, ...), custom_call_target="tpu_custom_call" | custom-call | flops 33554432 | tf_op jit(solution)/shard_map/pack_more/pallas_call | solution.py:46
  13.4 1.5 %collective-permute-start.11 = (bf16[128,256]{1,0:T(8,128)(2,1)S(1)}, bf16[128,256]{1,0:T(8,128)(2,1)S(1)}, u32[]{:S(2)}, u32[]{:S(2)}) collective-permute-start(bf16[128,256]{1,0:T(8,128)(2,1)S(1)} %slice_bitcast_fusion), channel_id=1, source_target_pairs={{0,2},{2,0},{1,3},{3,1},{4,6},{6,4},{5,7},{7,5},{8,10},{10,8},{9,1... | collective-permute-start | bytes 196616 | tf_op jit(solution)/shard_map/latent_tp/ppermute | solution.py:27
  14.9 0.9 %collective-permute-start.1 = (bf16[72,896]{1,0:T(8,128)(2,1)S(1)}, bf16[72,896]{1,0:T(8,128)(2,1)S(1)}, u32[]{:S(2)}, u32[]{:S(2)}) collective-permute-start(bf16[72,896]{1,0:T(8,128)(2,1)S(1)} %collective-permute-done.refs_0_), channel_id=1, source_target_pairs={{0,2},{2,0},{1,3},{3,1},{4,6},{6,4},{5,7},{7,5},{8,10},{10,8},{9,1... | collective-permute-start | bytes 387080 | tf_op jit(solution)/shard_map/rows3_tp/ppermute | solution.py:27
  15.8 3.5 %collective-permute-done.3.value_ref = bf16[72,896]{1,0:T(8,128)(2,1)S(1)} collective-permute-done((bf16[72,896]{1,0:T(8,128)(2,1)S(1)}, bf16[72,896]{1,0:T(8,128)(2,1)S(1)}, u32[]{:S(2)}, u32[]{:S(2)}) %collective-permute-start.3) | collective-permute-done | bytes 129056 | tf_op jit(solution)/shard_map/rows1_tp/ppermute | solution.py:27
  19.3 2.1 %collective-permute-done.1.refs_1_ = bf16[72,896]{1,0:T(8,128)(2,1)S(1)} collective-permute-done((bf16[72,896]{1,0:T(8,128)(2,1)S(1)}, bf16[72,896]{1,0:T(8,128)(2,1)S(1)}, u32[]{:S(2)}, u32[]{:S(2)}) %collective-permute-start.1) | collective-permute-done | bytes 129056 | tf_op jit(solution)/shard_map/rows3_tp/ppermute | solution.py:27
  21.4 0.8 %hidden.2 = (f32[216,512]{1,0:T(8,128)S(1)}, bf16[216,512]{1,0:T(8,128)(2,1)S(1)}) custom-call(bf16[72,896]{1,0:T(8,128)(2,1)S(1)} %collective-permute-done.refs_0_, bf16[72,896]{1,0:T(8,128)(2,1)S(1)} %collective-permute-done.1.refs_1_, bf16[72,896]{1,0:T(8,128)(2,1)S(1)} %collective-permute-done.2.refs_2_, bf16[72,896]{1,0:T(8,128)(2,1)S(1)} %after.7.refs_3_, ...), custom_call_target="tpu_custom_call" | custom-call | tf_op jit(solution)/shard_map/hidden/pallas_call | solution.py:46
  22.9 0.8 %collective-permute-done.5.other_ref = bf16[216,512]{1,0:T(8,128)(2,1)S(1)} collective-permute-done((bf16[216,512]{1,0:T(8,128)(2,1)S(1)}, bf16[216,512]{1,0:T(8,128)(2,1)S(1)}, u32[]{:S(2)}, u32[]{:S(2)}) %collective-permute-start.5) | collective-permute-done | bytes 221216 | tf_op jit(solution)/shard_map/hidden3_sub/ppermute | solution.py:27
  23.7 1.3 %back.2 = (bf16[72,896]{1,0:T(8,128)(2,1)S(1)}, bf16[72,896]{1,0:T(8,128)(2,1)S(1)}, bf16[72,896]{1,0:T(8,128)(2,1)S(1)}, bf16[72,896]{1,0:T(8,128)(2,1)S(1)}, b...) custom-call(f32[216,512]{1,0:T(8,128)S(1)} %get-tuple-element.37.sum_ref.earlier_ref, ...), custom_call_target="tpu_custom_call" | custom-call | tf_op jit(solution)/shard_map/back/pallas_call | solution.py:46
  25.9 2.4 %collective-permute-done.10.value_ref = bf16[72,896]{1,0:T(8,128)(2,1)S(1)} collective-permute-done((bf16[72,896]{1,0:T(8,128)(2,1)S(1)}, bf16[72,896]{1,0:T(8,128)(2,1)S(1)}, u32[]{:S(2)}, u32[]{:S(2)}) %collective-permute-start.10) | collective-permute-done | bytes 129056 | tf_op jit(solution)/shard_map/rows2_tp/ppermute | solution.py:27
  29.1 1.8 %collective-permute-done.6 = bf16[72,896]{1,0:T(8,128)(2,1)S(1)} collective-permute-done((bf16[72,896]{1,0:T(8,128)(2,1)S(1)}, bf16[72,896]{1,0:T(8,128)(2,1)S(1)}, u32[]{:S(2)}, u32[]{:S(2)}) %collective-permute-start.6) | collective-permute-done | bytes 129056 | tf_op jit(solution)/shard_map/back3_tp/ppermute | solution.py:27
  30.9 2.7 %collective-permute-start.15 = (bf16[72,896]{1,0:T(8,128)(2,1)S(1)}, bf16[72,896]{1,0:T(8,128)(2,1)S(1)}, u32[]{:S(2)}, u32[]{:S(2)}) collective-permute-start(bf16[72,896]{1,0:T(8,128)(2,1)S(1)} %add_convert_fusion.2.earlier_ref), channel_id=1, source_target_pairs={{0,12},{4,8},{8,4},{12,0},{1,13},{5,9},{9,5},{13,1},{2,14},{6,10},... | collective-permute-start | bytes 387080 | tf_op jit(solution)/shard_map/back3_ep/ppermute | solution.py:27
  34.2 1.2 %back.3 = (bf16[72,896]{1,0:T(8,128)(2,1)S(1)}, bf16[72,896]{1,0:T(8,128)(2,1)S(1)}) custom-call(f32[72,512]{1,0:T(8,128)S(1)} %get-tuple-element.51.sum_ref, bf16[88,512]{1,0:T(8,128)(2,1)S(1)} %after.12.other_ref, bf16[2,4,72,512]{3,2,1,0:T(8,128)(2,1)S(1)} %get-tuple-element.39.pre_ref, bf16[1792,512]{1,0:T(8,128)(2,1)S(1)} %get-tuple-element.40.gate_ref, ...), custom_call_target="tpu_custom_call" | custom-call | tf_op jit(solution)/shard_map/back/pallas_call | solution.py:46
  35.4 1.5 %collective-permute-start.13 = (bf16[72,896]{1,0:T(8,128)(2,1)S(1)}, bf16[72,896]{1,0:T(8,128)(2,1)S(1)}, u32[]{:S(2)}, u32[]{:S(2)}) collective-permute-start(bf16[72,896]{1,0:T(8,128)(2,1)S(1)} %get-tuple-element.54), channel_id=1, source_target_pairs={{0,2},{2,0},{1,3},{3,1},{4,6},{6,4},{5,7},{7,5},{8,10},{10,8},{9,1... | collective-permute-start | bytes 387080 | tf_op jit(solution)/shard_map/back2_tp/ppermute | solution.py:27
  37.0 2.7 %collective-permute-done.7 = bf16[72,896]{1,0:T(8,128)(2,1)S(1)} collective-permute-done((bf16[72,896]{1,0:T(8,128)(2,1)S(1)}, bf16[72,896]{1,0:T(8,128)(2,1)S(1)}, u32[]{:S(2)}, u32[]{:S(2)}) %collective-permute-start.7) | collective-permute-done | bytes 129056 | tf_op jit(solution)/shard_map/back1_tp/ppermute | solution.py:27
  41.1 1.3 %collective-permute-start.14 = (bf16[72,896]{1,0:T(8,128)(2,1)S(1)}, bf16[72,896]{1,0:T(8,128)(2,1)S(1)}, u32[]{:S(2)}, u32[]{:S(2)}) collective-permute-start(bf16[72,896]{1,0:T(8,128)(2,1)S(1)} %add_convert_fusion.earlier_ref), channel_id=1, source_target_pairs={{0,8},{4,12},{8,0},{12,4},{1,9},{5,13},{9,1},{13,5},{2,10},{6,14},... | collective-permute-start | bytes 387080 | tf_op jit(solution)/shard_map/back2_ep/ppermute | solution.py:27
  42.5 1.5 %collective-permute-start.16 = (bf16[72,896]{1,0:T(8,128)(2,1)S(1)}, bf16[72,896]{1,0:T(8,128)(2,1)S(1)}, u32[]{:S(2)}, u32[]{:S(2)}) collective-permute-start(bf16[72,896]{1,0:T(8,128)(2,1)S(1)} %after.13), channel_id=1, source_target_pairs={{0,2},{2,0},{1,3},{3,1},{4,6},{6,4},{5,7},{7,5},{8,10},{10,8},{9,1... | collective-permute-start | bytes 387080 | tf_op jit(solution)/shard_map/back0_tp/ppermute | solution.py:27
  43.9 0.8 %fusion.5 = bf16[128,256]{1,0:T(8,128)(2,1)} fusion(bf16[128,256]{1,0:T(8,128)(2,1)S(1)} %get-tuple-element.48, bf16[128,256]{1,0:T(8,128)(2,1)S(1)} %after.11, f32[128]{0:T(128)S(1)} %slice_bitcast_fusion.1, f32[128]{0:T(128)S(1)} %get-tuple-element.58, f32[128]{0:T(128)S(1)} %get-tuple-element.59, f32[256]{0:T(256)S(1)} %bitcast.24, ...), kind=kLoop, calls=%fused_computation.11 | loop fusion | flops 360448 | bytes 264704 | tf_op jit(solution)/shard_map/convert_element_type | solution.py:383
  44.7 1.3 %collective-permute-done.8.refs_1_ = bf16[72,896]{1,0:T(8,128)(2,1)S(1)} collective-permute-done((bf16[72,896]{1,0:T(8,128)(2,1)S(1)}, bf16[72,896]{1,0:T(8,128)(2,1)S(1)}, u32[]{:S(2)}, u32[]{:S(2)}) %collective-permute-start.8) | collective-permute-done | bytes 129056 | tf_op jit(solution)/shard_map/back1_ep/ppermute | solution.py:27
  45.9 2.8 %collective-permute-done.14.refs_2_ = bf16[72,896]{1,0:T(8,128)(2,1)S(1)} collective-permute-done((bf16[72,896]{1,0:T(8,128)(2,1)S(1)}, bf16[72,896]{1,0:T(8,128)(2,1)S(1)}, u32[]{:S(2)}, u32[]{:S(2)}) %collective-permute-start.14) | collective-permute-done | bytes 129056 | tf_op jit(solution)/shard_map/back2_ep/ppermute | solution.py:27
  48.7 1.5 %unpack.1 = bf16[128,1792]{1,0:T(8,128)(2,1)} custom-call(bf16[2,4,72,128]{3,2,1,0:T(8,128)(2,1)S(1)} %get-tuple-element.29.place_ref, bf16[72,896]{1,0:T(8,128)(2,1)S(1)} %get-tuple-element.42.refs_0_, bf16[72,896]{1,0:T(8,128)(2,1)S(1)} %collective-permute-done.8.refs_1_, bf16[72,896]{1,0:T(8,128)(2,1)S(1)} %collective-permute-done.14.refs_2_, ...), custom_call_target="tpu_custom_call" | custom-call | tf_op jit(solution)/shard_map/unpack/pallas_call | solution.py:46
  (35 shorter events, 5.0 us)
Async XLA Ops:
  2.7 10.2 %collective-permute-start.2 = (bf16[72,896]{1,0:T(8,128)(2,1)S(1)}, bf16[72,896]{1,0:T(8,128)(2,1)S(1)}, u32[]{:S(2)}, u32[]{:S(2)}) collective-permute-start(bf16[72,896]{1,0:T(8,128)(2,1)S(1)} %get-tuple-element.31), channel_id=1, source_target_pairs={{0,4},{4,0},{8,12},{12,8},{1,5},{5,1},{9,13},{13,9},{2,6},{6,2},{1... | collective-permute-start | bytes 387080 | tf_op jit(solution)/shard_map/rows1_ep/ppermute | solution.py:27
  5.8 9.1 %collective-permute-start = (bf16[72,896]{1,0:T(8,128)(2,1)S(1)}, bf16[72,896]{1,0:T(8,128)(2,1)S(1)}, u32[]{:S(2)}, u32[]{:S(2)}) collective-permute-start(bf16[72,896]{1,0:T(8,128)(2,1)S(1)} %get-tuple-element.30.earlier_ref), channel_id=1, source_target_pairs={{0,12},{4,8},{8,4},{12,0},{1,13},{5,9},{9,5},{13,1},{2,14},{6,10},... | collective-permute-start | bytes 387080 | tf_op jit(solution)/shard_map/rows3_ep/ppermute | solution.py:27
  8.3 11.0 %collective-permute-start.4 = (bf16[72,896]{1,0:T(8,128)(2,1)S(1)}, bf16[72,896]{1,0:T(8,128)(2,1)S(1)}, u32[]{:S(2)}, u32[]{:S(2)}) collective-permute-start(bf16[72,896]{1,0:T(8,128)(2,1)S(1)} %get-tuple-element.32.refs_4_), channel_id=1, source_target_pairs={{0,2},{2,0},{1,3},{3,1},{4,6},{6,4},{5,7},{7,5},{8,10},{10,8},{9,1... | collective-permute-start | bytes 387080 | tf_op jit(solution)/shard_map/rows0_tp/ppermute | solution.py:27
  12.7 9.6 %collective-permute-start.9 = (bf16[72,896]{1,0:T(8,128)(2,1)S(1)}, bf16[72,896]{1,0:T(8,128)(2,1)S(1)}, u32[]{:S(2)}, u32[]{:S(2)}) collective-permute-start(bf16[72,896]{1,0:T(8,128)(2,1)S(1)} %get-tuple-element.47), channel_id=1, source_target_pairs={{0,8},{4,12},{8,0},{12,4},{1,9},{5,13},{9,1},{13,5},{2,10},{6,14},... | collective-permute-start | bytes 387080 | tf_op jit(solution)/shard_map/rows2_ep/ppermute | solution.py:27
  12.9 6.4 %collective-permute-start.3 = (bf16[72,896]{1,0:T(8,128)(2,1)S(1)}, bf16[72,896]{1,0:T(8,128)(2,1)S(1)}, u32[]{:S(2)}, u32[]{:S(2)}) collective-permute-start(bf16[72,896]{1,0:T(8,128)(2,1)S(1)} %collective-permute-done.2.refs_2_), channel_id=1, source_target_pairs={{0,2},{2,0},{1,3},{3,1},{4,6},{6,4},{5,7},{7,5},{8,10},{10,8},{9,1... | collective-permute-start | bytes 387080 | tf_op jit(solution)/shard_map/rows1_tp/ppermute | solution.py:27
  13.4 9.5 %collective-permute-start.11 = (bf16[128,256]{1,0:T(8,128)(2,1)S(1)}, bf16[128,256]{1,0:T(8,128)(2,1)S(1)}, u32[]{:S(2)}, u32[]{:S(2)}) collective-permute-start(bf16[128,256]{1,0:T(8,128)(2,1)S(1)} %slice_bitcast_fusion), channel_id=1, source_target_pairs={{0,2},{2,0},{1,3},{3,1},{4,6},{6,4},{5,7},{7,5},{8,10},{10,8},{9,1... | collective-permute-start | bytes 196616 | tf_op jit(solution)/shard_map/latent_tp/ppermute | solution.py:27
  14.9 6.5 %collective-permute-start.1 = (bf16[72,896]{1,0:T(8,128)(2,1)S(1)}, bf16[72,896]{1,0:T(8,128)(2,1)S(1)}, u32[]{:S(2)}, u32[]{:S(2)}) collective-permute-start(bf16[72,896]{1,0:T(8,128)(2,1)S(1)} %collective-permute-done.refs_0_), channel_id=1, source_target_pairs={{0,2},{2,0},{1,3},{3,1},{4,6},{6,4},{5,7},{7,5},{8,10},{10,8},{9,1... | collective-permute-start | bytes 387080 | tf_op jit(solution)/shard_map/rows3_tp/ppermute | solution.py:27
  22.2 1.5 %collective-permute-start.5 = (bf16[216,512]{1,0:T(8,128)(2,1)S(1)}, bf16[216,512]{1,0:T(8,128)(2,1)S(1)}, u32[]{:S(2)}, u32[]{:S(2)}) collective-permute-start(bf16[216,512]{1,0:T(8,128)(2,1)S(1)} %get-tuple-element.38), channel_id=1, source_target_pairs={{0,1},{1,0},{2,3},{3,2},{4,5},{5,4},{6,7},{7,6},{8,9},{9,8},{10,11... | collective-permute-start | bytes 663560 | tf_op jit(solution)/shard_map/hidden3_sub/ppermute | solution.py:27
  22.3 6.1 %collective-permute-start.10 = (bf16[72,896]{1,0:T(8,128)(2,1)S(1)}, bf16[72,896]{1,0:T(8,128)(2,1)S(1)}, u32[]{:S(2)}, u32[]{:S(2)}) collective-permute-start(bf16[72,896]{1,0:T(8,128)(2,1)S(1)} %after.9.refs_0_), channel_id=1, source_target_pairs={{0,2},{2,0},{1,3},{3,1},{4,6},{6,4},{5,7},{7,5},{8,10},{10,8},{9,1... | collective-permute-start | bytes 387080 | tf_op jit(solution)/shard_map/rows2_tp/ppermute | solution.py:27
  25.0 5.8 %collective-permute-start.6 = (bf16[72,896]{1,0:T(8,128)(2,1)S(1)}, bf16[72,896]{1,0:T(8,128)(2,1)S(1)}, u32[]{:S(2)}, u32[]{:S(2)}) collective-permute-start(bf16[72,896]{1,0:T(8,128)(2,1)S(1)} %get-tuple-element.46), channel_id=1, source_target_pairs={{0,2},{2,0},{1,3},{3,1},{4,6},{6,4},{5,7},{7,5},{8,10},{10,8},{9,1... | collective-permute-start | bytes 387080 | tf_op jit(solution)/shard_map/back3_tp/ppermute | solution.py:27
  29.0 5.1 %collective-permute-start.12 = (bf16[88,512]{1,0:T(8,128)(2,1)S(1)}, bf16[88,512]{1,0:T(8,128)(2,1)S(1)}, u32[]{:S(2)}, u32[]{:S(2)}) collective-permute-start(bf16[88,512]{1,0:T(8,128)(2,1)S(1)} %get-tuple-element.52), channel_id=1, source_target_pairs={{0,1},{1,0},{2,3},{3,2},{4,5},{5,4},{6,7},{7,6},{8,9},{9,8},{10,11... | collective-permute-start | bytes 270344 | tf_op jit(solution)/shard_map/hidden2_sub/ppermute | solution.py:27
  30.9 13.8 %collective-permute-start.15 = (bf16[72,896]{1,0:T(8,128)(2,1)S(1)}, bf16[72,896]{1,0:T(8,128)(2,1)S(1)}, u32[]{:S(2)}, u32[]{:S(2)}) collective-permute-start(bf16[72,896]{1,0:T(8,128)(2,1)S(1)} %add_convert_fusion.2.earlier_ref), channel_id=1, source_target_pairs={{0,12},{4,8},{8,4},{12,0},{1,13},{5,9},{9,5},{13,1},{2,14},{6,10},... | collective-permute-start | bytes 387080 | tf_op jit(solution)/shard_map/back3_ep/ppermute | solution.py:27
  33.6 6.1 %collective-permute-start.7 = (bf16[72,896]{1,0:T(8,128)(2,1)S(1)}, bf16[72,896]{1,0:T(8,128)(2,1)S(1)}, u32[]{:S(2)}, u32[]{:S(2)}) collective-permute-start(bf16[72,896]{1,0:T(8,128)(2,1)S(1)} %after.8), channel_id=1, source_target_pairs={{0,2},{2,0},{1,3},{3,1},{4,6},{6,4},{5,7},{7,5},{8,10},{10,8},{9,1... | collective-permute-start | bytes 387080 | tf_op jit(solution)/shard_map/back1_tp/ppermute | solution.py:27
  35.4 5.7 %collective-permute-start.13 = (bf16[72,896]{1,0:T(8,128)(2,1)S(1)}, bf16[72,896]{1,0:T(8,128)(2,1)S(1)}, u32[]{:S(2)}, u32[]{:S(2)}) collective-permute-start(bf16[72,896]{1,0:T(8,128)(2,1)S(1)} %get-tuple-element.54), channel_id=1, source_target_pairs={{0,2},{2,0},{1,3},{3,1},{4,6},{6,4},{5,7},{7,5},{8,10},{10,8},{9,1... | collective-permute-start | bytes 387080 | tf_op jit(solution)/shard_map/back2_tp/ppermute | solution.py:27
  39.7 6.2 %collective-permute-start.8 = (bf16[72,896]{1,0:T(8,128)(2,1)S(1)}, bf16[72,896]{1,0:T(8,128)(2,1)S(1)}, u32[]{:S(2)}, u32[]{:S(2)}) collective-permute-start(bf16[72,896]{1,0:T(8,128)(2,1)S(1)} %add_convert_fusion.1), channel_id=1, source_target_pairs={{0,4},{4,0},{8,12},{12,8},{1,5},{5,1},{9,13},{13,9},{2,6},{6,2},{1... | collective-permute-start | bytes 387080 | tf_op jit(solution)/shard_map/back1_ep/ppermute | solution.py:27
  41.1 7.6 %collective-permute-start.14 = (bf16[72,896]{1,0:T(8,128)(2,1)S(1)}, bf16[72,896]{1,0:T(8,128)(2,1)S(1)}, u32[]{:S(2)}, u32[]{:S(2)}) collective-permute-start(bf16[72,896]{1,0:T(8,128)(2,1)S(1)} %add_convert_fusion.earlier_ref), channel_id=1, source_target_pairs={{0,8},{4,12},{8,0},{12,4},{1,9},{5,13},{9,1},{13,5},{2,10},{6,14},... | collective-permute-start | bytes 387080 | tf_op jit(solution)/shard_map/back2_ep/ppermute | solution.py:27
  42.5 6.3 %collective-permute-start.16 = (bf16[72,896]{1,0:T(8,128)(2,1)S(1)}, bf16[72,896]{1,0:T(8,128)(2,1)S(1)}, u32[]{:S(2)}, u32[]{:S(2)}) collective-permute-start(bf16[72,896]{1,0:T(8,128)(2,1)S(1)} %after.13), channel_id=1, source_target_pairs={{0,2},{2,0},{1,3},{3,1},{4,6},{6,4},{5,7},{7,5},{8,10},{10,8},{9,1... | collective-permute-start | bytes 387080 | tf_op jit(solution)/shard_map/back0_tp/ppermute | solution.py:27

commit v6 on v5

--- a/solution.py
+++ b/solution.py
@@ -199,22 +199,23 @@
         out[...] = jnp.concatenate(pieces, axis=0).astype(jnp.bfloat16)
 
 
-def unpack_kernel(wide, place_ref, *refs):
-    blocks, out_ref = refs[:-1], refs[-1]
+def unpack_kernel(distances, started, place_ref, *refs):
+    blocks, others, out_ref = refs[: len(distances)], refs[len(distances) : -1], refs[-1]
+    if started:
+        others, so_far_ref = others[:-1], others[-1]
     half = out_ref.shape[1] // 2
     for side in range(2):
-        total = None
-        for k in range(wide):
+        columns = slice(side * half, (side + 1) * half)
+        total = so_far_ref[:, columns].astype(jnp.float32) if started else 0.0
+        for k, block_ref in zip(distances, blocks):
+            rows = block_ref[...]
             if k == 0:
-                rows = blocks[0][...].astype(jnp.float32)
-                for other in blocks[wide:]:
-                    rows += other[...].astype(jnp.float32)
+                rows = rows.astype(jnp.float32)
+                for other_ref in others:
+                    rows += other_ref[...].astype(jnp.float32)
                 rows = rows.astype(jnp.bfloat16)
-            else:
-                rows = blocks[k][...]
-            term = dot(place_ref[side, k], rows, TN)
-            total = term if total is None else total + term
-        out_ref[:, side * half : (side + 1) * half] = total.astype(jnp.bfloat16)
+            total = total + dot(place_ref[side, k], rows, TN)
+        out_ref[:, columns] = total.astype(jnp.bfloat16)
 
 
 def groups_of(wide):
@@ -309,8 +310,16 @@
         swap(shares[j], "tp", j, "latent") for j in range(1, narrow)
     ]
 
+    def give_back(k, mine, others):
+        others = [swap(other, "tp", j + 1, f"back{k}") for j, other in enumerate(others)]
+        total = mine.astype(f32)
+        for other in others:
+            total += other.astype(f32)
+        total = total.astype(bf16)
+        return total, swap(total, "ep", k, f"back{k}")
+
     returned = {}
-    own = []
+    own, waiting = [], []
     values = latent.astype(f32)
     received, products, moved = None, None, None
     for group in groups:
@@ -344,6 +353,10 @@
             name="hidden",
             earlier=products[:1] if products else (),
         )
+        for k, mine, others in waiting:
+            others = [after(other, summed) for other in others]
+            returned[k] = give_back(k, mine, others)[1]
+        waiting = []
         received = swap(sent, "sub", 1, f"hidden{group[0]}")
         if moved is not None:
             received = after(received, moved)
@@ -358,22 +371,15 @@
             name="back",
         )
         for at, k in enumerate(group):
-            mine = products[at * narrow]
+            mine, others = products[at * narrow], products[at * narrow + 1 : (at + 1) * narrow]
             if k == 0:
-                returned[0] = mine
-                own = products[1 + at * narrow : (at + 1) * narrow]
-                continue
-            others = products[at * narrow + 1 : (at + 1) * narrow]
-            if k != group[0]:
-                others = [after(other, moved) for other in others]
-            others = [swap(other, "tp", j + 1, f"back{k}") for j, other in enumerate(others)]
-            total = mine.astype(f32)
-            for other in others:
-                total += other.astype(f32)
-            total = total.astype(bf16)
-            returned[k] = swap(total, "ep", k, f"back{k}")
-            if k == group[0]:
-                moved = total
+                returned[0], own = mine, others
+            elif k != group[0] and not extra:
+                waiting.append((k, mine, others))
+            else:
+                total, returned[k] = give_back(k, mine, others)
+                if k == group[0]:
+                    moved = total
     own = [swap(after(value, moved), "tp", j + 1, "back0") for j, value in enumerate(own)]
     tail = received[count : count + 4, :tokens].astype(f32)
     row_sums = row_sums + tail[:2] + tail[2:]
@@ -381,14 +387,25 @@
     d_latent = (
         inverse_rms * gained - values * inverse_rms**3 * row_sums[1][:, None] / LAT
     ).astype(bf16)
+    latest = groups[-1][:1] if len(groups) > 1 else []
+    distances = [k for k in sorted(returned, reverse=True) if k not in latest]
     (grad_input,) = call(
-        functools.partial(unpack_kernel, wide),
-        [jax.ShapeDtypeStruct((tokens, width), bf16)],
+        functools.partial(unpack_kernel, distances, False),
+        [pltpu.VMEM((tokens, width), bf16) if latest else jax.ShapeDtypeStruct((tokens, width), bf16)],
         place,
-        *[returned[k] for k in range(wide)],
+        *[returned[k] for k in distances],
         *own,
         name="unpack",
     )
+    if latest:
+        (grad_input,) = call(
+            functools.partial(unpack_kernel, latest, True),
+            [jax.ShapeDtypeStruct((tokens, width), bf16)],
+            place,
+            *[returned[k] for k in latest],
+            grad_input,
+            name="unpack_latest",
+        )
     return (grad_input, d_latent)
 
 

time: 50.3 us -> 48.4 us (0.962)
  waiting for transfers between devices: 18.1 us -> 15.1 us
  starting transfers between devices: 19.8 us -> 20.7 us
    ppermute x17, waiting for transfers between devices: 18.1 us -> 15.1 us  [swap(): return lax.ppermute(value, axis, [(i, i ^ step) for i in range(count)])]
    ppermute x17, starting transfers between devices: 19.8 us -> 20.7 us  [swap(): return lax.ppermute(value, axis, [(i, i ^ step) for i in range(count)])]
    pallas_call x7 -> x8, Pallas kernels: 10.4 us -> 10.6 us  [call(): pl.pallas_call(kernel, out_shape=outs, in_specs=specs, out_specs=[VMEM] *...]
  transfers between devices with their start and end apart: 17 -> 17, of which waited for: 9 -> 9; matrix products, arithmetic and copies ran while one was open for 2% -> 2% of each run, Pallas kernels for 14% -> 15%
where the time goes in v6:
time: 48.4 us; the launch traced here: 48.2 us
  starting transfers between devices  20.7 us (43%)
  waiting for transfers between devices  15.1 us (31%)
  Pallas kernels  10.6 us (22%)
  other arithmetic  1 us (2%)
  between operations  0.77 us (2%)
    ppermute x17, starting transfers between devices, swap(): return lax.ppermute(value, axis, [(i, i ^ step) for i in range(count)])  20.7 us
    ppermute x17, waiting for transfers between devices, swap(): return lax.ppermute(value, axis, [(i, i ^ step) for i in range(count)])  15.1 us
    pallas_call x8, Pallas kernels, call(): pl.pallas_call(kernel, out_shape=outs, in_specs=specs, out_specs=[VMEM] *...  10.6 us
  transfers between devices with their start and end apart: 17, of which 9 were waited for; matrix products, arithmetic and copies ran while one was open for 2% of the time, Pallas kernels for 15%

profile of v6, /device:TPU:0, one launch (start us, length us, event | category | flops | bytes accessed | tf_op | source)
XLA Modules:
  0.0 48.2 jit_solution(16412741234466499951)
XLA Ops:
  0.6 2.1 %pack.1 = (bf16[72,896]{1,0:T(8,128)(2,1)S(1)}, bf16[72,896]{1,0:T(8,128)(2,1)S(1)}, bf16[72,896]{1,0:T(8,128)(2,1)S(1)}, bf16[2,4,72,128]{3,2,1,0:T(8,128)(2,1)...) custom-call(s32[1,128]{1,0:T(1,128)} %bitcast.36, f32[1,128]{1,0:T(1,128)} %bitcast.37, ...), custom_call_target="tpu_custom_call" | custom-call | tf_op jit(solution)/shard_map/pack/pallas_call | solution.py:46
  2.7 3.1 %collective-permute-start.4 = (bf16[72,896]{1,0:T(8,128)(2,1)S(1)}, bf16[72,896]{1,0:T(8,128)(2,1)S(1)}, u32[]{:S(2)}, u32[]{:S(2)}) collective-permute-start(bf16[72,896]{1,0:T(8,128)(2,1)S(1)} %get-tuple-element.35), channel_id=1, source_target_pairs={{0,4},{4,0},{8,12},{12,8},{1,5},{5,1},{9,13},{13,9},{2,6},{6,2},{1... | collective-permute-start | bytes 387080 | tf_op jit(solution)/shard_map/rows1_ep/ppermute | solution.py:27
  5.8 2.5 %collective-permute-start.2 = (bf16[72,896]{1,0:T(8,128)(2,1)S(1)}, bf16[72,896]{1,0:T(8,128)(2,1)S(1)}, u32[]{:S(2)}, u32[]{:S(2)}) collective-permute-start(bf16[72,896]{1,0:T(8,128)(2,1)S(1)} %get-tuple-element.34.earlier_ref), channel_id=1, source_target_pairs={{0,12},{4,8},{8,4},{12,0},{1,13},{5,9},{9,5},{13,1},{2,14},{6,10},... | collective-permute-start | bytes 387080 | tf_op jit(solution)/shard_map/rows3_ep/ppermute | solution.py:27
  8.3 1.5 %collective-permute-start.6 = (bf16[72,896]{1,0:T(8,128)(2,1)S(1)}, bf16[72,896]{1,0:T(8,128)(2,1)S(1)}, u32[]{:S(2)}, u32[]{:S(2)}) collective-permute-start(bf16[72,896]{1,0:T(8,128)(2,1)S(1)} %get-tuple-element.36.refs_4_), channel_id=1, source_target_pairs={{0,2},{2,0},{1,3},{3,1},{4,6},{6,4},{5,7},{7,5},{8,10},{10,8},{9,1... | collective-permute-start | bytes 387080 | tf_op jit(solution)/shard_map/rows0_tp/ppermute | solution.py:27
  9.8 2.9 %pack_more.1 = (bf16[72,896]{1,0:T(8,128)(2,1)S(1)}, bf16[2,128,256]{2,1,0:T(8,128)(2,1)S(1)}, bf16[512,1792]{1,0:T(8,128)(2,1)S(1)}, bf16[2,4,72,512]{3,2,1,0:T...) custom-call(bf16[2,4,72,128]{3,2,1,0:T(8,128)(2,1)S(1)} %get-tuple-e, ...), custom_call_target="tpu_custom_call" | custom-call | flops 33554432 | tf_op jit(solution)/shard_map/pack_more/pallas_call | solution.py:46
  13.3 1.5 %collective-permute-start.8 = (bf16[128,256]{1,0:T(8,128)(2,1)S(1)}, bf16[128,256]{1,0:T(8,128)(2,1)S(1)}, u32[]{:S(2)}, u32[]{:S(2)}) collective-permute-start(bf16[128,256]{1,0:T(8,128)(2,1)S(1)} %slice_bitcast_fusion), channel_id=1, source_target_pairs={{0,2},{2,0},{1,3},{3,1},{4,6},{6,4},{5,7},{7,5},{8,10},{10,8},{9,1... | collective-permute-start | bytes 196616 | tf_op jit(solution)/shard_map/latent_tp/ppermute | solution.py:27
  15.2 1.5 %collective-permute-start.3 = (bf16[72,896]{1,0:T(8,128)(2,1)S(1)}, bf16[72,896]{1,0:T(8,128)(2,1)S(1)}, u32[]{:S(2)}, u32[]{:S(2)}) collective-permute-start(bf16[72,896]{1,0:T(8,128)(2,1)S(1)} %collective-permute-done.2.refs_0_), channel_id=1, source_target_pairs={{0,2},{2,0},{1,3},{3,1},{4,6},{6,4},{5,7},{7,5},{8,10},{10,8},{9,1... | collective-permute-start | bytes 387080 | tf_op jit(solution)/shard_map/rows3_tp/ppermute | solution.py:27
  16.7 2.5 %collective-permute-done.5.value_ref = bf16[72,896]{1,0:T(8,128)(2,1)S(1)} collective-permute-done((bf16[72,896]{1,0:T(8,128)(2,1)S(1)}, bf16[72,896]{1,0:T(8,128)(2,1)S(1)}, u32[]{:S(2)}, u32[]{:S(2)}) %collective-permute-start.5) | collective-permute-done | bytes 129056 | tf_op jit(solution)/shard_map/rows1_tp/ppermute | solution.py:27
  19.1 2.1 %collective-permute-done.3.refs_1_ = bf16[72,896]{1,0:T(8,128)(2,1)S(1)} collective-permute-done((bf16[72,896]{1,0:T(8,128)(2,1)S(1)}, bf16[72,896]{1,0:T(8,128)(2,1)S(1)}, u32[]{:S(2)}, u32[]{:S(2)}) %collective-permute-start.3) | collective-permute-done | bytes 129056 | tf_op jit(solution)/shard_map/rows3_tp/ppermute | solution.py:27
  22.8 0.8 %collective-permute-done.7.other_ref = bf16[216,512]{1,0:T(8,128)(2,1)S(1)} collective-permute-done((bf16[216,512]{1,0:T(8,128)(2,1)S(1)}, bf16[216,512]{1,0:T(8,128)(2,1)S(1)}, u32[]{:S(2)}, u32[]{:S(2)}) %collective-permute-start.7) | collective-permute-done | bytes 221216 | tf_op jit(solution)/shard_map/hidden3_sub/ppermute | solution.py:27
  23.6 1.3 %back.2 = (bf16[72,896]{1,0:T(8,128)(2,1)S(1)}, bf16[72,896]{1,0:T(8,128)(2,1)S(1)}, bf16[72,896]{1,0:T(8,128)(2,1)S(1)}, bf16[72,896]{1,0:T(8,128)(2,1)S(1)}, b...) custom-call(f32[216,512]{1,0:T(8,128)S(1)} %get-tuple-element.38.sum_ref.earlier_ref, ...), custom_call_target="tpu_custom_call" | custom-call | tf_op jit(solution)/shard_map/back/pallas_call | solution.py:46
  24.9 0.8 %collective-permute-start.10 = (bf16[72,896]{1,0:T(8,128)(2,1)S(1)}, bf16[72,896]{1,0:T(8,128)(2,1)S(1)}, u32[]{:S(2)}, u32[]{:S(2)}) collective-permute-start(bf16[72,896]{1,0:T(8,128)(2,1)S(1)} %get-tuple-element.49), channel_id=1, source_target_pairs={{0,2},{2,0},{1,3},{3,1},{4,6},{6,4},{5,7},{7,5},{8,10},{10,8},{9,1... | collective-permute-start | bytes 387080 | tf_op jit(solution)/shard_map/back3_tp/ppermute | solution.py:27
  25.8 2.3 %collective-permute-done.1.value_ref = bf16[72,896]{1,0:T(8,128)(2,1)S(1)} collective-permute-done((bf16[72,896]{1,0:T(8,128)(2,1)S(1)}, bf16[72,896]{1,0:T(8,128)(2,1)S(1)}, u32[]{:S(2)}, u32[]{:S(2)}) %collective-permute-start.1) | collective-permute-done | bytes 129056 | tf_op jit(solution)/shard_map/rows2_tp/ppermute | solution.py:27
  29.4 1.3 %collective-permute-done.10 = bf16[72,896]{1,0:T(8,128)(2,1)S(1)} collective-permute-done((bf16[72,896]{1,0:T(8,128)(2,1)S(1)}, bf16[72,896]{1,0:T(8,128)(2,1)S(1)}, u32[]{:S(2)}, u32[]{:S(2)}) %collective-permute-start.10) | collective-permute-done | bytes 129056 | tf_op jit(solution)/shard_map/back3_tp/ppermute | solution.py:27
  30.8 1.2 %back.3 = (bf16[72,896]{1,0:T(8,128)(2,1)S(1)}, bf16[72,896]{1,0:T(8,128)(2,1)S(1)}) custom-call(f32[72,512]{1,0:T(8,128)S(1)} %get-tuple-element.47.sum_ref.earlier_ref, bf16[88,512]{1,0:T(8,128)(2,1)S(1)} %after.11.other_ref, bf16[2,4,72,512]{3,2,1,0:T(8,128)(2,1)S(1)} %get-tuple-element.40.pre_ref, bf16[1792,512]{1,0:T(8,128)(2,1)S(1)} %get-tuple-element.41.gate_ref, ...), custom_call_target="tpu_custom_call" | custom-call | tf_op jit(solution)/shard_map/back/pallas_call | solution.py:46
  32.0 2.2 %collective-permute-start.13 = (bf16[72,896]{1,0:T(8,128)(2,1)S(1)}, bf16[72,896]{1,0:T(8,128)(2,1)S(1)}, u32[]{:S(2)}, u32[]{:S(2)}) collective-permute-start(bf16[72,896]{1,0:T(8,128)(2,1)S(1)} %add_convert_fusion.2.earlier_ref), channel_id=1, source_target_pairs={{0,12},{4,8},{8,4},{12,0},{1,13},{5,9},{9,5},{13,1},{2,14},{6,10},... | collective-permute-start | bytes 387080 | tf_op jit(solution)/shard_map/back3_ep/ppermute | solution.py:27
  34.3 0.9 %collective-permute-start.11 = (bf16[72,896]{1,0:T(8,128)(2,1)S(1)}, bf16[72,896]{1,0:T(8,128)(2,1)S(1)}, u32[]{:S(2)}, u32[]{:S(2)}) collective-permute-start(bf16[72,896]{1,0:T(8,128)(2,1)S(1)} %get-tuple-element.51), channel_id=1, source_target_pairs={{0,2},{2,0},{1,3},{3,1},{4,6},{6,4},{5,7},{7,5},{8,10},{10,8},{9,1... | collective-permute-start | bytes 387080 | tf_op jit(solution)/shard_map/back2_tp/ppermute | solution.py:27
  35.3 1.6 %collective-permute-start.15 = (bf16[72,896]{1,0:T(8,128)(2,1)S(1)}, bf16[72,896]{1,0:T(8,128)(2,1)S(1)}, u32[]{:S(2)}, u32[]{:S(2)}) collective-permute-start(bf16[72,896]{1,0:T(8,128)(2,1)S(1)} %add_convert_fusion), channel_id=1, source_target_pairs={{0,4},{4,0},{8,12},{12,8},{1,5},{5,1},{9,13},{13,9},{2,6},{6,2},{1... | collective-permute-start | bytes 387080 | tf_op jit(solution)/shard_map/back1_ep/ppermute | solution.py:27
  36.9 2.4 %collective-permute-done.11 = bf16[72,896]{1,0:T(8,128)(2,1)S(1)} collective-permute-done((bf16[72,896]{1,0:T(8,128)(2,1)S(1)}, bf16[72,896]{1,0:T(8,128)(2,1)S(1)}, u32[]{:S(2)}, u32[]{:S(2)}) %collective-permute-start.11) | collective-permute-done | bytes 129056 | tf_op jit(solution)/shard_map/back2_tp/ppermute | solution.py:27
  39.3 1.5 %collective-permute-start.12 = (bf16[72,896]{1,0:T(8,128)(2,1)S(1)}, bf16[72,896]{1,0:T(8,128)(2,1)S(1)}, u32[]{:S(2)}, u32[]{:S(2)}) collective-permute-start(bf16[72,896]{1,0:T(8,128)(2,1)S(1)} %add_convert_fusion.1.earlier_ref), channel_id=1, source_target_pairs={{0,8},{4,12},{8,0},{12,4},{1,9},{5,13},{9,1},{13,5},{2,10},{6,14},... | collective-permute-start | bytes 387080 | tf_op jit(solution)/shard_map/back2_ep/ppermute | solution.py:27
  40.8 1.4 %collective-permute-start.16 = (bf16[72,896]{1,0:T(8,128)(2,1)S(1)}, bf16[72,896]{1,0:T(8,128)(2,1)S(1)}, u32[]{:S(2)}, u32[]{:S(2)}) collective-permute-start(bf16[72,896]{1,0:T(8,128)(2,1)S(1)} %after.13), channel_id=1, source_target_pairs={{0,2},{2,0},{1,3},{3,1},{4,6},{6,4},{5,7},{7,5},{8,10},{10,8},{9,1... | collective-permute-start | bytes 387080 | tf_op jit(solution)/shard_map/back0_tp/ppermute | solution.py:27
  43.0 2.8 %collective-permute-done.16.refs_3_ = bf16[72,896]{1,0:T(8,128)(2,1)S(1)} collective-permute-done((bf16[72,896]{1,0:T(8,128)(2,1)S(1)}, bf16[72,896]{1,0:T(8,128)(2,1)S(1)}, u32[]{:S(2)}, u32[]{:S(2)}) %collective-permute-start.16) | collective-permute-done | bytes 129056 | tf_op jit(solution)/shard_map/back0_tp/ppermute | solution.py:27
  46.3 0.8 %collective-permute-done.12.refs_0_ = bf16[72,896]{1,0:T(8,128)(2,1)S(1)} collective-permute-done((bf16[72,896]{1,0:T(8,128)(2,1)S(1)}, bf16[72,896]{1,0:T(8,128)(2,1)S(1)}, u32[]{:S(2)}, u32[]{:S(2)}) %collective-permute-start.12) | collective-permute-done | bytes 129056 | tf_op jit(solution)/shard_map/back2_ep/ppermute | solution.py:27
  47.1 1.1 %unpack_latest.1 = bf16[128,1792]{1,0:T(8,128)(2,1)} custom-call(bf16[2,4,72,128]{3,2,1,0:T(8,128)(2,1)S(1)} %get-tuple-element.29.place_ref, bf16[72,896]{1,0:T(8,128)(2,1)S(1)} %collective-permute-done.12.refs_0_, bf16[128,1792]{1,0:T(8,128)(2,1)S(1)} %unpack.1.refs_1_), custom_call_target="tpu_custom_call" | custom-call | tf_op jit(solution)/shard_map/unpack_latest/pallas_call | solution.py:46
  (36 shorter events, 5.4 us)
Async XLA Ops:
  2.7 10.0 %collective-permute-start.4 = (bf16[72,896]{1,0:T(8,128)(2,1)S(1)}, bf16[72,896]{1,0:T(8,128)(2,1)S(1)}, u32[]{:S(2)}, u32[]{:S(2)}) collective-permute-start(bf16[72,896]{1,0:T(8,128)(2,1)S(1)} %get-tuple-element.35), channel_id=1, source_target_pairs={{0,4},{4,0},{8,12},{12,8},{1,5},{5,1},{9,13},{13,9},{2,6},{6,2},{1... | collective-permute-start | bytes 387080 | tf_op jit(solution)/shard_map/rows1_ep/ppermute | solution.py:27
  5.8 9.4 %collective-permute-start.2 = (bf16[72,896]{1,0:T(8,128)(2,1)S(1)}, bf16[72,896]{1,0:T(8,128)(2,1)S(1)}, u32[]{:S(2)}, u32[]{:S(2)}) collective-permute-start(bf16[72,896]{1,0:T(8,128)(2,1)S(1)} %get-tuple-element.34.earlier_ref), channel_id=1, source_target_pairs={{0,12},{4,8},{8,4},{12,0},{1,13},{5,9},{9,5},{13,1},{2,14},{6,10},... | collective-permute-start | bytes 387080 | tf_op jit(solution)/shard_map/rows3_ep/ppermute | solution.py:27
  8.3 10.9 %collective-permute-start.6 = (bf16[72,896]{1,0:T(8,128)(2,1)S(1)}, bf16[72,896]{1,0:T(8,128)(2,1)S(1)}, u32[]{:S(2)}, u32[]{:S(2)}) collective-permute-start(bf16[72,896]{1,0:T(8,128)(2,1)S(1)} %get-tuple-element.36.refs_4_), channel_id=1, source_target_pairs={{0,2},{2,0},{1,3},{3,1},{4,6},{6,4},{5,7},{7,5},{8,10},{10,8},{9,1... | collective-permute-start | bytes 387080 | tf_op jit(solution)/shard_map/rows0_tp/ppermute | solution.py:27
  12.7 6.5 %collective-permute-start.5 = (bf16[72,896]{1,0:T(8,128)(2,1)S(1)}, bf16[72,896]{1,0:T(8,128)(2,1)S(1)}, u32[]{:S(2)}, u32[]{:S(2)}) collective-permute-start(bf16[72,896]{1,0:T(8,128)(2,1)S(1)} %collective-permute-done.4.refs_2_), channel_id=1, source_target_pairs={{0,2},{2,0},{1,3},{3,1},{4,6},{6,4},{5,7},{7,5},{8,10},{10,8},{9,1... | collective-permute-start | bytes 387080 | tf_op jit(solution)/shard_map/rows1_tp/ppermute | solution.py:27
  13.3 9.5 %collective-permute-start.8 = (bf16[128,256]{1,0:T(8,128)(2,1)S(1)}, bf16[128,256]{1,0:T(8,128)(2,1)S(1)}, u32[]{:S(2)}, u32[]{:S(2)}) collective-permute-start(bf16[128,256]{1,0:T(8,128)(2,1)S(1)} %slice_bitcast_fusion), channel_id=1, source_target_pairs={{0,2},{2,0},{1,3},{3,1},{4,6},{6,4},{5,7},{7,5},{8,10},{10,8},{9,1... | collective-permute-start | bytes 196616 | tf_op jit(solution)/shard_map/latent_tp/ppermute | solution.py:27
  14.8 7.5 %collective-permute-start = (bf16[72,896]{1,0:T(8,128)(2,1)S(1)}, bf16[72,896]{1,0:T(8,128)(2,1)S(1)}, u32[]{:S(2)}, u32[]{:S(2)}) collective-permute-start(bf16[72,896]{1,0:T(8,128)(2,1)S(1)} %get-tuple-element.33), channel_id=1, source_target_pairs={{0,8},{4,12},{8,0},{12,4},{1,9},{5,13},{9,1},{13,5},{2,10},{6,14},... | collective-permute-start | bytes 387080 | tf_op jit(solution)/shard_map/rows2_ep/ppermute | solution.py:27
  15.2 6.1 %collective-permute-start.3 = (bf16[72,896]{1,0:T(8,128)(2,1)S(1)}, bf16[72,896]{1,0:T(8,128)(2,1)S(1)}, u32[]{:S(2)}, u32[]{:S(2)}) collective-permute-start(bf16[72,896]{1,0:T(8,128)(2,1)S(1)} %collective-permute-done.2.refs_0_), channel_id=1, source_target_pairs={{0,2},{2,0},{1,3},{3,1},{4,6},{6,4},{5,7},{7,5},{8,10},{10,8},{9,1... | collective-permute-start | bytes 387080 | tf_op jit(solution)/shard_map/rows3_tp/ppermute | solution.py:27
  22.0 1.5 %collective-permute-start.7 = (bf16[216,512]{1,0:T(8,128)(2,1)S(1)}, bf16[216,512]{1,0:T(8,128)(2,1)S(1)}, u32[]{:S(2)}, u32[]{:S(2)}) collective-permute-start(bf16[216,512]{1,0:T(8,128)(2,1)S(1)} %get-tuple-element.39), channel_id=1, source_target_pairs={{0,1},{1,0},{2,3},{3,2},{4,5},{5,4},{6,7},{7,6},{8,9},{9,8},{10,11... | collective-permute-start | bytes 663560 | tf_op jit(solution)/shard_map/hidden3_sub/ppermute | solution.py:27
  22.2 5.9 %collective-permute-start.1 = (bf16[72,896]{1,0:T(8,128)(2,1)S(1)}, bf16[72,896]{1,0:T(8,128)(2,1)S(1)}, u32[]{:S(2)}, u32[]{:S(2)}) collective-permute-start(bf16[72,896]{1,0:T(8,128)(2,1)S(1)} %after.7.refs_0_), channel_id=1, source_target_pairs={{0,2},{2,0},{1,3},{3,1},{4,6},{6,4},{5,7},{7,5},{8,10},{10,8},{9,1... | collective-permute-start | bytes 387080 | tf_op jit(solution)/shard_map/rows2_tp/ppermute | solution.py:27
  24.9 5.8 %collective-permute-start.10 = (bf16[72,896]{1,0:T(8,128)(2,1)S(1)}, bf16[72,896]{1,0:T(8,128)(2,1)S(1)}, u32[]{:S(2)}, u32[]{:S(2)}) collective-permute-start(bf16[72,896]{1,0:T(8,128)(2,1)S(1)} %get-tuple-element.49), channel_id=1, source_target_pairs={{0,2},{2,0},{1,3},{3,1},{4,6},{6,4},{5,7},{7,5},{8,10},{10,8},{9,1... | collective-permute-start | bytes 387080 | tf_op jit(solution)/shard_map/back3_tp/ppermute | solution.py:27
  28.9 1.9 %collective-permute-start.9 = (bf16[88,512]{1,0:T(8,128)(2,1)S(1)}, bf16[88,512]{1,0:T(8,128)(2,1)S(1)}, u32[]{:S(2)}, u32[]{:S(2)}) collective-permute-start(bf16[88,512]{1,0:T(8,128)(2,1)S(1)} %get-tuple-element.48), channel_id=1, source_target_pairs={{0,1},{1,0},{2,3},{3,2},{4,5},{5,4},{6,7},{7,6},{8,9},{9,8},{10,11... | collective-permute-start | bytes 270344 | tf_op jit(solution)/shard_map/hidden2_sub/ppermute | solution.py:27
  28.9 6.3 %collective-permute-start.14 = (bf16[72,896]{1,0:T(8,128)(2,1)S(1)}, bf16[72,896]{1,0:T(8,128)(2,1)S(1)}, u32[]{:S(2)}, u32[]{:S(2)}) collective-permute-start(bf16[72,896]{1,0:T(8,128)(2,1)S(1)} %after.12), channel_id=1, source_target_pairs={{0,2},{2,0},{1,3},{3,1},{4,6},{6,4},{5,7},{7,5},{8,10},{10,8},{9,1... | collective-permute-start | bytes 387080 | tf_op jit(solution)/shard_map/back1_tp/ppermute | solution.py:27
  32.0 11.0 %collective-permute-start.13 = (bf16[72,896]{1,0:T(8,128)(2,1)S(1)}, bf16[72,896]{1,0:T(8,128)(2,1)S(1)}, u32[]{:S(2)}, u32[]{:S(2)}) collective-permute-start(bf16[72,896]{1,0:T(8,128)(2,1)S(1)} %add_convert_fusion.2.earlier_ref), channel_id=1, source_target_pairs={{0,12},{4,8},{8,4},{12,0},{1,13},{5,9},{9,5},{13,1},{2,14},{6,10},... | collective-permute-start | bytes 387080 | tf_op jit(solution)/shard_map/back3_ep/ppermute | solution.py:27
  34.3 5.0 %collective-permute-start.11 = (bf16[72,896]{1,0:T(8,128)(2,1)S(1)}, bf16[72,896]{1,0:T(8,128)(2,1)S(1)}, u32[]{:S(2)}, u32[]{:S(2)}) collective-permute-start(bf16[72,896]{1,0:T(8,128)(2,1)S(1)} %get-tuple-element.51), channel_id=1, source_target_pairs={{0,2},{2,0},{1,3},{3,1},{4,6},{6,4},{5,7},{7,5},{8,10},{10,8},{9,1... | collective-permute-start | bytes 387080 | tf_op jit(solution)/shard_map/back2_tp/ppermute | solution.py:27
  35.3 7.7 %collective-permute-start.15 = (bf16[72,896]{1,0:T(8,128)(2,1)S(1)}, bf16[72,896]{1,0:T(8,128)(2,1)S(1)}, u32[]{:S(2)}, u32[]{:S(2)}) collective-permute-start(bf16[72,896]{1,0:T(8,128)(2,1)S(1)} %add_convert_fusion), channel_id=1, source_target_pairs={{0,4},{4,0},{8,12},{12,8},{1,5},{5,1},{9,13},{13,9},{2,6},{6,2},{1... | collective-permute-start | bytes 387080 | tf_op jit(solution)/shard_map/back1_ep/ppermute | solution.py:27
  39.3 7.8 %collective-permute-start.12 = (bf16[72,896]{1,0:T(8,128)(2,1)S(1)}, bf16[72,896]{1,0:T(8,128)(2,1)S(1)}, u32[]{:S(2)}, u32[]{:S(2)}) collective-permute-start(bf16[72,896]{1,0:T(8,128)(2,1)S(1)} %add_convert_fusion.1.earlier_ref), channel_id=1, source_target_pairs={{0,8},{4,12},{8,0},{12,4},{1,9},{5,13},{9,1},{13,5},{2,10},{6,14},... | collective-permute-start | bytes 387080 | tf_op jit(solution)/shard_map/back2_ep/ppermute | solution.py:27
  40.8 4.9 %collective-permute-start.16 = (bf16[72,896]{1,0:T(8,128)(2,1)S(1)}, bf16[72,896]{1,0:T(8,128)(2,1)S(1)}, u32[]{:S(2)}, u32[]{:S(2)}) collective-permute-start(bf16[72,896]{1,0:T(8,128)(2,1)S(1)} %after.13), channel_id=1, source_target_pairs={{0,2},{2,0},{1,3},{3,1},{4,6},{6,4},{5,7},{7,5},{8,10},{10,8},{9,1... | collective-permute-start | bytes 387080 | tf_op jit(solution)/shard_map/back0_tp/ppermute | solution.py:27

commit v7 on v6

--- a/solution.py
+++ b/solution.py
@@ -94,18 +94,23 @@
     return copies
 
 
-def pack_kernel(wide, most, order, *refs):
-    given, refs = refs[:4], refs[4:]
-    blocks, (place_ref, *held) = refs[: len(order)], refs[len(order) : -2]
-    ids_ref, sems = refs[-2:]
-    held = [ids_ref] + held
+def pack_kernel(most, order, *refs):
+    given, partial_ref, refs = refs[:4], refs[4], refs[5:]
+    blocks, (place_ref, share_ref), refs = refs[: len(order)], refs[len(order) :][:2], refs[-6:]
+    held, sems, share_sems = refs[:4], refs[4], refs[5]
+    lane, count = lax.axis_index("tp"), partial_ref.shape[0]
     copies = fetch(given, held, sems)
+    shares = fetch(
+        [partial_ref.at[lane ^ j] for j in range(count)],
+        [share_ref.at[j] for j in range(count)],
+        share_sems,
+    )
     copies[0].wait()
-    weights_ref, scales_ref, grad_ref = held[1:]
+    ids_ref, weights_ref, scales_ref, grad_ref = held
     tokens, rows = grad_ref.shape[0], blocks[0].shape[0]
     me = lax.axis_index("ep")
     ids = ids_ref[...]
-    expert = lax.broadcasted_iota(jnp.int32, (max(8, wide), tokens), 0)
+    expert = lax.broadcasted_iota(jnp.int32, (max(8, len(order)), tokens), 0)
     named = expert == ids
     before = lax.broadcasted_iota(jnp.int32, (tokens, tokens), 0) < lax.broadcasted_iota(
         jnp.int32, (tokens, tokens), 1
@@ -116,32 +121,23 @@
     position = jnp.sum(jnp.where(named, earlier, 0.0), axis=0, keepdims=True).astype(jnp.int32)
     row = lax.broadcasted_iota(jnp.int32, (rows, tokens), 0)
     found = []
-    for k in range(wide):
+    for k in order:
         local = jnp.where(ids == (me ^ k), position, -2 * rows)
-        found.append((row == local, row - most == local))
-        place_ref[0, k] = found[k][0].astype(jnp.bfloat16)
-        place_ref[1, k] = found[k][1].astype(jnp.bfloat16)
+        low, high = row == local, row - most == local
+        found.append((low, high))
+        place_ref[0, k] = low.astype(jnp.bfloat16)
+        place_ref[1, k] = high.astype(jnp.bfloat16)
     for copy in copies[1:]:
         copy.wait()
-    for block_ref, k in zip(blocks, order):
-        fill(block_ref, most, *found[k], weights_ref, scales_ref, grad_ref)
-
-
-def pack_more_kernel(most, order, place_ref, weights_ref, scales_ref, grad_ref, partial_ref, *refs):
-    taken = (len(refs) - 3 - len(order)) // 2
-    given, blocks, (share_ref, *held) = refs[:taken], refs[taken : -taken - 3], refs[-taken - 3 : -2]
-    sems, share_sems = refs[-2:]
-    lane, count = lax.axis_index("tp"), partial_ref.shape[0]
-    copies = fetch(
-        [partial_ref.at[lane ^ j] for j in range(count)],
-        [share_ref.at[j] for j in range(count)],
-        share_sems,
-    )
-    copies += fetch(given, held, sems)
-    for block_ref, k in zip(blocks, order):
-        low, high = place_ref[0, k] != 0, place_ref[1, k] != 0
+    for block_ref, (low, high) in zip(blocks, found):
         fill(block_ref, most, low, high, weights_ref, scales_ref, grad_ref)
-    for copy in copies:
+    for copy in shares:
+        copy.wait()
+
+
+def fetch_kernel(*refs):
+    count = len(refs) // 2
+    for copy in fetch(refs[:count], refs[count : 2 * count], refs[-1]):
         copy.wait()
 
 
@@ -247,29 +243,43 @@
     f32, bf16 = jnp.float32, jnp.bfloat16
     block = pltpu.VMEM((rows, half), bf16)
     groups = groups_of(wide)
-    order, more = groups[0], [k for group in groups[1:] for k in group]
+    order = [k for group in groups for k in group]
+    partials = latent_partials.reshape(narrow, tokens, latent.shape[1])
     packed = call(
-        functools.partial(pack_kernel, wide, most, order),
-        [block] * len(order)
-        + [
-            pltpu.VMEM((2, wide, rows, tokens), bf16),
-            pltpu.VMEM((1, tokens), f32),
-            pltpu.VMEM((grad_scales.shape[1], tokens), f32),
-            pltpu.VMEM((tokens, width), bf16),
-        ],
+        functools.partial(pack_kernel, most, order),
+        [block] * wide + [pltpu.VMEM((2, wide, rows, tokens), bf16), like(partials)],
         *pinned(
             expert_ids.reshape(1, tokens),
             route_weights.reshape(1, tokens),
             grad_scales.T,
             grad_values,
+            partials,
         ),
-        specs=[HBM] * 4,
-        scratch=[pltpu.VMEM((1, tokens), jnp.int32), pltpu.SemaphoreType.DMA((4,))],
+        specs=[HBM] * 5,
+        scratch=[
+            pltpu.VMEM((1, tokens), jnp.int32),
+            pltpu.VMEM((1, tokens), f32),
+            pltpu.VMEM((grad_scales.shape[1], tokens), f32),
+            pltpu.VMEM((tokens, width), bf16),
+            pltpu.SemaphoreType.DMA((4,)),
+            pltpu.SemaphoreType.DMA((narrow,)),
+        ],
         name="pack",
     )
-    place, *fillers = packed[len(order) :]
+    place, shares = packed[wide:]
     packed = dict(zip(order, packed))
-    partials = latent_partials.reshape(narrow, tokens, latent.shape[1])
+
+    def across(k, rows_of_k):
+        return [rows_of_k] + [swap(rows_of_k, "tp", j, f"rows{k}") for j in range(1, narrow)]
+
+    taken = {0: across(0, packed[0])}
+    first = groups[0][0]
+    arrived = {}
+    for k in order:
+        if k:
+            arrived[k] = swap(packed[k], "ep", k, f"rows{k}")
+            if len(groups) > 1 and k == groups[1][0]:
+                arrived[k] = after(arrived[k], packed[first], 1 << 31)
     fetched = [
         w_down[0],
         pre_acts.reshape(2, wide, narrow * most, hidden_width),
@@ -278,34 +288,16 @@
         latent,
         latent_gain.reshape(1, -1),
     ]
-    blocks = call(
-        functools.partial(pack_more_kernel, most, more),
-        [block] * len(more) + [like(partials)] + [like(array) for array in fetched],
-        place,
-        *fillers,
-        *pinned(partials, *fetched),
-        specs=[VMEM] * 4 + [HBM] * (1 + len(fetched)),
-        scratch=[
-            pltpu.SemaphoreType.DMA((len(fetched),)),
-            pltpu.SemaphoreType.DMA((narrow,)),
-        ],
-        cost=1 << 25,
-        name="pack_more",
-    )
-    packed.update(zip(more, blocks))
-    shares, down, pre, gate, up, latent, latent_gain = blocks[len(more) :]
-
-    def across(k, rows_of_k):
-        return [rows_of_k] + [swap(rows_of_k, "tp", j, f"rows{k}") for j in range(1, narrow)]
-
-    taken = {0: across(0, packed[0])}
-    first = groups[0][0]
-    arrived = {}
-    for k in order + more:
-        if k:
-            arrived[k] = swap(packed[k], "ep", k, f"rows{k}")
-            if len(groups) > 1 and k == groups[1][0]:
-                arrived[k] = after(arrived[k], packed[first], 1 << 31)
+    down, pre, gate, up, latent, latent_gain = call(
+        fetch_kernel,
+        [like(array) for array in fetched],
+        *pinned(*fetched),
+        specs=[HBM] * len(fetched),
+        scratch=[pltpu.SemaphoreType.DMA((len(fetched),))],
+        cost=1 << 31,
+        earlier=[arrived[first]],
+        name="fetch",
+    )
     latent_parts = [shares[0]] + [
         swap(shares[j], "tp", j, "latent") for j in range(1, narrow)
     ]

time: 48.4 us -> 48.6 us (level)
  waiting for transfers between devices: 15.1 us -> 16 us
  starting transfers between devices: 20.7 us -> 19.8 us
    ppermute x17, waiting for transfers between devices: 15.1 us -> 16 us  [swap(): return lax.ppermute(value, axis, [(i, i ^ step) for i in range(count)])]
    ppermute x17, starting transfers between devices: 20.7 us -> 19.8 us  [swap(): return lax.ppermute(value, axis, [(i, i ^ step) for i in range(count)])]
  transfers between devices with their start and end apart: 17 -> 17, of which waited for: 9 -> 10; matrix products, arithmetic and copies ran while one was open for 2% -> 2% of each run, Pallas kernels for 15% -> 15%
where the time goes in v7:
time: 48.6 us; the launch traced here: 48.5 us
  starting transfers between devices  19.8 us (41%)
  waiting for transfers between devices  16 us (33%)
  Pallas kernels  10.8 us (22%)
  other arithmetic  1 us (2%)
  between operations  0.78 us (2%)
    ppermute x17, starting transfers between devices, swap(): return lax.ppermute(value, axis, [(i, i ^ step) for i in range(count)])  19.8 us
    ppermute x17, waiting for transfers between devices, swap(): return lax.ppermute(value, axis, [(i, i ^ step) for i in range(count)])  16 us
    pallas_call x8, Pallas kernels, call(): pl.pallas_call(kernel, out_shape=outs, in_specs=specs, out_specs=[VMEM] *...  10.8 us
  transfers between devices with their start and end apart: 17, of which 10 were waited for; matrix products, arithmetic and copies ran while one was open for 2% of the time, Pallas kernels for 15%

profile of v7, /device:TPU:0, one launch (start us, length us, event | category | flops | bytes accessed | tf_op | source)
XLA Modules:
  0.0 48.5 jit_solution(7443691683315297995)
XLA Ops:
  0.6 2.3 %pack.1 = (bf16[72,896]{1,0:T(8,128)(2,1)S(1)}, bf16[72,896]{1,0:T(8,128)(2,1)S(1)}, bf16[72,896]{1,0:T(8,128)(2,1)S(1)}, bf16[72,896]{1,0:T(8,128)(2,1)S(1)}, b...) custom-call(s32[1,128]{1,0:T(1,128)} %bitcast.31, f32[1,128]{1,0:T(1,128)} %bitcast.32, ...), custom_call_target="tpu_custom_call" | custom-call | tf_op jit(solution)/shard_map/pack/pallas_call | solution.py:46
  3.0 5.1 %collective-permute-start.2 = (bf16[72,896]{1,0:T(8,128)(2,1)S(1)}, bf16[72,896]{1,0:T(8,128)(2,1)S(1)}, u32[]{:S(2)}, u32[]{:S(2)}) collective-permute-start(bf16[72,896]{1,0:T(8,128)(2,1)S(1)} %get-tuple-element.28.earlier_ref), channel_id=1, source_target_pairs={{0,12},{4,8},{8,4},{12,0},{1,13},{5,9},{9,5},{13,1},{2,14},{6,10},... | collective-permute-start | bytes 387080 | tf_op jit(solution)/shard_map/rows3_ep/ppermute | solution.py:27
  8.1 1.5 %collective-permute-start.6 = (bf16[72,896]{1,0:T(8,128)(2,1)S(1)}, bf16[72,896]{1,0:T(8,128)(2,1)S(1)}, u32[]{:S(2)}, u32[]{:S(2)}) collective-permute-start(bf16[72,896]{1,0:T(8,128)(2,1)S(1)} %get-tuple-element.30.refs_4_), channel_id=1, source_target_pairs={{0,2},{2,0},{1,3},{3,1},{4,6},{6,4},{5,7},{7,5},{8,10},{10,8},{9,1... | collective-permute-start | bytes 387080 | tf_op jit(solution)/shard_map/rows0_tp/ppermute | solution.py:27
  10.8 4.6 %collective-permute-done.4.refs_2_ = bf16[72,896]{1,0:T(8,128)(2,1)S(1)} collective-permute-done((bf16[72,896]{1,0:T(8,128)(2,1)S(1)}, bf16[72,896]{1,0:T(8,128)(2,1)S(1)}, u32[]{:S(2)}, u32[]{:S(2)}) %collective-permute-start.4) | collective-permute-done | bytes 129056 | tf_op jit(solution)/shard_map/rows1_ep/ppermute | solution.py:27
  15.4 1.5 %collective-permute-start.5 = (bf16[72,896]{1,0:T(8,128)(2,1)S(1)}, bf16[72,896]{1,0:T(8,128)(2,1)S(1)}, u32[]{:S(2)}, u32[]{:S(2)}) collective-permute-start(bf16[72,896]{1,0:T(8,128)(2,1)S(1)} %collective-permute-done.4.refs_2_), channel_id=1, source_target_pairs={{0,2},{2,0},{1,3},{3,1},{4,6},{6,4},{5,7},{7,5},{8,10},{10,8},{9,1... | collective-permute-start | bytes 387080 | tf_op jit(solution)/shard_map/rows1_tp/ppermute | solution.py:27
  17.4 2.8 %fetch.1 = (bf16[512,1792]{1,0:T(8,128)(2,1)S(1)}, bf16[2,4,72,512]{3,2,1,0:T(8,128)(2,1)S(1)}, bf16[1792,512]{1,0:T(8,128)(2,1)S(1)}, bf16[1792,512]{1,0:T(8,12...) custom-call(bf16[512,1792]{1,0:T(8,128)(2,1)} %bitcast.33, bf16[2,4,72,512]{3,2,1,0:T(8,128)(2,1)} %bitcast.36, ...), custom_call_target="tpu_custom_call" | custom-call | flops 2147483648 | tf_op jit(solution)/shard_map/fetch/pallas_call | solution.py:46
  20.3 1.4 %collective-permute-done.5.value_ref = bf16[72,896]{1,0:T(8,128)(2,1)S(1)} collective-permute-done((bf16[72,896]{1,0:T(8,128)(2,1)S(1)}, bf16[72,896]{1,0:T(8,128)(2,1)S(1)}, u32[]{:S(2)}, u32[]{:S(2)}) %collective-permute-start.5) | collective-permute-done | bytes 129056 | tf_op jit(solution)/shard_map/rows1_tp/ppermute | solution.py:27
  21.7 1.4 %collective-permute-done.3.refs_1_ = bf16[72,896]{1,0:T(8,128)(2,1)S(1)} collective-permute-done((bf16[72,896]{1,0:T(8,128)(2,1)S(1)}, bf16[72,896]{1,0:T(8,128)(2,1)S(1)}, u32[]{:S(2)}, u32[]{:S(2)}) %collective-permute-start.3) | collective-permute-done | bytes 129056 | tf_op jit(solution)/shard_map/rows3_tp/ppermute | solution.py:27
  23.1 0.8 %hidden.2 = (f32[216,512]{1,0:T(8,128)S(1)}, bf16[216,512]{1,0:T(8,128)(2,1)S(1)}) custom-call(bf16[72,896]{1,0:T(8,128)(2,1)S(1)} %collective-permute-done.2.refs_6_.refs_0_, bf16[72,896]{1,0:T(8,128)(2,1)S(1)} %collective-permute-done.3.refs_1_, bf16[72,896]{1,0:T(8,128)(2,1)S(1)} %collective-permute-done.4.refs_2_, bf16[72,896]{1,0:T(8,128)(2,1)S(1)} %after.8.refs_3_, ...), custom_call_target="tpu_custom_call" | custom-call | tf_op jit(solution)/shard_map/hidden/pallas_call | solution.py:46
  24.0 1.4 %collective-permute-start.1 = (bf16[72,896]{1,0:T(8,128)(2,1)S(1)}, bf16[72,896]{1,0:T(8,128)(2,1)S(1)}, u32[]{:S(2)}, u32[]{:S(2)}) collective-permute-start(bf16[72,896]{1,0:T(8,128)(2,1)S(1)} %after.7.refs_0_), channel_id=1, source_target_pairs={{0,2},{2,0},{1,3},{3,1},{4,6},{6,4},{5,7},{7,5},{8,10},{10,8},{9,1... | collective-permute-start | bytes 387080 | tf_op jit(solution)/shard_map/rows2_tp/ppermute | solution.py:27
  25.4 1.4 %back.2 = (bf16[72,896]{1,0:T(8,128)(2,1)S(1)}, bf16[72,896]{1,0:T(8,128)(2,1)S(1)}, bf16[72,896]{1,0:T(8,128)(2,1)S(1)}, bf16[72,896]{1,0:T(8,128)(2,1)S(1)}, b...) custom-call(f32[216,512]{1,0:T(8,128)S(1)} %get-tuple-element.32.sum_ref.earlier_ref, ...), custom_call_target="tpu_custom_call" | custom-call | tf_op jit(solution)/shard_map/back/pallas_call | solution.py:46
  26.8 1.4 %collective-permute-start.10 = (bf16[72,896]{1,0:T(8,128)(2,1)S(1)}, bf16[72,896]{1,0:T(8,128)(2,1)S(1)}, u32[]{:S(2)}, u32[]{:S(2)}) collective-permute-start(bf16[72,896]{1,0:T(8,128)(2,1)S(1)} %get-tuple-element.43), channel_id=1, source_target_pairs={{0,2},{2,0},{1,3},{3,1},{4,6},{6,4},{5,7},{7,5},{8,10},{10,8},{9,1... | collective-permute-start | bytes 387080 | tf_op jit(solution)/shard_map/back3_tp/ppermute | solution.py:27
  28.3 1.7 %collective-permute-done.1.value_ref = bf16[72,896]{1,0:T(8,128)(2,1)S(1)} collective-permute-done((bf16[72,896]{1,0:T(8,128)(2,1)S(1)}, bf16[72,896]{1,0:T(8,128)(2,1)S(1)}, u32[]{:S(2)}, u32[]{:S(2)}) %collective-permute-start.1) | collective-permute-done | bytes 129056 | tf_op jit(solution)/shard_map/rows2_tp/ppermute | solution.py:27
  30.7 1.4 %collective-permute-start.14 = (bf16[72,896]{1,0:T(8,128)(2,1)S(1)}, bf16[72,896]{1,0:T(8,128)(2,1)S(1)}, u32[]{:S(2)}, u32[]{:S(2)}) collective-permute-start(bf16[72,896]{1,0:T(8,128)(2,1)S(1)} %after.12), channel_id=1, source_target_pairs={{0,2},{2,0},{1,3},{3,1},{4,6},{6,4},{5,7},{7,5},{8,10},{10,8},{9,1... | collective-permute-start | bytes 387080 | tf_op jit(solution)/shard_map/back1_tp/ppermute | solution.py:27
  32.6 1.2 %back.3 = (bf16[72,896]{1,0:T(8,128)(2,1)S(1)}, bf16[72,896]{1,0:T(8,128)(2,1)S(1)}) custom-call(f32[72,512]{1,0:T(8,128)S(1)} %get-tuple-element.41.sum_ref.earlier_ref, bf16[88,512]{1,0:T(8,128)(2,1)S(1)} %after.11.other_ref, bf16[2,4,72,512]{3,2,1,0:T(8,128)(2,1)S(1)} %get-tuple-element.34.pre_ref, bf16[1792,512]{1,0:T(8,128)(2,1)S(1)} %get-tuple-element.35.gate_ref, ...), custom_call_target="tpu_custom_call" | custom-call | tf_op jit(solution)/shard_map/back/pallas_call | solution.py:46
  34.5 1.5 %collective-permute-start.11 = (bf16[72,896]{1,0:T(8,128)(2,1)S(1)}, bf16[72,896]{1,0:T(8,128)(2,1)S(1)}, u32[]{:S(2)}, u32[]{:S(2)}) collective-permute-start(bf16[72,896]{1,0:T(8,128)(2,1)S(1)} %get-tuple-element.45), channel_id=1, source_target_pairs={{0,2},{2,0},{1,3},{3,1},{4,6},{6,4},{5,7},{7,5},{8,10},{10,8},{9,1... | collective-permute-start | bytes 387080 | tf_op jit(solution)/shard_map/back2_tp/ppermute | solution.py:27
  36.6 0.7 %collective-permute-start.15 = (bf16[72,896]{1,0:T(8,128)(2,1)S(1)}, bf16[72,896]{1,0:T(8,128)(2,1)S(1)}, u32[]{:S(2)}, u32[]{:S(2)}) collective-permute-start(bf16[72,896]{1,0:T(8,128)(2,1)S(1)} %add_convert_fusion), channel_id=1, source_target_pairs={{0,4},{4,0},{8,12},{12,8},{1,5},{5,1},{9,13},{13,9},{2,6},{6,2},{1... | collective-permute-start | bytes 387080 | tf_op jit(solution)/shard_map/back1_ep/ppermute | solution.py:27
  37.3 2.1 %collective-permute-done.11 = bf16[72,896]{1,0:T(8,128)(2,1)S(1)} collective-permute-done((bf16[72,896]{1,0:T(8,128)(2,1)S(1)}, bf16[72,896]{1,0:T(8,128)(2,1)S(1)}, u32[]{:S(2)}, u32[]{:S(2)}) %collective-permute-start.11) | collective-permute-done | bytes 129056 | tf_op jit(solution)/shard_map/back2_tp/ppermute | solution.py:27
  39.5 1.6 %collective-permute-start.12 = (bf16[72,896]{1,0:T(8,128)(2,1)S(1)}, bf16[72,896]{1,0:T(8,128)(2,1)S(1)}, u32[]{:S(2)}, u32[]{:S(2)}) collective-permute-start(bf16[72,896]{1,0:T(8,128)(2,1)S(1)} %add_convert_fusion.1.earlier_ref), channel_id=1, source_target_pairs={{0,8},{4,12},{8,0},{12,4},{1,9},{5,13},{9,1},{13,5},{2,10},{6,14},... | collective-permute-start | bytes 387080 | tf_op jit(solution)/shard_map/back2_ep/ppermute | solution.py:27
  41.1 1.4 %collective-permute-start.16 = (bf16[72,896]{1,0:T(8,128)(2,1)S(1)}, bf16[72,896]{1,0:T(8,128)(2,1)S(1)}, u32[]{:S(2)}, u32[]{:S(2)}) collective-permute-start(bf16[72,896]{1,0:T(8,128)(2,1)S(1)} %after.13), channel_id=1, source_target_pairs={{0,2},{2,0},{1,3},{3,1},{4,6},{6,4},{5,7},{7,5},{8,10},{10,8},{9,1... | collective-permute-start | bytes 387080 | tf_op jit(solution)/shard_map/back0_tp/ppermute | solution.py:27
  42.5 0.7 %fusion.5 = bf16[128,256]{1,0:T(8,128)(2,1)} fusion(bf16[128,256]{1,0:T(8,128)(2,1)S(1)} %get-tuple-element.38, bf16[128,256]{1,0:T(8,128)(2,1)S(1)} %after.10, f32[128]{0:T(128)S(1)} %slice_bitcast_fusion.1, f32[128]{0:T(128)S(1)} %get-tuple-element.52, f32[128]{0:T(128)S(1)} %get-tuple-element.53, f32[256]{0:T(256)S(1)} %bitcast.24, ...), kind=kLoop, calls=%fused_computation.11 | loop fusion | flops 360448 | bytes 264704 | tf_op jit(solution)/shard_map/convert_element_type | solution.py:381
  43.2 2.3 %collective-permute-done.15.refs_1_ = bf16[72,896]{1,0:T(8,128)(2,1)S(1)} collective-permute-done((bf16[72,896]{1,0:T(8,128)(2,1)S(1)}, bf16[72,896]{1,0:T(8,128)(2,1)S(1)}, u32[]{:S(2)}, u32[]{:S(2)}) %collective-permute-start.15) | collective-permute-done | bytes 129056 | tf_op jit(solution)/shard_map/back1_ep/ppermute | solution.py:27
  46.6 0.8 %collective-permute-done.12.refs_0_ = bf16[72,896]{1,0:T(8,128)(2,1)S(1)} collective-permute-done((bf16[72,896]{1,0:T(8,128)(2,1)S(1)}, bf16[72,896]{1,0:T(8,128)(2,1)S(1)}, u32[]{:S(2)}, u32[]{:S(2)}) %collective-permute-start.12) | collective-permute-done | bytes 129056 | tf_op jit(solution)/shard_map/back2_ep/ppermute | solution.py:27
  47.4 1.1 %unpack_latest.1 = bf16[128,1792]{1,0:T(8,128)(2,1)} custom-call(bf16[2,4,72,128]{3,2,1,0:T(8,128)(2,1)S(1)} %get-tuple-element.26.place_ref, bf16[72,896]{1,0:T(8,128)(2,1)S(1)} %collective-permute-done.12.refs_0_, bf16[128,1792]{1,0:T(8,128)(2,1)S(1)} %unpack.1.refs_1_), custom_call_target="tpu_custom_call" | custom-call | tf_op jit(solution)/shard_map/unpack_latest/pallas_call | solution.py:46
  (36 shorter events, 5.6 us)
Async XLA Ops:
  3.0 13.9 %collective-permute-start.2 = (bf16[72,896]{1,0:T(8,128)(2,1)S(1)}, bf16[72,896]{1,0:T(8,128)(2,1)S(1)}, u32[]{:S(2)}, u32[]{:S(2)}) collective-permute-start(bf16[72,896]{1,0:T(8,128)(2,1)S(1)} %get-tuple-element.28.earlier_ref), channel_id=1, source_target_pairs={{0,12},{4,8},{8,4},{12,0},{1,13},{5,9},{9,5},{13,1},{2,14},{6,10},... | collective-permute-start | bytes 387080 | tf_op jit(solution)/shard_map/rows3_ep/ppermute | solution.py:27
  8.1 7.3 %collective-permute-start.4 = (bf16[72,896]{1,0:T(8,128)(2,1)S(1)}, bf16[72,896]{1,0:T(8,128)(2,1)S(1)}, u32[]{:S(2)}, u32[]{:S(2)}) collective-permute-start(bf16[72,896]{1,0:T(8,128)(2,1)S(1)} %get-tuple-element.29), channel_id=1, source_target_pairs={{0,4},{4,0},{8,12},{12,8},{1,5},{5,1},{9,13},{13,9},{2,6},{6,2},{1... | collective-permute-start | bytes 387080 | tf_op jit(solution)/shard_map/rows1_ep/ppermute | solution.py:27
  8.1 13.6 %collective-permute-start.6 = (bf16[72,896]{1,0:T(8,128)(2,1)S(1)}, bf16[72,896]{1,0:T(8,128)(2,1)S(1)}, u32[]{:S(2)}, u32[]{:S(2)}) collective-permute-start(bf16[72,896]{1,0:T(8,128)(2,1)S(1)} %get-tuple-element.30.refs_4_), channel_id=1, source_target_pairs={{0,2},{2,0},{1,3},{3,1},{4,6},{6,4},{5,7},{7,5},{8,10},{10,8},{9,1... | collective-permute-start | bytes 387080 | tf_op jit(solution)/shard_map/rows0_tp/ppermute | solution.py:27
  9.6 15.8 %collective-permute-start.8 = (bf16[128,256]{1,0:T(8,128)(2,1)S(1)}, bf16[128,256]{1,0:T(8,128)(2,1)S(1)}, u32[]{:S(2)}, u32[]{:S(2)}) collective-permute-start(bf16[128,256]{1,0:T(8,128)(2,1)S(1)} %slice_bitcast_fusion), channel_id=1, source_target_pairs={{0,2},{2,0},{1,3},{3,1},{4,6},{6,4},{5,7},{7,5},{8,10},{10,8},{9,1... | collective-permute-start | bytes 196616 | tf_op jit(solution)/shard_map/latent_tp/ppermute | solution.py:27
  10.1 13.8 %collective-permute-start = (bf16[72,896]{1,0:T(8,128)(2,1)S(1)}, bf16[72,896]{1,0:T(8,128)(2,1)S(1)}, u32[]{:S(2)}, u32[]{:S(2)}) collective-permute-start(bf16[72,896]{1,0:T(8,128)(2,1)S(1)} %get-tuple-element.27), channel_id=1, source_target_pairs={{0,8},{4,12},{8,0},{12,4},{1,9},{5,13},{9,1},{13,5},{2,10},{6,14},... | collective-permute-start | bytes 387080 | tf_op jit(solution)/shard_map/rows2_ep/ppermute | solution.py:27
  15.4 6.3 %collective-permute-start.5 = (bf16[72,896]{1,0:T(8,128)(2,1)S(1)}, bf16[72,896]{1,0:T(8,128)(2,1)S(1)}, u32[]{:S(2)}, u32[]{:S(2)}) collective-permute-start(bf16[72,896]{1,0:T(8,128)(2,1)S(1)} %collective-permute-done.4.refs_2_), channel_id=1, source_target_pairs={{0,2},{2,0},{1,3},{3,1},{4,6},{6,4},{5,7},{7,5},{8,10},{10,8},{9,1... | collective-permute-start | bytes 387080 | tf_op jit(solution)/shard_map/rows1_tp/ppermute | solution.py:27
  16.9 6.2 %collective-permute-start.3 = (bf16[72,896]{1,0:T(8,128)(2,1)S(1)}, bf16[72,896]{1,0:T(8,128)(2,1)S(1)}, u32[]{:S(2)}, u32[]{:S(2)}) collective-permute-start(bf16[72,896]{1,0:T(8,128)(2,1)S(1)} %collective-permute-done.2.refs_6_.refs_0_), channel_id=1, source_target_pairs={{0,2},{2,0},{1,3},{3,1},{4,6},{6,4},{5,7},{7,5},{8,10},{10,8},{9,1... | collective-permute-start | bytes 387080 | tf_op jit(solution)/shard_map/rows3_tp/ppermute | solution.py:27
  23.9 1.5 %collective-permute-start.7 = (bf16[216,512]{1,0:T(8,128)(2,1)S(1)}, bf16[216,512]{1,0:T(8,128)(2,1)S(1)}, u32[]{:S(2)}, u32[]{:S(2)}) collective-permute-start(bf16[216,512]{1,0:T(8,128)(2,1)S(1)} %get-tuple-element.33), channel_id=1, source_target_pairs={{0,1},{1,0},{2,3},{3,2},{4,5},{5,4},{6,7},{7,6},{8,9},{9,8},{10,11... | collective-permute-start | bytes 663560 | tf_op jit(solution)/shard_map/hidden3_sub/ppermute | solution.py:27
  24.0 6.0 %collective-permute-start.1 = (bf16[72,896]{1,0:T(8,128)(2,1)S(1)}, bf16[72,896]{1,0:T(8,128)(2,1)S(1)}, u32[]{:S(2)}, u32[]{:S(2)}) collective-permute-start(bf16[72,896]{1,0:T(8,128)(2,1)S(1)} %after.7.refs_0_), channel_id=1, source_target_pairs={{0,2},{2,0},{1,3},{3,1},{4,6},{6,4},{5,7},{7,5},{8,10},{10,8},{9,1... | collective-permute-start | bytes 387080 | tf_op jit(solution)/shard_map/rows2_tp/ppermute | solution.py:27
  26.8 5.8 %collective-permute-start.10 = (bf16[72,896]{1,0:T(8,128)(2,1)S(1)}, bf16[72,896]{1,0:T(8,128)(2,1)S(1)}, u32[]{:S(2)}, u32[]{:S(2)}) collective-permute-start(bf16[72,896]{1,0:T(8,128)(2,1)S(1)} %get-tuple-element.43), channel_id=1, source_target_pairs={{0,2},{2,0},{1,3},{3,1},{4,6},{6,4},{5,7},{7,5},{8,10},{10,8},{9,1... | collective-permute-start | bytes 387080 | tf_op jit(solution)/shard_map/back3_tp/ppermute | solution.py:27
  30.7 2.0 %collective-permute-start.9 = (bf16[88,512]{1,0:T(8,128)(2,1)S(1)}, bf16[88,512]{1,0:T(8,128)(2,1)S(1)}, u32[]{:S(2)}, u32[]{:S(2)}) collective-permute-start(bf16[88,512]{1,0:T(8,128)(2,1)S(1)} %get-tuple-element.42), channel_id=1, source_target_pairs={{0,1},{1,0},{2,3},{3,2},{4,5},{5,4},{6,7},{7,6},{8,9},{9,8},{10,11... | collective-permute-start | bytes 270344 | tf_op jit(solution)/shard_map/hidden2_sub/ppermute | solution.py:27
  30.7 5.9 %collective-permute-start.14 = (bf16[72,896]{1,0:T(8,128)(2,1)S(1)}, bf16[72,896]{1,0:T(8,128)(2,1)S(1)}, u32[]{:S(2)}, u32[]{:S(2)}) collective-permute-start(bf16[72,896]{1,0:T(8,128)(2,1)S(1)} %after.12), channel_id=1, source_target_pairs={{0,2},{2,0},{1,3},{3,1},{4,6},{6,4},{5,7},{7,5},{8,10},{10,8},{9,1... | collective-permute-start | bytes 387080 | tf_op jit(solution)/shard_map/back1_tp/ppermute | solution.py:27
  33.9 11.6 %collective-permute-start.13 = (bf16[72,896]{1,0:T(8,128)(2,1)S(1)}, bf16[72,896]{1,0:T(8,128)(2,1)S(1)}, u32[]{:S(2)}, u32[]{:S(2)}) collective-permute-start(bf16[72,896]{1,0:T(8,128)(2,1)S(1)} %add_convert_fusion.2.earlier_ref), channel_id=1, source_target_pairs={{0,12},{4,8},{8,4},{12,0},{1,13},{5,9},{9,5},{13,1},{2,14},{6,10},... | collective-permute-start | bytes 387080 | tf_op jit(solution)/shard_map/back3_ep/ppermute | solution.py:27
  34.5 5.0 %collective-permute-start.11 = (bf16[72,896]{1,0:T(8,128)(2,1)S(1)}, bf16[72,896]{1,0:T(8,128)(2,1)S(1)}, u32[]{:S(2)}, u32[]{:S(2)}) collective-permute-start(bf16[72,896]{1,0:T(8,128)(2,1)S(1)} %get-tuple-element.45), channel_id=1, source_target_pairs={{0,2},{2,0},{1,3},{3,1},{4,6},{6,4},{5,7},{7,5},{8,10},{10,8},{9,1... | collective-permute-start | bytes 387080 | tf_op jit(solution)/shard_map/back2_tp/ppermute | solution.py:27
  36.6 8.8 %collective-permute-start.15 = (bf16[72,896]{1,0:T(8,128)(2,1)S(1)}, bf16[72,896]{1,0:T(8,128)(2,1)S(1)}, u32[]{:S(2)}, u32[]{:S(2)}) collective-permute-start(bf16[72,896]{1,0:T(8,128)(2,1)S(1)} %add_convert_fusion), channel_id=1, source_target_pairs={{0,4},{4,0},{8,12},{12,8},{1,5},{5,1},{9,13},{13,9},{2,6},{6,2},{1... | collective-permute-start | bytes 387080 | tf_op jit(solution)/shard_map/back1_ep/ppermute | solution.py:27
  39.5 7.9 %collective-permute-start.12 = (bf16[72,896]{1,0:T(8,128)(2,1)S(1)}, bf16[72,896]{1,0:T(8,128)(2,1)S(1)}, u32[]{:S(2)}, u32[]{:S(2)}) collective-permute-start(bf16[72,896]{1,0:T(8,128)(2,1)S(1)} %add_convert_fusion.1.earlier_ref), channel_id=1, source_target_pairs={{0,8},{4,12},{8,0},{12,4},{1,9},{5,13},{9,1},{13,5},{2,10},{6,14},... | collective-permute-start | bytes 387080 | tf_op jit(solution)/shard_map/back2_ep/ppermute | solution.py:27
  41.1 4.9 %collective-permute-start.16 = (bf16[72,896]{1,0:T(8,128)(2,1)S(1)}, bf16[72,896]{1,0:T(8,128)(2,1)S(1)}, u32[]{:S(2)}, u32[]{:S(2)}) collective-permute-start(bf16[72,896]{1,0:T(8,128)(2,1)S(1)} %after.13), channel_id=1, source_target_pairs={{0,2},{2,0},{1,3},{3,1},{4,6},{6,4},{5,7},{7,5},{8,10},{10,8},{9,1... | collective-permute-start | bytes 387080 | tf_op jit(solution)/shard_map/back0_tp/ppermute | solution.py:27

commit v8 on v7

--- a/solution.py
+++ b/solution.py
@@ -277,7 +277,8 @@
     arrived = {}
     for k in order:
         if k:
-            arrived[k] = swap(packed[k], "ep", k, f"rows{k}")
+            given = packed[k] if k in groups[0] else after(packed[k], arrived[1])
+            arrived[k] = swap(given, "ep", k, f"rows{k}")
             if len(groups) > 1 and k == groups[1][0]:
                 arrived[k] = after(arrived[k], packed[first], 1 << 31)
     fetched = [

time: 48.6 us -> 48.4 us (level)
  waiting for transfers between devices: 16 us -> 5.86 us
  starting transfers between devices: 19.8 us -> 29.7 us
    ppermute x17, waiting for transfers between devices: 16 us -> 5.86 us  [swap(): return lax.ppermute(value, axis, [(i, i ^ step) for i in range(count)])]
    ppermute x17, starting transfers between devices: 19.8 us -> 29.7 us  [swap(): return lax.ppermute(value, axis, [(i, i ^ step) for i in range(count)])]
  transfers between devices with their start and end apart: 17 -> 17, of which waited for: 10 -> 6; matrix products, arithmetic and copies ran while one was open for 2% -> 2% of each run, Pallas kernels for 15% -> 15%
where the time goes in v8:
time: 48.4 us; the launch traced here: 48.2 us
  starting transfers between devices  29.7 us (61%)
  Pallas kernels  10.9 us (23%)
  waiting for transfers between devices  5.86 us (12%)
  other arithmetic  1 us (2%)
  between operations  0.8 us (2%)
    ppermute x17, starting transfers between devices, swap(): return lax.ppermute(value, axis, [(i, i ^ step) for i in range(count)])  29.7 us
    pallas_call x8, Pallas kernels, call(): pl.pallas_call(kernel, out_shape=outs, in_specs=specs, out_specs=[VMEM] *...  10.8 us
    ppermute x17, waiting for transfers between devices, swap(): return lax.ppermute(value, axis, [(i, i ^ step) for i in range(count)])  5.86 us
  transfers between devices with their start and end apart: 17, of which 6 were waited for; matrix products, arithmetic and copies ran while one was open for 2% of the time, Pallas kernels for 15%

profile of v8, /device:TPU:0, one launch (start us, length us, event | category | flops | bytes accessed | tf_op | source)
XLA Modules:
  0.0 48.2 jit_solution(8189139363643081047)
XLA Ops:
  0.6 2.3 %pack.1 = (bf16[72,896]{1,0:T(8,128)(2,1)S(1)}, bf16[72,896]{1,0:T(8,128)(2,1)S(1)}, bf16[72,896]{1,0:T(8,128)(2,1)S(1)}, bf16[72,896]{1,0:T(8,128)(2,1)S(1)}, b...) custom-call(s32[1,128]{1,0:T(1,128)} %bitcast.31, f32[1,128]{1,0:T(1,128)} %bitcast.32, ...), custom_call_target="tpu_custom_call" | custom-call | tf_op jit(solution)/shard_map/pack/pallas_call | solution.py:46
  3.0 3.1 %collective-permute-start = (bf16[72,896]{1,0:T(8,128)(2,1)S(1)}, bf16[72,896]{1,0:T(8,128)(2,1)S(1)}, u32[]{:S(2)}, u32[]{:S(2)}) collective-permute-start(bf16[72,896]{1,0:T(8,128)(2,1)S(1)} %get-tuple-element.28), channel_id=1, source_target_pairs={{0,4},{4,0},{8,12},{12,8},{1,5},{5,1},{9,13},{13,9},{2,6},{6,2},{1... | collective-permute-start | bytes 387080 | tf_op jit(solution)/shard_map/rows1_ep/ppermute | solution.py:27
  6.1 2.5 %collective-permute-start.3 = (bf16[72,896]{1,0:T(8,128)(2,1)S(1)}, bf16[72,896]{1,0:T(8,128)(2,1)S(1)}, u32[]{:S(2)}, u32[]{:S(2)}) collective-permute-start(bf16[72,896]{1,0:T(8,128)(2,1)S(1)} %get-tuple-element.29.earlier_ref), channel_id=1, source_target_pairs={{0,12},{4,8},{8,4},{12,0},{1,13},{5,9},{9,5},{13,1},{2,14},{6,10},... | collective-permute-start | bytes 387080 | tf_op jit(solution)/shard_map/rows3_ep/ppermute | solution.py:27
  8.5 1.5 %collective-permute-start.6 = (bf16[72,896]{1,0:T(8,128)(2,1)S(1)}, bf16[72,896]{1,0:T(8,128)(2,1)S(1)}, u32[]{:S(2)}, u32[]{:S(2)}) collective-permute-start(bf16[72,896]{1,0:T(8,128)(2,1)S(1)} %get-tuple-element.30.refs_4_), channel_id=1, source_target_pairs={{0,2},{2,0},{1,3},{3,1},{4,6},{6,4},{5,7},{7,5},{8,10},{10,8},{9,1... | collective-permute-start | bytes 387080 | tf_op jit(solution)/shard_map/rows0_tp/ppermute | solution.py:27
  10.6 2.8 %collective-permute-start.1 = (bf16[72,896]{1,0:T(8,128)(2,1)S(1)}, bf16[72,896]{1,0:T(8,128)(2,1)S(1)}, u32[]{:S(2)}, u32[]{:S(2)}) collective-permute-start(bf16[72,896]{1,0:T(8,128)(2,1)S(1)} %after.8), channel_id=1, source_target_pairs={{0,8},{4,12},{8,0},{12,4},{1,9},{5,13},{9,1},{13,5},{2,10},{6,14},... | collective-permute-start | bytes 387080 | tf_op jit(solution)/shard_map/rows2_ep/ppermute | solution.py:27
  13.4 1.5 %collective-permute-start.5 = (bf16[72,896]{1,0:T(8,128)(2,1)S(1)}, bf16[72,896]{1,0:T(8,128)(2,1)S(1)}, u32[]{:S(2)}, u32[]{:S(2)}) collective-permute-start(bf16[72,896]{1,0:T(8,128)(2,1)S(1)} %collective-permute-done.earlier_ref.refs_2_), channel_id=1, source_target_pairs={{0,2},{2,0},{1,3},{3,1},{4,6},{6,4},{5,7},{7,5},{8,10},{10,8},{9,1... | collective-permute-start | bytes 387080 | tf_op jit(solution)/shard_map/rows1_tp/ppermute | solution.py:27
  14.9 0.8 %collective-permute-done.3.refs_6_.refs_0_ = bf16[72,896]{1,0:T(8,128)(2,1)S(1)} collective-permute-done((bf16[72,896]{1,0:T(8,128)(2,1)S(1)}, bf16[72,896]{1,0:T(8,128)(2,1)S(1)}, u32[]{:S(2)}, u32[]{:S(2)}) %collective-permute-start.3) | collective-permute-done | bytes 129056 | tf_op jit(solution)/shard_map/rows3_ep/ppermute | solution.py:27
  15.7 1.5 %collective-permute-start.4 = (bf16[72,896]{1,0:T(8,128)(2,1)S(1)}, bf16[72,896]{1,0:T(8,128)(2,1)S(1)}, u32[]{:S(2)}, u32[]{:S(2)}) collective-permute-start(bf16[72,896]{1,0:T(8,128)(2,1)S(1)} %collective-permute-done.3.refs_6_.refs_0_), channel_id=1, source_target_pairs={{0,2},{2,0},{1,3},{3,1},{4,6},{6,4},{5,7},{7,5},{8,10},{10,8},{9,1... | collective-permute-start | bytes 387080 | tf_op jit(solution)/shard_map/rows3_tp/ppermute | solution.py:27
  17.2 2.8 %fetch.1 = (bf16[512,1792]{1,0:T(8,128)(2,1)S(1)}, bf16[2,4,72,512]{3,2,1,0:T(8,128)(2,1)S(1)}, bf16[1792,512]{1,0:T(8,128)(2,1)S(1)}, bf16[1792,512]{1,0:T(8,12...) custom-call(bf16[512,1792]{1,0:T(8,128)(2,1)} %bitcast.33, bf16[2,4,72,512]{3,2,1,0:T(8,128)(2,1)} %bitcast.36, ...), custom_call_target="tpu_custom_call" | custom-call | flops 2147483648 | tf_op jit(solution)/shard_map/fetch/pallas_call | solution.py:46
  20.7 0.8 %hidden.2 = (f32[216,512]{1,0:T(8,128)S(1)}, bf16[216,512]{1,0:T(8,128)(2,1)S(1)}) custom-call(bf16[72,896]{1,0:T(8,128)(2,1)S(1)} %collective-permute-done.3.refs_6_.refs_0_, bf16[72,896]{1,0:T(8,128)(2,1)S(1)} %collective-permute-done.4.refs_1_, bf16[72,896]{1,0:T(8,128)(2,1)S(1)} %collective-permute-done.earlier_ref.refs_2_, ...), custom_call_target="tpu_custom_call" | custom-call | tf_op jit(solution)/shard_map/hidden/pallas_call | solution.py:46
  21.5 1.5 %collective-permute-start.2 = (bf16[72,896]{1,0:T(8,128)(2,1)S(1)}, bf16[72,896]{1,0:T(8,128)(2,1)S(1)}, u32[]{:S(2)}, u32[]{:S(2)}) collective-permute-start(bf16[72,896]{1,0:T(8,128)(2,1)S(1)} %after.9.refs_0_), channel_id=1, source_target_pairs={{0,2},{2,0},{1,3},{3,1},{4,6},{6,4},{5,7},{7,5},{8,10},{10,8},{9,1... | collective-permute-start | bytes 387080 | tf_op jit(solution)/shard_map/rows2_tp/ppermute | solution.py:27
  23.1 1.4 %back.2 = (bf16[72,896]{1,0:T(8,128)(2,1)S(1)}, bf16[72,896]{1,0:T(8,128)(2,1)S(1)}, bf16[72,896]{1,0:T(8,128)(2,1)S(1)}, bf16[72,896]{1,0:T(8,128)(2,1)S(1)}, b...) custom-call(f32[216,512]{1,0:T(8,128)S(1)} %get-tuple-element.32.sum_ref.earlier_ref, ...), custom_call_target="tpu_custom_call" | custom-call | tf_op jit(solution)/shard_map/back/pallas_call | solution.py:46
  24.5 1.4 %collective-permute-start.10 = (bf16[72,896]{1,0:T(8,128)(2,1)S(1)}, bf16[72,896]{1,0:T(8,128)(2,1)S(1)}, u32[]{:S(2)}, u32[]{:S(2)}) collective-permute-start(bf16[72,896]{1,0:T(8,128)(2,1)S(1)} %get-tuple-element.43), channel_id=1, source_target_pairs={{0,2},{2,0},{1,3},{3,1},{4,6},{6,4},{5,7},{7,5},{8,10},{10,8},{9,1... | collective-permute-start | bytes 387080 | tf_op jit(solution)/shard_map/back3_tp/ppermute | solution.py:27
  26.0 1.4 %collective-permute-done.2.value_ref = bf16[72,896]{1,0:T(8,128)(2,1)S(1)} collective-permute-done((bf16[72,896]{1,0:T(8,128)(2,1)S(1)}, bf16[72,896]{1,0:T(8,128)(2,1)S(1)}, u32[]{:S(2)}, u32[]{:S(2)}) %collective-permute-start.2) | collective-permute-done | bytes 129056 | tf_op jit(solution)/shard_map/rows2_tp/ppermute | solution.py:27
  28.2 1.7 %collective-permute-start.14 = (bf16[72,896]{1,0:T(8,128)(2,1)S(1)}, bf16[72,896]{1,0:T(8,128)(2,1)S(1)}, u32[]{:S(2)}, u32[]{:S(2)}) collective-permute-start(bf16[72,896]{1,0:T(8,128)(2,1)S(1)} %after.14), channel_id=1, source_target_pairs={{0,2},{2,0},{1,3},{3,1},{4,6},{6,4},{5,7},{7,5},{8,10},{10,8},{9,1... | collective-permute-start | bytes 387080 | tf_op jit(solution)/shard_map/back1_tp/ppermute | solution.py:27
  30.2 1.8 %collective-permute-start.13 = (bf16[72,896]{1,0:T(8,128)(2,1)S(1)}, bf16[72,896]{1,0:T(8,128)(2,1)S(1)}, u32[]{:S(2)}, u32[]{:S(2)}) collective-permute-start(bf16[72,896]{1,0:T(8,128)(2,1)S(1)} %add_convert_fusion.2.earlier_ref), channel_id=1, source_target_pairs={{0,12},{4,8},{8,4},{12,0},{1,13},{5,9},{9,5},{13,1},{2,14},{6,10},... | collective-permute-start | bytes 387080 | tf_op jit(solution)/shard_map/back3_ep/ppermute | solution.py:27
  32.0 1.2 %back.3 = (bf16[72,896]{1,0:T(8,128)(2,1)S(1)}, bf16[72,896]{1,0:T(8,128)(2,1)S(1)}) custom-call(f32[72,512]{1,0:T(8,128)S(1)} %get-tuple-element.41.sum_ref.earlier_ref, bf16[88,512]{1,0:T(8,128)(2,1)S(1)} %after.13.other_ref, bf16[2,4,72,512]{3,2,1,0:T(8,128)(2,1)S(1)} %get-tuple-element.34.pre_ref, bf16[1792,512]{1,0:T(8,128)(2,1)S(1)} %get-tuple-element.35.gate_ref, ...), custom_call_target="tpu_custom_call" | custom-call | tf_op jit(solution)/shard_map/back/pallas_call | solution.py:46
  33.3 1.4 %collective-permute-start.11 = (bf16[72,896]{1,0:T(8,128)(2,1)S(1)}, bf16[72,896]{1,0:T(8,128)(2,1)S(1)}, u32[]{:S(2)}, u32[]{:S(2)}) collective-permute-start(bf16[72,896]{1,0:T(8,128)(2,1)S(1)} %get-tuple-element.45), channel_id=1, source_target_pairs={{0,2},{2,0},{1,3},{3,1},{4,6},{6,4},{5,7},{7,5},{8,10},{10,8},{9,1... | collective-permute-start | bytes 387080 | tf_op jit(solution)/shard_map/back2_tp/ppermute | solution.py:27
  34.8 3.5 %collective-permute-start.15 = (bf16[72,896]{1,0:T(8,128)(2,1)S(1)}, bf16[72,896]{1,0:T(8,128)(2,1)S(1)}, u32[]{:S(2)}, u32[]{:S(2)}) collective-permute-start(bf16[72,896]{1,0:T(8,128)(2,1)S(1)} %add_convert_fusion), channel_id=1, source_target_pairs={{0,4},{4,0},{8,12},{12,8},{1,5},{5,1},{9,13},{13,9},{2,6},{6,2},{1... | collective-permute-start | bytes 387080 | tf_op jit(solution)/shard_map/back1_ep/ppermute | solution.py:27
  38.3 3.1 %collective-permute-start.12 = (bf16[72,896]{1,0:T(8,128)(2,1)S(1)}, bf16[72,896]{1,0:T(8,128)(2,1)S(1)}, u32[]{:S(2)}, u32[]{:S(2)}) collective-permute-start(bf16[72,896]{1,0:T(8,128)(2,1)S(1)} %add_convert_fusion.1.earlier_ref), channel_id=1, source_target_pairs={{0,8},{4,12},{8,0},{12,4},{1,9},{5,13},{9,1},{13,5},{2,10},{6,14},... | collective-permute-start | bytes 387080 | tf_op jit(solution)/shard_map/back2_ep/ppermute | solution.py:27
  41.5 1.6 %collective-permute-start.16 = (bf16[72,896]{1,0:T(8,128)(2,1)S(1)}, bf16[72,896]{1,0:T(8,128)(2,1)S(1)}, u32[]{:S(2)}, u32[]{:S(2)}) collective-permute-start(bf16[72,896]{1,0:T(8,128)(2,1)S(1)} %after.15), channel_id=1, source_target_pairs={{0,2},{2,0},{1,3},{3,1},{4,6},{6,4},{5,7},{7,5},{8,10},{10,8},{9,1... | collective-permute-start | bytes 387080 | tf_op jit(solution)/shard_map/back0_tp/ppermute | solution.py:27
  43.1 0.8 %fusion.5 = bf16[128,256]{1,0:T(8,128)(2,1)} fusion(bf16[128,256]{1,0:T(8,128)(2,1)S(1)} %get-tuple-element.38, bf16[128,256]{1,0:T(8,128)(2,1)S(1)} %after.12, f32[128]{0:T(128)S(1)} %slice_bitcast_fusion.1, f32[128]{0:T(128)S(1)} %get-tuple-element.52, f32[128]{0:T(128)S(1)} %get-tuple-element.53, f32[256]{0:T(256)S(1)} %bitcast.24, ...), kind=kLoop, calls=%fused_computation.11 | loop fusion | flops 360448 | bytes 264704 | tf_op jit(solution)/shard_map/convert_element_type | solution.py:382
  43.8 2.6 %collective-permute-done.16.refs_3_ = bf16[72,896]{1,0:T(8,128)(2,1)S(1)} collective-permute-done((bf16[72,896]{1,0:T(8,128)(2,1)S(1)}, bf16[72,896]{1,0:T(8,128)(2,1)S(1)}, u32[]{:S(2)}, u32[]{:S(2)}) %collective-permute-start.16) | collective-permute-done | bytes 129056 | tf_op jit(solution)/shard_map/back0_tp/ppermute | solution.py:27
  47.2 1.1 %unpack_latest.1 = bf16[128,1792]{1,0:T(8,128)(2,1)} custom-call(bf16[2,4,72,128]{3,2,1,0:T(8,128)(2,1)S(1)} %get-tuple-element.26.place_ref, bf16[72,896]{1,0:T(8,128)(2,1)S(1)} %collective-permute-done.12.refs_0_, bf16[128,1792]{1,0:T(8,128)(2,1)S(1)} %unpack.1.refs_1_), custom_call_target="tpu_custom_call" | custom-call | tf_op jit(solution)/shard_map/unpack_latest/pallas_call | solution.py:46
  (37 shorter events, 3.2 us)
Async XLA Ops:
  3.0 7.6 %collective-permute-start = (bf16[72,896]{1,0:T(8,128)(2,1)S(1)}, bf16[72,896]{1,0:T(8,128)(2,1)S(1)}, u32[]{:S(2)}, u32[]{:S(2)}) collective-permute-start(bf16[72,896]{1,0:T(8,128)(2,1)S(1)} %get-tuple-element.28), channel_id=1, source_target_pairs={{0,4},{4,0},{8,12},{12,8},{1,5},{5,1},{9,13},{13,9},{2,6},{6,2},{1... | collective-permute-start | bytes 387080 | tf_op jit(solution)/shard_map/rows1_ep/ppermute | solution.py:27
  6.1 9.7 %collective-permute-start.3 = (bf16[72,896]{1,0:T(8,128)(2,1)S(1)}, bf16[72,896]{1,0:T(8,128)(2,1)S(1)}, u32[]{:S(2)}, u32[]{:S(2)}) collective-permute-start(bf16[72,896]{1,0:T(8,128)(2,1)S(1)} %get-tuple-element.29.earlier_ref), channel_id=1, source_target_pairs={{0,12},{4,8},{8,4},{12,0},{1,13},{5,9},{9,5},{13,1},{2,14},{6,10},... | collective-permute-start | bytes 387080 | tf_op jit(solution)/shard_map/rows3_ep/ppermute | solution.py:27
  8.5 11.5 %collective-permute-start.6 = (bf16[72,896]{1,0:T(8,128)(2,1)S(1)}, bf16[72,896]{1,0:T(8,128)(2,1)S(1)}, u32[]{:S(2)}, u32[]{:S(2)}) collective-permute-start(bf16[72,896]{1,0:T(8,128)(2,1)S(1)} %get-tuple-element.30.refs_4_), channel_id=1, source_target_pairs={{0,2},{2,0},{1,3},{3,1},{4,6},{6,4},{5,7},{7,5},{8,10},{10,8},{9,1... | collective-permute-start | bytes 387080 | tf_op jit(solution)/shard_map/rows0_tp/ppermute | solution.py:27
  10.0 13.1 %collective-permute-start.8 = (bf16[128,256]{1,0:T(8,128)(2,1)S(1)}, bf16[128,256]{1,0:T(8,128)(2,1)S(1)}, u32[]{:S(2)}, u32[]{:S(2)}) collective-permute-start(bf16[128,256]{1,0:T(8,128)(2,1)S(1)} %slice_bitcast_fusion), channel_id=1, source_target_pairs={{0,2},{2,0},{1,3},{3,1},{4,6},{6,4},{5,7},{7,5},{8,10},{10,8},{9,1... | collective-permute-start | bytes 196616 | tf_op jit(solution)/shard_map/latent_tp/ppermute | solution.py:27
  10.6 10.9 %collective-permute-start.1 = (bf16[72,896]{1,0:T(8,128)(2,1)S(1)}, bf16[72,896]{1,0:T(8,128)(2,1)S(1)}, u32[]{:S(2)}, u32[]{:S(2)}) collective-permute-start(bf16[72,896]{1,0:T(8,128)(2,1)S(1)} %after.8), channel_id=1, source_target_pairs={{0,8},{4,12},{8,0},{12,4},{1,9},{5,13},{9,1},{13,5},{2,10},{6,14},... | collective-permute-start | bytes 387080 | tf_op jit(solution)/shard_map/rows2_ep/ppermute | solution.py:27
  13.4 6.6 %collective-permute-start.5 = (bf16[72,896]{1,0:T(8,128)(2,1)S(1)}, bf16[72,896]{1,0:T(8,128)(2,1)S(1)}, u32[]{:S(2)}, u32[]{:S(2)}) collective-permute-start(bf16[72,896]{1,0:T(8,128)(2,1)S(1)} %collective-permute-done.earlier_ref.refs_2_), channel_id=1, source_target_pairs={{0,2},{2,0},{1,3},{3,1},{4,6},{6,4},{5,7},{7,5},{8,10},{10,8},{9,1... | collective-permute-start | bytes 387080 | tf_op jit(solution)/shard_map/rows1_tp/ppermute | solution.py:27
  15.7 4.9 %collective-permute-start.4 = (bf16[72,896]{1,0:T(8,128)(2,1)S(1)}, bf16[72,896]{1,0:T(8,128)(2,1)S(1)}, u32[]{:S(2)}, u32[]{:S(2)}) collective-permute-start(bf16[72,896]{1,0:T(8,128)(2,1)S(1)} %collective-permute-done.3.refs_6_.refs_0_), channel_id=1, source_target_pairs={{0,2},{2,0},{1,3},{3,1},{4,6},{6,4},{5,7},{7,5},{8,10},{10,8},{9,1... | collective-permute-start | bytes 387080 | tf_op jit(solution)/shard_map/rows3_tp/ppermute | solution.py:27
  21.4 1.7 %collective-permute-start.7 = (bf16[216,512]{1,0:T(8,128)(2,1)S(1)}, bf16[216,512]{1,0:T(8,128)(2,1)S(1)}, u32[]{:S(2)}, u32[]{:S(2)}) collective-permute-start(bf16[216,512]{1,0:T(8,128)(2,1)S(1)} %get-tuple-element.33), channel_id=1, source_target_pairs={{0,1},{1,0},{2,3},{3,2},{4,5},{5,4},{6,7},{7,6},{8,9},{9,8},{10,11... | collective-permute-start | bytes 663560 | tf_op jit(solution)/shard_map/hidden3_sub/ppermute | solution.py:27
  21.5 5.9 %collective-permute-start.2 = (bf16[72,896]{1,0:T(8,128)(2,1)S(1)}, bf16[72,896]{1,0:T(8,128)(2,1)S(1)}, u32[]{:S(2)}, u32[]{:S(2)}) collective-permute-start(bf16[72,896]{1,0:T(8,128)(2,1)S(1)} %after.9.refs_0_), channel_id=1, source_target_pairs={{0,2},{2,0},{1,3},{3,1},{4,6},{6,4},{5,7},{7,5},{8,10},{10,8},{9,1... | collective-permute-start | bytes 387080 | tf_op jit(solution)/shard_map/rows2_tp/ppermute | solution.py:27
  24.5 5.7 %collective-permute-start.10 = (bf16[72,896]{1,0:T(8,128)(2,1)S(1)}, bf16[72,896]{1,0:T(8,128)(2,1)S(1)}, u32[]{:S(2)}, u32[]{:S(2)}) collective-permute-start(bf16[72,896]{1,0:T(8,128)(2,1)S(1)} %get-tuple-element.43), channel_id=1, source_target_pairs={{0,2},{2,0},{1,3},{3,1},{4,6},{6,4},{5,7},{7,5},{8,10},{10,8},{9,1... | collective-permute-start | bytes 387080 | tf_op jit(solution)/shard_map/back3_tp/ppermute | solution.py:27
  28.1 3.9 %collective-permute-start.9 = (bf16[88,512]{1,0:T(8,128)(2,1)S(1)}, bf16[88,512]{1,0:T(8,128)(2,1)S(1)}, u32[]{:S(2)}, u32[]{:S(2)}) collective-permute-start(bf16[88,512]{1,0:T(8,128)(2,1)S(1)} %get-tuple-element.42), channel_id=1, source_target_pairs={{0,1},{1,0},{2,3},{3,2},{4,5},{5,4},{6,7},{7,6},{8,9},{9,8},{10,11... | collective-permute-start | bytes 270344 | tf_op jit(solution)/shard_map/hidden2_sub/ppermute | solution.py:27
  28.2 6.5 %collective-permute-start.14 = (bf16[72,896]{1,0:T(8,128)(2,1)S(1)}, bf16[72,896]{1,0:T(8,128)(2,1)S(1)}, u32[]{:S(2)}, u32[]{:S(2)}) collective-permute-start(bf16[72,896]{1,0:T(8,128)(2,1)S(1)} %after.14), channel_id=1, source_target_pairs={{0,2},{2,0},{1,3},{3,1},{4,6},{6,4},{5,7},{7,5},{8,10},{10,8},{9,1... | collective-permute-start | bytes 387080 | tf_op jit(solution)/shard_map/back1_tp/ppermute | solution.py:27
  30.2 13.6 %collective-permute-start.13 = (bf16[72,896]{1,0:T(8,128)(2,1)S(1)}, bf16[72,896]{1,0:T(8,128)(2,1)S(1)}, u32[]{:S(2)}, u32[]{:S(2)}) collective-permute-start(bf16[72,896]{1,0:T(8,128)(2,1)S(1)} %add_convert_fusion.2.earlier_ref), channel_id=1, source_target_pairs={{0,12},{4,8},{8,4},{12,0},{1,13},{5,9},{9,5},{13,1},{2,14},{6,10},... | collective-permute-start | bytes 387080 | tf_op jit(solution)/shard_map/back3_ep/ppermute | solution.py:27
  33.3 5.0 %collective-permute-start.11 = (bf16[72,896]{1,0:T(8,128)(2,1)S(1)}, bf16[72,896]{1,0:T(8,128)(2,1)S(1)}, u32[]{:S(2)}, u32[]{:S(2)}) collective-permute-start(bf16[72,896]{1,0:T(8,128)(2,1)S(1)} %get-tuple-element.45), channel_id=1, source_target_pairs={{0,2},{2,0},{1,3},{3,1},{4,6},{6,4},{5,7},{7,5},{8,10},{10,8},{9,1... | collective-permute-start | bytes 387080 | tf_op jit(solution)/shard_map/back2_tp/ppermute | solution.py:27
  34.8 9.1 %collective-permute-start.15 = (bf16[72,896]{1,0:T(8,128)(2,1)S(1)}, bf16[72,896]{1,0:T(8,128)(2,1)S(1)}, u32[]{:S(2)}, u32[]{:S(2)}) collective-permute-start(bf16[72,896]{1,0:T(8,128)(2,1)S(1)} %add_convert_fusion), channel_id=1, source_target_pairs={{0,4},{4,0},{8,12},{12,8},{1,5},{5,1},{9,13},{13,9},{2,6},{6,2},{1... | collective-permute-start | bytes 387080 | tf_op jit(solution)/shard_map/back1_ep/ppermute | solution.py:27
  38.3 8.8 %collective-permute-start.12 = (bf16[72,896]{1,0:T(8,128)(2,1)S(1)}, bf16[72,896]{1,0:T(8,128)(2,1)S(1)}, u32[]{:S(2)}, u32[]{:S(2)}) collective-permute-start(bf16[72,896]{1,0:T(8,128)(2,1)S(1)} %add_convert_fusion.1.earlier_ref), channel_id=1, source_target_pairs={{0,8},{4,12},{8,0},{12,4},{1,9},{5,13},{9,1},{13,5},{2,10},{6,14},... | collective-permute-start | bytes 387080 | tf_op jit(solution)/shard_map/back2_ep/ppermute | solution.py:27
  41.5 4.9 %collective-permute-start.16 = (bf16[72,896]{1,0:T(8,128)(2,1)S(1)}, bf16[72,896]{1,0:T(8,128)(2,1)S(1)}, u32[]{:S(2)}, u32[]{:S(2)}) collective-permute-start(bf16[72,896]{1,0:T(8,128)(2,1)S(1)} %after.15), channel_id=1, source_target_pairs={{0,2},{2,0},{1,3},{3,1},{4,6},{6,4},{5,7},{7,5},{8,10},{10,8},{9,1... | collective-permute-start | bytes 387080 | tf_op jit(solution)/shard_map/back0_tp/ppermute | solution.py:27

commit v9 on v8

--- a/solution.py
+++ b/solution.py
@@ -277,7 +277,7 @@
     arrived = {}
     for k in order:
         if k:
-            given = packed[k] if k in groups[0] else after(packed[k], arrived[1])
+            given = packed[k] if k in groups[0] else after(packed[k], arrived[first])
             arrived[k] = swap(given, "ep", k, f"rows{k}")
             if len(groups) > 1 and k == groups[1][0]:
                 arrived[k] = after(arrived[k], packed[first], 1 << 31)
@@ -295,7 +295,6 @@
         *pinned(*fetched),
         specs=[HBM] * len(fetched),
         scratch=[pltpu.SemaphoreType.DMA((len(fetched),))],
-        cost=1 << 31,
         earlier=[arrived[first]],
         name="fetch",
     )

time: 48.4 us -> 48 us (level)
  starting transfers between devices: 29.7 us -> 25.6 us
  waiting for transfers between devices: 5.86 us -> 9.62 us
    ppermute x17, starting transfers between devices: 29.7 us -> 25.6 us  [swap(): return lax.ppermute(value, axis, [(i, i ^ step) for i in range(count)])]
    ppermute x17, waiting for transfers between devices: 5.86 us -> 9.62 us  [swap(): return lax.ppermute(value, axis, [(i, i ^ step) for i in range(count)])]
  transfers between devices with their start and end apart: 17 -> 17, of which waited for: 6 -> 7; matrix products, arithmetic and copies ran while one was open for 2% -> 2% of each run, Pallas kernels for 15% -> 16%
where the time goes in v9:
time: 48 us; the launch traced here: 47.8 us
  starting transfers between devices  25.6 us (53%)
  Pallas kernels  10.8 us (22%)
  waiting for transfers between devices  9.62 us (20%)
  other arithmetic  1 us (2%)
  between operations  0.79 us (2%)
    ppermute x17, starting transfers between devices, swap(): return lax.ppermute(value, axis, [(i, i ^ step) for i in range(count)])  25.6 us
    pallas_call x8, Pallas kernels, call(): pl.pallas_call(kernel, out_shape=outs, in_specs=specs, out_specs=[VMEM] *...  10.8 us
    ppermute x17, waiting for transfers between devices, swap(): return lax.ppermute(value, axis, [(i, i ^ step) for i in range(count)])  9.62 us
  transfers between devices with their start and end apart: 17, of which 7 were waited for; matrix products, arithmetic and copies ran while one was open for 2% of the time, Pallas kernels for 16%

profile of v9, /device:TPU:0, one launch (start us, length us, event | category | flops | bytes accessed | tf_op | source)
XLA Modules:
  0.0 47.8 jit_solution(15510350569774307582)
XLA Ops:
  0.6 2.3 %pack.1 = (bf16[72,896]{1,0:T(8,128)(2,1)S(1)}, bf16[72,896]{1,0:T(8,128)(2,1)S(1)}, bf16[72,896]{1,0:T(8,128)(2,1)S(1)}, bf16[72,896]{1,0:T(8,128)(2,1)S(1)}, b...) custom-call(s32[1,128]{1,0:T(1,128)} %bitcast.36, f32[1,128]{1,0:T(1,128)} %bitcast.37, ...), custom_call_target="tpu_custom_call" | custom-call | tf_op jit(solution)/shard_map/pack/pallas_call | solution.py:46
  3.0 3.1 %collective-permute-start.4 = (bf16[72,896]{1,0:T(8,128)(2,1)S(1)}, bf16[72,896]{1,0:T(8,128)(2,1)S(1)}, u32[]{:S(2)}, u32[]{:S(2)}) collective-permute-start(bf16[72,896]{1,0:T(8,128)(2,1)S(1)} %get-tuple-element.29), channel_id=1, source_target_pairs={{0,4},{4,0},{8,12},{12,8},{1,5},{5,1},{9,13},{13,9},{2,6},{6,2},{1... | collective-permute-start | bytes 387080 | tf_op jit(solution)/shard_map/rows1_ep/ppermute | solution.py:27
  6.1 2.5 %collective-permute-start = (bf16[72,896]{1,0:T(8,128)(2,1)S(1)}, bf16[72,896]{1,0:T(8,128)(2,1)S(1)}, u32[]{:S(2)}, u32[]{:S(2)}) collective-permute-start(bf16[72,896]{1,0:T(8,128)(2,1)S(1)} %get-tuple-element.28.earlier_ref), channel_id=1, source_target_pairs={{0,12},{4,8},{8,4},{12,0},{1,13},{5,9},{9,5},{13,1},{2,14},{6,10},... | collective-permute-start | bytes 387080 | tf_op jit(solution)/shard_map/rows3_ep/ppermute | solution.py:27
  8.5 1.5 %collective-permute-start.6 = (bf16[72,896]{1,0:T(8,128)(2,1)S(1)}, bf16[72,896]{1,0:T(8,128)(2,1)S(1)}, u32[]{:S(2)}, u32[]{:S(2)}) collective-permute-start(bf16[72,896]{1,0:T(8,128)(2,1)S(1)} %get-tuple-element.30.refs_4_), channel_id=1, source_target_pairs={{0,2},{2,0},{1,3},{3,1},{4,6},{6,4},{5,7},{7,5},{8,10},{10,8},{9,1... | collective-permute-start | bytes 387080 | tf_op jit(solution)/shard_map/rows0_tp/ppermute | solution.py:27
  10.0 1.1 %collective-permute-start.5 = (bf16[72,896]{1,0:T(8,128)(2,1)S(1)}, bf16[72,896]{1,0:T(8,128)(2,1)S(1)}, u32[]{:S(2)}, u32[]{:S(2)}) collective-permute-start(bf16[72,896]{1,0:T(8,128)(2,1)S(1)} %collective-permute-done.4.refs_2_), channel_id=1, source_target_pairs={{0,2},{2,0},{1,3},{3,1},{4,6},{6,4},{5,7},{7,5},{8,10},{10,8},{9,1... | collective-permute-start | bytes 387080 | tf_op jit(solution)/shard_map/rows1_tp/ppermute | solution.py:27
  11.2 0.9 %collective-permute-start.8 = (bf16[128,256]{1,0:T(8,128)(2,1)S(1)}, bf16[128,256]{1,0:T(8,128)(2,1)S(1)}, u32[]{:S(2)}, u32[]{:S(2)}) collective-permute-start(bf16[128,256]{1,0:T(8,128)(2,1)S(1)} %slice_bitcast_fusion), channel_id=1, source_target_pairs={{0,2},{2,0},{1,3},{3,1},{4,6},{6,4},{5,7},{7,5},{8,10},{10,8},{9,1... | collective-permute-start | bytes 196616 | tf_op jit(solution)/shard_map/latent_tp/ppermute | solution.py:27
  12.1 2.5 %collective-permute-done.earlier_ref.refs_6_.refs_0_ = bf16[72,896]{1,0:T(8,128)(2,1)S(1)} collective-permute-done((bf16[72,896]{1,0:T(8,128)(2,1)S(1)}, bf16[72,896]{1,0:T(8,128)(2,1)S(1)}, u32[]{:S(2)}, u32[]{:S(2)}) %collective-permute-start) | collective-permute-done | bytes 129056 | tf_op jit(solution)/shard_map/rows3_ep/ppermute | solution.py:27
  14.6 1.8 %collective-permute-start.1 = (bf16[72,896]{1,0:T(8,128)(2,1)S(1)}, bf16[72,896]{1,0:T(8,128)(2,1)S(1)}, u32[]{:S(2)}, u32[]{:S(2)}) collective-permute-start(bf16[72,896]{1,0:T(8,128)(2,1)S(1)} %after.8), channel_id=1, source_target_pairs={{0,8},{4,12},{8,0},{12,4},{1,9},{5,13},{9,1},{13,5},{2,10},{6,14},... | collective-permute-start | bytes 387080 | tf_op jit(solution)/shard_map/rows2_ep/ppermute | solution.py:27
  16.3 1.5 %collective-permute-start.3 = (bf16[72,896]{1,0:T(8,128)(2,1)S(1)}, bf16[72,896]{1,0:T(8,128)(2,1)S(1)}, u32[]{:S(2)}, u32[]{:S(2)}) collective-permute-start(bf16[72,896]{1,0:T(8,128)(2,1)S(1)} %collective-permute-done.earlier_ref.refs_6_.refs_0_), channel_id=1, source_target_pairs={{0,2},{2,0},{1,3},{3,1},{4,6},{6,4},{5,7},{7,5},{8,10},{10,8},{9,1... | collective-permute-start | bytes 387080 | tf_op jit(solution)/shard_map/rows3_tp/ppermute | solution.py:27
  17.8 2.8 %fetch.1 = (bf16[512,1792]{1,0:T(8,128)(2,1)S(1)}, bf16[2,4,72,512]{3,2,1,0:T(8,128)(2,1)S(1)}, bf16[1792,512]{1,0:T(8,128)(2,1)S(1)}, bf16[1792,512]{1,0:T(8,12...) custom-call(bf16[512,1792]{1,0:T(8,128)(2,1)} %bitcast.25, bf16[2,4,72,512]{3,2,1,0:T(8,128)(2,1)} %bitcast.28, ...), custom_call_target="tpu_custom_call" | custom-call | tf_op jit(solution)/shard_map/fetch/pallas_call | solution.py:46
  22.1 1.6 %collective-permute-start.2 = (bf16[72,896]{1,0:T(8,128)(2,1)S(1)}, bf16[72,896]{1,0:T(8,128)(2,1)S(1)}, u32[]{:S(2)}, u32[]{:S(2)}) collective-permute-start(bf16[72,896]{1,0:T(8,128)(2,1)S(1)} %after.9.refs_0_), channel_id=1, source_target_pairs={{0,2},{2,0},{1,3},{3,1},{4,6},{6,4},{5,7},{7,5},{8,10},{10,8},{9,1... | collective-permute-start | bytes 387080 | tf_op jit(solution)/shard_map/rows2_tp/ppermute | solution.py:27
  23.7 1.4 %back.2 = (bf16[72,896]{1,0:T(8,128)(2,1)S(1)}, bf16[72,896]{1,0:T(8,128)(2,1)S(1)}, bf16[72,896]{1,0:T(8,128)(2,1)S(1)}, bf16[72,896]{1,0:T(8,128)(2,1)S(1)}, b...) custom-call(f32[216,512]{1,0:T(8,128)S(1)} %get-tuple-element.32.sum_ref.earlier_ref, ...), custom_call_target="tpu_custom_call" | custom-call | tf_op jit(solution)/shard_map/back/pallas_call | solution.py:46
  25.1 1.4 %collective-permute-start.10 = (bf16[72,896]{1,0:T(8,128)(2,1)S(1)}, bf16[72,896]{1,0:T(8,128)(2,1)S(1)}, u32[]{:S(2)}, u32[]{:S(2)}) collective-permute-start(bf16[72,896]{1,0:T(8,128)(2,1)S(1)} %get-tuple-element.43), channel_id=1, source_target_pairs={{0,2},{2,0},{1,3},{3,1},{4,6},{6,4},{5,7},{7,5},{8,10},{10,8},{9,1... | collective-permute-start | bytes 387080 | tf_op jit(solution)/shard_map/back3_tp/ppermute | solution.py:27
  26.7 1.4 %collective-permute-done.2.value_ref = bf16[72,896]{1,0:T(8,128)(2,1)S(1)} collective-permute-done((bf16[72,896]{1,0:T(8,128)(2,1)S(1)}, bf16[72,896]{1,0:T(8,128)(2,1)S(1)}, u32[]{:S(2)}, u32[]{:S(2)}) %collective-permute-start.2) | collective-permute-done | bytes 129056 | tf_op jit(solution)/shard_map/rows2_tp/ppermute | solution.py:27
  28.8 1.7 %collective-permute-start.14 = (bf16[72,896]{1,0:T(8,128)(2,1)S(1)}, bf16[72,896]{1,0:T(8,128)(2,1)S(1)}, u32[]{:S(2)}, u32[]{:S(2)}) collective-permute-start(bf16[72,896]{1,0:T(8,128)(2,1)S(1)} %after.14), channel_id=1, source_target_pairs={{0,2},{2,0},{1,3},{3,1},{4,6},{6,4},{5,7},{7,5},{8,10},{10,8},{9,1... | collective-permute-start | bytes 387080 | tf_op jit(solution)/shard_map/back1_tp/ppermute | solution.py:27
  30.8 2.0 %collective-permute-start.13 = (bf16[72,896]{1,0:T(8,128)(2,1)S(1)}, bf16[72,896]{1,0:T(8,128)(2,1)S(1)}, u32[]{:S(2)}, u32[]{:S(2)}) collective-permute-start(bf16[72,896]{1,0:T(8,128)(2,1)S(1)} %add_convert_fusion.2.earlier_ref), channel_id=1, source_target_pairs={{0,12},{4,8},{8,4},{12,0},{1,13},{5,9},{9,5},{13,1},{2,14},{6,10},... | collective-permute-start | bytes 387080 | tf_op jit(solution)/shard_map/back3_ep/ppermute | solution.py:27
  32.8 1.2 %back.3 = (bf16[72,896]{1,0:T(8,128)(2,1)S(1)}, bf16[72,896]{1,0:T(8,128)(2,1)S(1)}) custom-call(f32[72,512]{1,0:T(8,128)S(1)} %get-tuple-element.41.sum_ref.earlier_ref, bf16[88,512]{1,0:T(8,128)(2,1)S(1)} %after.13.other_ref, bf16[2,4,72,512]{3,2,1,0:T(8,128)(2,1)S(1)} %get-tuple-element.34.pre_ref, bf16[1792,512]{1,0:T(8,128)(2,1)S(1)} %get-tuple-element.35.gate_ref, ...), custom_call_target="tpu_custom_call" | custom-call | tf_op jit(solution)/shard_map/back/pallas_call | solution.py:46
  34.0 1.4 %collective-permute-start.11 = (bf16[72,896]{1,0:T(8,128)(2,1)S(1)}, bf16[72,896]{1,0:T(8,128)(2,1)S(1)}, u32[]{:S(2)}, u32[]{:S(2)}) collective-permute-start(bf16[72,896]{1,0:T(8,128)(2,1)S(1)} %get-tuple-element.45), channel_id=1, source_target_pairs={{0,2},{2,0},{1,3},{3,1},{4,6},{6,4},{5,7},{7,5},{8,10},{10,8},{9,1... | collective-permute-start | bytes 387080 | tf_op jit(solution)/shard_map/back2_tp/ppermute | solution.py:27
  35.5 1.6 %collective-permute-start.15 = (bf16[72,896]{1,0:T(8,128)(2,1)S(1)}, bf16[72,896]{1,0:T(8,128)(2,1)S(1)}, u32[]{:S(2)}, u32[]{:S(2)}) collective-permute-start(bf16[72,896]{1,0:T(8,128)(2,1)S(1)} %add_convert_fusion), channel_id=1, source_target_pairs={{0,4},{4,0},{8,12},{12,8},{1,5},{5,1},{9,13},{13,9},{2,6},{6,2},{1... | collective-permute-start | bytes 387080 | tf_op jit(solution)/shard_map/back1_ep/ppermute | solution.py:27
  37.1 1.9 %collective-permute-done.11 = bf16[72,896]{1,0:T(8,128)(2,1)S(1)} collective-permute-done((bf16[72,896]{1,0:T(8,128)(2,1)S(1)}, bf16[72,896]{1,0:T(8,128)(2,1)S(1)}, u32[]{:S(2)}, u32[]{:S(2)}) %collective-permute-start.11) | collective-permute-done | bytes 129056 | tf_op jit(solution)/shard_map/back2_tp/ppermute | solution.py:27
  39.1 2.0 %collective-permute-start.12 = (bf16[72,896]{1,0:T(8,128)(2,1)S(1)}, bf16[72,896]{1,0:T(8,128)(2,1)S(1)}, u32[]{:S(2)}, u32[]{:S(2)}) collective-permute-start(bf16[72,896]{1,0:T(8,128)(2,1)S(1)} %add_convert_fusion.1.earlier_ref), channel_id=1, source_target_pairs={{0,8},{4,12},{8,0},{12,4},{1,9},{5,13},{9,1},{13,5},{2,10},{6,14},... | collective-permute-start | bytes 387080 | tf_op jit(solution)/shard_map/back2_ep/ppermute | solution.py:27
  41.0 1.5 %collective-permute-start.16 = (bf16[72,896]{1,0:T(8,128)(2,1)S(1)}, bf16[72,896]{1,0:T(8,128)(2,1)S(1)}, u32[]{:S(2)}, u32[]{:S(2)}) collective-permute-start(bf16[72,896]{1,0:T(8,128)(2,1)S(1)} %after.15), channel_id=1, source_target_pairs={{0,2},{2,0},{1,3},{3,1},{4,6},{6,4},{5,7},{7,5},{8,10},{10,8},{9,1... | collective-permute-start | bytes 387080 | tf_op jit(solution)/shard_map/back0_tp/ppermute | solution.py:27
  43.2 2.7 %collective-permute-done.16.refs_3_ = bf16[72,896]{1,0:T(8,128)(2,1)S(1)} collective-permute-done((bf16[72,896]{1,0:T(8,128)(2,1)S(1)}, bf16[72,896]{1,0:T(8,128)(2,1)S(1)}, u32[]{:S(2)}, u32[]{:S(2)}) %collective-permute-start.16) | collective-permute-done | bytes 129056 | tf_op jit(solution)/shard_map/back0_tp/ppermute | solution.py:27
  46.8 1.1 %unpack_latest.1 = bf16[128,1792]{1,0:T(8,128)(2,1)} custom-call(bf16[2,4,72,128]{3,2,1,0:T(8,128)(2,1)S(1)} %get-tuple-element.26.place_ref, bf16[72,896]{1,0:T(8,128)(2,1)S(1)} %collective-permute-done.12.refs_0_, bf16[128,1792]{1,0:T(8,128)(2,1)S(1)} %unpack.1.refs_1_), custom_call_target="tpu_custom_call" | custom-call | tf_op jit(solution)/shard_map/unpack_latest/pallas_call | solution.py:46
  (37 shorter events, 4.3 us)
Async XLA Ops:
  3.0 7.1 %collective-permute-start.4 = (bf16[72,896]{1,0:T(8,128)(2,1)S(1)}, bf16[72,896]{1,0:T(8,128)(2,1)S(1)}, u32[]{:S(2)}, u32[]{:S(2)}) collective-permute-start(bf16[72,896]{1,0:T(8,128)(2,1)S(1)} %get-tuple-element.29), channel_id=1, source_target_pairs={{0,4},{4,0},{8,12},{12,8},{1,5},{5,1},{9,13},{13,9},{2,6},{6,2},{1... | collective-permute-start | bytes 387080 | tf_op jit(solution)/shard_map/rows1_ep/ppermute | solution.py:27
  6.1 8.5 %collective-permute-start = (bf16[72,896]{1,0:T(8,128)(2,1)S(1)}, bf16[72,896]{1,0:T(8,128)(2,1)S(1)}, u32[]{:S(2)}, u32[]{:S(2)}) collective-permute-start(bf16[72,896]{1,0:T(8,128)(2,1)S(1)} %get-tuple-element.28.earlier_ref), channel_id=1, source_target_pairs={{0,12},{4,8},{8,4},{12,0},{1,13},{5,9},{9,5},{13,1},{2,14},{6,10},... | collective-permute-start | bytes 387080 | tf_op jit(solution)/shard_map/rows3_ep/ppermute | solution.py:27
  8.5 12.2 %collective-permute-start.6 = (bf16[72,896]{1,0:T(8,128)(2,1)S(1)}, bf16[72,896]{1,0:T(8,128)(2,1)S(1)}, u32[]{:S(2)}, u32[]{:S(2)}) collective-permute-start(bf16[72,896]{1,0:T(8,128)(2,1)S(1)} %get-tuple-element.30.refs_4_), channel_id=1, source_target_pairs={{0,2},{2,0},{1,3},{3,1},{4,6},{6,4},{5,7},{7,5},{8,10},{10,8},{9,1... | collective-permute-start | bytes 387080 | tf_op jit(solution)/shard_map/rows0_tp/ppermute | solution.py:27
  10.0 10.6 %collective-permute-start.5 = (bf16[72,896]{1,0:T(8,128)(2,1)S(1)}, bf16[72,896]{1,0:T(8,128)(2,1)S(1)}, u32[]{:S(2)}, u32[]{:S(2)}) collective-permute-start(bf16[72,896]{1,0:T(8,128)(2,1)S(1)} %collective-permute-done.4.refs_2_), channel_id=1, source_target_pairs={{0,2},{2,0},{1,3},{3,1},{4,6},{6,4},{5,7},{7,5},{8,10},{10,8},{9,1... | collective-permute-start | bytes 387080 | tf_op jit(solution)/shard_map/rows1_tp/ppermute | solution.py:27
  11.2 12.5 %collective-permute-start.8 = (bf16[128,256]{1,0:T(8,128)(2,1)S(1)}, bf16[128,256]{1,0:T(8,128)(2,1)S(1)}, u32[]{:S(2)}, u32[]{:S(2)}) collective-permute-start(bf16[128,256]{1,0:T(8,128)(2,1)S(1)} %slice_bitcast_fusion), channel_id=1, source_target_pairs={{0,2},{2,0},{1,3},{3,1},{4,6},{6,4},{5,7},{7,5},{8,10},{10,8},{9,1... | collective-permute-start | bytes 196616 | tf_op jit(solution)/shard_map/latent_tp/ppermute | solution.py:27
  14.6 7.6 %collective-permute-start.1 = (bf16[72,896]{1,0:T(8,128)(2,1)S(1)}, bf16[72,896]{1,0:T(8,128)(2,1)S(1)}, u32[]{:S(2)}, u32[]{:S(2)}) collective-permute-start(bf16[72,896]{1,0:T(8,128)(2,1)S(1)} %after.8), channel_id=1, source_target_pairs={{0,8},{4,12},{8,0},{12,4},{1,9},{5,13},{9,1},{13,5},{2,10},{6,14},... | collective-permute-start | bytes 387080 | tf_op jit(solution)/shard_map/rows2_ep/ppermute | solution.py:27
  16.3 4.9 %collective-permute-start.3 = (bf16[72,896]{1,0:T(8,128)(2,1)S(1)}, bf16[72,896]{1,0:T(8,128)(2,1)S(1)}, u32[]{:S(2)}, u32[]{:S(2)}) collective-permute-start(bf16[72,896]{1,0:T(8,128)(2,1)S(1)} %collective-permute-done.earlier_ref.refs_6_.refs_0_), channel_id=1, source_target_pairs={{0,2},{2,0},{1,3},{3,1},{4,6},{6,4},{5,7},{7,5},{8,10},{10,8},{9,1... | collective-permute-start | bytes 387080 | tf_op jit(solution)/shard_map/rows3_tp/ppermute | solution.py:27
  22.0 1.7 %collective-permute-start.7 = (bf16[216,512]{1,0:T(8,128)(2,1)S(1)}, bf16[216,512]{1,0:T(8,128)(2,1)S(1)}, u32[]{:S(2)}, u32[]{:S(2)}) collective-permute-start(bf16[216,512]{1,0:T(8,128)(2,1)S(1)} %get-tuple-element.33), channel_id=1, source_target_pairs={{0,1},{1,0},{2,3},{3,2},{4,5},{5,4},{6,7},{7,6},{8,9},{9,8},{10,11... | collective-permute-start | bytes 663560 | tf_op jit(solution)/shard_map/hidden3_sub/ppermute | solution.py:27
  22.1 5.9 %collective-permute-start.2 = (bf16[72,896]{1,0:T(8,128)(2,1)S(1)}, bf16[72,896]{1,0:T(8,128)(2,1)S(1)}, u32[]{:S(2)}, u32[]{:S(2)}) collective-permute-start(bf16[72,896]{1,0:T(8,128)(2,1)S(1)} %after.9.refs_0_), channel_id=1, source_target_pairs={{0,2},{2,0},{1,3},{3,1},{4,6},{6,4},{5,7},{7,5},{8,10},{10,8},{9,1... | collective-permute-start | bytes 387080 | tf_op jit(solution)/shard_map/rows2_tp/ppermute | solution.py:27
  25.1 5.7 %collective-permute-start.10 = (bf16[72,896]{1,0:T(8,128)(2,1)S(1)}, bf16[72,896]{1,0:T(8,128)(2,1)S(1)}, u32[]{:S(2)}, u32[]{:S(2)}) collective-permute-start(bf16[72,896]{1,0:T(8,128)(2,1)S(1)} %get-tuple-element.43), channel_id=1, source_target_pairs={{0,2},{2,0},{1,3},{3,1},{4,6},{6,4},{5,7},{7,5},{8,10},{10,8},{9,1... | collective-permute-start | bytes 387080 | tf_op jit(solution)/shard_map/back3_tp/ppermute | solution.py:27
  28.7 4.1 %collective-permute-start.9 = (bf16[88,512]{1,0:T(8,128)(2,1)S(1)}, bf16[88,512]{1,0:T(8,128)(2,1)S(1)}, u32[]{:S(2)}, u32[]{:S(2)}) collective-permute-start(bf16[88,512]{1,0:T(8,128)(2,1)S(1)} %get-tuple-element.42), channel_id=1, source_target_pairs={{0,1},{1,0},{2,3},{3,2},{4,5},{5,4},{6,7},{7,6},{8,9},{9,8},{10,11... | collective-permute-start | bytes 270344 | tf_op jit(solution)/shard_map/hidden2_sub/ppermute | solution.py:27
  28.8 6.6 %collective-permute-start.14 = (bf16[72,896]{1,0:T(8,128)(2,1)S(1)}, bf16[72,896]{1,0:T(8,128)(2,1)S(1)}, u32[]{:S(2)}, u32[]{:S(2)}) collective-permute-start(bf16[72,896]{1,0:T(8,128)(2,1)S(1)} %after.14), channel_id=1, source_target_pairs={{0,2},{2,0},{1,3},{3,1},{4,6},{6,4},{5,7},{7,5},{8,10},{10,8},{9,1... | collective-permute-start | bytes 387080 | tf_op jit(solution)/shard_map/back1_tp/ppermute | solution.py:27
  30.8 12.4 %collective-permute-start.13 = (bf16[72,896]{1,0:T(8,128)(2,1)S(1)}, bf16[72,896]{1,0:T(8,128)(2,1)S(1)}, u32[]{:S(2)}, u32[]{:S(2)}) collective-permute-start(bf16[72,896]{1,0:T(8,128)(2,1)S(1)} %add_convert_fusion.2.earlier_ref), channel_id=1, source_target_pairs={{0,12},{4,8},{8,4},{12,0},{1,13},{5,9},{9,5},{13,1},{2,14},{6,10},... | collective-permute-start | bytes 387080 | tf_op jit(solution)/shard_map/back3_ep/ppermute | solution.py:27
  34.0 5.0 %collective-permute-start.11 = (bf16[72,896]{1,0:T(8,128)(2,1)S(1)}, bf16[72,896]{1,0:T(8,128)(2,1)S(1)}, u32[]{:S(2)}, u32[]{:S(2)}) collective-permute-start(bf16[72,896]{1,0:T(8,128)(2,1)S(1)} %get-tuple-element.45), channel_id=1, source_target_pairs={{0,2},{2,0},{1,3},{3,1},{4,6},{6,4},{5,7},{7,5},{8,10},{10,8},{9,1... | collective-permute-start | bytes 387080 | tf_op jit(solution)/shard_map/back2_tp/ppermute | solution.py:27
  35.5 7.8 %collective-permute-start.15 = (bf16[72,896]{1,0:T(8,128)(2,1)S(1)}, bf16[72,896]{1,0:T(8,128)(2,1)S(1)}, u32[]{:S(2)}, u32[]{:S(2)}) collective-permute-start(bf16[72,896]{1,0:T(8,128)(2,1)S(1)} %add_convert_fusion), channel_id=1, source_target_pairs={{0,4},{4,0},{8,12},{12,8},{1,5},{5,1},{9,13},{13,9},{2,6},{6,2},{1... | collective-permute-start | bytes 387080 | tf_op jit(solution)/shard_map/back1_ep/ppermute | solution.py:27
  39.1 7.7 %collective-permute-start.12 = (bf16[72,896]{1,0:T(8,128)(2,1)S(1)}, bf16[72,896]{1,0:T(8,128)(2,1)S(1)}, u32[]{:S(2)}, u32[]{:S(2)}) collective-permute-start(bf16[72,896]{1,0:T(8,128)(2,1)S(1)} %add_convert_fusion.1.earlier_ref), channel_id=1, source_target_pairs={{0,8},{4,12},{8,0},{12,4},{1,9},{5,13},{9,1},{13,5},{2,10},{6,14},... | collective-permute-start | bytes 387080 | tf_op jit(solution)/shard_map/back2_ep/ppermute | solution.py:27
  41.0 4.9 %collective-permute-start.16 = (bf16[72,896]{1,0:T(8,128)(2,1)S(1)}, bf16[72,896]{1,0:T(8,128)(2,1)S(1)}, u32[]{:S(2)}, u32[]{:S(2)}) collective-permute-start(bf16[72,896]{1,0:T(8,128)(2,1)S(1)} %after.15), channel_id=1, source_target_pairs={{0,2},{2,0},{1,3},{3,1},{4,6},{6,4},{5,7},{7,5},{8,10},{10,8},{9,1... | collective-permute-start | bytes 387080 | tf_op jit(solution)/shard_map/back0_tp/ppermute | solution.py:27

commit v10 on v9

--- a/solution.py
+++ b/solution.py
@@ -2,6 +2,7 @@
 
 import jax
 import jax.numpy as jnp
+import numpy as np
 from jax import lax
 from jax.experimental import pallas as pl
 from jax.experimental.pallas import tpu as pltpu
@@ -21,10 +22,14 @@
     return lax.dot_general(a, b, dims, precision=precision, preferred_element_type=jnp.float32)
 
 
-def swap(value, axis, step, what):
-    count = lax.axis_size(axis)
-    with jax.named_scope(f"{what}_{axis}"):
-        return lax.ppermute(value, axis, [(i, i ^ step) for i in range(count)])
+def swap(value, what, **steps):
+    counts = [lax.axis_size(axis) for axis in steps]
+    pairs = []
+    for place in np.ndindex(*counts):
+        other = [index ^ step for index, step in zip(place, steps.values())]
+        pairs.append(tuple(int(np.ravel_multi_index(p, counts)) for p in (place, other)))
+    with jax.named_scope("_".join([what, *steps])):
+        return lax.ppermute(value, tuple(steps), pairs)
 
 
 def pinned(*arrays):
@@ -195,21 +200,19 @@
         out[...] = jnp.concatenate(pieces, axis=0).astype(jnp.bfloat16)
 
 
-def unpack_kernel(distances, started, place_ref, *refs):
-    blocks, others, out_ref = refs[: len(distances)], refs[len(distances) : -1], refs[-1]
-    if started:
-        others, so_far_ref = others[:-1], others[-1]
+def unpack_kernel(parts, started, place_ref, *refs):
+    given, out_ref = list(refs[:-1]), refs[-1]
     half = out_ref.shape[1] // 2
+    blocks = {}
+    for k, count in parts.items():
+        rows = given.pop(0)[...].astype(jnp.float32)
+        for _ in range(count - 1):
+            rows += given.pop(0)[...].astype(jnp.float32)
+        blocks[k] = rows.astype(jnp.bfloat16)
     for side in range(2):
         columns = slice(side * half, (side + 1) * half)
-        total = so_far_ref[:, columns].astype(jnp.float32) if started else 0.0
-        for k, block_ref in zip(distances, blocks):
-            rows = block_ref[...]
-            if k == 0:
-                rows = rows.astype(jnp.float32)
-                for other_ref in others:
-                    rows += other_ref[...].astype(jnp.float32)
-                rows = rows.astype(jnp.bfloat16)
+        total = given[0][:, columns].astype(jnp.float32) if started else 0.0
+        for k, rows in blocks.items():
             total = total + dot(place_ref[side, k], rows, TN)
         out_ref[:, columns] = total.astype(jnp.bfloat16)
 
@@ -269,17 +272,14 @@
     place, shares = packed[wide:]
     packed = dict(zip(order, packed))
 
-    def across(k, rows_of_k):
-        return [rows_of_k] + [swap(rows_of_k, "tp", j, f"rows{k}") for j in range(1, narrow)]
-
-    taken = {0: across(0, packed[0])}
-    first = groups[0][0]
+    first, staged = groups[0][0], len(groups) > 1
+    taken = {0: [packed[0]] + [swap(packed[0], "rows0", tp=j) for j in range(1, narrow)]}
     arrived = {}
     for k in order:
         if k:
             given = packed[k] if k in groups[0] else after(packed[k], arrived[first])
-            arrived[k] = swap(given, "ep", k, f"rows{k}")
-            if len(groups) > 1 and k == groups[1][0]:
+            arrived[k] = swap(given, f"rows{k}", ep=k)
+            if staged and k == groups[1][0]:
                 arrived[k] = after(arrived[k], packed[first], 1 << 31)
     fetched = [
         w_down[0],
@@ -299,30 +299,29 @@
         name="fetch",
     )
     latent_parts = [shares[0]] + [
-        swap(shares[j], "tp", j, "latent") for j in range(1, narrow)
+        swap(shares[j], "latent", tp=j) for j in range(1, narrow)
     ]
 
-    def give_back(k, mine, others):
-        others = [swap(other, "tp", j + 1, f"back{k}") for j, other in enumerate(others)]
-        total = mine.astype(f32)
-        for other in others:
-            total += other.astype(f32)
-        total = total.astype(bf16)
-        return total, swap(total, "ep", k, f"back{k}")
-
-    returned = {}
-    own, waiting = [], []
+    def straight(k, mine, others):
+        return [swap(mine, f"back{k}", ep=k)] + [
+            swap(other, f"back{k}", ep=k, tp=j + 1) for j, other in enumerate(others)
+        ]
+
+    returned, waiting = {}, []
     values = latent.astype(f32)
     received, products, moved = None, None, None
     for group in groups:
         for k in group:
-            if k == 0:
-                continue
-            taken[k] = across(k, arrived[k])
-            if received is not None:
-                taken[k][-1] = after(taken[k][-1], products[0])
-            elif k != first and narrow > 1:
-                taken[k][-1] = after(taken[k][-1], packed[first], 1 << 31)
+            if staged and k == 1:
+                crossing = [swap(packed[k], f"rows{k}", ep=k, tp=j) for j in range(1, narrow)]
+            elif k:
+                if products:
+                    arrived[k] = after(arrived[k], summed)
+                crossing = [swap(arrived[k], f"rows{k}", tp=j) for j in range(1, narrow)]
+                if products:
+                    crossing[-1] = after(crossing[-1], products[0])
+            if k:
+                taken[k] = [arrived[k]] + crossing
         count = len(group) * narrow * most
         extra = group is groups[-1]
         if extra:
@@ -345,11 +344,7 @@
             name="hidden",
             earlier=products[:1] if products else (),
         )
-        for k, mine, others in waiting:
-            others = [after(other, summed) for other in others]
-            returned[k] = give_back(k, mine, others)[1]
-        waiting = []
-        received = swap(sent, "sub", 1, f"hidden{group[0]}")
+        received = swap(sent, f"hidden{group[0]}", sub=1)
         if moved is not None:
             received = after(received, moved)
         products = call(
@@ -365,36 +360,45 @@
         for at, k in enumerate(group):
             mine, others = products[at * narrow], products[at * narrow + 1 : (at + 1) * narrow]
             if k == 0:
-                returned[0], own = mine, others
-            elif k != group[0] and not extra:
+                kept = mine, others
+            elif staged and k == 1:
                 waiting.append((k, mine, others))
             else:
-                total, returned[k] = give_back(k, mine, others)
+                total = mine.astype(f32)
+                for j, other in enumerate(others):
+                    total += swap(other, f"back{k}", tp=j + 1).astype(f32)
+                total = total.astype(bf16)
+                returned[k] = [swap(total, f"back{k}", ep=k)]
                 if k == group[0]:
                     moved = total
-    own = [swap(after(value, moved), "tp", j + 1, "back0") for j, value in enumerate(own)]
+    for k, mine, others in waiting:
+        returned[k] = straight(k, after(mine, products[0]), [after(other, products[0]) for other in others])
+    mine, others = kept
+    returned[0] = [mine] + [
+        swap(after(other, moved) if staged else other, "back0", tp=j + 1)
+        for j, other in enumerate(others)
+    ]
     tail = received[count : count + 4, :tokens].astype(f32)
     row_sums = row_sums + tail[:2] + tail[2:]
     inverse_rms = lax.rsqrt(row_sums[0] / LAT + 1e-06)[:, None]
     d_latent = (
         inverse_rms * gained - values * inverse_rms**3 * row_sums[1][:, None] / LAT
     ).astype(bf16)
-    latest = groups[-1][:1] if len(groups) > 1 else []
-    distances = [k for k in sorted(returned, reverse=True) if k not in latest]
+    latest = groups[-1][:1] if staged else []
+    distances = [k for k in order if k not in latest]
     (grad_input,) = call(
-        functools.partial(unpack_kernel, distances, False),
-        [pltpu.VMEM((tokens, width), bf16) if latest else jax.ShapeDtypeStruct((tokens, width), bf16)],
+        functools.partial(unpack_kernel, {k: len(returned[k]) for k in distances}, False),
+        [pltpu.VMEM((tokens, width), bf16) if staged else jax.ShapeDtypeStruct((tokens, width), bf16)],
         place,
-        *[returned[k] for k in distances],
-        *own,
+        *[part for k in distances for part in returned[k]],
         name="unpack",
     )
-    if latest:
+    if staged:
         (grad_input,) = call(
-            functools.partial(unpack_kernel, latest, True),
+            functools.partial(unpack_kernel, {k: len(returned[k]) for k in latest}, True),
             [jax.ShapeDtypeStruct((tokens, width), bf16)],
             place,
-            *[returned[k] for k in latest],
+            *[part for k in latest for part in returned[k]],
             grad_input,
             name="unpack_latest",
         )

time: 48 us -> 48.7 us (1.015)
  waiting for transfers between devices: 9.62 us -> 13.3 us
  starting transfers between devices: 25.6 us -> 22.7 us
    ppermute x17, waiting for transfers between devices: 9.62 us -> 13.3 us  [swap(): return lax.ppermute(value, tuple(steps), pairs)]
    ppermute x17, starting transfers between devices: 25.6 us -> 22.7 us  [swap(): return lax.ppermute(value, tuple(steps), pairs)]
  transfers between devices with their start and end apart: 17 -> 17, of which waited for: 7 -> 10; matrix products, arithmetic and copies ran while one was open for 2% -> 2% of each run, Pallas kernels for 16% -> 15%
where the time goes in v10:
time: 48.7 us; the launch traced here: 48.5 us
  starting transfers between devices  22.7 us (47%)
  waiting for transfers between devices  13.3 us (27%)
  Pallas kernels  10.8 us (22%)
  other arithmetic  0.97 us (2%)
  between operations  0.78 us (2%)
    ppermute x17, starting transfers between devices, swap(): return lax.ppermute(value, tuple(steps), pairs)  22.7 us
    ppermute x17, waiting for transfers between devices, swap(): return lax.ppermute(value, tuple(steps), pairs)  13.3 us
    pallas_call x8, Pallas kernels, call(): pl.pallas_call(kernel, out_shape=outs, in_specs=specs, out_specs=[VMEM] *...  10.8 us
  transfers between devices with their start and end apart: 17, of which 10 were waited for; matrix products, arithmetic and copies ran while one was open for 2% of the time, Pallas kernels for 15%

profile of v10, /device:TPU:0, one launch (start us, length us, event | category | flops | bytes accessed | tf_op | source)
XLA Modules:
  0.0 48.5 jit_solution(9123068568677915599)
XLA Ops:
  0.6 2.3 %pack.1 = (bf16[72,896]{1,0:T(8,128)(2,1)S(1)}, bf16[72,896]{1,0:T(8,128)(2,1)S(1)}, bf16[72,896]{1,0:T(8,128)(2,1)S(1)}, bf16[72,896]{1,0:T(8,128)(2,1)S(1)}, b...) custom-call(s32[1,128]{1,0:T(1,128)} %bitcast.36, f32[1,128]{1,0:T(1,128)} %bitcast.37, ...), custom_call_target="tpu_custom_call" | custom-call | tf_op jit(solution)/shard_map/pack/pallas_call | solution.py:51
  3.0 5.1 %collective-permute-start = (bf16[72,896]{1,0:T(8,128)(2,1)S(1)}, bf16[72,896]{1,0:T(8,128)(2,1)S(1)}, u32[]{:S(2)}, u32[]{:S(2)}) collective-permute-start(bf16[72,896]{1,0:T(8,128)(2,1)S(1)} %get-tuple-element.28.earlier_ref), channel_id=1, source_target_pairs={{0,12},{4,8},{8,4},{12,0},{1,13},{5,9},{9,5},{13,1},{2,14},{6,10},... | collective-permute-start | bytes 387080 | tf_op jit(solution)/shard_map/rows3_ep/ppermute | solution.py:32
  8.1 2.9 %collective-permute-start.4 = (bf16[72,896]{1,0:T(8,128)(2,1)S(1)}, bf16[72,896]{1,0:T(8,128)(2,1)S(1)}, u32[]{:S(2)}, u32[]{:S(2)}) collective-permute-start(bf16[72,896]{1,0:T(8,128)(2,1)S(1)} %get-tuple-element.29), channel_id=1, source_target_pairs={{0,6},{2,4},{4,2},{6,0},{8,14},{10,12},{12,10},{14,8},{1,7},{3,5},... | collective-permute-start | bytes 387080 | tf_op jit(solution)/shard_map/rows1_ep_tp/ppermute | solution.py:32
  11.6 0.8 %collective-permute-done.earlier_ref.refs_6_.refs_0_ = bf16[72,896]{1,0:T(8,128)(2,1)S(1)} collective-permute-done((bf16[72,896]{1,0:T(8,128)(2,1)S(1)}, bf16[72,896]{1,0:T(8,128)(2,1)S(1)}, u32[]{:S(2)}, u32[]{:S(2)}) %collective-permute-start) | collective-permute-done | bytes 129056 | tf_op jit(solution)/shard_map/rows3_ep/ppermute | solution.py:32
  12.4 2.3 %collective-permute-start.1 = (bf16[72,896]{1,0:T(8,128)(2,1)S(1)}, bf16[72,896]{1,0:T(8,128)(2,1)S(1)}, u32[]{:S(2)}, u32[]{:S(2)}) collective-permute-start(bf16[72,896]{1,0:T(8,128)(2,1)S(1)} %after.9), channel_id=1, source_target_pairs={{0,8},{4,12},{8,0},{12,4},{1,9},{5,13},{9,1},{13,5},{2,10},{6,14},... | collective-permute-start | bytes 387080 | tf_op jit(solution)/shard_map/rows2_ep/ppermute | solution.py:32
  14.7 1.5 %collective-permute-start.2 = (bf16[72,896]{1,0:T(8,128)(2,1)S(1)}, bf16[72,896]{1,0:T(8,128)(2,1)S(1)}, u32[]{:S(2)}, u32[]{:S(2)}) collective-permute-start(bf16[72,896]{1,0:T(8,128)(2,1)S(1)} %collective-permute-done.earlier_ref.refs_6_.refs_0_), channel_id=1, source_target_pairs={{0,2},{2,0},{1,3},{3,1},{4,6},{6,4},{5,7},{7,5},{8,10},{10,8},{9,1... | collective-permute-start | bytes 387080 | tf_op jit(solution)/shard_map/rows3_tp/ppermute | solution.py:32
  16.2 2.8 %fetch.1 = (bf16[512,1792]{1,0:T(8,128)(2,1)S(1)}, bf16[2,4,72,512]{3,2,1,0:T(8,128)(2,1)S(1)}, bf16[1792,512]{1,0:T(8,128)(2,1)S(1)}, bf16[1792,512]{1,0:T(8,12...) custom-call(bf16[512,1792]{1,0:T(8,128)(2,1)} %bitcast.25, bf16[2,4,72,512]{3,2,1,0:T(8,128)(2,1)} %bitcast.28, ...), custom_call_target="tpu_custom_call" | custom-call | tf_op jit(solution)/shard_map/fetch/pallas_call | solution.py:51
  20.2 1.5 %collective-permute-done.2.refs_1_ = bf16[72,896]{1,0:T(8,128)(2,1)S(1)} collective-permute-done((bf16[72,896]{1,0:T(8,128)(2,1)S(1)}, bf16[72,896]{1,0:T(8,128)(2,1)S(1)}, u32[]{:S(2)}, u32[]{:S(2)}) %collective-permute-start.2) | collective-permute-done | bytes 129056 | tf_op jit(solution)/shard_map/rows3_tp/ppermute | solution.py:32
  21.7 0.8 %hidden.2 = (f32[216,512]{1,0:T(8,128)S(1)}, bf16[216,512]{1,0:T(8,128)(2,1)S(1)}) custom-call(bf16[72,896]{1,0:T(8,128)(2,1)S(1)} %collective-permute-done.earlier_ref.refs_6_.refs_0_, bf16[72,896]{1,0:T(8,128)(2,1)S(1)} %collective-permute-done.2.refs_1_, bf16[72,896]{1,0:T(8,128)(2,1)S(1)} %collective-permute-done.3.refs_2_, ...), custom_call_target="tpu_custom_call" | custom-call | tf_op jit(solution)/shard_map/hidden/pallas_call | solution.py:51
  22.6 1.1 %collective-permute-start.6 = (bf16[72,896]{1,0:T(8,128)(2,1)S(1)}, bf16[72,896]{1,0:T(8,128)(2,1)S(1)}, u32[]{:S(2)}, u32[]{:S(2)}) collective-permute-start(bf16[72,896]{1,0:T(8,128)(2,1)S(1)} %after.11.refs_0_), channel_id=1, source_target_pairs={{0,2},{2,0},{1,3},{3,1},{4,6},{6,4},{5,7},{7,5},{8,10},{10,8},{9,1... | collective-permute-start | bytes 387080 | tf_op jit(solution)/shard_map/rows2_tp/ppermute | solution.py:32
  24.0 1.4 %back.2 = (bf16[72,896]{1,0:T(8,128)(2,1)S(1)}, bf16[72,896]{1,0:T(8,128)(2,1)S(1)}, bf16[72,896]{1,0:T(8,128)(2,1)S(1)}, bf16[72,896]{1,0:T(8,128)(2,1)S(1)}, b...) custom-call(f32[216,512]{1,0:T(8,128)S(1)} %get-tuple-element.32.earlier_ref.sum_ref, ...), custom_call_target="tpu_custom_call" | custom-call | tf_op jit(solution)/shard_map/back/pallas_call | solution.py:51
  25.4 1.1 %collective-permute-start.10 = (bf16[72,896]{1,0:T(8,128)(2,1)S(1)}, bf16[72,896]{1,0:T(8,128)(2,1)S(1)}, u32[]{:S(2)}, u32[]{:S(2)}) collective-permute-start(bf16[72,896]{1,0:T(8,128)(2,1)S(1)} %get-tuple-element.43), channel_id=1, source_target_pairs={{0,2},{2,0},{1,3},{3,1},{4,6},{6,4},{5,7},{7,5},{8,10},{10,8},{9,1... | collective-permute-start | bytes 387080 | tf_op jit(solution)/shard_map/back3_tp/ppermute | solution.py:32
  26.6 1.9 %collective-permute-done.6.value_ref = bf16[72,896]{1,0:T(8,128)(2,1)S(1)} collective-permute-done((bf16[72,896]{1,0:T(8,128)(2,1)S(1)}, bf16[72,896]{1,0:T(8,128)(2,1)S(1)}, u32[]{:S(2)}, u32[]{:S(2)}) %collective-permute-start.6) | collective-permute-done | bytes 129056 | tf_op jit(solution)/shard_map/rows2_tp/ppermute | solution.py:32
  29.3 1.8 %collective-permute-done.10 = bf16[72,896]{1,0:T(8,128)(2,1)S(1)} collective-permute-done((bf16[72,896]{1,0:T(8,128)(2,1)S(1)}, bf16[72,896]{1,0:T(8,128)(2,1)S(1)}, u32[]{:S(2)}, u32[]{:S(2)}) %collective-permute-start.10) | collective-permute-done | bytes 129056 | tf_op jit(solution)/shard_map/back3_tp/ppermute | solution.py:32
  31.2 1.4 %collective-permute-start.13 = (bf16[72,896]{1,0:T(8,128)(2,1)S(1)}, bf16[72,896]{1,0:T(8,128)(2,1)S(1)}, u32[]{:S(2)}, u32[]{:S(2)}) collective-permute-start(bf16[72,896]{1,0:T(8,128)(2,1)S(1)} %add_convert_fusion.1.earlier_ref), channel_id=1, source_target_pairs={{0,12},{4,8},{8,4},{12,0},{1,13},{5,9},{9,5},{13,1},{2,14},{6,10},... | collective-permute-start | bytes 387080 | tf_op jit(solution)/shard_map/back3_ep/ppermute | solution.py:32
  32.6 1.2 %back.3 = (bf16[72,896]{1,0:T(8,128)(2,1)S(1)}, bf16[72,896]{1,0:T(8,128)(2,1)S(1)}) custom-call(f32[72,512]{1,0:T(8,128)S(1)} %get-tuple-element.41.sum_ref, bf16[88,512]{1,0:T(8,128)(2,1)S(1)} %after.14.other_ref, bf16[2,4,72,512]{3,2,1,0:T(8,128)(2,1)S(1)} %get-tuple-element.34.pre_ref, bf16[1792,512]{1,0:T(8,128)(2,1)S(1)} %get-tuple-element.35.gate_ref, ...), custom_call_target="tpu_custom_call" | custom-call | tf_op jit(solution)/shard_map/back/pallas_call | solution.py:51
  33.9 1.0 %collective-permute-start.11 = (bf16[72,896]{1,0:T(8,128)(2,1)S(1)}, bf16[72,896]{1,0:T(8,128)(2,1)S(1)}, u32[]{:S(2)}, u32[]{:S(2)}) collective-permute-start(bf16[72,896]{1,0:T(8,128)(2,1)S(1)} %get-tuple-element.45), channel_id=1, source_target_pairs={{0,2},{2,0},{1,3},{3,1},{4,6},{6,4},{5,7},{7,5},{8,10},{10,8},{9,1... | collective-permute-start | bytes 387080 | tf_op jit(solution)/shard_map/back2_tp/ppermute | solution.py:32
  34.9 2.5 %collective-permute-start.15 = (bf16[72,896]{1,0:T(8,128)(2,1)S(1)}, bf16[72,896]{1,0:T(8,128)(2,1)S(1)}, u32[]{:S(2)}, u32[]{:S(2)}) collective-permute-start(bf16[72,896]{1,0:T(8,128)(2,1)S(1)} %after.16), channel_id=1, source_target_pairs={{0,6},{2,4},{4,2},{6,0},{8,14},{10,12},{12,10},{14,8},{1,7},{3,5},... | collective-permute-start | bytes 387080 | tf_op jit(solution)/shard_map/back1_ep_tp/ppermute | solution.py:32
  37.5 1.4 %collective-permute-done.11 = bf16[72,896]{1,0:T(8,128)(2,1)S(1)} collective-permute-done((bf16[72,896]{1,0:T(8,128)(2,1)S(1)}, bf16[72,896]{1,0:T(8,128)(2,1)S(1)}, u32[]{:S(2)}, u32[]{:S(2)}) %collective-permute-start.11) | collective-permute-done | bytes 129056 | tf_op jit(solution)/shard_map/back2_tp/ppermute | solution.py:32
  38.9 1.2 %collective-permute-start.12 = (bf16[72,896]{1,0:T(8,128)(2,1)S(1)}, bf16[72,896]{1,0:T(8,128)(2,1)S(1)}, u32[]{:S(2)}, u32[]{:S(2)}) collective-permute-start(bf16[72,896]{1,0:T(8,128)(2,1)S(1)} %add_convert_fusion.earlier_ref), channel_id=1, source_target_pairs={{0,8},{4,12},{8,0},{12,4},{1,9},{5,13},{9,1},{13,5},{2,10},{6,14},... | collective-permute-start | bytes 387080 | tf_op jit(solution)/shard_map/back2_ep/ppermute | solution.py:32
  40.1 1.1 %collective-permute-start.16 = (bf16[72,896]{1,0:T(8,128)(2,1)S(1)}, bf16[72,896]{1,0:T(8,128)(2,1)S(1)}, u32[]{:S(2)}, u32[]{:S(2)}) collective-permute-start(bf16[72,896]{1,0:T(8,128)(2,1)S(1)} %after.17), channel_id=1, source_target_pairs={{0,2},{2,0},{1,3},{3,1},{4,6},{6,4},{5,7},{7,5},{8,10},{10,8},{9,1... | collective-permute-start | bytes 387080 | tf_op jit(solution)/shard_map/back0_tp/ppermute | solution.py:32
  41.9 0.9 %collective-permute-done.14.refs_1_ = bf16[72,896]{1,0:T(8,128)(2,1)S(1)} collective-permute-done((bf16[72,896]{1,0:T(8,128)(2,1)S(1)}, bf16[72,896]{1,0:T(8,128)(2,1)S(1)}, u32[]{:S(2)}, u32[]{:S(2)}) %collective-permute-start.14) | collective-permute-done | bytes 129056 | tf_op jit(solution)/shard_map/back1_ep/ppermute | solution.py:32
  42.8 3.5 %collective-permute-done.15.refs_2_ = bf16[72,896]{1,0:T(8,128)(2,1)S(1)} collective-permute-done((bf16[72,896]{1,0:T(8,128)(2,1)S(1)}, bf16[72,896]{1,0:T(8,128)(2,1)S(1)}, u32[]{:S(2)}, u32[]{:S(2)}) %collective-permute-start.15) | collective-permute-done | bytes 129056 | tf_op jit(solution)/shard_map/back1_ep_tp/ppermute | solution.py:32
  47.5 1.1 %unpack_latest.1 = bf16[128,1792]{1,0:T(8,128)(2,1)} custom-call(bf16[2,4,72,128]{3,2,1,0:T(8,128)(2,1)S(1)} %get-tuple-element.26.place_ref, bf16[72,896]{1,0:T(8,128)(2,1)S(1)} %collective-permute-done.12.refs_0_, bf16[128,1792]{1,0:T(8,128)(2,1)S(1)} %unpack.1.refs_1_), custom_call_target="tpu_custom_call" | custom-call | tf_op jit(solution)/shard_map/unpack_latest/pallas_call | solution.py:51
  (37 shorter events, 4.9 us)
Async XLA Ops:
  3.0 9.5 %collective-permute-start = (bf16[72,896]{1,0:T(8,128)(2,1)S(1)}, bf16[72,896]{1,0:T(8,128)(2,1)S(1)}, u32[]{:S(2)}, u32[]{:S(2)}) collective-permute-start(bf16[72,896]{1,0:T(8,128)(2,1)S(1)} %get-tuple-element.28.earlier_ref), channel_id=1, source_target_pairs={{0,12},{4,8},{8,4},{12,0},{1,13},{5,9},{9,5},{13,1},{2,14},{6,10},... | collective-permute-start | bytes 387080 | tf_op jit(solution)/shard_map/rows3_ep/ppermute | solution.py:32
  8.1 11.0 %collective-permute-start.3 = (bf16[72,896]{1,0:T(8,128)(2,1)S(1)}, bf16[72,896]{1,0:T(8,128)(2,1)S(1)}, u32[]{:S(2)}, u32[]{:S(2)}) collective-permute-start(bf16[72,896]{1,0:T(8,128)(2,1)S(1)} %get-tuple-element.29), channel_id=1, source_target_pairs={{0,4},{4,0},{8,12},{12,8},{1,5},{5,1},{9,13},{13,9},{2,6},{6,2},{1... | collective-permute-start | bytes 387080 | tf_op jit(solution)/shard_map/rows1_ep/ppermute | solution.py:32
  8.1 12.1 %collective-permute-start.4 = (bf16[72,896]{1,0:T(8,128)(2,1)S(1)}, bf16[72,896]{1,0:T(8,128)(2,1)S(1)}, u32[]{:S(2)}, u32[]{:S(2)}) collective-permute-start(bf16[72,896]{1,0:T(8,128)(2,1)S(1)} %get-tuple-element.29), channel_id=1, source_target_pairs={{0,6},{2,4},{4,2},{6,0},{8,14},{10,12},{12,10},{14,8},{1,7},{3,5},... | collective-permute-start | bytes 387080 | tf_op jit(solution)/shard_map/rows1_ep_tp/ppermute | solution.py:32
  11.0 9.1 %collective-permute-start.5 = (bf16[72,896]{1,0:T(8,128)(2,1)S(1)}, bf16[72,896]{1,0:T(8,128)(2,1)S(1)}, u32[]{:S(2)}, u32[]{:S(2)}) collective-permute-start(bf16[72,896]{1,0:T(8,128)(2,1)S(1)} %get-tuple-element.30.refs_4_), channel_id=1, source_target_pairs={{0,2},{2,0},{1,3},{3,1},{4,6},{6,4},{5,7},{7,5},{8,10},{10,8},{9,1... | collective-permute-start | bytes 387080 | tf_op jit(solution)/shard_map/rows0_tp/ppermute | solution.py:32
  12.4 10.1 %collective-permute-start.1 = (bf16[72,896]{1,0:T(8,128)(2,1)S(1)}, bf16[72,896]{1,0:T(8,128)(2,1)S(1)}, u32[]{:S(2)}, u32[]{:S(2)}) collective-permute-start(bf16[72,896]{1,0:T(8,128)(2,1)S(1)} %after.9), channel_id=1, source_target_pairs={{0,8},{4,12},{8,0},{12,4},{1,9},{5,13},{9,1},{13,5},{2,10},{6,14},... | collective-permute-start | bytes 387080 | tf_op jit(solution)/shard_map/rows2_ep/ppermute | solution.py:32
  14.7 7.0 %collective-permute-start.2 = (bf16[72,896]{1,0:T(8,128)(2,1)S(1)}, bf16[72,896]{1,0:T(8,128)(2,1)S(1)}, u32[]{:S(2)}, u32[]{:S(2)}) collective-permute-start(bf16[72,896]{1,0:T(8,128)(2,1)S(1)} %collective-permute-done.earlier_ref.refs_6_.refs_0_), channel_id=1, source_target_pairs={{0,2},{2,0},{1,3},{3,1},{4,6},{6,4},{5,7},{7,5},{8,10},{10,8},{9,1... | collective-permute-start | bytes 387080 | tf_op jit(solution)/shard_map/rows3_tp/ppermute | solution.py:32
  19.1 4.6 %collective-permute-start.8 = (bf16[128,256]{1,0:T(8,128)(2,1)S(1)}, bf16[128,256]{1,0:T(8,128)(2,1)S(1)}, u32[]{:S(2)}, u32[]{:S(2)}) collective-permute-start(bf16[128,256]{1,0:T(8,128)(2,1)S(1)} %slice_bitcast_fusion), channel_id=1, source_target_pairs={{0,2},{2,0},{1,3},{3,1},{4,6},{6,4},{5,7},{7,5},{8,10},{10,8},{9,1... | collective-permute-start | bytes 196616 | tf_op jit(solution)/shard_map/latent_tp/ppermute | solution.py:32
  22.5 1.5 %collective-permute-start.7 = (bf16[216,512]{1,0:T(8,128)(2,1)S(1)}, bf16[216,512]{1,0:T(8,128)(2,1)S(1)}, u32[]{:S(2)}, u32[]{:S(2)}) collective-permute-start(bf16[216,512]{1,0:T(8,128)(2,1)S(1)} %get-tuple-element.33), channel_id=1, source_target_pairs={{0,1},{1,0},{2,3},{3,2},{4,5},{5,4},{6,7},{7,6},{8,9},{9,8},{10,11... | collective-permute-start | bytes 663560 | tf_op jit(solution)/shard_map/hidden3_sub/ppermute | solution.py:32
  22.6 6.0 %collective-permute-start.6 = (bf16[72,896]{1,0:T(8,128)(2,1)S(1)}, bf16[72,896]{1,0:T(8,128)(2,1)S(1)}, u32[]{:S(2)}, u32[]{:S(2)}) collective-permute-start(bf16[72,896]{1,0:T(8,128)(2,1)S(1)} %after.11.refs_0_), channel_id=1, source_target_pairs={{0,2},{2,0},{1,3},{3,1},{4,6},{6,4},{5,7},{7,5},{8,10},{10,8},{9,1... | collective-permute-start | bytes 387080 | tf_op jit(solution)/shard_map/rows2_tp/ppermute | solution.py:32
  25.4 5.8 %collective-permute-start.10 = (bf16[72,896]{1,0:T(8,128)(2,1)S(1)}, bf16[72,896]{1,0:T(8,128)(2,1)S(1)}, u32[]{:S(2)}, u32[]{:S(2)}) collective-permute-start(bf16[72,896]{1,0:T(8,128)(2,1)S(1)} %get-tuple-element.43), channel_id=1, source_target_pairs={{0,2},{2,0},{1,3},{3,1},{4,6},{6,4},{5,7},{7,5},{8,10},{10,8},{9,1... | collective-permute-start | bytes 387080 | tf_op jit(solution)/shard_map/back3_tp/ppermute | solution.py:32
  29.3 3.4 %collective-permute-start.9 = (bf16[88,512]{1,0:T(8,128)(2,1)S(1)}, bf16[88,512]{1,0:T(8,128)(2,1)S(1)}, u32[]{:S(2)}, u32[]{:S(2)}) collective-permute-start(bf16[88,512]{1,0:T(8,128)(2,1)S(1)} %get-tuple-element.42), channel_id=1, source_target_pairs={{0,1},{1,0},{2,3},{3,2},{4,5},{5,4},{6,7},{7,6},{8,9},{9,8},{10,11... | collective-permute-start | bytes 270344 | tf_op jit(solution)/shard_map/hidden2_sub/ppermute | solution.py:32
  31.2 10.7 %collective-permute-start.13 = (bf16[72,896]{1,0:T(8,128)(2,1)S(1)}, bf16[72,896]{1,0:T(8,128)(2,1)S(1)}, u32[]{:S(2)}, u32[]{:S(2)}) collective-permute-start(bf16[72,896]{1,0:T(8,128)(2,1)S(1)} %add_convert_fusion.1.earlier_ref), channel_id=1, source_target_pairs={{0,12},{4,8},{8,4},{12,0},{1,13},{5,9},{9,5},{13,1},{2,14},{6,10},... | collective-permute-start | bytes 387080 | tf_op jit(solution)/shard_map/back3_ep/ppermute | solution.py:32
  33.9 5.0 %collective-permute-start.11 = (bf16[72,896]{1,0:T(8,128)(2,1)S(1)}, bf16[72,896]{1,0:T(8,128)(2,1)S(1)}, u32[]{:S(2)}, u32[]{:S(2)}) collective-permute-start(bf16[72,896]{1,0:T(8,128)(2,1)S(1)} %get-tuple-element.45), channel_id=1, source_target_pairs={{0,2},{2,0},{1,3},{3,1},{4,6},{6,4},{5,7},{7,5},{8,10},{10,8},{9,1... | collective-permute-start | bytes 387080 | tf_op jit(solution)/shard_map/back2_tp/ppermute | solution.py:32
  34.9 7.9 %collective-permute-start.14 = (bf16[72,896]{1,0:T(8,128)(2,1)S(1)}, bf16[72,896]{1,0:T(8,128)(2,1)S(1)}, u32[]{:S(2)}, u32[]{:S(2)}) collective-permute-start(bf16[72,896]{1,0:T(8,128)(2,1)S(1)} %after.15), channel_id=1, source_target_pairs={{0,4},{4,0},{8,12},{12,8},{1,5},{5,1},{9,13},{13,9},{2,6},{6,2},{1... | collective-permute-start | bytes 387080 | tf_op jit(solution)/shard_map/back1_ep/ppermute | solution.py:32
  34.9 11.4 %collective-permute-start.15 = (bf16[72,896]{1,0:T(8,128)(2,1)S(1)}, bf16[72,896]{1,0:T(8,128)(2,1)S(1)}, u32[]{:S(2)}, u32[]{:S(2)}) collective-permute-start(bf16[72,896]{1,0:T(8,128)(2,1)S(1)} %after.16), channel_id=1, source_target_pairs={{0,6},{2,4},{4,2},{6,0},{8,14},{10,12},{12,10},{14,8},{1,7},{3,5},... | collective-permute-start | bytes 387080 | tf_op jit(solution)/shard_map/back1_ep_tp/ppermute | solution.py:32
  38.9 8.5 %collective-permute-start.12 = (bf16[72,896]{1,0:T(8,128)(2,1)S(1)}, bf16[72,896]{1,0:T(8,128)(2,1)S(1)}, u32[]{:S(2)}, u32[]{:S(2)}) collective-permute-start(bf16[72,896]{1,0:T(8,128)(2,1)S(1)} %add_convert_fusion.earlier_ref), channel_id=1, source_target_pairs={{0,8},{4,12},{8,0},{12,4},{1,9},{5,13},{9,1},{13,5},{2,10},{6,14},... | collective-permute-start | bytes 387080 | tf_op jit(solution)/shard_map/back2_ep/ppermute | solution.py:32
  40.1 6.7 %collective-permute-start.16 = (bf16[72,896]{1,0:T(8,128)(2,1)S(1)}, bf16[72,896]{1,0:T(8,128)(2,1)S(1)}, u32[]{:S(2)}, u32[]{:S(2)}) collective-permute-start(bf16[72,896]{1,0:T(8,128)(2,1)S(1)} %after.17), channel_id=1, source_target_pairs={{0,2},{2,0},{1,3},{3,1},{4,6},{6,4},{5,7},{7,5},{8,10},{10,8},{9,1... | collective-permute-start | bytes 387080 | tf_op jit(solution)/shard_map/back0_tp/ppermute | solution.py:32

commit v11 on v10

--- a/solution.py
+++ b/solution.py
@@ -99,19 +99,13 @@
     return copies
 
 
-def pack_kernel(most, order, *refs):
-    given, partial_ref, refs = refs[:4], refs[4], refs[5:]
-    blocks, (place_ref, share_ref), refs = refs[: len(order)], refs[len(order) :][:2], refs[-6:]
-    held, sems, share_sems = refs[:4], refs[4], refs[5]
-    lane, count = lax.axis_index("tp"), partial_ref.shape[0]
+def pack_kernel(most, order, leading, *refs):
+    given, refs = refs[:4], refs[4:]
+    blocks, (place_ref, *held), (ids_ref, sems) = refs[:leading], refs[leading:-2], refs[-2:]
+    held = [ids_ref] + held
     copies = fetch(given, held, sems)
-    shares = fetch(
-        [partial_ref.at[lane ^ j] for j in range(count)],
-        [share_ref.at[j] for j in range(count)],
-        share_sems,
-    )
     copies[0].wait()
-    ids_ref, weights_ref, scales_ref, grad_ref = held
+    weights_ref, scales_ref, grad_ref = held[1:]
     tokens, rows = grad_ref.shape[0], blocks[0].shape[0]
     me = lax.axis_index("ep")
     ids = ids_ref[...]
@@ -136,13 +130,50 @@
         copy.wait()
     for block_ref, (low, high) in zip(blocks, found):
         fill(block_ref, most, low, high, weights_ref, scales_ref, grad_ref)
+
+
+def pack_more_kernel(most, order, place_ref, weights_ref, scales_ref, grad_ref, partial_ref, *refs):
+    blocks, (share_ref, sems) = refs[:-2], refs[-2:]
+    lane, count = lax.axis_index("tp"), partial_ref.shape[0]
+    shares = fetch(
+        [partial_ref.at[lane ^ j] for j in range(count)],
+        [share_ref.at[j] for j in range(count)],
+        sems,
+    )
+    for block_ref, k in zip(blocks, order):
+        low, high = place_ref[0, k] != 0, place_ref[1, k] != 0
+        fill(block_ref, most, low, high, weights_ref, scales_ref, grad_ref)
     for copy in shares:
         copy.wait()
 
 
-def fetch_kernel(*refs):
-    count = len(refs) // 2
-    for copy in fetch(refs[:count], refs[count : 2 * count], refs[-1]):
+def by_xor(value, most, narrow, lane):
+    step = 1
+    while step < narrow:
+        pieces = [value[i * most : (i + step) * most] for i in range(0, narrow, step)]
+        turned = [pieces[i ^ 1] for i in range(len(pieces))]
+        value = jnp.where((lane & step) != 0, jnp.concatenate(turned, axis=0), value)
+        step *= 2
+    return value
+
+
+def fetch_kernel(most, *refs):
+    pre_ref, sems = refs[-2:]
+    wide = pre_ref.shape[1]
+    narrow = pre_ref.shape[2] // most
+    count = (len(refs) - 3) // 2
+    given, (up_ref, gate_ref, *held) = refs[:count], refs[count:-2]
+    copies = fetch(given, [pre_ref] + held, sems)
+    me, lane = lax.axis_index("ep"), lax.axis_index("tp")
+    copies[0].wait()
+    for k in range(wide):
+        gate_pre, up_pre = [
+            by_xor(pre_ref[i, me ^ k].astype(jnp.float32), most, narrow, lane) for i in range(2)
+        ]
+        sig = 1.0 / (1.0 + jnp.exp(-gate_pre))
+        up_ref[k] = gate_pre * sig
+        gate_ref[k] = up_pre * sig * (1.0 + gate_pre * (1.0 - sig))
+    for copy in copies[1:]:
         copy.wait()
 
 
@@ -165,30 +196,14 @@
     sent_ref[:count, :] = total.astype(jnp.bfloat16)
 
 
-def by_xor(value, most, narrow, lane):
-    step = 1
-    while step < narrow:
-        pieces = [value[i * most : (i + step) * most] for i in range(0, narrow, step)]
-        turned = [pieces[i ^ 1] for i in range(len(pieces))]
-        value = jnp.where((lane & step) != 0, jnp.concatenate(turned, axis=0), value)
-        step *= 2
-    return value
-
-
-def back_kernel(most, narrow, group, sum_ref, other_ref, pre_ref, gate_ref, up_ref, *outs):
+def back_kernel(most, group, sum_ref, other_ref, up_by_ref, gate_by_ref, gate_ref, up_ref, *outs):
     half = gate_ref.shape[0] // 2
-    me, lane = lax.axis_index("ep"), lax.axis_index("tp")
     hidden = sum_ref[...] + other_ref[: sum_ref.shape[0], :].astype(jnp.float32)
-    gate_pre, up_pre = [
-        jnp.concatenate(
-            [by_xor(pre_ref[i, me ^ k].astype(jnp.float32), most, narrow, lane) for k in group],
-            axis=0,
-        )
-        for i in range(2)
+    up_by, gate_by = [
+        jnp.concatenate([by_ref[k] for k in group], axis=0) for by_ref in (up_by_ref, gate_by_ref)
     ]
-    sig = 1.0 / (1.0 + jnp.exp(-gate_pre))
-    up_grad = (hidden * gate_pre * sig).astype(jnp.bfloat16)
-    gate_grad = (hidden * up_pre * sig * (1.0 + gate_pre * (1.0 - sig))).astype(jnp.bfloat16)
+    up_grad = (hidden * up_by).astype(jnp.bfloat16)
+    gate_grad = (hidden * gate_by).astype(jnp.bfloat16)
     low = dot(gate_grad, gate_ref[:half], NT) + dot(up_grad, up_ref[:half], NT)
     high = dot(gate_grad, gate_ref[half:], NT) + dot(up_grad, up_ref[half:], NT)
     for i, out in enumerate(outs):
@@ -248,29 +263,36 @@
     groups = groups_of(wide)
     order = [k for group in groups for k in group]
     partials = latent_partials.reshape(narrow, tokens, latent.shape[1])
-    packed = call(
-        functools.partial(pack_kernel, most, order),
-        [block] * wide + [pltpu.VMEM((2, wide, rows, tokens), bf16), like(partials)],
+    leading, place, *fillers = call(
+        functools.partial(pack_kernel, most, order, 1),
+        [
+            block,
+            pltpu.VMEM((2, wide, rows, tokens), bf16),
+            pltpu.VMEM((1, tokens), f32),
+            pltpu.VMEM((grad_scales.shape[1], tokens), f32),
+            pltpu.VMEM((tokens, width), bf16),
+        ],
         *pinned(
             expert_ids.reshape(1, tokens),
             route_weights.reshape(1, tokens),
             grad_scales.T,
             grad_values,
-            partials,
         ),
-        specs=[HBM] * 5,
-        scratch=[
-            pltpu.VMEM((1, tokens), jnp.int32),
-            pltpu.VMEM((1, tokens), f32),
-            pltpu.VMEM((grad_scales.shape[1], tokens), f32),
-            pltpu.VMEM((tokens, width), bf16),
-            pltpu.SemaphoreType.DMA((4,)),
-            pltpu.SemaphoreType.DMA((narrow,)),
-        ],
+        specs=[HBM] * 4,
+        scratch=[pltpu.VMEM((1, tokens), jnp.int32), pltpu.SemaphoreType.DMA((4,))],
         name="pack",
     )
-    place, shares = packed[wide:]
-    packed = dict(zip(order, packed))
+    *packed, shares = call(
+        functools.partial(pack_more_kernel, most, order[1:]),
+        [block] * (wide - 1) + [like(partials)],
+        place,
+        *fillers,
+        *pinned(partials),
+        specs=[VMEM] * 4 + [HBM],
+        scratch=[pltpu.SemaphoreType.DMA((narrow,))],
+        name="pack_more",
+    )
+    packed = dict(zip(order, [leading] + packed))
 
     first, staged = groups[0][0], len(groups) > 1
     taken = {0: [packed[0]] + [swap(packed[0], "rows0", tp=j) for j in range(1, narrow)]}
@@ -282,19 +304,20 @@
             if staged and k == groups[1][0]:
                 arrived[k] = after(arrived[k], packed[first], 1 << 31)
     fetched = [
+        pre_acts.reshape(2, wide, narrow * most, hidden_width),
         w_down[0],
-        pre_acts.reshape(2, wide, narrow * most, hidden_width),
         w_gate[0],
         w_up[0],
         latent,
         latent_gain.reshape(1, -1),
     ]
-    down, pre, gate, up, latent, latent_gain = call(
-        fetch_kernel,
-        [like(array) for array in fetched],
+    factors = pltpu.VMEM((wide, narrow * most, hidden_width), f32)
+    up_by, gate_by, down, gate, up, latent, latent_gain = call(
+        functools.partial(fetch_kernel, most),
+        [factors, factors] + [like(array) for array in fetched[1:]],
         *pinned(*fetched),
         specs=[HBM] * len(fetched),
-        scratch=[pltpu.SemaphoreType.DMA((len(fetched),))],
+        scratch=[like(fetched[0]), pltpu.SemaphoreType.DMA((len(fetched),))],
         earlier=[arrived[first]],
         name="fetch",
     )
@@ -348,11 +371,12 @@
         if moved is not None:
             received = after(received, moved)
         products = call(
-            functools.partial(back_kernel, most, narrow, group),
+            functools.partial(back_kernel, most, group),
             [block] * (len(group) * narrow),
             summed,
             received,
-            pre,
+            up_by,
+            gate_by,
             gate,
             up,
             name="back",

time: 48.7 us -> 49.3 us (1.012)
  starting transfers between devices: 22.7 us -> 19.7 us
  waiting for transfers between devices: 13.3 us -> 15.8 us
  Pallas kernels: 10.8 us -> 11.8 us
    ppermute x17, starting transfers between devices: 22.7 us -> 19.7 us  [swap(): return lax.ppermute(value, tuple(steps), pairs)]
    ppermute x17, waiting for transfers between devices: 13.3 us -> 15.8 us  [swap(): return lax.ppermute(value, tuple(steps), pairs)]
    pallas_call x8 -> x9, Pallas kernels: 10.8 us -> 11.8 us  [call(): pl.pallas_call(kernel, out_shape=outs, in_specs=specs, out_specs=[VMEM] *...]
  transfers between devices with their start and end apart: 17 -> 17, of which waited for: 10 -> 11; matrix products, arithmetic and copies ran while one was open for 2% -> 2% of each run, Pallas kernels for 15% -> 19%
where the time goes in v11:
time: 49.3 us; the launch traced here: 49.1 us
  starting transfers between devices  19.7 us (40%)
  waiting for transfers between devices  15.8 us (32%)
  Pallas kernels  11.8 us (24%)
  other arithmetic  0.97 us (2%)
  between operations  0.78 us (2%)
    ppermute x17, starting transfers between devices, swap(): return lax.ppermute(value, tuple(steps), pairs)  19.7 us
    ppermute x17, waiting for transfers between devices, swap(): return lax.ppermute(value, tuple(steps), pairs)  15.8 us
    pallas_call x9, Pallas kernels, call(): pl.pallas_call(kernel, out_shape=outs, in_specs=specs, out_specs=[VMEM] *...  11.8 us
  transfers between devices with their start and end apart: 17, of which 11 were waited for; matrix products, arithmetic and copies ran while one was open for 2% of the time, Pallas kernels for 19%

profile of v11, /device:TPU:0, one launch (start us, length us, event | category | flops | bytes accessed | tf_op | source)
XLA Modules:
  0.0 49.1 jit_solution(11312229061433443997)
XLA Ops:
  0.6 1.6 %pack.1 = (bf16[72,896]{1,0:T(8,128)(2,1)S(1)}, bf16[2,4,72,128]{3,2,1,0:T(8,128)(2,1)S(1)}, f32[1,128]{1,0:T(1,128)S(1)}, f32[14,128]{1,0:T(8,128)S(1)}, bf16[128,1792]{1,0:T(8,128)(2,1)S(1)}) custom-call(s32[1,128]{1,0:T(1,128)} %bitcast.36, f32[1,128]{1,0:T(1,128)} %bitcast.37, f32[14,128]{1,0:T(8,128)} %bitcast.30, bf16[128,1792]{1,0:T(8,128)(2,1)} %refs_3_.1), custom_call_target="tpu_custom_call" | custom-call | tf_op jit(solution)/shard_map/pack/pallas_call | solution.py:51
  2.2 5.1 %collective-permute-start = (bf16[72,896]{1,0:T(8,128)(2,1)S(1)}, bf16[72,896]{1,0:T(8,128)(2,1)S(1)}, u32[]{:S(2)}, u32[]{:S(2)}) collective-permute-start(bf16[72,896]{1,0:T(8,128)(2,1)S(1)} %get-tuple-element.35.earlier_ref), channel_id=1, source_target_pairs={{0,12},{4,8},{8,4},{12,0},{1,13},{5,9},{9,5},{13,1},{2,14},{6,10},... | collective-permute-start | bytes 387080 | tf_op jit(solution)/shard_map/rows3_ep/ppermute | solution.py:32
  7.4 1.8 %pack_more.1 = (bf16[72,896]{1,0:T(8,128)(2,1)S(1)}, bf16[72,896]{1,0:T(8,128)(2,1)S(1)}, bf16[72,896]{1,0:T(8,128)(2,1)S(1)}, bf16[2,128,256]{2,1,0:T(8,128)(2,1)S(1)}) custom-call(bf16[2,4,72,128]{3,2,1,0:T(8,128)(2,1)S(1)} %get-tuple-element.30.place_ref, f32[1,128]{1,0:T(1,128)S(1)} %get-tuple-element.31.weights_ref, ...), custom_call_target="tpu_custom_call" | custom-call | tf_op jit(solution)/shard_map/pack_more/pallas_call | solution.py:51
  9.2 2.9 %collective-permute-start.4 = (bf16[72,896]{1,0:T(8,128)(2,1)S(1)}, bf16[72,896]{1,0:T(8,128)(2,1)S(1)}, u32[]{:S(2)}, u32[]{:S(2)}) collective-permute-start(bf16[72,896]{1,0:T(8,128)(2,1)S(1)} %get-tuple-element.36), channel_id=1, source_target_pairs={{0,6},{2,4},{4,2},{6,0},{8,14},{10,12},{12,10},{14,8},{1,7},{3,5},... | collective-permute-start | bytes 387080 | tf_op jit(solution)/shard_map/rows1_ep_tp/ppermute | solution.py:32
  12.7 1.4 %collective-permute-start.1 = (bf16[72,896]{1,0:T(8,128)(2,1)S(1)}, bf16[72,896]{1,0:T(8,128)(2,1)S(1)}, u32[]{:S(2)}, u32[]{:S(2)}) collective-permute-start(bf16[72,896]{1,0:T(8,128)(2,1)S(1)} %after.9), channel_id=1, source_target_pairs={{0,8},{4,12},{8,0},{12,4},{1,9},{5,13},{9,1},{13,5},{2,10},{6,14},... | collective-permute-start | bytes 387080 | tf_op jit(solution)/shard_map/rows2_ep/ppermute | solution.py:32
  14.1 1.5 %collective-permute-start.2 = (bf16[72,896]{1,0:T(8,128)(2,1)S(1)}, bf16[72,896]{1,0:T(8,128)(2,1)S(1)}, u32[]{:S(2)}, u32[]{:S(2)}) collective-permute-start(bf16[72,896]{1,0:T(8,128)(2,1)S(1)} %collective-permute-done.earlier_ref.refs_6_.refs_0_), channel_id=1, source_target_pairs={{0,2},{2,0},{1,3},{3,1},{4,6},{6,4},{5,7},{7,5},{8,10},{10,8},{9,1... | collective-permute-start | bytes 387080 | tf_op jit(solution)/shard_map/rows3_tp/ppermute | solution.py:32
  15.6 2.9 %fetch.1 = (f32[4,72,512]{2,1,0:T(8,128)S(1)}, f32[4,72,512]{2,1,0:T(8,128)S(1)}, bf16[512,1792]{1,0:T(8,128)(2,1)S(1)}, bf16[1792,512]{1,0:T(8,128)(2,1)S(1)}, ...) custom-call(bf16[2,4,72,512]{3,2,1,0:T(8,128)(2,1)} %bitcast.28, ...), custom_call_target="tpu_custom_call" | custom-call | tf_op jit(solution)/shard_map/fetch/pallas_call | solution.py:51
  19.5 0.8 %collective-permute-done.5.refs_5_ = bf16[72,896]{1,0:T(8,128)(2,1)S(1)} collective-permute-done((bf16[72,896]{1,0:T(8,128)(2,1)S(1)}, bf16[72,896]{1,0:T(8,128)(2,1)S(1)}, u32[]{:S(2)}, u32[]{:S(2)}) %collective-permute-start.5) | collective-permute-done | bytes 129056 | tf_op jit(solution)/shard_map/rows0_tp/ppermute | solution.py:32
  20.3 2.4 %collective-permute-done.2.refs_1_ = bf16[72,896]{1,0:T(8,128)(2,1)S(1)} collective-permute-done((bf16[72,896]{1,0:T(8,128)(2,1)S(1)}, bf16[72,896]{1,0:T(8,128)(2,1)S(1)}, u32[]{:S(2)}, u32[]{:S(2)}) %collective-permute-start.2) | collective-permute-done | bytes 129056 | tf_op jit(solution)/shard_map/rows3_tp/ppermute | solution.py:32
  22.7 0.8 %hidden.2 = (f32[216,512]{1,0:T(8,128)S(1)}, bf16[216,512]{1,0:T(8,128)(2,1)S(1)}) custom-call(bf16[72,896]{1,0:T(8,128)(2,1)S(1)} %collective-permute-done.earlier_ref.refs_6_.refs_0_, bf16[72,896]{1,0:T(8,128)(2,1)S(1)} %collective-permute-done.2.refs_1_, bf16[72,896]{1,0:T(8,128)(2,1)S(1)} %collective-permute-done.3.refs_2_, ...), custom_call_target="tpu_custom_call" | custom-call | tf_op jit(solution)/shard_map/hidden/pallas_call | solution.py:51
  24.2 0.8 %collective-permute-done.7.other_ref = bf16[216,512]{1,0:T(8,128)(2,1)S(1)} collective-permute-done((bf16[216,512]{1,0:T(8,128)(2,1)S(1)}, bf16[216,512]{1,0:T(8,128)(2,1)S(1)}, u32[]{:S(2)}, u32[]{:S(2)}) %collective-permute-start.7) | collective-permute-done | bytes 221216 | tf_op jit(solution)/shard_map/hidden3_sub/ppermute | solution.py:32
  25.0 1.3 %back.2 = (bf16[72,896]{1,0:T(8,128)(2,1)S(1)}, bf16[72,896]{1,0:T(8,128)(2,1)S(1)}, bf16[72,896]{1,0:T(8,128)(2,1)S(1)}, bf16[72,896]{1,0:T(8,128)(2,1)S(1)}, b...) custom-call(f32[216,512]{1,0:T(8,128)S(1)} %get-tuple-element.39.earlier_ref.sum_ref, ...), custom_call_target="tpu_custom_call" | custom-call | tf_op jit(solution)/shard_map/back/pallas_call | solution.py:51
  26.3 0.7 %collective-permute-start.10 = (bf16[72,896]{1,0:T(8,128)(2,1)S(1)}, bf16[72,896]{1,0:T(8,128)(2,1)S(1)}, u32[]{:S(2)}, u32[]{:S(2)}) collective-permute-start(bf16[72,896]{1,0:T(8,128)(2,1)S(1)} %get-tuple-element.51), channel_id=1, source_target_pairs={{0,2},{2,0},{1,3},{3,1},{4,6},{6,4},{5,7},{7,5},{8,10},{10,8},{9,1... | collective-permute-start | bytes 387080 | tf_op jit(solution)/shard_map/back3_tp/ppermute | solution.py:32
  27.2 2.5 %collective-permute-done.6.value_ref = bf16[72,896]{1,0:T(8,128)(2,1)S(1)} collective-permute-done((bf16[72,896]{1,0:T(8,128)(2,1)S(1)}, bf16[72,896]{1,0:T(8,128)(2,1)S(1)}, u32[]{:S(2)}, u32[]{:S(2)}) %collective-permute-start.6) | collective-permute-done | bytes 129056 | tf_op jit(solution)/shard_map/rows2_tp/ppermute | solution.py:32
  30.5 1.8 %collective-permute-done.10 = bf16[72,896]{1,0:T(8,128)(2,1)S(1)} collective-permute-done((bf16[72,896]{1,0:T(8,128)(2,1)S(1)}, bf16[72,896]{1,0:T(8,128)(2,1)S(1)}, u32[]{:S(2)}, u32[]{:S(2)}) %collective-permute-start.10) | collective-permute-done | bytes 129056 | tf_op jit(solution)/shard_map/back3_tp/ppermute | solution.py:32
  32.3 1.4 %collective-permute-start.13 = (bf16[72,896]{1,0:T(8,128)(2,1)S(1)}, bf16[72,896]{1,0:T(8,128)(2,1)S(1)}, u32[]{:S(2)}, u32[]{:S(2)}) collective-permute-start(bf16[72,896]{1,0:T(8,128)(2,1)S(1)} %add_convert_fusion.1.earlier_ref), channel_id=1, source_target_pairs={{0,12},{4,8},{8,4},{12,0},{1,13},{5,9},{9,5},{13,1},{2,14},{6,10},... | collective-permute-start | bytes 387080 | tf_op jit(solution)/shard_map/back3_ep/ppermute | solution.py:32
  33.7 1.2 %back.3 = (bf16[72,896]{1,0:T(8,128)(2,1)S(1)}, bf16[72,896]{1,0:T(8,128)(2,1)S(1)}) custom-call(f32[72,512]{1,0:T(8,128)S(1)} %get-tuple-element.49.sum_ref, bf16[88,512]{1,0:T(8,128)(2,1)S(1)} %after.14.other_ref, f32[4,72,512]{2,1,0:T(8,128)S(1)} %get-tuple-element.41.up_by_ref, f32[4,72,512]{2,1,0:T(8,128)S(1)} %get-tuple-element.42.gate_by_ref, ...), custom_call_target="tpu_custom_call" | custom-call | tf_op jit(solution)/shard_map/back/pallas_call | solution.py:51
  34.9 0.8 %collective-permute-start.11 = (bf16[72,896]{1,0:T(8,128)(2,1)S(1)}, bf16[72,896]{1,0:T(8,128)(2,1)S(1)}, u32[]{:S(2)}, u32[]{:S(2)}) collective-permute-start(bf16[72,896]{1,0:T(8,128)(2,1)S(1)} %get-tuple-element.53), channel_id=1, source_target_pairs={{0,2},{2,0},{1,3},{3,1},{4,6},{6,4},{5,7},{7,5},{8,10},{10,8},{9,1... | collective-permute-start | bytes 387080 | tf_op jit(solution)/shard_map/back2_tp/ppermute | solution.py:32
  35.8 2.7 %collective-permute-start.15 = (bf16[72,896]{1,0:T(8,128)(2,1)S(1)}, bf16[72,896]{1,0:T(8,128)(2,1)S(1)}, u32[]{:S(2)}, u32[]{:S(2)}) collective-permute-start(bf16[72,896]{1,0:T(8,128)(2,1)S(1)} %after.16), channel_id=1, source_target_pairs={{0,6},{2,4},{4,2},{6,0},{8,14},{10,12},{12,10},{14,8},{1,7},{3,5},... | collective-permute-start | bytes 387080 | tf_op jit(solution)/shard_map/back1_ep_tp/ppermute | solution.py:32
  38.5 1.4 %collective-permute-done.11 = bf16[72,896]{1,0:T(8,128)(2,1)S(1)} collective-permute-done((bf16[72,896]{1,0:T(8,128)(2,1)S(1)}, bf16[72,896]{1,0:T(8,128)(2,1)S(1)}, u32[]{:S(2)}, u32[]{:S(2)}) %collective-permute-start.11) | collective-permute-done | bytes 129056 | tf_op jit(solution)/shard_map/back2_tp/ppermute | solution.py:32
  41.1 0.8 %fusion.5 = bf16[128,256]{1,0:T(8,128)(2,1)} fusion(bf16[128,256]{1,0:T(8,128)(2,1)S(1)} %get-tuple-element.46, bf16[128,256]{1,0:T(8,128)(2,1)S(1)} %after.13, f32[128]{0:T(128)S(1)} %slice_bitcast_fusion.1, f32[128]{0:T(128)S(1)} %get-tuple-element.60, f32[128]{0:T(128)S(1)} %get-tuple-element.61, f32[256]{0:T(256)S(1)} %bitcast.24, ...), kind=kLoop, calls=%fused_computation.10 | loop fusion | flops 360448 | bytes 264704 | tf_op jit(solution)/shard_map/convert_element_type | solution.py:410
  41.9 2.2 %collective-permute-done.14.refs_1_ = bf16[72,896]{1,0:T(8,128)(2,1)S(1)} collective-permute-done((bf16[72,896]{1,0:T(8,128)(2,1)S(1)}, bf16[72,896]{1,0:T(8,128)(2,1)S(1)}, u32[]{:S(2)}, u32[]{:S(2)}) %collective-permute-start.14) | collective-permute-done | bytes 129056 | tf_op jit(solution)/shard_map/back1_ep/ppermute | solution.py:32
  44.1 2.7 %collective-permute-done.15.refs_2_ = bf16[72,896]{1,0:T(8,128)(2,1)S(1)} collective-permute-done((bf16[72,896]{1,0:T(8,128)(2,1)S(1)}, bf16[72,896]{1,0:T(8,128)(2,1)S(1)}, u32[]{:S(2)}, u32[]{:S(2)}) %collective-permute-start.15) | collective-permute-done | bytes 129056 | tf_op jit(solution)/shard_map/back1_ep_tp/ppermute | solution.py:32
  48.1 1.1 %unpack_latest.1 = bf16[128,1792]{1,0:T(8,128)(2,1)} custom-call(bf16[2,4,72,128]{3,2,1,0:T(8,128)(2,1)S(1)} %get-tuple-element.30.place_ref, bf16[72,896]{1,0:T(8,128)(2,1)S(1)} %collective-permute-done.12.refs_0_, bf16[128,1792]{1,0:T(8,128)(2,1)S(1)} %unpack.1.refs_1_), custom_call_target="tpu_custom_call" | custom-call | tf_op jit(solution)/shard_map/unpack_latest/pallas_call | solution.py:51
  (38 shorter events, 5.6 us)
Async XLA Ops:
  2.2 10.5 %collective-permute-start = (bf16[72,896]{1,0:T(8,128)(2,1)S(1)}, bf16[72,896]{1,0:T(8,128)(2,1)S(1)}, u32[]{:S(2)}, u32[]{:S(2)}) collective-permute-start(bf16[72,896]{1,0:T(8,128)(2,1)S(1)} %get-tuple-element.35.earlier_ref), channel_id=1, source_target_pairs={{0,12},{4,8},{8,4},{12,0},{1,13},{5,9},{9,5},{13,1},{2,14},{6,10},... | collective-permute-start | bytes 387080 | tf_op jit(solution)/shard_map/rows3_ep/ppermute | solution.py:32
  9.1 9.3 %collective-permute-start.3 = (bf16[72,896]{1,0:T(8,128)(2,1)S(1)}, bf16[72,896]{1,0:T(8,128)(2,1)S(1)}, u32[]{:S(2)}, u32[]{:S(2)}) collective-permute-start(bf16[72,896]{1,0:T(8,128)(2,1)S(1)} %get-tuple-element.36), channel_id=1, source_target_pairs={{0,4},{4,0},{8,12},{12,8},{1,5},{5,1},{9,13},{13,9},{2,6},{6,2},{1... | collective-permute-start | bytes 387080 | tf_op jit(solution)/shard_map/rows1_ep/ppermute | solution.py:32
  9.2 10.2 %collective-permute-start.4 = (bf16[72,896]{1,0:T(8,128)(2,1)S(1)}, bf16[72,896]{1,0:T(8,128)(2,1)S(1)}, u32[]{:S(2)}, u32[]{:S(2)}) collective-permute-start(bf16[72,896]{1,0:T(8,128)(2,1)S(1)} %get-tuple-element.36), channel_id=1, source_target_pairs={{0,6},{2,4},{4,2},{6,0},{8,14},{10,12},{12,10},{14,8},{1,7},{3,5},... | collective-permute-start | bytes 387080 | tf_op jit(solution)/shard_map/rows1_ep_tp/ppermute | solution.py:32
  12.2 8.1 %collective-permute-start.5 = (bf16[72,896]{1,0:T(8,128)(2,1)S(1)}, bf16[72,896]{1,0:T(8,128)(2,1)S(1)}, u32[]{:S(2)}, u32[]{:S(2)}) collective-permute-start(bf16[72,896]{1,0:T(8,128)(2,1)S(1)} %get-tuple-element.37.refs_4_), channel_id=1, source_target_pairs={{0,2},{2,0},{1,3},{3,1},{4,6},{6,4},{5,7},{7,5},{8,10},{10,8},{9,1... | collective-permute-start | bytes 387080 | tf_op jit(solution)/shard_map/rows0_tp/ppermute | solution.py:32
  12.7 10.9 %collective-permute-start.1 = (bf16[72,896]{1,0:T(8,128)(2,1)S(1)}, bf16[72,896]{1,0:T(8,128)(2,1)S(1)}, u32[]{:S(2)}, u32[]{:S(2)}) collective-permute-start(bf16[72,896]{1,0:T(8,128)(2,1)S(1)} %after.9), channel_id=1, source_target_pairs={{0,8},{4,12},{8,0},{12,4},{1,9},{5,13},{9,1},{13,5},{2,10},{6,14},... | collective-permute-start | bytes 387080 | tf_op jit(solution)/shard_map/rows2_ep/ppermute | solution.py:32
  14.1 8.6 %collective-permute-start.2 = (bf16[72,896]{1,0:T(8,128)(2,1)S(1)}, bf16[72,896]{1,0:T(8,128)(2,1)S(1)}, u32[]{:S(2)}, u32[]{:S(2)}) collective-permute-start(bf16[72,896]{1,0:T(8,128)(2,1)S(1)} %collective-permute-done.earlier_ref.refs_6_.refs_0_), channel_id=1, source_target_pairs={{0,2},{2,0},{1,3},{3,1},{4,6},{6,4},{5,7},{7,5},{8,10},{10,8},{9,1... | collective-permute-start | bytes 387080 | tf_op jit(solution)/shard_map/rows3_tp/ppermute | solution.py:32
  18.5 5.7 %collective-permute-start.8 = (bf16[128,256]{1,0:T(8,128)(2,1)S(1)}, bf16[128,256]{1,0:T(8,128)(2,1)S(1)}, u32[]{:S(2)}, u32[]{:S(2)}) collective-permute-start(bf16[128,256]{1,0:T(8,128)(2,1)S(1)} %slice_bitcast_fusion), channel_id=1, source_target_pairs={{0,2},{2,0},{1,3},{3,1},{4,6},{6,4},{5,7},{7,5},{8,10},{10,8},{9,1... | collective-permute-start | bytes 196616 | tf_op jit(solution)/shard_map/latent_tp/ppermute | solution.py:32
  23.5 1.5 %collective-permute-start.7 = (bf16[216,512]{1,0:T(8,128)(2,1)S(1)}, bf16[216,512]{1,0:T(8,128)(2,1)S(1)}, u32[]{:S(2)}, u32[]{:S(2)}) collective-permute-start(bf16[216,512]{1,0:T(8,128)(2,1)S(1)} %get-tuple-element.40), channel_id=1, source_target_pairs={{0,1},{1,0},{2,3},{3,2},{4,5},{5,4},{6,7},{7,6},{8,9},{9,8},{10,11... | collective-permute-start | bytes 663560 | tf_op jit(solution)/shard_map/hidden3_sub/ppermute | solution.py:32
  23.6 6.1 %collective-permute-start.6 = (bf16[72,896]{1,0:T(8,128)(2,1)S(1)}, bf16[72,896]{1,0:T(8,128)(2,1)S(1)}, u32[]{:S(2)}, u32[]{:S(2)}) collective-permute-start(bf16[72,896]{1,0:T(8,128)(2,1)S(1)} %after.11.refs_0_), channel_id=1, source_target_pairs={{0,2},{2,0},{1,3},{3,1},{4,6},{6,4},{5,7},{7,5},{8,10},{10,8},{9,1... | collective-permute-start | bytes 387080 | tf_op jit(solution)/shard_map/rows2_tp/ppermute | solution.py:32
  26.3 5.9 %collective-permute-start.10 = (bf16[72,896]{1,0:T(8,128)(2,1)S(1)}, bf16[72,896]{1,0:T(8,128)(2,1)S(1)}, u32[]{:S(2)}, u32[]{:S(2)}) collective-permute-start(bf16[72,896]{1,0:T(8,128)(2,1)S(1)} %get-tuple-element.51), channel_id=1, source_target_pairs={{0,2},{2,0},{1,3},{3,1},{4,6},{6,4},{5,7},{7,5},{8,10},{10,8},{9,1... | collective-permute-start | bytes 387080 | tf_op jit(solution)/shard_map/back3_tp/ppermute | solution.py:32
  30.4 3.3 %collective-permute-start.9 = (bf16[88,512]{1,0:T(8,128)(2,1)S(1)}, bf16[88,512]{1,0:T(8,128)(2,1)S(1)}, u32[]{:S(2)}, u32[]{:S(2)}) collective-permute-start(bf16[88,512]{1,0:T(8,128)(2,1)S(1)} %get-tuple-element.50), channel_id=1, source_target_pairs={{0,1},{1,0},{2,3},{3,2},{4,5},{5,4},{6,7},{7,6},{8,9},{9,8},{10,11... | collective-permute-start | bytes 270344 | tf_op jit(solution)/shard_map/hidden2_sub/ppermute | solution.py:32
  32.3 9.6 %collective-permute-start.13 = (bf16[72,896]{1,0:T(8,128)(2,1)S(1)}, bf16[72,896]{1,0:T(8,128)(2,1)S(1)}, u32[]{:S(2)}, u32[]{:S(2)}) collective-permute-start(bf16[72,896]{1,0:T(8,128)(2,1)S(1)} %add_convert_fusion.1.earlier_ref), channel_id=1, source_target_pairs={{0,12},{4,8},{8,4},{12,0},{1,13},{5,9},{9,5},{13,1},{2,14},{6,10},... | collective-permute-start | bytes 387080 | tf_op jit(solution)/shard_map/back3_ep/ppermute | solution.py:32
  34.9 5.0 %collective-permute-start.11 = (bf16[72,896]{1,0:T(8,128)(2,1)S(1)}, bf16[72,896]{1,0:T(8,128)(2,1)S(1)}, u32[]{:S(2)}, u32[]{:S(2)}) collective-permute-start(bf16[72,896]{1,0:T(8,128)(2,1)S(1)} %get-tuple-element.53), channel_id=1, source_target_pairs={{0,2},{2,0},{1,3},{3,1},{4,6},{6,4},{5,7},{7,5},{8,10},{10,8},{9,1... | collective-permute-start | bytes 387080 | tf_op jit(solution)/shard_map/back2_tp/ppermute | solution.py:32
  35.8 8.4 %collective-permute-start.14 = (bf16[72,896]{1,0:T(8,128)(2,1)S(1)}, bf16[72,896]{1,0:T(8,128)(2,1)S(1)}, u32[]{:S(2)}, u32[]{:S(2)}) collective-permute-start(bf16[72,896]{1,0:T(8,128)(2,1)S(1)} %after.15), channel_id=1, source_target_pairs={{0,4},{4,0},{8,12},{12,8},{1,5},{5,1},{9,13},{13,9},{2,6},{6,2},{1... | collective-permute-start | bytes 387080 | tf_op jit(solution)/shard_map/back1_ep/ppermute | solution.py:32
  35.8 11.1 %collective-permute-start.15 = (bf16[72,896]{1,0:T(8,128)(2,1)S(1)}, bf16[72,896]{1,0:T(8,128)(2,1)S(1)}, u32[]{:S(2)}, u32[]{:S(2)}) collective-permute-start(bf16[72,896]{1,0:T(8,128)(2,1)S(1)} %after.16), channel_id=1, source_target_pairs={{0,6},{2,4},{4,2},{6,0},{8,14},{10,12},{12,10},{14,8},{1,7},{3,5},... | collective-permute-start | bytes 387080 | tf_op jit(solution)/shard_map/back1_ep_tp/ppermute | solution.py:32
  40.0 8.1 %collective-permute-start.12 = (bf16[72,896]{1,0:T(8,128)(2,1)S(1)}, bf16[72,896]{1,0:T(8,128)(2,1)S(1)}, u32[]{:S(2)}, u32[]{:S(2)}) collective-permute-start(bf16[72,896]{1,0:T(8,128)(2,1)S(1)} %add_convert_fusion.earlier_ref), channel_id=1, source_target_pairs={{0,8},{4,12},{8,0},{12,4},{1,9},{5,13},{9,1},{13,5},{2,10},{6,14},... | collective-permute-start | bytes 387080 | tf_op jit(solution)/shard_map/back2_ep/ppermute | solution.py:32
  40.6 6.8 %collective-permute-start.16 = (bf16[72,896]{1,0:T(8,128)(2,1)S(1)}, bf16[72,896]{1,0:T(8,128)(2,1)S(1)}, u32[]{:S(2)}, u32[]{:S(2)}) collective-permute-start(bf16[72,896]{1,0:T(8,128)(2,1)S(1)} %after.17), channel_id=1, source_target_pairs={{0,2},{2,0},{1,3},{3,1},{4,6},{6,4},{5,7},{7,5},{8,10},{10,8},{9,1... | collective-permute-start | bytes 387080 | tf_op jit(solution)/shard_map/back0_tp/ppermute | solution.py:32

commit v12 on v11

--- a/solution.py
+++ b/solution.py
@@ -132,18 +132,32 @@
         fill(block_ref, most, low, high, weights_ref, scales_ref, grad_ref)
 
 
+def shares_of(tokens, columns, width):
+    across = width // columns
+    deep = -(-tokens // across // 16) * 16
+    return deep, [(at, i * columns) for i, at in enumerate(range(0, tokens, deep))]
+
+
 def pack_more_kernel(most, order, place_ref, weights_ref, scales_ref, grad_ref, partial_ref, *refs):
-    blocks, (share_ref, sems) = refs[:-2], refs[-2:]
-    lane, count = lax.axis_index("tp"), partial_ref.shape[0]
-    shares = fetch(
-        [partial_ref.at[lane ^ j] for j in range(count)],
-        [share_ref.at[j] for j in range(count)],
-        sems,
-    )
+    count, tokens, columns = partial_ref.shape
+    blocks, crossing = refs[: len(order)], refs[len(order) : len(order) + count - 1]
+    own_ref, sems = refs[-2:]
+    lane, rows = lax.axis_index("tp"), blocks[0].shape[0]
+    deep, parts = shares_of(tokens, columns, blocks[0].shape[1])
+    sources, targets = [partial_ref.at[lane]], [own_ref]
+    for j in range(1, count):
+        for at, column in parts:
+            size = min(deep, tokens - at)
+            sources.append(partial_ref.at[lane ^ j, pl.ds(at, size)])
+            targets.append(crossing[j - 1].at[pl.ds(0, size), pl.ds(column, columns)])
+    copies = fetch(sources, targets, sems)
     for block_ref, k in zip(blocks, order):
         low, high = place_ref[0, k] != 0, place_ref[1, k] != 0
         fill(block_ref, most, low, high, weights_ref, scales_ref, grad_ref)
-    for copy in shares:
+        if k == 0:
+            for both_ref in crossing:
+                both_ref[deep:, :] = block_ref[...]
+    for copy in copies:
         copy.wait()
 
 
@@ -177,7 +191,7 @@
         copy.wait()
 
 
-def hidden_kernel(most, extra, *refs):
+def hidden_kernel(most, extra, skips, *refs):
     blocks, (down_ref, sum_ref, sent_ref) = refs[:-3], refs[-3:]
     half = down_ref.shape[1] // 2
     count = sum_ref.shape[0]
@@ -188,7 +202,7 @@
         tail = jnp.concatenate([high, row_sums - high, spare], axis=0)
         sent_ref[count:, :] = jnp.zeros((EXTRA, sent_ref.shape[1]), jnp.bfloat16)
         sent_ref[count:, : row_sums.shape[1]] = tail.astype(jnp.bfloat16)
-    values = [b[...].astype(jnp.float32) for b in blocks]
+    values = [b[skip:, :].astype(jnp.float32) for b, skip in zip(blocks, skips)]
     low = jnp.concatenate([v[:most] for v in values], axis=0).astype(jnp.bfloat16)
     high = jnp.concatenate([v[most : 2 * most] for v in values], axis=0).astype(jnp.bfloat16)
     total = dot(low, down_ref[:, :half], NT) + dot(high, down_ref[:, half:], NT)
@@ -233,10 +247,10 @@
 
 
 def groups_of(wide):
+    left = list(range(wide - 1, -1, -1))
     if wide < 4:
-        return [list(range(wide - 1, -1, -1))]
-    left = list(range(wide - 2, 1, -1))
-    return [[wide - 1, 1, 0]] + [left[i : i + 2] for i in range(0, len(left), 2)]
+        return [left]
+    return [[left[0], 0]] + [left[i : min(i + 2, wide - 1)] for i in range(1, wide - 1, 2)]
 
 
 def local(
@@ -282,27 +296,33 @@
         scratch=[pltpu.VMEM((1, tokens), jnp.int32), pltpu.SemaphoreType.DMA((4,))],
         name="pack",
     )
-    *packed, shares = call(
+    deep, parts = shares_of(tokens, latent.shape[1], half)
+    more = call(
         functools.partial(pack_more_kernel, most, order[1:]),
-        [block] * (wide - 1) + [like(partials)],
+        [block] * (wide - 1)
+        + [pltpu.VMEM((deep + rows, half), bf16)] * (narrow - 1)
+        + [pltpu.VMEM(latent.shape, bf16)],
         place,
         *fillers,
         *pinned(partials),
         specs=[VMEM] * 4 + [HBM],
-        scratch=[pltpu.SemaphoreType.DMA((narrow,))],
+        scratch=[pltpu.SemaphoreType.DMA((1 + (narrow - 1) * len(parts),))],
         name="pack_more",
     )
-    packed = dict(zip(order, [leading] + packed))
+    packed = dict(zip(order, [leading, *more]))
 
     first, staged = groups[0][0], len(groups) > 1
-    taken = {0: [packed[0]] + [swap(packed[0], "rows0", tp=j) for j in range(1, narrow)]}
+    both = [swap(more[wide - 2 + j], "rows0", tp=j) for j in range(1, narrow)]
+    if staged and narrow > 1:
+        both[-1] = after(both[-1], place, 1 << 27)
+    taken = {0: [packed[0]] + both}
     arrived = {}
     for k in order:
         if k:
-            given = packed[k] if k in groups[0] else after(packed[k], arrived[first])
+            given = packed[k] if k in (first, 1) else after(packed[k], arrived[first])
             arrived[k] = swap(given, f"rows{k}", ep=k)
             if staged and k == groups[1][0]:
-                arrived[k] = after(arrived[k], packed[first], 1 << 31)
+                arrived[k] = after(arrived[k], packed[first], 1 << 28)
     fetched = [
         pre_acts.reshape(2, wide, narrow * most, hidden_width),
         w_down[0],
@@ -321,25 +341,16 @@
         earlier=[arrived[first]],
         name="fetch",
     )
-    latent_parts = [shares[0]] + [
-        swap(shares[j], "latent", tp=j) for j in range(1, narrow)
-    ]
-
-    def straight(k, mine, others):
-        return [swap(mine, f"back{k}", ep=k)] + [
-            swap(other, f"back{k}", ep=k, tp=j + 1) for j, other in enumerate(others)
-        ]
-
-    returned, waiting = {}, []
+    returned = {}
     values = latent.astype(f32)
     received, products, moved = None, None, None
     for group in groups:
         for k in group:
-            if staged and k == 1:
-                crossing = [swap(packed[k], f"rows{k}", ep=k, tp=j) for j in range(1, narrow)]
-            elif k:
-                if products:
+            if k:
+                if products and k == group[0]:
                     arrived[k] = after(arrived[k], summed)
+                if products and k == 1:
+                    arrived[k] = after(arrived[k], down)
                 crossing = [swap(arrived[k], f"rows{k}", tp=j) for j in range(1, narrow)]
                 if products:
                     crossing[-1] = after(crossing[-1], products[0])
@@ -348,15 +359,21 @@
         count = len(group) * narrow * most
         extra = group is groups[-1]
         if extra:
-            if received is not None:
-                latent_parts[-1] = after(latent_parts[-1], summed, 1 << 30)
-            own_grad = sum(part.astype(f32) for part in latent_parts)
+            if staged:
+                both[-1] = after(both[-1], summed)
+            own_grad = more[-1].astype(f32)
+            for value in both:
+                pieces = [
+                    value[: min(deep, tokens - at), column : column + latent.shape[1]]
+                    for at, column in parts
+                ]
+                own_grad += jnp.concatenate(pieces, axis=0).astype(f32)
             gained = own_grad * latent_gain
             row_sums = jnp.stack(
                 [jnp.sum(values * values, axis=1), jnp.sum(gained * values, axis=1)]
             )
         summed, sent = call(
-            functools.partial(hidden_kernel, most, extra),
+            functools.partial(hidden_kernel, most, extra, [0 if j == 0 or k else deep for k in group for j in range(narrow)]),
             [
                 pltpu.VMEM((count, hidden_width), f32),
                 pltpu.VMEM((count + (EXTRA if extra else 0), hidden_width), bf16),
@@ -385,8 +402,6 @@
             mine, others = products[at * narrow], products[at * narrow + 1 : (at + 1) * narrow]
             if k == 0:
                 kept = mine, others
-            elif staged and k == 1:
-                waiting.append((k, mine, others))
             else:
                 total = mine.astype(f32)
                 for j, other in enumerate(others):
@@ -395,8 +410,6 @@
                 returned[k] = [swap(total, f"back{k}", ep=k)]
                 if k == group[0]:
                     moved = total
-    for k, mine, others in waiting:
-        returned[k] = straight(k, after(mine, products[0]), [after(other, products[0]) for other in others])
     mine, others = kept
     returned[0] = [mine] + [
         swap(after(other, moved) if staged else other, "back0", tp=j + 1)

time: 49.3 us -> 49.7 us (level)
  starting transfers between devices: 19.7 us -> 21.6 us
  waiting for transfers between devices: 15.8 us -> 14.8 us
  Pallas kernels: 11.8 us -> 11.2 us
    ppermute x17 -> x16, starting transfers between devices: 19.7 us -> 21.6 us  [swap(): return lax.ppermute(value, tuple(steps), pairs)]
    ppermute x17 -> x16, waiting for transfers between devices: 15.8 us -> 14.8 us  [swap(): return lax.ppermute(value, tuple(steps), pairs)]
    pallas_call x9, Pallas kernels: 11.8 us -> 11.2 us  [call(): pl.pallas_call(kernel, out_shape=outs, in_specs=specs, out_specs=[VMEM] *...]
  transfers between devices with their start and end apart: 17 -> 16, of which waited for: 11 -> 9; matrix products, arithmetic and copies ran while one was open for 2% -> 2% of each run, Pallas kernels for 19% -> 17%
where the time goes in v12:
time: 49.7 us; the launch traced here: 49.5 us
  starting transfers between devices  21.6 us (43%)
  waiting for transfers between devices  14.8 us (30%)
  Pallas kernels  11.2 us (23%)
  other arithmetic  1 us (2%)
  between operations  0.79 us (2%)
    ppermute x16, starting transfers between devices, swap(): return lax.ppermute(value, tuple(steps), pairs)  21.6 us
    ppermute x16, waiting for transfers between devices, swap(): return lax.ppermute(value, tuple(steps), pairs)  14.8 us
    pallas_call x9, Pallas kernels, call(): pl.pallas_call(kernel, out_shape=outs, in_specs=specs, out_specs=[VMEM] *...  11.2 us
  transfers between devices with their start and end apart: 16, of which 9 were waited for; matrix products, arithmetic and copies ran while one was open for 2% of the time, Pallas kernels for 17%

profile of v12, /device:TPU:0, one launch (start us, length us, event | category | flops | bytes accessed | tf_op | source)
XLA Modules:
  0.0 49.5 jit_solution(10397809607178001381)
XLA Ops:
  0.6 1.6 %pack.1 = (bf16[72,896]{1,0:T(8,128)(2,1)S(1)}, bf16[2,4,72,128]{3,2,1,0:T(8,128)(2,1)S(1)}, f32[1,128]{1,0:T(1,128)S(1)}, f32[14,128]{1,0:T(8,128)S(1)}, bf16[128,1792]{1,0:T(8,128)(2,1)S(1)}) custom-call(s32[1,128]{1,0:T(1,128)} %bitcast.30, f32[1,128]{1,0:T(1,128)} %bitcast.31, f32[14,128]{1,0:T(8,128)} %bitcast.24, bf16[128,1792]{1,0:T(8,128)(2,1)} %refs_3_.1), custom_call_target="tpu_custom_call" | custom-call | tf_op jit(solution)/shard_map/pack/pallas_call | solution.py:51
  2.2 5.1 %collective-permute-start = (bf16[72,896]{1,0:T(8,128)(2,1)S(1)}, bf16[72,896]{1,0:T(8,128)(2,1)S(1)}, u32[]{:S(2)}, u32[]{:S(2)}) collective-permute-start(bf16[72,896]{1,0:T(8,128)(2,1)S(1)} %get-tuple-element.36.earlier_ref), channel_id=1, source_target_pairs={{0,12},{4,8},{8,4},{12,0},{1,13},{5,9},{9,5},{13,1},{2,14},{6,10},... | collective-permute-start | bytes 387080 | tf_op jit(solution)/shard_map/rows3_ep/ppermute | solution.py:32
  7.4 1.1 %pack_more.1 = (bf16[72,896]{1,0:T(8,128)(2,1)S(1)}, bf16[72,896]{1,0:T(8,128)(2,1)S(1)}, bf16[72,896]{1,0:T(8,128)(2,1)S(1)}, bf16[120,896]{1,0:T(8,128)(2,1)S(1)}, bf16[128,256]{1,0:T(8,128)(2,1)S(1)}) custom-call(bf16[2,4,72,128]{3,2,1,0:T(8,128)(2,1)S(1)} %get-tuple-element.31.place_ref.earlier_ref, f32[1,128]{1,0:T(1,128)S(1)} %get-tuple-element.32.weights_ref, ...), custom_call_target="tpu_custom_call" | custom-call | tf_op jit(solution)/shard_map/pack_more/pallas_call | solution.py:51
  8.5 1.6 %collective-permute-start.3 = (bf16[120,896]{1,0:T(8,128)(2,1)S(1)}, bf16[120,896]{1,0:T(8,128)(2,1)S(1)}, u32[]{:S(2)}, u32[]{:S(2)}) collective-permute-start(bf16[120,896]{1,0:T(8,128)(2,1)S(1)} %get-tuple-element.38), channel_id=1, source_target_pairs={{0,2},{2,0},{1,3},{3,1},{4,6},{6,4},{5,7},{7,5},{8,10},{10,8},{9,1... | collective-permute-start | bytes 645128 | tf_op jit(solution)/shard_map/rows0_tp/ppermute | solution.py:32
  10.0 0.9 %collective-permute-done.earlier_ref.refs_6_.refs_0_ = bf16[72,896]{1,0:T(8,128)(2,1)S(1)} collective-permute-done((bf16[72,896]{1,0:T(8,128)(2,1)S(1)}, bf16[72,896]{1,0:T(8,128)(2,1)S(1)}, u32[]{:S(2)}, u32[]{:S(2)}) %collective-permute-start) | collective-permute-done | bytes 129056 | tf_op jit(solution)/shard_map/rows3_ep/ppermute | solution.py:32
  10.9 2.5 %collective-permute-start.2 = (bf16[72,896]{1,0:T(8,128)(2,1)S(1)}, bf16[72,896]{1,0:T(8,128)(2,1)S(1)}, u32[]{:S(2)}, u32[]{:S(2)}) collective-permute-start(bf16[72,896]{1,0:T(8,128)(2,1)S(1)} %collective-permute-done.earlier_ref.refs_6_.refs_0_), channel_id=1, source_target_pairs={{0,2},{2,0},{1,3},{3,1},{4,6},{6,4},{5,7},{7,5},{8,10},{10,8},{9,1... | collective-permute-start | bytes 387080 | tf_op jit(solution)/shard_map/rows3_tp/ppermute | solution.py:32
  13.4 2.1 %collective-permute-start.1 = (bf16[72,896]{1,0:T(8,128)(2,1)S(1)}, bf16[72,896]{1,0:T(8,128)(2,1)S(1)}, u32[]{:S(2)}, u32[]{:S(2)}) collective-permute-start(bf16[72,896]{1,0:T(8,128)(2,1)S(1)} %after.10), channel_id=1, source_target_pairs={{0,8},{4,12},{8,0},{12,4},{1,9},{5,13},{9,1},{13,5},{2,10},{6,14},... | collective-permute-start | bytes 387080 | tf_op jit(solution)/shard_map/rows2_ep/ppermute | solution.py:32
  15.5 2.9 %fetch.1 = (f32[4,72,512]{2,1,0:T(8,128)S(1)}, f32[4,72,512]{2,1,0:T(8,128)S(1)}, bf16[512,1792]{1,0:T(8,128)(2,1)S(1)}, bf16[1792,512]{1,0:T(8,128)(2,1)S(1)}, ...) custom-call(bf16[2,4,72,512]{3,2,1,0:T(8,128)(2,1)} %bitcast.22, ...), custom_call_target="tpu_custom_call" | custom-call | tf_op jit(solution)/shard_map/fetch/pallas_call | solution.py:51
  18.4 0.9 %collective-permute-start.7 = (bf16[72,896]{1,0:T(8,128)(2,1)S(1)}, bf16[72,896]{1,0:T(8,128)(2,1)S(1)}, u32[]{:S(2)}, u32[]{:S(2)}) collective-permute-start(bf16[72,896]{1,0:T(8,128)(2,1)S(1)} %after.15.refs_2_), channel_id=1, source_target_pairs={{0,2},{2,0},{1,3},{3,1},{4,6},{6,4},{5,7},{7,5},{8,10},{10,8},{9,1... | collective-permute-start | bytes 387080 | tf_op jit(solution)/shard_map/rows1_tp/ppermute | solution.py:32
  20.6 0.8 %collective-permute-start.4 = (bf16[72,896]{1,0:T(8,128)(2,1)S(1)}, bf16[72,896]{1,0:T(8,128)(2,1)S(1)}, u32[]{:S(2)}, u32[]{:S(2)}) collective-permute-start(bf16[72,896]{1,0:T(8,128)(2,1)S(1)} %after.13.refs_0_), channel_id=1, source_target_pairs={{0,2},{2,0},{1,3},{3,1},{4,6},{6,4},{5,7},{7,5},{8,10},{10,8},{9,1... | collective-permute-start | bytes 387080 | tf_op jit(solution)/shard_map/rows2_tp/ppermute | solution.py:32
  21.5 1.4 %collective-permute-done.5.other_ref = bf16[144,512]{1,0:T(8,128)(2,1)S(1)} collective-permute-done((bf16[144,512]{1,0:T(8,128)(2,1)S(1)}, bf16[144,512]{1,0:T(8,128)(2,1)S(1)}, u32[]{:S(2)}, u32[]{:S(2)}) %collective-permute-start.5) | collective-permute-done | bytes 147488 | tf_op jit(solution)/shard_map/hidden3_sub/ppermute | solution.py:32
  22.9 1.3 %back.2 = (bf16[72,896]{1,0:T(8,128)(2,1)S(1)}, bf16[72,896]{1,0:T(8,128)(2,1)S(1)}, bf16[72,896]{1,0:T(8,128)(2,1)S(1)}, bf16[72,896]{1,0:T(8,128)(2,1)S(1)}) custom-call(f32[144,512]{1,0:T(8,128)S(1)} %get-tuple-element.40.earlier_ref.sum_ref, bf16[144,512]{1,0:T(8,128)(2,1)S(1)} %collective-permute-done.5.other_ref, ...), custom_call_target="tpu_custom_call" | custom-call | tf_op jit(solution)/shard_map/back/pallas_call | solution.py:51
  24.1 1.3 %collective-permute-start.9 = (bf16[72,896]{1,0:T(8,128)(2,1)S(1)}, bf16[72,896]{1,0:T(8,128)(2,1)S(1)}, u32[]{:S(2)}, u32[]{:S(2)}) collective-permute-start(bf16[72,896]{1,0:T(8,128)(2,1)S(1)} %get-tuple-element.53), channel_id=1, source_target_pairs={{0,2},{2,0},{1,3},{3,1},{4,6},{6,4},{5,7},{7,5},{8,10},{10,8},{9,1... | collective-permute-start | bytes 387080 | tf_op jit(solution)/shard_map/back3_tp/ppermute | solution.py:32
  26.4 3.3 %collective-permute-done.9 = bf16[72,896]{1,0:T(8,128)(2,1)S(1)} collective-permute-done((bf16[72,896]{1,0:T(8,128)(2,1)S(1)}, bf16[72,896]{1,0:T(8,128)(2,1)S(1)}, u32[]{:S(2)}, u32[]{:S(2)}) %collective-permute-start.9) | collective-permute-done | bytes 129056 | tf_op jit(solution)/shard_map/back3_tp/ppermute | solution.py:32
  29.7 2.8 %collective-permute-start.12 = (bf16[72,896]{1,0:T(8,128)(2,1)S(1)}, bf16[72,896]{1,0:T(8,128)(2,1)S(1)}, u32[]{:S(2)}, u32[]{:S(2)}) collective-permute-start(bf16[72,896]{1,0:T(8,128)(2,1)S(1)} %add_convert_fusion.2.earlier_ref), channel_id=1, source_target_pairs={{0,12},{4,8},{8,4},{12,0},{1,13},{5,9},{9,5},{13,1},{2,14},{6,10},... | collective-permute-start | bytes 387080 | tf_op jit(solution)/shard_map/back3_ep/ppermute | solution.py:32
  32.5 1.3 %back.3 = (bf16[72,896]{1,0:T(8,128)(2,1)S(1)}, bf16[72,896]{1,0:T(8,128)(2,1)S(1)}, bf16[72,896]{1,0:T(8,128)(2,1)S(1)}, bf16[72,896]{1,0:T(8,128)(2,1)S(1)}) custom-call(f32[144,512]{1,0:T(8,128)S(1)} %get-tuple-element.51.sum_ref, bf16[160,512]{1,0:T(8,128)(2,1)S(1)} %after.18.other_ref, f32[4,72,512]{2,1,0:T(8,128)S(1)} %get-tuple-element.42.up_by_ref, ...), custom_call_target="tpu_custom_call" | custom-call | tf_op jit(solution)/shard_map/back/pallas_call | solution.py:51
  33.8 1.5 %collective-permute-start.10 = (bf16[72,896]{1,0:T(8,128)(2,1)S(1)}, bf16[72,896]{1,0:T(8,128)(2,1)S(1)}, u32[]{:S(2)}, u32[]{:S(2)}) collective-permute-start(bf16[72,896]{1,0:T(8,128)(2,1)S(1)} %get-tuple-element.55), channel_id=1, source_target_pairs={{0,2},{2,0},{1,3},{3,1},{4,6},{6,4},{5,7},{7,5},{8,10},{10,8},{9,1... | collective-permute-start | bytes 387080 | tf_op jit(solution)/shard_map/back2_tp/ppermute | solution.py:32
  35.9 3.7 %collective-permute-done.10 = bf16[72,896]{1,0:T(8,128)(2,1)S(1)} collective-permute-done((bf16[72,896]{1,0:T(8,128)(2,1)S(1)}, bf16[72,896]{1,0:T(8,128)(2,1)S(1)}, u32[]{:S(2)}, u32[]{:S(2)}) %collective-permute-start.10) | collective-permute-done | bytes 129056 | tf_op jit(solution)/shard_map/back2_tp/ppermute | solution.py:32
  40.4 0.9 %collective-permute-start.13 = (bf16[72,896]{1,0:T(8,128)(2,1)S(1)}, bf16[72,896]{1,0:T(8,128)(2,1)S(1)}, u32[]{:S(2)}, u32[]{:S(2)}) collective-permute-start(bf16[72,896]{1,0:T(8,128)(2,1)S(1)} %after.19), channel_id=1, source_target_pairs={{0,2},{2,0},{1,3},{3,1},{4,6},{6,4},{5,7},{7,5},{8,10},{10,8},{9,1... | collective-permute-start | bytes 387080 | tf_op jit(solution)/shard_map/back0_tp/ppermute | solution.py:32
  42.0 0.8 %collective-permute-start.15 = (bf16[72,896]{1,0:T(8,128)(2,1)S(1)}, bf16[72,896]{1,0:T(8,128)(2,1)S(1)}, u32[]{:S(2)}, u32[]{:S(2)}) collective-permute-start(bf16[72,896]{1,0:T(8,128)(2,1)S(1)} %add_convert_fusion), channel_id=1, source_target_pairs={{0,4},{4,0},{8,12},{12,8},{1,5},{5,1},{9,13},{13,9},{2,6},{6,2},{1... | collective-permute-start | bytes 387080 | tf_op jit(solution)/shard_map/back1_ep/ppermute | solution.py:32
  42.8 0.7 %fusion.5 = bf16[128,256]{1,0:T(8,128)(2,1)} fusion(bf16[128,256]{1,0:T(8,128)(2,1)S(1)} %get-tuple-element.48, bf16[128,256]{1,0:T(8,128)(2,1)S(1)} %get-tuple-element.49, f32[128]{0:T(128)S(1)} %slice_bitcast_fusion, f32[128]{0:T(128)S(1)} %get-tuple-element.62, f32[128]{0:T(128)S(1)} %get-tuple-element.63, f32[256]{0:T(256)S(1)} %bitcast.18, ...), kind=kLoop, calls=%fused_computation.11 | loop fusion | flops 524288 | bytes 264704 | tf_op jit(solution)/shard_map/convert_element_type | solution.py:423
  43.5 1.9 %collective-permute-done.13.refs_2_ = bf16[72,896]{1,0:T(8,128)(2,1)S(1)} collective-permute-done((bf16[72,896]{1,0:T(8,128)(2,1)S(1)}, bf16[72,896]{1,0:T(8,128)(2,1)S(1)}, u32[]{:S(2)}, u32[]{:S(2)}) %collective-permute-start.13) | collective-permute-done | bytes 129056 | tf_op jit(solution)/shard_map/back0_tp/ppermute | solution.py:32
  45.4 2.4 %collective-permute-done.15.refs_3_ = bf16[72,896]{1,0:T(8,128)(2,1)S(1)} collective-permute-done((bf16[72,896]{1,0:T(8,128)(2,1)S(1)}, bf16[72,896]{1,0:T(8,128)(2,1)S(1)}, u32[]{:S(2)}, u32[]{:S(2)}) %collective-permute-start.15) | collective-permute-done | bytes 129056 | tf_op jit(solution)/shard_map/back1_ep/ppermute | solution.py:32
  48.4 1.1 %unpack_latest.1 = bf16[128,1792]{1,0:T(8,128)(2,1)} custom-call(bf16[2,4,72,128]{3,2,1,0:T(8,128)(2,1)S(1)} %get-tuple-element.31.place_ref.earlier_ref, bf16[72,896]{1,0:T(8,128)(2,1)S(1)} %collective-permute-done.11.refs_0_, bf16[128,1792]{1,0:T(8,128)(2,1)S(1)} %unpack.1.refs_1_), custom_call_target="tpu_custom_call" | custom-call | tf_op jit(solution)/shard_map/unpack_latest/pallas_call | solution.py:51
  (39 shorter events, 5.0 us)
Async XLA Ops:
  2.2 8.7 %collective-permute-start = (bf16[72,896]{1,0:T(8,128)(2,1)S(1)}, bf16[72,896]{1,0:T(8,128)(2,1)S(1)}, u32[]{:S(2)}, u32[]{:S(2)}) collective-permute-start(bf16[72,896]{1,0:T(8,128)(2,1)S(1)} %get-tuple-element.36.earlier_ref), channel_id=1, source_target_pairs={{0,12},{4,8},{8,4},{12,0},{1,13},{5,9},{9,5},{13,1},{2,14},{6,10},... | collective-permute-start | bytes 387080 | tf_op jit(solution)/shard_map/rows3_ep/ppermute | solution.py:32
  8.5 10.8 %collective-permute-start.3 = (bf16[120,896]{1,0:T(8,128)(2,1)S(1)}, bf16[120,896]{1,0:T(8,128)(2,1)S(1)}, u32[]{:S(2)}, u32[]{:S(2)}) collective-permute-start(bf16[120,896]{1,0:T(8,128)(2,1)S(1)} %get-tuple-element.38), channel_id=1, source_target_pairs={{0,2},{2,0},{1,3},{3,1},{4,6},{6,4},{5,7},{7,5},{8,10},{10,8},{9,1... | collective-permute-start | bytes 645128 | tf_op jit(solution)/shard_map/rows0_tp/ppermute | solution.py:32
  10.0 8.3 %collective-permute-start.6 = (bf16[72,896]{1,0:T(8,128)(2,1)S(1)}, bf16[72,896]{1,0:T(8,128)(2,1)S(1)}, u32[]{:S(2)}, u32[]{:S(2)}) collective-permute-start(bf16[72,896]{1,0:T(8,128)(2,1)S(1)} %get-tuple-element.47), channel_id=1, source_target_pairs={{0,4},{4,0},{8,12},{12,8},{1,5},{5,1},{9,13},{13,9},{2,6},{6,2},{1... | collective-permute-start | bytes 387080 | tf_op jit(solution)/shard_map/rows1_ep/ppermute | solution.py:32
  10.9 8.4 %collective-permute-start.2 = (bf16[72,896]{1,0:T(8,128)(2,1)S(1)}, bf16[72,896]{1,0:T(8,128)(2,1)S(1)}, u32[]{:S(2)}, u32[]{:S(2)}) collective-permute-start(bf16[72,896]{1,0:T(8,128)(2,1)S(1)} %collective-permute-done.earlier_ref.refs_6_.refs_0_), channel_id=1, source_target_pairs={{0,2},{2,0},{1,3},{3,1},{4,6},{6,4},{5,7},{7,5},{8,10},{10,8},{9,1... | collective-permute-start | bytes 387080 | tf_op jit(solution)/shard_map/rows3_tp/ppermute | solution.py:32
  13.4 7.2 %collective-permute-start.1 = (bf16[72,896]{1,0:T(8,128)(2,1)S(1)}, bf16[72,896]{1,0:T(8,128)(2,1)S(1)}, u32[]{:S(2)}, u32[]{:S(2)}) collective-permute-start(bf16[72,896]{1,0:T(8,128)(2,1)S(1)} %after.10), channel_id=1, source_target_pairs={{0,8},{4,12},{8,0},{12,4},{1,9},{5,13},{9,1},{13,5},{2,10},{6,14},... | collective-permute-start | bytes 387080 | tf_op jit(solution)/shard_map/rows2_ep/ppermute | solution.py:32
  18.4 7.1 %collective-permute-start.7 = (bf16[72,896]{1,0:T(8,128)(2,1)S(1)}, bf16[72,896]{1,0:T(8,128)(2,1)S(1)}, u32[]{:S(2)}, u32[]{:S(2)}) collective-permute-start(bf16[72,896]{1,0:T(8,128)(2,1)S(1)} %after.15.refs_2_), channel_id=1, source_target_pairs={{0,2},{2,0},{1,3},{3,1},{4,6},{6,4},{5,7},{7,5},{8,10},{10,8},{9,1... | collective-permute-start | bytes 387080 | tf_op jit(solution)/shard_map/rows1_tp/ppermute | solution.py:32
  20.6 4.9 %collective-permute-start.4 = (bf16[72,896]{1,0:T(8,128)(2,1)S(1)}, bf16[72,896]{1,0:T(8,128)(2,1)S(1)}, u32[]{:S(2)}, u32[]{:S(2)}) collective-permute-start(bf16[72,896]{1,0:T(8,128)(2,1)S(1)} %after.13.refs_0_), channel_id=1, source_target_pairs={{0,2},{2,0},{1,3},{3,1},{4,6},{6,4},{5,7},{7,5},{8,10},{10,8},{9,1... | collective-permute-start | bytes 387080 | tf_op jit(solution)/shard_map/rows2_tp/ppermute | solution.py:32
  21.5 1.4 %collective-permute-start.5 = (bf16[144,512]{1,0:T(8,128)(2,1)S(1)}, bf16[144,512]{1,0:T(8,128)(2,1)S(1)}, u32[]{:S(2)}, u32[]{:S(2)}) collective-permute-start(bf16[144,512]{1,0:T(8,128)(2,1)S(1)} %get-tuple-element.41), channel_id=1, source_target_pairs={{0,1},{1,0},{2,3},{3,2},{4,5},{5,4},{6,7},{7,6},{8,9},{9,8},{10,11... | collective-permute-start | bytes 442376 | tf_op jit(solution)/shard_map/hidden3_sub/ppermute | solution.py:32
  24.1 5.6 %collective-permute-start.9 = (bf16[72,896]{1,0:T(8,128)(2,1)S(1)}, bf16[72,896]{1,0:T(8,128)(2,1)S(1)}, u32[]{:S(2)}, u32[]{:S(2)}) collective-permute-start(bf16[72,896]{1,0:T(8,128)(2,1)S(1)} %get-tuple-element.53), channel_id=1, source_target_pairs={{0,2},{2,0},{1,3},{3,1},{4,6},{6,4},{5,7},{7,5},{8,10},{10,8},{9,1... | collective-permute-start | bytes 387080 | tf_op jit(solution)/shard_map/back3_tp/ppermute | solution.py:32
  26.3 6.2 %collective-permute-start.8 = (bf16[160,512]{1,0:T(8,128)(2,1)S(1)}, bf16[160,512]{1,0:T(8,128)(2,1)S(1)}, u32[]{:S(2)}, u32[]{:S(2)}) collective-permute-start(bf16[160,512]{1,0:T(8,128)(2,1)S(1)} %get-tuple-element.52), channel_id=1, source_target_pairs={{0,1},{1,0},{2,3},{3,2},{4,5},{5,4},{6,7},{7,6},{8,9},{9,8},{10,11... | collective-permute-start | bytes 491528 | tf_op jit(solution)/shard_map/hidden2_sub/ppermute | solution.py:32
  29.7 13.8 %collective-permute-start.12 = (bf16[72,896]{1,0:T(8,128)(2,1)S(1)}, bf16[72,896]{1,0:T(8,128)(2,1)S(1)}, u32[]{:S(2)}, u32[]{:S(2)}) collective-permute-start(bf16[72,896]{1,0:T(8,128)(2,1)S(1)} %add_convert_fusion.2.earlier_ref), channel_id=1, source_target_pairs={{0,12},{4,8},{8,4},{12,0},{1,13},{5,9},{9,5},{13,1},{2,14},{6,10},... | collective-permute-start | bytes 387080 | tf_op jit(solution)/shard_map/back3_ep/ppermute | solution.py:32
  33.8 5.8 %collective-permute-start.10 = (bf16[72,896]{1,0:T(8,128)(2,1)S(1)}, bf16[72,896]{1,0:T(8,128)(2,1)S(1)}, u32[]{:S(2)}, u32[]{:S(2)}) collective-permute-start(bf16[72,896]{1,0:T(8,128)(2,1)S(1)} %get-tuple-element.55), channel_id=1, source_target_pairs={{0,2},{2,0},{1,3},{3,1},{4,6},{6,4},{5,7},{7,5},{8,10},{10,8},{9,1... | collective-permute-start | bytes 387080 | tf_op jit(solution)/shard_map/back2_tp/ppermute | solution.py:32
  35.3 6.6 %collective-permute-start.14 = (bf16[72,896]{1,0:T(8,128)(2,1)S(1)}, bf16[72,896]{1,0:T(8,128)(2,1)S(1)}, u32[]{:S(2)}, u32[]{:S(2)}) collective-permute-start(bf16[72,896]{1,0:T(8,128)(2,1)S(1)} %get-tuple-element.59), channel_id=1, source_target_pairs={{0,2},{2,0},{1,3},{3,1},{4,6},{6,4},{5,7},{7,5},{8,10},{10,8},{9,1... | collective-permute-start | bytes 387080 | tf_op jit(solution)/shard_map/back1_tp/ppermute | solution.py:32
  39.7 8.7 %collective-permute-start.11 = (bf16[72,896]{1,0:T(8,128)(2,1)S(1)}, bf16[72,896]{1,0:T(8,128)(2,1)S(1)}, u32[]{:S(2)}, u32[]{:S(2)}) collective-permute-start(bf16[72,896]{1,0:T(8,128)(2,1)S(1)} %add_convert_fusion.1.earlier_ref), channel_id=1, source_target_pairs={{0,8},{4,12},{8,0},{12,4},{1,9},{5,13},{9,1},{13,5},{2,10},{6,14},... | collective-permute-start | bytes 387080 | tf_op jit(solution)/shard_map/back2_ep/ppermute | solution.py:32
  40.4 4.9 %collective-permute-start.13 = (bf16[72,896]{1,0:T(8,128)(2,1)S(1)}, bf16[72,896]{1,0:T(8,128)(2,1)S(1)}, u32[]{:S(2)}, u32[]{:S(2)}) collective-permute-start(bf16[72,896]{1,0:T(8,128)(2,1)S(1)} %after.19), channel_id=1, source_target_pairs={{0,2},{2,0},{1,3},{3,1},{4,6},{6,4},{5,7},{7,5},{8,10},{10,8},{9,1... | collective-permute-start | bytes 387080 | tf_op jit(solution)/shard_map/back0_tp/ppermute | solution.py:32
  42.0 5.8 %collective-permute-start.15 = (bf16[72,896]{1,0:T(8,128)(2,1)S(1)}, bf16[72,896]{1,0:T(8,128)(2,1)S(1)}, u32[]{:S(2)}, u32[]{:S(2)}) collective-permute-start(bf16[72,896]{1,0:T(8,128)(2,1)S(1)} %add_convert_fusion), channel_id=1, source_target_pairs={{0,4},{4,0},{8,12},{12,8},{1,5},{5,1},{9,13},{13,9},{2,6},{6,2},{1... | collective-permute-start | bytes 387080 | tf_op jit(solution)/shard_map/back1_ep/ppermute | solution.py:32

commit v13 on v12

--- a/solution.py
+++ b/solution.py
@@ -200,14 +200,14 @@
         high = row_sums.astype(jnp.bfloat16).astype(jnp.float32)
         spare = jnp.zeros((EXTRA - 4, row_sums.shape[1]), jnp.float32)
         tail = jnp.concatenate([high, row_sums - high, spare], axis=0)
-        sent_ref[count:, :] = jnp.zeros((EXTRA, sent_ref.shape[1]), jnp.bfloat16)
-        sent_ref[count:, : row_sums.shape[1]] = tail.astype(jnp.bfloat16)
+        sent_ref[count:, :] = jnp.zeros((EXTRA, sent_ref.shape[1]), sent_ref.dtype)
+        sent_ref[count:, : row_sums.shape[1]] = tail.astype(sent_ref.dtype)
     values = [b[skip:, :].astype(jnp.float32) for b, skip in zip(blocks, skips)]
     low = jnp.concatenate([v[:most] for v in values], axis=0).astype(jnp.bfloat16)
     high = jnp.concatenate([v[most : 2 * most] for v in values], axis=0).astype(jnp.bfloat16)
     total = dot(low, down_ref[:, :half], NT) + dot(high, down_ref[:, half:], NT)
     sum_ref[...] = total
-    sent_ref[:count, :] = total.astype(jnp.bfloat16)
+    sent_ref[:count, :] = total.astype(sent_ref.dtype)
 
 
 def back_kernel(most, group, sum_ref, other_ref, up_by_ref, gate_by_ref, gate_ref, up_ref, *outs):
@@ -353,7 +353,7 @@
                     arrived[k] = after(arrived[k], down)
                 crossing = [swap(arrived[k], f"rows{k}", tp=j) for j in range(1, narrow)]
                 if products:
-                    crossing[-1] = after(crossing[-1], products[0])
+                    crossing[-1] = after(crossing[-1], products[0], (1 << 31) * (k == 1))
             if k:
                 taken[k] = [arrived[k]] + crossing
         count = len(group) * narrow * most
@@ -376,7 +376,7 @@
             functools.partial(hidden_kernel, most, extra, [0 if j == 0 or k else deep for k in group for j in range(narrow)]),
             [
                 pltpu.VMEM((count, hidden_width), f32),
-                pltpu.VMEM((count + (EXTRA if extra else 0), hidden_width), bf16),
+                pltpu.VMEM((count + (EXTRA if extra else 0), hidden_width), bf16 if products else f32),
             ],
             *[rows_of_k for k in group for rows_of_k in taken[k]],
             *([row_sums] if extra else []),

time: 49.7 us -> 49.1 us (0.988)
  waiting for transfers between devices: 14.8 us -> 13.5 us
  starting transfers between devices: 21.6 us -> 22.4 us
    ppermute x16, waiting for transfers between devices: 14.8 us -> 13.5 us  [swap(): return lax.ppermute(value, tuple(steps), pairs)]
    ppermute x16, starting transfers between devices: 21.6 us -> 22.4 us  [swap(): return lax.ppermute(value, tuple(steps), pairs)]
  transfers between devices with their start and end apart: 16 -> 16, of which waited for: 9 -> 7; matrix products, arithmetic and copies ran while one was open for 2% -> 2% of each run, Pallas kernels for 17% -> 17%
where the time goes in v13:
time: 49.1 us; the launch traced here: 48.9 us
  starting transfers between devices  22.4 us (46%)
  waiting for transfers between devices  13.5 us (27%)
  Pallas kernels  11.2 us (23%)
  other arithmetic  1 us (2%)
  between operations  0.81 us (2%)
    ppermute x16, starting transfers between devices, swap(): return lax.ppermute(value, tuple(steps), pairs)  22.4 us
    ppermute x16, waiting for transfers between devices, swap(): return lax.ppermute(value, tuple(steps), pairs)  13.5 us
    pallas_call x9, Pallas kernels, call(): pl.pallas_call(kernel, out_shape=outs, in_specs=specs, out_specs=[VMEM] *...  11.2 us
  transfers between devices with their start and end apart: 16, of which 7 were waited for; matrix products, arithmetic and copies ran while one was open for 2% of the time, Pallas kernels for 17%

profile of v13, /device:TPU:0, one launch (start us, length us, event | category | flops | bytes accessed | tf_op | source)
XLA Modules:
  0.0 48.9 jit_solution(14102075907664280302)
XLA Ops:
  0.6 1.6 %pack.1 = (bf16[72,896]{1,0:T(8,128)(2,1)S(1)}, bf16[2,4,72,128]{3,2,1,0:T(8,128)(2,1)S(1)}, f32[1,128]{1,0:T(1,128)S(1)}, f32[14,128]{1,0:T(8,128)S(1)}, bf16[128,1792]{1,0:T(8,128)(2,1)S(1)}) custom-call(s32[1,128]{1,0:T(1,128)} %bitcast.30, f32[1,128]{1,0:T(1,128)} %bitcast.31, f32[14,128]{1,0:T(8,128)} %bitcast.24, bf16[128,1792]{1,0:T(8,128)(2,1)} %refs_3_.1), custom_call_target="tpu_custom_call" | custom-call | tf_op jit(solution)/shard_map/pack/pallas_call | solution.py:51
  2.2 5.1 %collective-permute-start = (bf16[72,896]{1,0:T(8,128)(2,1)S(1)}, bf16[72,896]{1,0:T(8,128)(2,1)S(1)}, u32[]{:S(2)}, u32[]{:S(2)}) collective-permute-start(bf16[72,896]{1,0:T(8,128)(2,1)S(1)} %get-tuple-element.36.earlier_ref), channel_id=1, source_target_pairs={{0,12},{4,8},{8,4},{12,0},{1,13},{5,9},{9,5},{13,1},{2,14},{6,10},... | collective-permute-start | bytes 387080 | tf_op jit(solution)/shard_map/rows3_ep/ppermute | solution.py:32
  7.4 1.1 %pack_more.1 = (bf16[72,896]{1,0:T(8,128)(2,1)S(1)}, bf16[72,896]{1,0:T(8,128)(2,1)S(1)}, bf16[72,896]{1,0:T(8,128)(2,1)S(1)}, bf16[120,896]{1,0:T(8,128)(2,1)S(1)}, bf16[128,256]{1,0:T(8,128)(2,1)S(1)}) custom-call(bf16[2,4,72,128]{3,2,1,0:T(8,128)(2,1)S(1)} %get-tuple-element.31.place_ref.earlier_ref, f32[1,128]{1,0:T(1,128)S(1)} %get-tuple-element.32.weights_ref, ...), custom_call_target="tpu_custom_call" | custom-call | tf_op jit(solution)/shard_map/pack_more/pallas_call | solution.py:51
  8.5 1.6 %collective-permute-start.3 = (bf16[120,896]{1,0:T(8,128)(2,1)S(1)}, bf16[120,896]{1,0:T(8,128)(2,1)S(1)}, u32[]{:S(2)}, u32[]{:S(2)}) collective-permute-start(bf16[120,896]{1,0:T(8,128)(2,1)S(1)} %get-tuple-element.38), channel_id=1, source_target_pairs={{0,2},{2,0},{1,3},{3,1},{4,6},{6,4},{5,7},{7,5},{8,10},{10,8},{9,1... | collective-permute-start | bytes 645128 | tf_op jit(solution)/shard_map/rows0_tp/ppermute | solution.py:32
  10.0 0.9 %collective-permute-done.earlier_ref.refs_6_.refs_0_ = bf16[72,896]{1,0:T(8,128)(2,1)S(1)} collective-permute-done((bf16[72,896]{1,0:T(8,128)(2,1)S(1)}, bf16[72,896]{1,0:T(8,128)(2,1)S(1)}, u32[]{:S(2)}, u32[]{:S(2)}) %collective-permute-start) | collective-permute-done | bytes 129056 | tf_op jit(solution)/shard_map/rows3_ep/ppermute | solution.py:32
  10.9 2.5 %collective-permute-start.2 = (bf16[72,896]{1,0:T(8,128)(2,1)S(1)}, bf16[72,896]{1,0:T(8,128)(2,1)S(1)}, u32[]{:S(2)}, u32[]{:S(2)}) collective-permute-start(bf16[72,896]{1,0:T(8,128)(2,1)S(1)} %collective-permute-done.earlier_ref.refs_6_.refs_0_), channel_id=1, source_target_pairs={{0,2},{2,0},{1,3},{3,1},{4,6},{6,4},{5,7},{7,5},{8,10},{10,8},{9,1... | collective-permute-start | bytes 387080 | tf_op jit(solution)/shard_map/rows3_tp/ppermute | solution.py:32
  13.4 2.1 %collective-permute-start.1 = (bf16[72,896]{1,0:T(8,128)(2,1)S(1)}, bf16[72,896]{1,0:T(8,128)(2,1)S(1)}, u32[]{:S(2)}, u32[]{:S(2)}) collective-permute-start(bf16[72,896]{1,0:T(8,128)(2,1)S(1)} %after.10), channel_id=1, source_target_pairs={{0,8},{4,12},{8,0},{12,4},{1,9},{5,13},{9,1},{13,5},{2,10},{6,14},... | collective-permute-start | bytes 387080 | tf_op jit(solution)/shard_map/rows2_ep/ppermute | solution.py:32
  15.5 2.9 %fetch.1 = (f32[4,72,512]{2,1,0:T(8,128)S(1)}, f32[4,72,512]{2,1,0:T(8,128)S(1)}, bf16[512,1792]{1,0:T(8,128)(2,1)S(1)}, bf16[1792,512]{1,0:T(8,128)(2,1)S(1)}, ...) custom-call(bf16[2,4,72,512]{3,2,1,0:T(8,128)(2,1)} %bitcast.22, ...), custom_call_target="tpu_custom_call" | custom-call | tf_op jit(solution)/shard_map/fetch/pallas_call | solution.py:51
  18.4 0.9 %collective-permute-start.7 = (bf16[72,896]{1,0:T(8,128)(2,1)S(1)}, bf16[72,896]{1,0:T(8,128)(2,1)S(1)}, u32[]{:S(2)}, u32[]{:S(2)}) collective-permute-start(bf16[72,896]{1,0:T(8,128)(2,1)S(1)} %after.15.refs_2_), channel_id=1, source_target_pairs={{0,2},{2,0},{1,3},{3,1},{4,6},{6,4},{5,7},{7,5},{8,10},{10,8},{9,1... | collective-permute-start | bytes 387080 | tf_op jit(solution)/shard_map/rows1_tp/ppermute | solution.py:32
  20.6 0.9 %collective-permute-start.4 = (bf16[72,896]{1,0:T(8,128)(2,1)S(1)}, bf16[72,896]{1,0:T(8,128)(2,1)S(1)}, u32[]{:S(2)}, u32[]{:S(2)}) collective-permute-start(bf16[72,896]{1,0:T(8,128)(2,1)S(1)} %after.13.refs_0_), channel_id=1, source_target_pairs={{0,2},{2,0},{1,3},{3,1},{4,6},{6,4},{5,7},{7,5},{8,10},{10,8},{9,1... | collective-permute-start | bytes 387080 | tf_op jit(solution)/shard_map/rows2_tp/ppermute | solution.py:32
  21.7 1.3 %back.2 = (bf16[72,896]{1,0:T(8,128)(2,1)S(1)}, bf16[72,896]{1,0:T(8,128)(2,1)S(1)}, bf16[72,896]{1,0:T(8,128)(2,1)S(1)}, bf16[72,896]{1,0:T(8,128)(2,1)S(1)}) custom-call(f32[144,512]{1,0:T(8,128)S(1)} %get-tuple-element.40.earlier_ref.sum_ref, f32[144,512]{1,0:T(8,128)S(1)} %collective-permute-done.5.other_ref, ...), custom_call_target="tpu_custom_call" | custom-call | tf_op jit(solution)/shard_map/back/pallas_call | solution.py:51
  23.0 1.4 %collective-permute-start.9 = (bf16[72,896]{1,0:T(8,128)(2,1)S(1)}, bf16[72,896]{1,0:T(8,128)(2,1)S(1)}, u32[]{:S(2)}, u32[]{:S(2)}) collective-permute-start(bf16[72,896]{1,0:T(8,128)(2,1)S(1)} %get-tuple-element.53), channel_id=1, source_target_pairs={{0,2},{2,0},{1,3},{3,1},{4,6},{6,4},{5,7},{7,5},{8,10},{10,8},{9,1... | collective-permute-start | bytes 387080 | tf_op jit(solution)/shard_map/back3_tp/ppermute | solution.py:32
  24.4 2.0 %collective-permute-done.4.value_ref = bf16[72,896]{1,0:T(8,128)(2,1)S(1)} collective-permute-done((bf16[72,896]{1,0:T(8,128)(2,1)S(1)}, bf16[72,896]{1,0:T(8,128)(2,1)S(1)}, u32[]{:S(2)}, u32[]{:S(2)}) %collective-permute-start.4) | collective-permute-done | bytes 129056 | tf_op jit(solution)/shard_map/rows2_tp/ppermute | solution.py:32
  27.2 1.7 %collective-permute-done.9 = bf16[72,896]{1,0:T(8,128)(2,1)S(1)} collective-permute-done((bf16[72,896]{1,0:T(8,128)(2,1)S(1)}, bf16[72,896]{1,0:T(8,128)(2,1)S(1)}, u32[]{:S(2)}, u32[]{:S(2)}) %collective-permute-start.9) | collective-permute-done | bytes 129056 | tf_op jit(solution)/shard_map/back3_tp/ppermute | solution.py:32
  29.0 2.5 %collective-permute-start.12 = (bf16[72,896]{1,0:T(8,128)(2,1)S(1)}, bf16[72,896]{1,0:T(8,128)(2,1)S(1)}, u32[]{:S(2)}, u32[]{:S(2)}) collective-permute-start(bf16[72,896]{1,0:T(8,128)(2,1)S(1)} %add_convert_fusion.2.earlier_ref), channel_id=1, source_target_pairs={{0,12},{4,8},{8,4},{12,0},{1,13},{5,9},{9,5},{13,1},{2,14},{6,10},... | collective-permute-start | bytes 387080 | tf_op jit(solution)/shard_map/back3_ep/ppermute | solution.py:32
  31.4 1.3 %back.3 = (bf16[72,896]{1,0:T(8,128)(2,1)S(1)}, bf16[72,896]{1,0:T(8,128)(2,1)S(1)}, bf16[72,896]{1,0:T(8,128)(2,1)S(1)}, bf16[72,896]{1,0:T(8,128)(2,1)S(1)}) custom-call(f32[144,512]{1,0:T(8,128)S(1)} %get-tuple-element.51.sum_ref, bf16[160,512]{1,0:T(8,128)(2,1)S(1)} %after.18.other_ref, f32[4,72,512]{2,1,0:T(8,128)S(1)} %get-tuple-element.42.up_by_ref, ...), custom_call_target="tpu_custom_call" | custom-call | tf_op jit(solution)/shard_map/back/pallas_call | solution.py:51
  33.5 1.3 %collective-permute-start.14 = (bf16[72,896]{1,0:T(8,128)(2,1)S(1)}, bf16[72,896]{1,0:T(8,128)(2,1)S(1)}, u32[]{:S(2)}, u32[]{:S(2)}) collective-permute-start(bf16[72,896]{1,0:T(8,128)(2,1)S(1)} %get-tuple-element.59), channel_id=1, source_target_pairs={{0,2},{2,0},{1,3},{3,1},{4,6},{6,4},{5,7},{7,5},{8,10},{10,8},{9,1... | collective-permute-start | bytes 387080 | tf_op jit(solution)/shard_map/back1_tp/ppermute | solution.py:32
  34.8 4.2 %collective-permute-done.10 = bf16[72,896]{1,0:T(8,128)(2,1)S(1)} collective-permute-done((bf16[72,896]{1,0:T(8,128)(2,1)S(1)}, bf16[72,896]{1,0:T(8,128)(2,1)S(1)}, u32[]{:S(2)}, u32[]{:S(2)}) %collective-permute-start.10) | collective-permute-done | bytes 129056 | tf_op jit(solution)/shard_map/back2_tp/ppermute | solution.py:32
  39.1 1.1 %collective-permute-start.11 = (bf16[72,896]{1,0:T(8,128)(2,1)S(1)}, bf16[72,896]{1,0:T(8,128)(2,1)S(1)}, u32[]{:S(2)}, u32[]{:S(2)}) collective-permute-start(bf16[72,896]{1,0:T(8,128)(2,1)S(1)} %add_convert_fusion.1.earlier_ref), channel_id=1, source_target_pairs={{0,8},{4,12},{8,0},{12,4},{1,9},{5,13},{9,1},{13,5},{2,10},{6,14},... | collective-permute-start | bytes 387080 | tf_op jit(solution)/shard_map/back2_ep/ppermute | solution.py:32
  40.2 1.0 %collective-permute-start.13 = (bf16[72,896]{1,0:T(8,128)(2,1)S(1)}, bf16[72,896]{1,0:T(8,128)(2,1)S(1)}, u32[]{:S(2)}, u32[]{:S(2)}) collective-permute-start(bf16[72,896]{1,0:T(8,128)(2,1)S(1)} %after.19), channel_id=1, source_target_pairs={{0,2},{2,0},{1,3},{3,1},{4,6},{6,4},{5,7},{7,5},{8,10},{10,8},{9,1... | collective-permute-start | bytes 387080 | tf_op jit(solution)/shard_map/back0_tp/ppermute | solution.py:32
  41.3 1.1 %collective-permute-start.15 = (bf16[72,896]{1,0:T(8,128)(2,1)S(1)}, bf16[72,896]{1,0:T(8,128)(2,1)S(1)}, u32[]{:S(2)}, u32[]{:S(2)}) collective-permute-start(bf16[72,896]{1,0:T(8,128)(2,1)S(1)} %add_convert_fusion), channel_id=1, source_target_pairs={{0,4},{4,0},{8,12},{12,8},{1,5},{5,1},{9,13},{13,9},{2,6},{6,2},{1... | collective-permute-start | bytes 387080 | tf_op jit(solution)/shard_map/back1_ep/ppermute | solution.py:32
  43.1 2.0 %collective-permute-done.13.refs_2_ = bf16[72,896]{1,0:T(8,128)(2,1)S(1)} collective-permute-done((bf16[72,896]{1,0:T(8,128)(2,1)S(1)}, bf16[72,896]{1,0:T(8,128)(2,1)S(1)}, u32[]{:S(2)}, u32[]{:S(2)}) %collective-permute-start.13) | collective-permute-done | bytes 129056 | tf_op jit(solution)/shard_map/back0_tp/ppermute | solution.py:32
  45.1 2.1 %collective-permute-done.15.refs_3_ = bf16[72,896]{1,0:T(8,128)(2,1)S(1)} collective-permute-done((bf16[72,896]{1,0:T(8,128)(2,1)S(1)}, bf16[72,896]{1,0:T(8,128)(2,1)S(1)}, u32[]{:S(2)}, u32[]{:S(2)}) %collective-permute-start.15) | collective-permute-done | bytes 129056 | tf_op jit(solution)/shard_map/back1_ep/ppermute | solution.py:32
  47.8 1.1 %unpack_latest.1 = bf16[128,1792]{1,0:T(8,128)(2,1)} custom-call(bf16[2,4,72,128]{3,2,1,0:T(8,128)(2,1)S(1)} %get-tuple-element.31.place_ref.earlier_ref, bf16[72,896]{1,0:T(8,128)(2,1)S(1)} %collective-permute-done.11.refs_0_, bf16[128,1792]{1,0:T(8,128)(2,1)S(1)} %unpack.1.refs_1_), custom_call_target="tpu_custom_call" | custom-call | tf_op jit(solution)/shard_map/unpack_latest/pallas_call | solution.py:51
  (39 shorter events, 4.5 us)
Async XLA Ops:
  2.2 8.7 %collective-permute-start = (bf16[72,896]{1,0:T(8,128)(2,1)S(1)}, bf16[72,896]{1,0:T(8,128)(2,1)S(1)}, u32[]{:S(2)}, u32[]{:S(2)}) collective-permute-start(bf16[72,896]{1,0:T(8,128)(2,1)S(1)} %get-tuple-element.36.earlier_ref), channel_id=1, source_target_pairs={{0,12},{4,8},{8,4},{12,0},{1,13},{5,9},{9,5},{13,1},{2,14},{6,10},... | collective-permute-start | bytes 387080 | tf_op jit(solution)/shard_map/rows3_ep/ppermute | solution.py:32
  8.5 10.8 %collective-permute-start.3 = (bf16[120,896]{1,0:T(8,128)(2,1)S(1)}, bf16[120,896]{1,0:T(8,128)(2,1)S(1)}, u32[]{:S(2)}, u32[]{:S(2)}) collective-permute-start(bf16[120,896]{1,0:T(8,128)(2,1)S(1)} %get-tuple-element.38), channel_id=1, source_target_pairs={{0,2},{2,0},{1,3},{3,1},{4,6},{6,4},{5,7},{7,5},{8,10},{10,8},{9,1... | collective-permute-start | bytes 645128 | tf_op jit(solution)/shard_map/rows0_tp/ppermute | solution.py:32
  10.0 8.3 %collective-permute-start.6 = (bf16[72,896]{1,0:T(8,128)(2,1)S(1)}, bf16[72,896]{1,0:T(8,128)(2,1)S(1)}, u32[]{:S(2)}, u32[]{:S(2)}) collective-permute-start(bf16[72,896]{1,0:T(8,128)(2,1)S(1)} %get-tuple-element.47), channel_id=1, source_target_pairs={{0,4},{4,0},{8,12},{12,8},{1,5},{5,1},{9,13},{13,9},{2,6},{6,2},{1... | collective-permute-start | bytes 387080 | tf_op jit(solution)/shard_map/rows1_ep/ppermute | solution.py:32
  10.9 8.4 %collective-permute-start.2 = (bf16[72,896]{1,0:T(8,128)(2,1)S(1)}, bf16[72,896]{1,0:T(8,128)(2,1)S(1)}, u32[]{:S(2)}, u32[]{:S(2)}) collective-permute-start(bf16[72,896]{1,0:T(8,128)(2,1)S(1)} %collective-permute-done.earlier_ref.refs_6_.refs_0_), channel_id=1, source_target_pairs={{0,2},{2,0},{1,3},{3,1},{4,6},{6,4},{5,7},{7,5},{8,10},{10,8},{9,1... | collective-permute-start | bytes 387080 | tf_op jit(solution)/shard_map/rows3_tp/ppermute | solution.py:32
  13.4 7.2 %collective-permute-start.1 = (bf16[72,896]{1,0:T(8,128)(2,1)S(1)}, bf16[72,896]{1,0:T(8,128)(2,1)S(1)}, u32[]{:S(2)}, u32[]{:S(2)}) collective-permute-start(bf16[72,896]{1,0:T(8,128)(2,1)S(1)} %after.10), channel_id=1, source_target_pairs={{0,8},{4,12},{8,0},{12,4},{1,9},{5,13},{9,1},{13,5},{2,10},{6,14},... | collective-permute-start | bytes 387080 | tf_op jit(solution)/shard_map/rows2_ep/ppermute | solution.py:32
  18.4 8.0 %collective-permute-start.7 = (bf16[72,896]{1,0:T(8,128)(2,1)S(1)}, bf16[72,896]{1,0:T(8,128)(2,1)S(1)}, u32[]{:S(2)}, u32[]{:S(2)}) collective-permute-start(bf16[72,896]{1,0:T(8,128)(2,1)S(1)} %after.15.refs_2_), channel_id=1, source_target_pairs={{0,2},{2,0},{1,3},{3,1},{4,6},{6,4},{5,7},{7,5},{8,10},{10,8},{9,1... | collective-permute-start | bytes 387080 | tf_op jit(solution)/shard_map/rows1_tp/ppermute | solution.py:32
  20.0 1.7 %collective-permute-start.5 = (f32[144,512]{1,0:T(8,128)S(1)}, f32[144,512]{1,0:T(8,128)S(1)}, u32[]{:S(2)}, u32[]{:S(2)}) collective-permute-start(f32[144,512]{1,0:T(8,128)S(1)} %get-tuple-element.41), channel_id=1, source_target_pairs={{0,1},{1,0},{2,3},{3,2},{4,5},{5,4},{6,7},{7,6},{8,9},{9,8},{10,11... | collective-permute-start | bytes 884744 | tf_op jit(solution)/shard_map/hidden3_sub/ppermute | solution.py:32
  20.6 5.7 %collective-permute-start.4 = (bf16[72,896]{1,0:T(8,128)(2,1)S(1)}, bf16[72,896]{1,0:T(8,128)(2,1)S(1)}, u32[]{:S(2)}, u32[]{:S(2)}) collective-permute-start(bf16[72,896]{1,0:T(8,128)(2,1)S(1)} %after.13.refs_0_), channel_id=1, source_target_pairs={{0,2},{2,0},{1,3},{3,1},{4,6},{6,4},{5,7},{7,5},{8,10},{10,8},{9,1... | collective-permute-start | bytes 387080 | tf_op jit(solution)/shard_map/rows2_tp/ppermute | solution.py:32
  23.0 5.9 %collective-permute-start.9 = (bf16[72,896]{1,0:T(8,128)(2,1)S(1)}, bf16[72,896]{1,0:T(8,128)(2,1)S(1)}, u32[]{:S(2)}, u32[]{:S(2)}) collective-permute-start(bf16[72,896]{1,0:T(8,128)(2,1)S(1)} %get-tuple-element.53), channel_id=1, source_target_pairs={{0,2},{2,0},{1,3},{3,1},{4,6},{6,4},{5,7},{7,5},{8,10},{10,8},{9,1... | collective-permute-start | bytes 387080 | tf_op jit(solution)/shard_map/back3_tp/ppermute | solution.py:32
  27.1 4.3 %collective-permute-start.8 = (bf16[160,512]{1,0:T(8,128)(2,1)S(1)}, bf16[160,512]{1,0:T(8,128)(2,1)S(1)}, u32[]{:S(2)}, u32[]{:S(2)}) collective-permute-start(bf16[160,512]{1,0:T(8,128)(2,1)S(1)} %get-tuple-element.52), channel_id=1, source_target_pairs={{0,1},{1,0},{2,3},{3,2},{4,5},{5,4},{6,7},{7,6},{8,9},{9,8},{10,11... | collective-permute-start | bytes 491528 | tf_op jit(solution)/shard_map/hidden2_sub/ppermute | solution.py:32
  29.0 14.1 %collective-permute-start.12 = (bf16[72,896]{1,0:T(8,128)(2,1)S(1)}, bf16[72,896]{1,0:T(8,128)(2,1)S(1)}, u32[]{:S(2)}, u32[]{:S(2)}) collective-permute-start(bf16[72,896]{1,0:T(8,128)(2,1)S(1)} %add_convert_fusion.2.earlier_ref), channel_id=1, source_target_pairs={{0,12},{4,8},{8,4},{12,0},{1,13},{5,9},{9,5},{13,1},{2,14},{6,10},... | collective-permute-start | bytes 387080 | tf_op jit(solution)/shard_map/back3_ep/ppermute | solution.py:32
  32.7 6.3 %collective-permute-start.10 = (bf16[72,896]{1,0:T(8,128)(2,1)S(1)}, bf16[72,896]{1,0:T(8,128)(2,1)S(1)}, u32[]{:S(2)}, u32[]{:S(2)}) collective-permute-start(bf16[72,896]{1,0:T(8,128)(2,1)S(1)} %get-tuple-element.55), channel_id=1, source_target_pairs={{0,2},{2,0},{1,3},{3,1},{4,6},{6,4},{5,7},{7,5},{8,10},{10,8},{9,1... | collective-permute-start | bytes 387080 | tf_op jit(solution)/shard_map/back2_tp/ppermute | solution.py:32
  33.5 7.7 %collective-permute-start.14 = (bf16[72,896]{1,0:T(8,128)(2,1)S(1)}, bf16[72,896]{1,0:T(8,128)(2,1)S(1)}, u32[]{:S(2)}, u32[]{:S(2)}) collective-permute-start(bf16[72,896]{1,0:T(8,128)(2,1)S(1)} %get-tuple-element.59), channel_id=1, source_target_pairs={{0,2},{2,0},{1,3},{3,1},{4,6},{6,4},{5,7},{7,5},{8,10},{10,8},{9,1... | collective-permute-start | bytes 387080 | tf_op jit(solution)/shard_map/back1_tp/ppermute | solution.py:32
  39.1 8.7 %collective-permute-start.11 = (bf16[72,896]{1,0:T(8,128)(2,1)S(1)}, bf16[72,896]{1,0:T(8,128)(2,1)S(1)}, u32[]{:S(2)}, u32[]{:S(2)}) collective-permute-start(bf16[72,896]{1,0:T(8,128)(2,1)S(1)} %add_convert_fusion.1.earlier_ref), channel_id=1, source_target_pairs={{0,8},{4,12},{8,0},{12,4},{1,9},{5,13},{9,1},{13,5},{2,10},{6,14},... | collective-permute-start | bytes 387080 | tf_op jit(solution)/shard_map/back2_ep/ppermute | solution.py:32
  40.2 4.9 %collective-permute-start.13 = (bf16[72,896]{1,0:T(8,128)(2,1)S(1)}, bf16[72,896]{1,0:T(8,128)(2,1)S(1)}, u32[]{:S(2)}, u32[]{:S(2)}) collective-permute-start(bf16[72,896]{1,0:T(8,128)(2,1)S(1)} %after.19), channel_id=1, source_target_pairs={{0,2},{2,0},{1,3},{3,1},{4,6},{6,4},{5,7},{7,5},{8,10},{10,8},{9,1... | collective-permute-start | bytes 387080 | tf_op jit(solution)/shard_map/back0_tp/ppermute | solution.py:32
  41.3 6.0 %collective-permute-start.15 = (bf16[72,896]{1,0:T(8,128)(2,1)S(1)}, bf16[72,896]{1,0:T(8,128)(2,1)S(1)}, u32[]{:S(2)}, u32[]{:S(2)}) collective-permute-start(bf16[72,896]{1,0:T(8,128)(2,1)S(1)} %add_convert_fusion), channel_id=1, source_target_pairs={{0,4},{4,0},{8,12},{12,8},{1,5},{5,1},{9,13},{13,9},{2,6},{6,2},{1... | collective-permute-start | bytes 387080 | tf_op jit(solution)/shard_map/back1_ep/ppermute | solution.py:32

commit v14 on v13

--- a/solution.py
+++ b/solution.py
@@ -247,10 +247,10 @@
 
 
 def groups_of(wide):
-    left = list(range(wide - 1, -1, -1))
     if wide < 4:
-        return [left]
-    return [[left[0], 0]] + [left[i : min(i + 2, wide - 1)] for i in range(1, wide - 1, 2)]
+        return [list(range(wide - 1, -1, -1))]
+    left = list(range(wide - 2, 1, -1))
+    return [[wide - 1, 0], [1]] + [left[i : i + 2] for i in range(0, len(left), 2)]
 
 
 def local(
@@ -321,7 +321,7 @@
         if k:
             given = packed[k] if k in (first, 1) else after(packed[k], arrived[first])
             arrived[k] = swap(given, f"rows{k}", ep=k)
-            if staged and k == groups[1][0]:
+            if staged and k == groups[2][0]:
                 arrived[k] = after(arrived[k], packed[first], 1 << 28)
     fetched = [
         pre_acts.reshape(2, wide, narrow * most, hidden_width),
@@ -341,52 +341,27 @@
         earlier=[arrived[first]],
         name="fetch",
     )
+    values = latent.astype(f32)
     returned = {}
-    values = latent.astype(f32)
-    received, products, moved = None, None, None
-    for group in groups:
-        for k in group:
-            if k:
-                if products and k == group[0]:
-                    arrived[k] = after(arrived[k], summed)
-                if products and k == 1:
-                    arrived[k] = after(arrived[k], down)
-                crossing = [swap(arrived[k], f"rows{k}", tp=j) for j in range(1, narrow)]
-                if products:
-                    crossing[-1] = after(crossing[-1], products[0], (1 << 31) * (k == 1))
-            if k:
-                taken[k] = [arrived[k]] + crossing
+
+    def forward(group, kind, earlier=(), row_sums=()):
         count = len(group) * narrow * most
-        extra = group is groups[-1]
-        if extra:
-            if staged:
-                both[-1] = after(both[-1], summed)
-            own_grad = more[-1].astype(f32)
-            for value in both:
-                pieces = [
-                    value[: min(deep, tokens - at), column : column + latent.shape[1]]
-                    for at, column in parts
-                ]
-                own_grad += jnp.concatenate(pieces, axis=0).astype(f32)
-            gained = own_grad * latent_gain
-            row_sums = jnp.stack(
-                [jnp.sum(values * values, axis=1), jnp.sum(gained * values, axis=1)]
-            )
+        skips = [0 if j == 0 or k else deep for k in group for j in range(narrow)]
         summed, sent = call(
-            functools.partial(hidden_kernel, most, extra, [0 if j == 0 or k else deep for k in group for j in range(narrow)]),
+            functools.partial(hidden_kernel, most, len(row_sums), skips),
             [
                 pltpu.VMEM((count, hidden_width), f32),
-                pltpu.VMEM((count + (EXTRA if extra else 0), hidden_width), bf16 if products else f32),
+                pltpu.VMEM((count + EXTRA * len(row_sums), hidden_width), kind),
             ],
             *[rows_of_k for k in group for rows_of_k in taken[k]],
-            *([row_sums] if extra else []),
+            *row_sums,
             down,
             name="hidden",
-            earlier=products[:1] if products else (),
+            earlier=earlier,
         )
-        received = swap(sent, f"hidden{group[0]}", sub=1)
-        if moved is not None:
-            received = after(received, moved)
+        return summed, swap(sent, f"hidden{group[0]}", sub=1)
+
+    def backward(group, summed, received):
         products = call(
             functools.partial(back_kernel, most, group),
             [block] * (len(group) * narrow),
@@ -398,23 +373,75 @@
             up,
             name="back",
         )
-        for at, k in enumerate(group):
-            mine, others = products[at * narrow], products[at * narrow + 1 : (at + 1) * narrow]
-            if k == 0:
-                kept = mine, others
-            else:
-                total = mine.astype(f32)
-                for j, other in enumerate(others):
-                    total += swap(other, f"back{k}", tp=j + 1).astype(f32)
-                total = total.astype(bf16)
-                returned[k] = [swap(total, f"back{k}", ep=k)]
-                if k == group[0]:
-                    moved = total
-    mine, others = kept
-    returned[0] = [mine] + [
-        swap(after(other, moved) if staged else other, "back0", tp=j + 1)
-        for j, other in enumerate(others)
+        return {k: products[i * narrow : (i + 1) * narrow] for i, k in enumerate(group)}
+
+    def give_back(k, products):
+        total = products[0].astype(f32)
+        for j in range(1, narrow):
+            total += swap(products[j], f"back{k}", tp=j).astype(f32)
+        total = total.astype(bf16)
+        returned[k] = [swap(total, f"back{k}", ep=k)]
+        return total
+
+    def row_sums_of(both):
+        own_grad = more[-1].astype(f32)
+        for value in both:
+            pieces = [
+                value[: min(deep, tokens - at), column : column + latent.shape[1]]
+                for at, column in parts
+            ]
+            own_grad += jnp.concatenate(pieces, axis=0).astype(f32)
+        gained = own_grad * latent_gain
+        return gained, jnp.stack(
+            [jnp.sum(values * values, axis=1), jnp.sum(gained * values, axis=1)]
+        )
+
+    def crossed(k, rows_of_k):
+        return [swap(rows_of_k, f"rows{k}", tp=j) for j in range(1, narrow)]
+
+    for k in groups[0]:
+        if k:
+            taken[k] = [arrived[k]] + crossed(k, arrived[k])
+    gained, row_sums = row_sums_of(both) if not staged else (None, None)
+    summed, received = forward(groups[0], f32, row_sums=() if staged else [row_sums])
+    products = backward(groups[0], summed, received)
+    kept = products[0]
+    moved = give_back(first, products[first]) if first else None
+    if staged:
+        first_summed, gate_open = summed, products[first][:1]
+        rows_of_k = after(arrived[1], down)
+        crossing = crossed(1, rows_of_k)
+        crossing[-1] = after(crossing[-1], gate_open[0], 1 << 31)
+        taken[1] = [rows_of_k] + crossing
+        near_summed, near_received = forward([1], bf16, earlier=gate_open)
+        gate_open, near = [near_summed], True
+        for group in groups[2:]:
+            for k in group:
+                rows_of_k = after(arrived[k], first_summed) if k == group[0] else arrived[k]
+                crossing = crossed(k, rows_of_k)
+                crossing[-1] = after(crossing[-1], gate_open[0])
+                taken[k] = [rows_of_k] + crossing
+            last = group is groups[-1]
+            if last:
+                both[-1] = after(both[-1], first_summed)
+                gained, row_sums = row_sums_of(both)
+            summed, received = forward(
+                group, f32, earlier=gate_open, row_sums=[row_sums] if last else ()
+            )
+            if near:
+                products = backward([1], near_summed, after(near_received, summed))
+                give_back(1, products[1])
+                near = False
+            products = backward(group, summed, after(received, moved))
+            gate_open = products[group[0]][:1]
+            moved = [give_back(k, products[k]) for k in group][0]
+    else:
+        for k in groups[0][1:-1]:
+            give_back(k, products[k])
+    returned[0] = [kept[0]] + [
+        swap(after(kept[j], moved) if staged else kept[j], "back0", tp=j) for j in range(1, narrow)
     ]
+    count = summed.shape[0]
     tail = received[count : count + 4, :tokens].astype(f32)
     row_sums = row_sums + tail[:2] + tail[2:]
     inverse_rms = lax.rsqrt(row_sums[0] / LAT + 1e-06)[:, None]

time: 49.1 us -> 48.7 us (level)
  waiting for transfers between devices: 13.5 us -> 9.6 us
  Pallas kernels: 11.2 us -> 13 us
  starting transfers between devices: 22.4 us -> 24 us
    ppermute x16 -> x17, waiting for transfers between devices: 13.5 us -> 9.6 us  [swap(): return lax.ppermute(value, tuple(steps), pairs)]
    pallas_call x9 -> x11, Pallas kernels: 11.2 us -> 13 us  [call(): pl.pallas_call(kernel, out_shape=outs, in_specs=specs, out_specs=[VMEM] *...]
    ppermute x16 -> x17, starting transfers between devices: 22.4 us -> 24 us  [swap(): return lax.ppermute(value, tuple(steps), pairs)]
  transfers between devices with their start and end apart: 16 -> 17, of which waited for: 7 -> 6; matrix products, arithmetic and copies ran while one was open for 2% -> 2% of each run, Pallas kernels for 17% -> 21%
where the time goes in v14:
time: 48.7 us; the launch traced here: 48.5 us
  starting transfers between devices  24 us (49%)
  Pallas kernels  13 us (27%)
  waiting for transfers between devices  9.6 us (20%)
  other arithmetic  1 us (2%)
  between operations  0.82 us (2%)
    ppermute x17, starting transfers between devices, swap(): return lax.ppermute(value, tuple(steps), pairs)  24 us
    pallas_call x11, Pallas kernels, call(): pl.pallas_call(kernel, out_shape=outs, in_specs=specs, out_specs=[VMEM] *...  13 us
    ppermute x17, waiting for transfers between devices, swap(): return lax.ppermute(value, tuple(steps), pairs)  9.6 us
  transfers between devices with their start and end apart: 17, of which 6 were waited for; matrix products, arithmetic and copies ran while one was open for 2% of the time, Pallas kernels for 21%

profile of v14, /device:TPU:0, one launch (start us, length us, event | category | flops | bytes accessed | tf_op | source)
XLA Modules:
  0.0 48.5 jit_solution(1702331697601323786)
XLA Ops:
  0.6 1.6 %pack.1 = (bf16[72,896]{1,0:T(8,128)(2,1)S(1)}, bf16[2,4,72,128]{3,2,1,0:T(8,128)(2,1)S(1)}, f32[1,128]{1,0:T(1,128)S(1)}, f32[14,128]{1,0:T(8,128)S(1)}, bf16[128,1792]{1,0:T(8,128)(2,1)S(1)}) custom-call(s32[1,128]{1,0:T(1,128)} %bitcast.30, f32[1,128]{1,0:T(1,128)} %bitcast.31, f32[14,128]{1,0:T(8,128)} %bitcast.24, bf16[128,1792]{1,0:T(8,128)(2,1)} %refs_3_.1), custom_call_target="tpu_custom_call" | custom-call | tf_op jit(solution)/shard_map/pack/pallas_call | solution.py:51
  2.2 5.1 %collective-permute-start = (bf16[72,896]{1,0:T(8,128)(2,1)S(1)}, bf16[72,896]{1,0:T(8,128)(2,1)S(1)}, u32[]{:S(2)}, u32[]{:S(2)}) collective-permute-start(bf16[72,896]{1,0:T(8,128)(2,1)S(1)} %get-tuple-element.38.earlier_ref), channel_id=1, source_target_pairs={{0,12},{4,8},{8,4},{12,0},{1,13},{5,9},{9,5},{13,1},{2,14},{6,10},... | collective-permute-start | bytes 387080 | tf_op jit(solution)/shard_map/rows3_ep/ppermute | solution.py:32
  7.4 1.1 %pack_more.1 = (bf16[72,896]{1,0:T(8,128)(2,1)S(1)}, bf16[72,896]{1,0:T(8,128)(2,1)S(1)}, bf16[72,896]{1,0:T(8,128)(2,1)S(1)}, bf16[120,896]{1,0:T(8,128)(2,1)S(1)}, bf16[128,256]{1,0:T(8,128)(2,1)S(1)}) custom-call(bf16[2,4,72,128]{3,2,1,0:T(8,128)(2,1)S(1)} %get-tuple-element.33.place_ref.earlier_ref, f32[1,128]{1,0:T(1,128)S(1)} %get-tuple-element.34.weights_ref, ...), custom_call_target="tpu_custom_call" | custom-call | tf_op jit(solution)/shard_map/pack_more/pallas_call | solution.py:51
  8.5 1.6 %collective-permute-start.3 = (bf16[120,896]{1,0:T(8,128)(2,1)S(1)}, bf16[120,896]{1,0:T(8,128)(2,1)S(1)}, u32[]{:S(2)}, u32[]{:S(2)}) collective-permute-start(bf16[120,896]{1,0:T(8,128)(2,1)S(1)} %get-tuple-element.40), channel_id=1, source_target_pairs={{0,2},{2,0},{1,3},{3,1},{4,6},{6,4},{5,7},{7,5},{8,10},{10,8},{9,1... | collective-permute-start | bytes 645128 | tf_op jit(solution)/shard_map/rows0_tp/ppermute | solution.py:32
  10.9 2.5 %collective-permute-start.2 = (bf16[72,896]{1,0:T(8,128)(2,1)S(1)}, bf16[72,896]{1,0:T(8,128)(2,1)S(1)}, u32[]{:S(2)}, u32[]{:S(2)}) collective-permute-start(bf16[72,896]{1,0:T(8,128)(2,1)S(1)} %collective-permute-done.earlier_ref.refs_6_.refs_0_), channel_id=1, source_target_pairs={{0,2},{2,0},{1,3},{3,1},{4,6},{6,4},{5,7},{7,5},{8,10},{10,8},{9,1... | collective-permute-start | bytes 387080 | tf_op jit(solution)/shard_map/rows3_tp/ppermute | solution.py:32
  13.4 2.1 %collective-permute-start.1 = (bf16[72,896]{1,0:T(8,128)(2,1)S(1)}, bf16[72,896]{1,0:T(8,128)(2,1)S(1)}, u32[]{:S(2)}, u32[]{:S(2)}) collective-permute-start(bf16[72,896]{1,0:T(8,128)(2,1)S(1)} %after.11), channel_id=1, source_target_pairs={{0,8},{4,12},{8,0},{12,4},{1,9},{5,13},{9,1},{13,5},{2,10},{6,14},... | collective-permute-start | bytes 387080 | tf_op jit(solution)/shard_map/rows2_ep/ppermute | solution.py:32
  15.5 2.9 %fetch.1 = (f32[4,72,512]{2,1,0:T(8,128)S(1)}, f32[4,72,512]{2,1,0:T(8,128)S(1)}, bf16[512,1792]{1,0:T(8,128)(2,1)S(1)}, bf16[1792,512]{1,0:T(8,128)(2,1)S(1)}, ...) custom-call(bf16[2,4,72,512]{3,2,1,0:T(8,128)(2,1)} %bitcast.22, ...), custom_call_target="tpu_custom_call" | custom-call | tf_op jit(solution)/shard_map/fetch/pallas_call | solution.py:51
  18.4 0.9 %collective-permute-start.6 = (bf16[72,896]{1,0:T(8,128)(2,1)S(1)}, bf16[72,896]{1,0:T(8,128)(2,1)S(1)}, u32[]{:S(2)}, u32[]{:S(2)}) collective-permute-start(bf16[72,896]{1,0:T(8,128)(2,1)S(1)} %after.15.refs_0_), channel_id=1, source_target_pairs={{0,2},{2,0},{1,3},{3,1},{4,6},{6,4},{5,7},{7,5},{8,10},{10,8},{9,1... | collective-permute-start | bytes 387080 | tf_op jit(solution)/shard_map/rows1_tp/ppermute | solution.py:32
  20.6 0.9 %collective-permute-start.4 = (bf16[72,896]{1,0:T(8,128)(2,1)S(1)}, bf16[72,896]{1,0:T(8,128)(2,1)S(1)}, u32[]{:S(2)}, u32[]{:S(2)}) collective-permute-start(bf16[72,896]{1,0:T(8,128)(2,1)S(1)} %after.14.refs_0_), channel_id=1, source_target_pairs={{0,2},{2,0},{1,3},{3,1},{4,6},{6,4},{5,7},{7,5},{8,10},{10,8},{9,1... | collective-permute-start | bytes 387080 | tf_op jit(solution)/shard_map/rows2_tp/ppermute | solution.py:32
  21.7 1.3 %back.3 = (bf16[72,896]{1,0:T(8,128)(2,1)S(1)}, bf16[72,896]{1,0:T(8,128)(2,1)S(1)}, bf16[72,896]{1,0:T(8,128)(2,1)S(1)}, bf16[72,896]{1,0:T(8,128)(2,1)S(1)}) custom-call(f32[144,512]{1,0:T(8,128)S(1)} %get-tuple-element.42.earlier_ref.sum_ref, f32[144,512]{1,0:T(8,128)S(1)} %collective-permute-done.7.other_ref, ...), custom_call_target="tpu_custom_call" | custom-call | tf_op jit(solution)/shard_map/back/pallas_call | solution.py:51
  23.0 1.4 %collective-permute-start.9 = (bf16[72,896]{1,0:T(8,128)(2,1)S(1)}, bf16[72,896]{1,0:T(8,128)(2,1)S(1)}, u32[]{:S(2)}, u32[]{:S(2)}) collective-permute-start(bf16[72,896]{1,0:T(8,128)(2,1)S(1)} %get-tuple-element.56), channel_id=1, source_target_pairs={{0,2},{2,0},{1,3},{3,1},{4,6},{6,4},{5,7},{7,5},{8,10},{10,8},{9,1... | collective-permute-start | bytes 387080 | tf_op jit(solution)/shard_map/back3_tp/ppermute | solution.py:32
  25.1 1.3 %collective-permute-done.4.value_ref = bf16[72,896]{1,0:T(8,128)(2,1)S(1)} collective-permute-done((bf16[72,896]{1,0:T(8,128)(2,1)S(1)}, bf16[72,896]{1,0:T(8,128)(2,1)S(1)}, u32[]{:S(2)}, u32[]{:S(2)}) %collective-permute-start.4) | collective-permute-done | bytes 129056 | tf_op jit(solution)/shard_map/rows2_tp/ppermute | solution.py:32
  27.2 1.2 %back.5 = (bf16[72,896]{1,0:T(8,128)(2,1)S(1)}, bf16[72,896]{1,0:T(8,128)(2,1)S(1)}) custom-call(f32[72,512]{1,0:T(8,128)S(1)} %get-tuple-element.50.earlier_ref.refs_4_.sum_ref, bf16[72,512]{1,0:T(8,128)(2,1)S(1)} %after.21.other_ref, f32[4,72,512]{2,1,0:T(8,128)S(1)} %get-tuple-element.45.up_by_ref, f32[4,72,512]{2,1,0:T(8,128)S(1)} %get-tuple-element.46.gate_by_ref, ...), custom_call_target="tpu_custom_call" | custom-call | tf_op jit(solution)/shard_map/back/pallas_call | solution.py:51
  28.4 1.3 %collective-permute-start.15 = (bf16[72,896]{1,0:T(8,128)(2,1)S(1)}, bf16[72,896]{1,0:T(8,128)(2,1)S(1)}, u32[]{:S(2)}, u32[]{:S(2)}) collective-permute-start(bf16[72,896]{1,0:T(8,128)(2,1)S(1)} %get-tuple-element.63), channel_id=1, source_target_pairs={{0,2},{2,0},{1,3},{3,1},{4,6},{6,4},{5,7},{7,5},{8,10},{10,8},{9,1... | collective-permute-start | bytes 387080 | tf_op jit(solution)/shard_map/back1_tp/ppermute | solution.py:32
  29.8 2.2 %collective-permute-start.12 = (bf16[72,896]{1,0:T(8,128)(2,1)S(1)}, bf16[72,896]{1,0:T(8,128)(2,1)S(1)}, u32[]{:S(2)}, u32[]{:S(2)}) collective-permute-start(bf16[72,896]{1,0:T(8,128)(2,1)S(1)} %add_convert_fusion.2.earlier_ref), channel_id=1, source_target_pairs={{0,12},{4,8},{8,4},{12,0},{1,13},{5,9},{9,5},{13,1},{2,14},{6,10},... | collective-permute-start | bytes 387080 | tf_op jit(solution)/shard_map/back3_ep/ppermute | solution.py:32
  32.0 1.2 %back.4 = (bf16[72,896]{1,0:T(8,128)(2,1)S(1)}, bf16[72,896]{1,0:T(8,128)(2,1)S(1)}) custom-call(f32[72,512]{1,0:T(8,128)S(1)} %get-tuple-element.54.sum_ref.earlier_ref, f32[88,512]{1,0:T(8,128)S(1)} %after.19.other_ref, f32[4,72,512]{2,1,0:T(8,128)S(1)} %get-tuple-element.45.up_by_ref, f32[4,72,512]{2,1,0:T(8,128)S(1)} %get-tuple-element.46.gate_by_ref, ...), custom_call_target="tpu_custom_call" | custom-call | tf_op jit(solution)/shard_map/back/pallas_call | solution.py:51
  33.3 2.1 %collective-permute-start.10 = (bf16[72,896]{1,0:T(8,128)(2,1)S(1)}, bf16[72,896]{1,0:T(8,128)(2,1)S(1)}, u32[]{:S(2)}, u32[]{:S(2)}) collective-permute-start(bf16[72,896]{1,0:T(8,128)(2,1)S(1)} %get-tuple-element.58), channel_id=1, source_target_pairs={{0,2},{2,0},{1,3},{3,1},{4,6},{6,4},{5,7},{7,5},{8,10},{10,8},{9,1... | collective-permute-start | bytes 387080 | tf_op jit(solution)/shard_map/back2_tp/ppermute | solution.py:32
  35.4 1.7 %collective-permute-start.16 = (bf16[72,896]{1,0:T(8,128)(2,1)S(1)}, bf16[72,896]{1,0:T(8,128)(2,1)S(1)}, u32[]{:S(2)}, u32[]{:S(2)}) collective-permute-start(bf16[72,896]{1,0:T(8,128)(2,1)S(1)} %add_convert_fusion), channel_id=1, source_target_pairs={{0,4},{4,0},{8,12},{12,8},{1,5},{5,1},{9,13},{13,9},{2,6},{6,2},{1... | collective-permute-start | bytes 387080 | tf_op jit(solution)/shard_map/back1_ep/ppermute | solution.py:32
  37.0 1.8 %collective-permute-done.10 = bf16[72,896]{1,0:T(8,128)(2,1)S(1)} collective-permute-done((bf16[72,896]{1,0:T(8,128)(2,1)S(1)}, bf16[72,896]{1,0:T(8,128)(2,1)S(1)}, u32[]{:S(2)}, u32[]{:S(2)}) %collective-permute-start.10) | collective-permute-done | bytes 129056 | tf_op jit(solution)/shard_map/back2_tp/ppermute | solution.py:32
  38.9 1.0 %collective-permute-start.11 = (bf16[72,896]{1,0:T(8,128)(2,1)S(1)}, bf16[72,896]{1,0:T(8,128)(2,1)S(1)}, u32[]{:S(2)}, u32[]{:S(2)}) collective-permute-start(bf16[72,896]{1,0:T(8,128)(2,1)S(1)} %add_convert_fusion.1.earlier_ref), channel_id=1, source_target_pairs={{0,8},{4,12},{8,0},{12,4},{1,9},{5,13},{9,1},{13,5},{2,10},{6,14},... | collective-permute-start | bytes 387080 | tf_op jit(solution)/shard_map/back2_ep/ppermute | solution.py:32
  40.0 1.1 %collective-permute-start.13 = (bf16[72,896]{1,0:T(8,128)(2,1)S(1)}, bf16[72,896]{1,0:T(8,128)(2,1)S(1)}, u32[]{:S(2)}, u32[]{:S(2)}) collective-permute-start(bf16[72,896]{1,0:T(8,128)(2,1)S(1)} %after.20), channel_id=1, source_target_pairs={{0,2},{2,0},{1,3},{3,1},{4,6},{6,4},{5,7},{7,5},{8,10},{10,8},{9,1... | collective-permute-start | bytes 387080 | tf_op jit(solution)/shard_map/back0_tp/ppermute | solution.py:32
  41.8 3.1 %collective-permute-done.13.refs_2_ = bf16[72,896]{1,0:T(8,128)(2,1)S(1)} collective-permute-done((bf16[72,896]{1,0:T(8,128)(2,1)S(1)}, bf16[72,896]{1,0:T(8,128)(2,1)S(1)}, u32[]{:S(2)}, u32[]{:S(2)}) %collective-permute-start.13) | collective-permute-done | bytes 129056 | tf_op jit(solution)/shard_map/back0_tp/ppermute | solution.py:32
  45.5 1.9 %collective-permute-done.11.refs_0_ = bf16[72,896]{1,0:T(8,128)(2,1)S(1)} collective-permute-done((bf16[72,896]{1,0:T(8,128)(2,1)S(1)}, bf16[72,896]{1,0:T(8,128)(2,1)S(1)}, u32[]{:S(2)}, u32[]{:S(2)}) %collective-permute-start.11) | collective-permute-done | bytes 129056 | tf_op jit(solution)/shard_map/back2_ep/ppermute | solution.py:32
  47.4 1.1 %unpack_latest.1 = bf16[128,1792]{1,0:T(8,128)(2,1)} custom-call(bf16[2,4,72,128]{3,2,1,0:T(8,128)(2,1)S(1)} %get-tuple-element.33.place_ref.earlier_ref, bf16[72,896]{1,0:T(8,128)(2,1)S(1)} %collective-permute-done.11.refs_0_, bf16[128,1792]{1,0:T(8,128)(2,1)S(1)} %unpack.1.refs_1_), custom_call_target="tpu_custom_call" | custom-call | tf_op jit(solution)/shard_map/unpack_latest/pallas_call | solution.py:51
  (43 shorter events, 5.3 us)
Async XLA Ops:
  2.2 8.7 %collective-permute-start = (bf16[72,896]{1,0:T(8,128)(2,1)S(1)}, bf16[72,896]{1,0:T(8,128)(2,1)S(1)}, u32[]{:S(2)}, u32[]{:S(2)}) collective-permute-start(bf16[72,896]{1,0:T(8,128)(2,1)S(1)} %get-tuple-element.38.earlier_ref), channel_id=1, source_target_pairs={{0,12},{4,8},{8,4},{12,0},{1,13},{5,9},{9,5},{13,1},{2,14},{6,10},... | collective-permute-start | bytes 387080 | tf_op jit(solution)/shard_map/rows3_ep/ppermute | solution.py:32
  8.5 10.8 %collective-permute-start.3 = (bf16[120,896]{1,0:T(8,128)(2,1)S(1)}, bf16[120,896]{1,0:T(8,128)(2,1)S(1)}, u32[]{:S(2)}, u32[]{:S(2)}) collective-permute-start(bf16[120,896]{1,0:T(8,128)(2,1)S(1)} %get-tuple-element.40), channel_id=1, source_target_pairs={{0,2},{2,0},{1,3},{3,1},{4,6},{6,4},{5,7},{7,5},{8,10},{10,8},{9,1... | collective-permute-start | bytes 645128 | tf_op jit(solution)/shard_map/rows0_tp/ppermute | solution.py:32
  10.0 8.3 %collective-permute-start.5 = (bf16[72,896]{1,0:T(8,128)(2,1)S(1)}, bf16[72,896]{1,0:T(8,128)(2,1)S(1)}, u32[]{:S(2)}, u32[]{:S(2)}) collective-permute-start(bf16[72,896]{1,0:T(8,128)(2,1)S(1)} %get-tuple-element.43), channel_id=1, source_target_pairs={{0,4},{4,0},{8,12},{12,8},{1,5},{5,1},{9,13},{13,9},{2,6},{6,2},{1... | collective-permute-start | bytes 387080 | tf_op jit(solution)/shard_map/rows1_ep/ppermute | solution.py:32
  10.9 8.4 %collective-permute-start.2 = (bf16[72,896]{1,0:T(8,128)(2,1)S(1)}, bf16[72,896]{1,0:T(8,128)(2,1)S(1)}, u32[]{:S(2)}, u32[]{:S(2)}) collective-permute-start(bf16[72,896]{1,0:T(8,128)(2,1)S(1)} %collective-permute-done.earlier_ref.refs_6_.refs_0_), channel_id=1, source_target_pairs={{0,2},{2,0},{1,3},{3,1},{4,6},{6,4},{5,7},{7,5},{8,10},{10,8},{9,1... | collective-permute-start | bytes 387080 | tf_op jit(solution)/shard_map/rows3_tp/ppermute | solution.py:32
  13.4 7.2 %collective-permute-start.1 = (bf16[72,896]{1,0:T(8,128)(2,1)S(1)}, bf16[72,896]{1,0:T(8,128)(2,1)S(1)}, u32[]{:S(2)}, u32[]{:S(2)}) collective-permute-start(bf16[72,896]{1,0:T(8,128)(2,1)S(1)} %after.11), channel_id=1, source_target_pairs={{0,8},{4,12},{8,0},{12,4},{1,9},{5,13},{9,1},{13,5},{2,10},{6,14},... | collective-permute-start | bytes 387080 | tf_op jit(solution)/shard_map/rows2_ep/ppermute | solution.py:32
  18.4 6.0 %collective-permute-start.6 = (bf16[72,896]{1,0:T(8,128)(2,1)S(1)}, bf16[72,896]{1,0:T(8,128)(2,1)S(1)}, u32[]{:S(2)}, u32[]{:S(2)}) collective-permute-start(bf16[72,896]{1,0:T(8,128)(2,1)S(1)} %after.15.refs_0_), channel_id=1, source_target_pairs={{0,2},{2,0},{1,3},{3,1},{4,6},{6,4},{5,7},{7,5},{8,10},{10,8},{9,1... | collective-permute-start | bytes 387080 | tf_op jit(solution)/shard_map/rows1_tp/ppermute | solution.py:32
  20.0 1.7 %collective-permute-start.7 = (f32[144,512]{1,0:T(8,128)S(1)}, f32[144,512]{1,0:T(8,128)S(1)}, u32[]{:S(2)}, u32[]{:S(2)}) collective-permute-start(f32[144,512]{1,0:T(8,128)S(1)} %get-tuple-element.44), channel_id=1, source_target_pairs={{0,1},{1,0},{2,3},{3,2},{4,5},{5,4},{6,7},{7,6},{8,9},{9,8},{10,11... | collective-permute-start | bytes 884744 | tf_op jit(solution)/shard_map/hidden3_sub/ppermute | solution.py:32
  20.6 5.8 %collective-permute-start.4 = (bf16[72,896]{1,0:T(8,128)(2,1)S(1)}, bf16[72,896]{1,0:T(8,128)(2,1)S(1)}, u32[]{:S(2)}, u32[]{:S(2)}) collective-permute-start(bf16[72,896]{1,0:T(8,128)(2,1)S(1)} %after.14.refs_0_), channel_id=1, source_target_pairs={{0,2},{2,0},{1,3},{3,1},{4,6},{6,4},{5,7},{7,5},{8,10},{10,8},{9,1... | collective-permute-start | bytes 387080 | tf_op jit(solution)/shard_map/rows2_tp/ppermute | solution.py:32
  23.0 6.8 %collective-permute-start.9 = (bf16[72,896]{1,0:T(8,128)(2,1)S(1)}, bf16[72,896]{1,0:T(8,128)(2,1)S(1)}, u32[]{:S(2)}, u32[]{:S(2)}) collective-permute-start(bf16[72,896]{1,0:T(8,128)(2,1)S(1)} %get-tuple-element.56), channel_id=1, source_target_pairs={{0,2},{2,0},{1,3},{3,1},{4,6},{6,4},{5,7},{7,5},{8,10},{10,8},{9,1... | collective-permute-start | bytes 387080 | tf_op jit(solution)/shard_map/back3_tp/ppermute | solution.py:32
  25.0 2.1 %collective-permute-start.14 = (bf16[72,512]{1,0:T(8,128)(2,1)S(1)}, bf16[72,512]{1,0:T(8,128)(2,1)S(1)}, u32[]{:S(2)}, u32[]{:S(2)}) collective-permute-start(bf16[72,512]{1,0:T(8,128)(2,1)S(1)} %get-tuple-element.61), channel_id=1, source_target_pairs={{0,1},{1,0},{2,3},{3,2},{4,5},{5,4},{6,7},{7,6},{8,9},{9,8},{10,11... | collective-permute-start | bytes 221192 | tf_op jit(solution)/shard_map/hidden1_sub/ppermute | solution.py:32
  27.1 4.9 %collective-permute-start.8 = (f32[88,512]{1,0:T(8,128)S(1)}, f32[88,512]{1,0:T(8,128)S(1)}, u32[]{:S(2)}, u32[]{:S(2)}) collective-permute-start(f32[88,512]{1,0:T(8,128)S(1)} %get-tuple-element.55), channel_id=1, source_target_pairs={{0,1},{1,0},{2,3},{3,2},{4,5},{5,4},{6,7},{7,6},{8,9},{9,8},{10,11... | collective-permute-start | bytes 540680 | tf_op jit(solution)/shard_map/hidden2_sub/ppermute | solution.py:32
  28.4 6.9 %collective-permute-start.15 = (bf16[72,896]{1,0:T(8,128)(2,1)S(1)}, bf16[72,896]{1,0:T(8,128)(2,1)S(1)}, u32[]{:S(2)}, u32[]{:S(2)}) collective-permute-start(bf16[72,896]{1,0:T(8,128)(2,1)S(1)} %get-tuple-element.63), channel_id=1, source_target_pairs={{0,2},{2,0},{1,3},{3,1},{4,6},{6,4},{5,7},{7,5},{8,10},{10,8},{9,1... | collective-permute-start | bytes 387080 | tf_op jit(solution)/shard_map/back1_tp/ppermute | solution.py:32
  29.8 12.0 %collective-permute-start.12 = (bf16[72,896]{1,0:T(8,128)(2,1)S(1)}, bf16[72,896]{1,0:T(8,128)(2,1)S(1)}, u32[]{:S(2)}, u32[]{:S(2)}) collective-permute-start(bf16[72,896]{1,0:T(8,128)(2,1)S(1)} %add_convert_fusion.2.earlier_ref), channel_id=1, source_target_pairs={{0,12},{4,8},{8,4},{12,0},{1,13},{5,9},{9,5},{13,1},{2,14},{6,10},... | collective-permute-start | bytes 387080 | tf_op jit(solution)/shard_map/back3_ep/ppermute | solution.py:32
  33.3 5.6 %collective-permute-start.10 = (bf16[72,896]{1,0:T(8,128)(2,1)S(1)}, bf16[72,896]{1,0:T(8,128)(2,1)S(1)}, u32[]{:S(2)}, u32[]{:S(2)}) collective-permute-start(bf16[72,896]{1,0:T(8,128)(2,1)S(1)} %get-tuple-element.58), channel_id=1, source_target_pairs={{0,2},{2,0},{1,3},{3,1},{4,6},{6,4},{5,7},{7,5},{8,10},{10,8},{9,1... | collective-permute-start | bytes 387080 | tf_op jit(solution)/shard_map/back2_tp/ppermute | solution.py:32
  35.4 6.4 %collective-permute-start.16 = (bf16[72,896]{1,0:T(8,128)(2,1)S(1)}, bf16[72,896]{1,0:T(8,128)(2,1)S(1)}, u32[]{:S(2)}, u32[]{:S(2)}) collective-permute-start(bf16[72,896]{1,0:T(8,128)(2,1)S(1)} %add_convert_fusion), channel_id=1, source_target_pairs={{0,4},{4,0},{8,12},{12,8},{1,5},{5,1},{9,13},{13,9},{2,6},{6,2},{1... | collective-permute-start | bytes 387080 | tf_op jit(solution)/shard_map/back1_ep/ppermute | solution.py:32
  38.9 8.5 %collective-permute-start.11 = (bf16[72,896]{1,0:T(8,128)(2,1)S(1)}, bf16[72,896]{1,0:T(8,128)(2,1)S(1)}, u32[]{:S(2)}, u32[]{:S(2)}) collective-permute-start(bf16[72,896]{1,0:T(8,128)(2,1)S(1)} %add_convert_fusion.1.earlier_ref), channel_id=1, source_target_pairs={{0,8},{4,12},{8,0},{12,4},{1,9},{5,13},{9,1},{13,5},{2,10},{6,14},... | collective-permute-start | bytes 387080 | tf_op jit(solution)/shard_map/back2_ep/ppermute | solution.py:32
  40.0 4.9 %collective-permute-start.13 = (bf16[72,896]{1,0:T(8,128)(2,1)S(1)}, bf16[72,896]{1,0:T(8,128)(2,1)S(1)}, u32[]{:S(2)}, u32[]{:S(2)}) collective-permute-start(bf16[72,896]{1,0:T(8,128)(2,1)S(1)} %after.20), channel_id=1, source_target_pairs={{0,2},{2,0},{1,3},{3,1},{4,6},{6,4},{5,7},{7,5},{8,10},{10,8},{9,1... | collective-permute-start | bytes 387080 | tf_op jit(solution)/shard_map/back0_tp/ppermute | solution.py:32

commit v15 on v14

--- a/solution.py
+++ b/solution.py
@@ -428,13 +428,13 @@
             summed, received = forward(
                 group, f32, earlier=gate_open, row_sums=[row_sums] if last else ()
             )
+            products = backward(group, summed, received)
+            gate_open = products[group[0]][:1]
+            moved = [give_back(k, products[k]) for k in group][0]
             if near:
-                products = backward([1], near_summed, after(near_received, summed))
+                products = backward([1], near_summed, after(near_received, gate_open[0], 0))
                 give_back(1, products[1])
                 near = False
-            products = backward(group, summed, after(received, moved))
-            gate_open = products[group[0]][:1]
-            moved = [give_back(k, products[k]) for k in group][0]
     else:
         for k in groups[0][1:-1]:
             give_back(k, products[k])
@@ -448,7 +448,7 @@
     d_latent = (
         inverse_rms * gained - values * inverse_rms**3 * row_sums[1][:, None] / LAT
     ).astype(bf16)
-    latest = groups[-1][:1] if staged else []
+    latest = [1, groups[-1][0]] if staged else []
     distances = [k for k in order if k not in latest]
     (grad_input,) = call(
         functools.partial(unpack_kernel, {k: len(returned[k]) for k in distances}, False),

time: 48.7 us -> 48.4 us (level)
  starting transfers between devices: 24 us -> 23 us
  waiting for transfers between devices: 9.6 us -> 10.3 us
    ppermute x17, starting transfers between devices: 24 us -> 23 us  [swap(): return lax.ppermute(value, tuple(steps), pairs)]
    ppermute x17, waiting for transfers between devices: 9.6 us -> 10.3 us  [swap(): return lax.ppermute(value, tuple(steps), pairs)]
  transfers between devices with their start and end apart: 17 -> 17, of which waited for: 6 -> 8; matrix products, arithmetic and copies ran while one was open for 2% -> 2% of each run, Pallas kernels for 21% -> 21%
where the time goes in v15:
time: 48.4 us; the launch traced here: 48.1 us
  starting transfers between devices  23 us (48%)
  Pallas kernels  13 us (27%)
  waiting for transfers between devices  10.3 us (21%)
  other arithmetic  1 us (2%)
  between operations  0.8 us (2%)
    ppermute x17, starting transfers between devices, swap(): return lax.ppermute(value, tuple(steps), pairs)  23 us
    pallas_call x11, Pallas kernels, call(): pl.pallas_call(kernel, out_shape=outs, in_specs=specs, out_specs=[VMEM] *...  13 us
    ppermute x17, waiting for transfers between devices, swap(): return lax.ppermute(value, tuple(steps), pairs)  10.3 us
  transfers between devices with their start and end apart: 17, of which 8 were waited for; matrix products, arithmetic and copies ran while one was open for 2% of the time, Pallas kernels for 21%

profile of v15, /device:TPU:0, one launch (start us, length us, event | category | flops | bytes accessed | tf_op | source)
XLA Modules:
  0.0 48.1 jit_solution(11208485406979928063)
XLA Ops:
  0.6 1.6 %pack.1 = (bf16[72,896]{1,0:T(8,128)(2,1)S(1)}, bf16[2,4,72,128]{3,2,1,0:T(8,128)(2,1)S(1)}, f32[1,128]{1,0:T(1,128)S(1)}, f32[14,128]{1,0:T(8,128)S(1)}, bf16[128,1792]{1,0:T(8,128)(2,1)S(1)}) custom-call(s32[1,128]{1,0:T(1,128)} %bitcast.30, f32[1,128]{1,0:T(1,128)} %bitcast.31, f32[14,128]{1,0:T(8,128)} %bitcast.24, bf16[128,1792]{1,0:T(8,128)(2,1)} %refs_3_.1), custom_call_target="tpu_custom_call" | custom-call | tf_op jit(solution)/shard_map/pack/pallas_call | solution.py:51
  2.2 5.1 %collective-permute-start.1 = (bf16[72,896]{1,0:T(8,128)(2,1)S(1)}, bf16[72,896]{1,0:T(8,128)(2,1)S(1)}, u32[]{:S(2)}, u32[]{:S(2)}) collective-permute-start(bf16[72,896]{1,0:T(8,128)(2,1)S(1)} %get-tuple-element.38.earlier_ref), channel_id=1, source_target_pairs={{0,12},{4,8},{8,4},{12,0},{1,13},{5,9},{9,5},{13,1},{2,14},{6,10},... | collective-permute-start | bytes 387080 | tf_op jit(solution)/shard_map/rows3_ep/ppermute | solution.py:32
  7.4 1.1 %pack_more.1 = (bf16[72,896]{1,0:T(8,128)(2,1)S(1)}, bf16[72,896]{1,0:T(8,128)(2,1)S(1)}, bf16[72,896]{1,0:T(8,128)(2,1)S(1)}, bf16[120,896]{1,0:T(8,128)(2,1)S(1)}, bf16[128,256]{1,0:T(8,128)(2,1)S(1)}) custom-call(bf16[2,4,72,128]{3,2,1,0:T(8,128)(2,1)S(1)} %get-tuple-element.33.place_ref.earlier_ref, f32[1,128]{1,0:T(1,128)S(1)} %get-tuple-element.34.weights_ref, ...), custom_call_target="tpu_custom_call" | custom-call | tf_op jit(solution)/shard_map/pack_more/pallas_call | solution.py:51
  8.5 1.6 %collective-permute-start.4 = (bf16[120,896]{1,0:T(8,128)(2,1)S(1)}, bf16[120,896]{1,0:T(8,128)(2,1)S(1)}, u32[]{:S(2)}, u32[]{:S(2)}) collective-permute-start(bf16[120,896]{1,0:T(8,128)(2,1)S(1)} %get-tuple-element.41), channel_id=1, source_target_pairs={{0,2},{2,0},{1,3},{3,1},{4,6},{6,4},{5,7},{7,5},{8,10},{10,8},{9,1... | collective-permute-start | bytes 645128 | tf_op jit(solution)/shard_map/rows0_tp/ppermute | solution.py:32
  10.0 0.9 %collective-permute-done.1.refs_6_.refs_0_.earlier_ref = bf16[72,896]{1,0:T(8,128)(2,1)S(1)} collective-permute-done((bf16[72,896]{1,0:T(8,128)(2,1)S(1)}, bf16[72,896]{1,0:T(8,128)(2,1)S(1)}, u32[]{:S(2)}, u32[]{:S(2)}) %collective-permute-start.1) | collective-permute-done | bytes 129056 | tf_op jit(solution)/shard_map/rows3_ep/ppermute | solution.py:32
  10.9 2.5 %collective-permute-start.3 = (bf16[72,896]{1,0:T(8,128)(2,1)S(1)}, bf16[72,896]{1,0:T(8,128)(2,1)S(1)}, u32[]{:S(2)}, u32[]{:S(2)}) collective-permute-start(bf16[72,896]{1,0:T(8,128)(2,1)S(1)} %collective-permute-done.1.refs_6_.refs_0_.earlier_ref), channel_id=1, source_target_pairs={{0,2},{2,0},{1,3},{3,1},{4,6},{6,4},{5,7},{7,5},{8,10},{10,8},{9,1... | collective-permute-start | bytes 387080 | tf_op jit(solution)/shard_map/rows3_tp/ppermute | solution.py:32
  13.4 2.1 %collective-permute-start.7 = (bf16[72,896]{1,0:T(8,128)(2,1)S(1)}, bf16[72,896]{1,0:T(8,128)(2,1)S(1)}, u32[]{:S(2)}, u32[]{:S(2)}) collective-permute-start(bf16[72,896]{1,0:T(8,128)(2,1)S(1)} %after.13), channel_id=1, source_target_pairs={{0,8},{4,12},{8,0},{12,4},{1,9},{5,13},{9,1},{13,5},{2,10},{6,14},... | collective-permute-start | bytes 387080 | tf_op jit(solution)/shard_map/rows2_ep/ppermute | solution.py:32
  15.5 2.9 %fetch.1 = (f32[4,72,512]{2,1,0:T(8,128)S(1)}, f32[4,72,512]{2,1,0:T(8,128)S(1)}, bf16[512,1792]{1,0:T(8,128)(2,1)S(1)}, bf16[1792,512]{1,0:T(8,128)(2,1)S(1)}, ...) custom-call(bf16[2,4,72,512]{3,2,1,0:T(8,128)(2,1)} %bitcast.22, ...), custom_call_target="tpu_custom_call" | custom-call | tf_op jit(solution)/shard_map/fetch/pallas_call | solution.py:51
  18.4 0.9 %collective-permute-start.2 = (bf16[72,896]{1,0:T(8,128)(2,1)S(1)}, bf16[72,896]{1,0:T(8,128)(2,1)S(1)}, u32[]{:S(2)}, u32[]{:S(2)}) collective-permute-start(bf16[72,896]{1,0:T(8,128)(2,1)S(1)} %after.10.refs_0_), channel_id=1, source_target_pairs={{0,2},{2,0},{1,3},{3,1},{4,6},{6,4},{5,7},{7,5},{8,10},{10,8},{9,1... | collective-permute-start | bytes 387080 | tf_op jit(solution)/shard_map/rows1_tp/ppermute | solution.py:32
  20.6 0.9 %collective-permute-start.8 = (bf16[72,896]{1,0:T(8,128)(2,1)S(1)}, bf16[72,896]{1,0:T(8,128)(2,1)S(1)}, u32[]{:S(2)}, u32[]{:S(2)}) collective-permute-start(bf16[72,896]{1,0:T(8,128)(2,1)S(1)} %after.15.refs_0_), channel_id=1, source_target_pairs={{0,2},{2,0},{1,3},{3,1},{4,6},{6,4},{5,7},{7,5},{8,10},{10,8},{9,1... | collective-permute-start | bytes 387080 | tf_op jit(solution)/shard_map/rows2_tp/ppermute | solution.py:32
  21.7 1.3 %back.3 = (bf16[72,896]{1,0:T(8,128)(2,1)S(1)}, bf16[72,896]{1,0:T(8,128)(2,1)S(1)}, bf16[72,896]{1,0:T(8,128)(2,1)S(1)}, bf16[72,896]{1,0:T(8,128)(2,1)S(1)}) custom-call(f32[144,512]{1,0:T(8,128)S(1)} %get-tuple-element.42.sum_ref.earlier_ref, f32[144,512]{1,0:T(8,128)S(1)} %collective-permute-done.5.other_ref, ...), custom_call_target="tpu_custom_call" | custom-call | tf_op jit(solution)/shard_map/back/pallas_call | solution.py:51
  23.0 1.4 %collective-permute-start.14 = (bf16[72,896]{1,0:T(8,128)(2,1)S(1)}, bf16[72,896]{1,0:T(8,128)(2,1)S(1)}, u32[]{:S(2)}, u32[]{:S(2)}) collective-permute-start(bf16[72,896]{1,0:T(8,128)(2,1)S(1)} %get-tuple-element.61), channel_id=1, source_target_pairs={{0,2},{2,0},{1,3},{3,1},{4,6},{6,4},{5,7},{7,5},{8,10},{10,8},{9,1... | collective-permute-start | bytes 387080 | tf_op jit(solution)/shard_map/back3_tp/ppermute | solution.py:32
  25.1 1.3 %collective-permute-done.8.value_ref = bf16[72,896]{1,0:T(8,128)(2,1)S(1)} collective-permute-done((bf16[72,896]{1,0:T(8,128)(2,1)S(1)}, bf16[72,896]{1,0:T(8,128)(2,1)S(1)}, u32[]{:S(2)}, u32[]{:S(2)}) %collective-permute-start.8) | collective-permute-done | bytes 129056 | tf_op jit(solution)/shard_map/rows2_tp/ppermute | solution.py:32
  27.6 1.3 %collective-permute-done.14 = bf16[72,896]{1,0:T(8,128)(2,1)S(1)} collective-permute-done((bf16[72,896]{1,0:T(8,128)(2,1)S(1)}, bf16[72,896]{1,0:T(8,128)(2,1)S(1)}, u32[]{:S(2)}, u32[]{:S(2)}) %collective-permute-start.14) | collective-permute-done | bytes 129056 | tf_op jit(solution)/shard_map/back3_tp/ppermute | solution.py:32
  28.9 2.5 %collective-permute-start.15 = (bf16[72,896]{1,0:T(8,128)(2,1)S(1)}, bf16[72,896]{1,0:T(8,128)(2,1)S(1)}, u32[]{:S(2)}, u32[]{:S(2)}) collective-permute-start(bf16[72,896]{1,0:T(8,128)(2,1)S(1)} %add_convert_fusion), channel_id=1, source_target_pairs={{0,12},{4,8},{8,4},{12,0},{1,13},{5,9},{9,5},{13,1},{2,14},{6,10},... | collective-permute-start | bytes 387080 | tf_op jit(solution)/shard_map/back3_ep/ppermute | solution.py:32
  31.5 1.2 %back.4 = (bf16[72,896]{1,0:T(8,128)(2,1)S(1)}, bf16[72,896]{1,0:T(8,128)(2,1)S(1)}) custom-call(f32[72,512]{1,0:T(8,128)S(1)} %get-tuple-element.55.sum_ref, f32[88,512]{1,0:T(8,128)S(1)} %collective-permute-done.9.other_ref, f32[4,72,512]{2,1,0:T(8,128)S(1)} %get-tuple-element.44.up_by_ref, f32[4,72,512]{2,1,0:T(8,128)S(1)} %get-tuple-element.45.gate_by_ref, ...), custom_call_target="tpu_custom_call" | custom-call | tf_op jit(solution)/shard_map/back/pallas_call | solution.py:51
  33.5 1.2 %back.5 = (bf16[72,896]{1,0:T(8,128)(2,1)S(1)}, bf16[72,896]{1,0:T(8,128)(2,1)S(1)}) custom-call(f32[72,512]{1,0:T(8,128)S(1)} %get-tuple-element.49.earlier_ref.refs_4_.sum_ref, bf16[72,512]{1,0:T(8,128)(2,1)S(1)} %after.18.other_ref, f32[4,72,512]{2,1,0:T(8,128)S(1)} %get-tuple-element.44.up_by_ref, f32[4,72,512]{2,1,0:T(8,128)S(1)} %get-tuple-element.45.gate_by_ref, ...), custom_call_target="tpu_custom_call" | custom-call | tf_op jit(solution)/shard_map/back/pallas_call | solution.py:51
  34.7 1.4 %collective-permute-start.10 = (bf16[72,896]{1,0:T(8,128)(2,1)S(1)}, bf16[72,896]{1,0:T(8,128)(2,1)S(1)}, u32[]{:S(2)}, u32[]{:S(2)}) collective-permute-start(bf16[72,896]{1,0:T(8,128)(2,1)S(1)} %get-tuple-element.59), channel_id=1, source_target_pairs={{0,2},{2,0},{1,3},{3,1},{4,6},{6,4},{5,7},{7,5},{8,10},{10,8},{9,1... | collective-permute-start | bytes 387080 | tf_op jit(solution)/shard_map/back1_tp/ppermute | solution.py:32
  36.1 2.9 %collective-permute-done.12 = bf16[72,896]{1,0:T(8,128)(2,1)S(1)} collective-permute-done((bf16[72,896]{1,0:T(8,128)(2,1)S(1)}, bf16[72,896]{1,0:T(8,128)(2,1)S(1)}, u32[]{:S(2)}, u32[]{:S(2)}) %collective-permute-start.12) | collective-permute-done | bytes 129056 | tf_op jit(solution)/shard_map/back2_tp/ppermute | solution.py:32
  39.8 1.3 %collective-permute-start.16 = (bf16[72,896]{1,0:T(8,128)(2,1)S(1)}, bf16[72,896]{1,0:T(8,128)(2,1)S(1)}, u32[]{:S(2)}, u32[]{:S(2)}) collective-permute-start(bf16[72,896]{1,0:T(8,128)(2,1)S(1)} %after.19), channel_id=1, source_target_pairs={{0,2},{2,0},{1,3},{3,1},{4,6},{6,4},{5,7},{7,5},{8,10},{10,8},{9,1... | collective-permute-start | bytes 387080 | tf_op jit(solution)/shard_map/back0_tp/ppermute | solution.py:32
  41.1 1.2 %collective-permute-start.11 = (bf16[72,896]{1,0:T(8,128)(2,1)S(1)}, bf16[72,896]{1,0:T(8,128)(2,1)S(1)}, u32[]{:S(2)}, u32[]{:S(2)}) collective-permute-start(bf16[72,896]{1,0:T(8,128)(2,1)S(1)} %add_convert_fusion.2), channel_id=1, source_target_pairs={{0,4},{4,0},{8,12},{12,8},{1,5},{5,1},{9,13},{13,9},{2,6},{6,2},{1... | collective-permute-start | bytes 387080 | tf_op jit(solution)/shard_map/back1_ep/ppermute | solution.py:32
  43.1 1.7 %collective-permute-done.16.refs_2_ = bf16[72,896]{1,0:T(8,128)(2,1)S(1)} collective-permute-done((bf16[72,896]{1,0:T(8,128)(2,1)S(1)}, bf16[72,896]{1,0:T(8,128)(2,1)S(1)}, u32[]{:S(2)}, u32[]{:S(2)}) %collective-permute-start.16) | collective-permute-done | bytes 129056 | tf_op jit(solution)/shard_map/back0_tp/ppermute | solution.py:32
  45.7 1.2 %collective-permute-done.11.refs_0_ = bf16[72,896]{1,0:T(8,128)(2,1)S(1)} collective-permute-done((bf16[72,896]{1,0:T(8,128)(2,1)S(1)}, bf16[72,896]{1,0:T(8,128)(2,1)S(1)}, u32[]{:S(2)}, u32[]{:S(2)}) %collective-permute-start.11) | collective-permute-done | bytes 129056 | tf_op jit(solution)/shard_map/back1_ep/ppermute | solution.py:32
  46.9 1.2 %unpack_latest.1 = bf16[128,1792]{1,0:T(8,128)(2,1)} custom-call(bf16[2,4,72,128]{3,2,1,0:T(8,128)(2,1)S(1)} %get-tuple-element.33.place_ref.earlier_ref, bf16[72,896]{1,0:T(8,128)(2,1)S(1)} %collective-permute-done.11.refs_0_, bf16[72,896]{1,0:T(8,128)(2,1)S(1)} %collective-permute-done.13.refs_1_, bf16[128,1792]{1,0:T(8,128)(2,1)S(1)} %unpack.1.refs_2_), custom_call_target="tpu_custom_call" | custom-call | tf_op jit(solution)/shard_map/unpack_latest/pallas_call | solution.py:51
  (42 shorter events, 6.8 us)
Async XLA Ops:
  2.2 8.7 %collective-permute-start.1 = (bf16[72,896]{1,0:T(8,128)(2,1)S(1)}, bf16[72,896]{1,0:T(8,128)(2,1)S(1)}, u32[]{:S(2)}, u32[]{:S(2)}) collective-permute-start(bf16[72,896]{1,0:T(8,128)(2,1)S(1)} %get-tuple-element.38.earlier_ref), channel_id=1, source_target_pairs={{0,12},{4,8},{8,4},{12,0},{1,13},{5,9},{9,5},{13,1},{2,14},{6,10},... | collective-permute-start | bytes 387080 | tf_op jit(solution)/shard_map/rows3_ep/ppermute | solution.py:32
  8.5 10.8 %collective-permute-start.4 = (bf16[120,896]{1,0:T(8,128)(2,1)S(1)}, bf16[120,896]{1,0:T(8,128)(2,1)S(1)}, u32[]{:S(2)}, u32[]{:S(2)}) collective-permute-start(bf16[120,896]{1,0:T(8,128)(2,1)S(1)} %get-tuple-element.41), channel_id=1, source_target_pairs={{0,2},{2,0},{1,3},{3,1},{4,6},{6,4},{5,7},{7,5},{8,10},{10,8},{9,1... | collective-permute-start | bytes 645128 | tf_op jit(solution)/shard_map/rows0_tp/ppermute | solution.py:32
  10.0 8.3 %collective-permute-start = (bf16[72,896]{1,0:T(8,128)(2,1)S(1)}, bf16[72,896]{1,0:T(8,128)(2,1)S(1)}, u32[]{:S(2)}, u32[]{:S(2)}) collective-permute-start(bf16[72,896]{1,0:T(8,128)(2,1)S(1)} %get-tuple-element.37), channel_id=1, source_target_pairs={{0,4},{4,0},{8,12},{12,8},{1,5},{5,1},{9,13},{13,9},{2,6},{6,2},{1... | collective-permute-start | bytes 387080 | tf_op jit(solution)/shard_map/rows1_ep/ppermute | solution.py:32
  10.9 8.4 %collective-permute-start.3 = (bf16[72,896]{1,0:T(8,128)(2,1)S(1)}, bf16[72,896]{1,0:T(8,128)(2,1)S(1)}, u32[]{:S(2)}, u32[]{:S(2)}) collective-permute-start(bf16[72,896]{1,0:T(8,128)(2,1)S(1)} %collective-permute-done.1.refs_6_.refs_0_.earlier_ref), channel_id=1, source_target_pairs={{0,2},{2,0},{1,3},{3,1},{4,6},{6,4},{5,7},{7,5},{8,10},{10,8},{9,1... | collective-permute-start | bytes 387080 | tf_op jit(solution)/shard_map/rows3_tp/ppermute | solution.py:32
  13.4 7.2 %collective-permute-start.7 = (bf16[72,896]{1,0:T(8,128)(2,1)S(1)}, bf16[72,896]{1,0:T(8,128)(2,1)S(1)}, u32[]{:S(2)}, u32[]{:S(2)}) collective-permute-start(bf16[72,896]{1,0:T(8,128)(2,1)S(1)} %after.13), channel_id=1, source_target_pairs={{0,8},{4,12},{8,0},{12,4},{1,9},{5,13},{9,1},{13,5},{2,10},{6,14},... | collective-permute-start | bytes 387080 | tf_op jit(solution)/shard_map/rows2_ep/ppermute | solution.py:32
  18.4 6.0 %collective-permute-start.2 = (bf16[72,896]{1,0:T(8,128)(2,1)S(1)}, bf16[72,896]{1,0:T(8,128)(2,1)S(1)}, u32[]{:S(2)}, u32[]{:S(2)}) collective-permute-start(bf16[72,896]{1,0:T(8,128)(2,1)S(1)} %after.10.refs_0_), channel_id=1, source_target_pairs={{0,2},{2,0},{1,3},{3,1},{4,6},{6,4},{5,7},{7,5},{8,10},{10,8},{9,1... | collective-permute-start | bytes 387080 | tf_op jit(solution)/shard_map/rows1_tp/ppermute | solution.py:32
  20.0 1.7 %collective-permute-start.5 = (f32[144,512]{1,0:T(8,128)S(1)}, f32[144,512]{1,0:T(8,128)S(1)}, u32[]{:S(2)}, u32[]{:S(2)}) collective-permute-start(f32[144,512]{1,0:T(8,128)S(1)} %get-tuple-element.43), channel_id=1, source_target_pairs={{0,1},{1,0},{2,3},{3,2},{4,5},{5,4},{6,7},{7,6},{8,9},{9,8},{10,11... | collective-permute-start | bytes 884744 | tf_op jit(solution)/shard_map/hidden3_sub/ppermute | solution.py:32
  20.6 5.7 %collective-permute-start.8 = (bf16[72,896]{1,0:T(8,128)(2,1)S(1)}, bf16[72,896]{1,0:T(8,128)(2,1)S(1)}, u32[]{:S(2)}, u32[]{:S(2)}) collective-permute-start(bf16[72,896]{1,0:T(8,128)(2,1)S(1)} %after.15.refs_0_), channel_id=1, source_target_pairs={{0,2},{2,0},{1,3},{3,1},{4,6},{6,4},{5,7},{7,5},{8,10},{10,8},{9,1... | collective-permute-start | bytes 387080 | tf_op jit(solution)/shard_map/rows2_tp/ppermute | solution.py:32
  23.0 5.9 %collective-permute-start.14 = (bf16[72,896]{1,0:T(8,128)(2,1)S(1)}, bf16[72,896]{1,0:T(8,128)(2,1)S(1)}, u32[]{:S(2)}, u32[]{:S(2)}) collective-permute-start(bf16[72,896]{1,0:T(8,128)(2,1)S(1)} %get-tuple-element.61), channel_id=1, source_target_pairs={{0,2},{2,0},{1,3},{3,1},{4,6},{6,4},{5,7},{7,5},{8,10},{10,8},{9,1... | collective-permute-start | bytes 387080 | tf_op jit(solution)/shard_map/back3_tp/ppermute | solution.py:32
  27.0 4.4 %collective-permute-start.9 = (f32[88,512]{1,0:T(8,128)S(1)}, f32[88,512]{1,0:T(8,128)S(1)}, u32[]{:S(2)}, u32[]{:S(2)}) collective-permute-start(f32[88,512]{1,0:T(8,128)S(1)} %get-tuple-element.56), channel_id=1, source_target_pairs={{0,1},{1,0},{2,3},{3,2},{4,5},{5,4},{6,7},{7,6},{8,9},{9,8},{10,11... | collective-permute-start | bytes 540680 | tf_op jit(solution)/shard_map/hidden2_sub/ppermute | solution.py:32
  27.1 6.4 %collective-permute-start.6 = (bf16[72,512]{1,0:T(8,128)(2,1)S(1)}, bf16[72,512]{1,0:T(8,128)(2,1)S(1)}, u32[]{:S(2)}, u32[]{:S(2)}) collective-permute-start(bf16[72,512]{1,0:T(8,128)(2,1)S(1)} %get-tuple-element.50), channel_id=1, source_target_pairs={{0,1},{1,0},{2,3},{3,2},{4,5},{5,4},{6,7},{7,6},{8,9},{9,8},{10,11... | collective-permute-start | bytes 221192 | tf_op jit(solution)/shard_map/hidden1_sub/ppermute | solution.py:32
  28.9 14.2 %collective-permute-start.15 = (bf16[72,896]{1,0:T(8,128)(2,1)S(1)}, bf16[72,896]{1,0:T(8,128)(2,1)S(1)}, u32[]{:S(2)}, u32[]{:S(2)}) collective-permute-start(bf16[72,896]{1,0:T(8,128)(2,1)S(1)} %add_convert_fusion), channel_id=1, source_target_pairs={{0,12},{4,8},{8,4},{12,0},{1,13},{5,9},{9,5},{13,1},{2,14},{6,10},... | collective-permute-start | bytes 387080 | tf_op jit(solution)/shard_map/back3_ep/ppermute | solution.py:32
  32.7 6.3 %collective-permute-start.12 = (bf16[72,896]{1,0:T(8,128)(2,1)S(1)}, bf16[72,896]{1,0:T(8,128)(2,1)S(1)}, u32[]{:S(2)}, u32[]{:S(2)}) collective-permute-start(bf16[72,896]{1,0:T(8,128)(2,1)S(1)} %get-tuple-element.60), channel_id=1, source_target_pairs={{0,2},{2,0},{1,3},{3,1},{4,6},{6,4},{5,7},{7,5},{8,10},{10,8},{9,1... | collective-permute-start | bytes 387080 | tf_op jit(solution)/shard_map/back2_tp/ppermute | solution.py:32
  34.7 6.4 %collective-permute-start.10 = (bf16[72,896]{1,0:T(8,128)(2,1)S(1)}, bf16[72,896]{1,0:T(8,128)(2,1)S(1)}, u32[]{:S(2)}, u32[]{:S(2)}) collective-permute-start(bf16[72,896]{1,0:T(8,128)(2,1)S(1)} %get-tuple-element.59), channel_id=1, source_target_pairs={{0,2},{2,0},{1,3},{3,1},{4,6},{6,4},{5,7},{7,5},{8,10},{10,8},{9,1... | collective-permute-start | bytes 387080 | tf_op jit(solution)/shard_map/back1_tp/ppermute | solution.py:32
  39.0 6.7 %collective-permute-start.13 = (bf16[72,896]{1,0:T(8,128)(2,1)S(1)}, bf16[72,896]{1,0:T(8,128)(2,1)S(1)}, u32[]{:S(2)}, u32[]{:S(2)}) collective-permute-start(bf16[72,896]{1,0:T(8,128)(2,1)S(1)} %add_convert_fusion.1.earlier_ref), channel_id=1, source_target_pairs={{0,8},{4,12},{8,0},{12,4},{1,9},{5,13},{9,1},{13,5},{2,10},{6,14},... | collective-permute-start | bytes 387080 | tf_op jit(solution)/shard_map/back2_ep/ppermute | solution.py:32
  39.8 4.9 %collective-permute-start.16 = (bf16[72,896]{1,0:T(8,128)(2,1)S(1)}, bf16[72,896]{1,0:T(8,128)(2,1)S(1)}, u32[]{:S(2)}, u32[]{:S(2)}) collective-permute-start(bf16[72,896]{1,0:T(8,128)(2,1)S(1)} %after.19), channel_id=1, source_target_pairs={{0,2},{2,0},{1,3},{3,1},{4,6},{6,4},{5,7},{7,5},{8,10},{10,8},{9,1... | collective-permute-start | bytes 387080 | tf_op jit(solution)/shard_map/back0_tp/ppermute | solution.py:32
  41.1 5.8 %collective-permute-start.11 = (bf16[72,896]{1,0:T(8,128)(2,1)S(1)}, bf16[72,896]{1,0:T(8,128)(2,1)S(1)}, u32[]{:S(2)}, u32[]{:S(2)}) collective-permute-start(bf16[72,896]{1,0:T(8,128)(2,1)S(1)} %add_convert_fusion.2), channel_id=1, source_target_pairs={{0,4},{4,0},{8,12},{12,8},{1,5},{5,1},{9,13},{13,9},{2,6},{6,2},{1... | collective-permute-start | bytes 387080 | tf_op jit(solution)/shard_map/back1_ep/ppermute | solution.py:32

commit v16 on v15

--- a/solution.py
+++ b/solution.py
@@ -439,7 +439,7 @@
         for k in groups[0][1:-1]:
             give_back(k, products[k])
     returned[0] = [kept[0]] + [
-        swap(after(kept[j], moved) if staged else kept[j], "back0", tp=j) for j in range(1, narrow)
+        swap(after(kept[j], summed) if staged else kept[j], "back0", tp=j) for j in range(1, narrow)
     ]
     count = summed.shape[0]
     tail = received[count : count + 4, :tokens].astype(f32)

time: 48.4 us -> 48.7 us (level)
  waiting for transfers between devices: 10.3 us -> 10.8 us
    ppermute x17, waiting for transfers between devices: 10.3 us -> 10.8 us  [swap(): return lax.ppermute(value, tuple(steps), pairs)]
where the time goes in v16:
time: 48.7 us; the launch traced here: 48.5 us
  starting transfers between devices  22.9 us (47%)
  Pallas kernels  13 us (27%)
  waiting for transfers between devices  10.8 us (22%)
  other arithmetic  1 us (2%)
  between operations  0.8 us (2%)
    ppermute x17, starting transfers between devices, swap(): return lax.ppermute(value, tuple(steps), pairs)  22.9 us
    pallas_call x11, Pallas kernels, call(): pl.pallas_call(kernel, out_shape=outs, in_specs=specs, out_specs=[VMEM] *...  13 us
    ppermute x17, waiting for transfers between devices, swap(): return lax.ppermute(value, tuple(steps), pairs)  10.8 us
  transfers between devices with their start and end apart: 17, of which 8 were waited for; matrix products, arithmetic and copies ran while one was open for 2% of the time, Pallas kernels for 21%

profile of v16, /device:TPU:0, one launch (start us, length us, event | category | flops | bytes accessed | tf_op | source)
XLA Modules:
  0.0 48.5 jit_solution(14713808867020182347)
XLA Ops:
  0.6 1.6 %pack.1 = (bf16[72,896]{1,0:T(8,128)(2,1)S(1)}, bf16[2,4,72,128]{3,2,1,0:T(8,128)(2,1)S(1)}, f32[1,128]{1,0:T(1,128)S(1)}, f32[14,128]{1,0:T(8,128)S(1)}, bf16[128,1792]{1,0:T(8,128)(2,1)S(1)}) custom-call(s32[1,128]{1,0:T(1,128)} %bitcast.30, f32[1,128]{1,0:T(1,128)} %bitcast.31, f32[14,128]{1,0:T(8,128)} %bitcast.24, bf16[128,1792]{1,0:T(8,128)(2,1)} %refs_3_.1), custom_call_target="tpu_custom_call" | custom-call | tf_op jit(solution)/shard_map/pack/pallas_call | solution.py:51
  2.2 5.1 %collective-permute-start.1 = (bf16[72,896]{1,0:T(8,128)(2,1)S(1)}, bf16[72,896]{1,0:T(8,128)(2,1)S(1)}, u32[]{:S(2)}, u32[]{:S(2)}) collective-permute-start(bf16[72,896]{1,0:T(8,128)(2,1)S(1)} %get-tuple-element.38.earlier_ref), channel_id=1, source_target_pairs={{0,12},{4,8},{8,4},{12,0},{1,13},{5,9},{9,5},{13,1},{2,14},{6,10},... | collective-permute-start | bytes 387080 | tf_op jit(solution)/shard_map/rows3_ep/ppermute | solution.py:32
  7.4 1.1 %pack_more.1 = (bf16[72,896]{1,0:T(8,128)(2,1)S(1)}, bf16[72,896]{1,0:T(8,128)(2,1)S(1)}, bf16[72,896]{1,0:T(8,128)(2,1)S(1)}, bf16[120,896]{1,0:T(8,128)(2,1)S(1)}, bf16[128,256]{1,0:T(8,128)(2,1)S(1)}) custom-call(bf16[2,4,72,128]{3,2,1,0:T(8,128)(2,1)S(1)} %get-tuple-element.33.place_ref.earlier_ref, f32[1,128]{1,0:T(1,128)S(1)} %get-tuple-element.34.weights_ref, ...), custom_call_target="tpu_custom_call" | custom-call | tf_op jit(solution)/shard_map/pack_more/pallas_call | solution.py:51
  8.5 1.6 %collective-permute-start.4 = (bf16[120,896]{1,0:T(8,128)(2,1)S(1)}, bf16[120,896]{1,0:T(8,128)(2,1)S(1)}, u32[]{:S(2)}, u32[]{:S(2)}) collective-permute-start(bf16[120,896]{1,0:T(8,128)(2,1)S(1)} %get-tuple-element.41), channel_id=1, source_target_pairs={{0,2},{2,0},{1,3},{3,1},{4,6},{6,4},{5,7},{7,5},{8,10},{10,8},{9,1... | collective-permute-start | bytes 645128 | tf_op jit(solution)/shard_map/rows0_tp/ppermute | solution.py:32
  10.0 0.9 %collective-permute-done.1.refs_6_.refs_0_.earlier_ref = bf16[72,896]{1,0:T(8,128)(2,1)S(1)} collective-permute-done((bf16[72,896]{1,0:T(8,128)(2,1)S(1)}, bf16[72,896]{1,0:T(8,128)(2,1)S(1)}, u32[]{:S(2)}, u32[]{:S(2)}) %collective-permute-start.1) | collective-permute-done | bytes 129056 | tf_op jit(solution)/shard_map/rows3_ep/ppermute | solution.py:32
  10.9 2.5 %collective-permute-start.3 = (bf16[72,896]{1,0:T(8,128)(2,1)S(1)}, bf16[72,896]{1,0:T(8,128)(2,1)S(1)}, u32[]{:S(2)}, u32[]{:S(2)}) collective-permute-start(bf16[72,896]{1,0:T(8,128)(2,1)S(1)} %collective-permute-done.1.refs_6_.refs_0_.earlier_ref), channel_id=1, source_target_pairs={{0,2},{2,0},{1,3},{3,1},{4,6},{6,4},{5,7},{7,5},{8,10},{10,8},{9,1... | collective-permute-start | bytes 387080 | tf_op jit(solution)/shard_map/rows3_tp/ppermute | solution.py:32
  13.4 2.1 %collective-permute-start.7 = (bf16[72,896]{1,0:T(8,128)(2,1)S(1)}, bf16[72,896]{1,0:T(8,128)(2,1)S(1)}, u32[]{:S(2)}, u32[]{:S(2)}) collective-permute-start(bf16[72,896]{1,0:T(8,128)(2,1)S(1)} %after.13), channel_id=1, source_target_pairs={{0,8},{4,12},{8,0},{12,4},{1,9},{5,13},{9,1},{13,5},{2,10},{6,14},... | collective-permute-start | bytes 387080 | tf_op jit(solution)/shard_map/rows2_ep/ppermute | solution.py:32
  15.5 2.9 %fetch.1 = (f32[4,72,512]{2,1,0:T(8,128)S(1)}, f32[4,72,512]{2,1,0:T(8,128)S(1)}, bf16[512,1792]{1,0:T(8,128)(2,1)S(1)}, bf16[1792,512]{1,0:T(8,128)(2,1)S(1)}, ...) custom-call(bf16[2,4,72,512]{3,2,1,0:T(8,128)(2,1)} %bitcast.22, ...), custom_call_target="tpu_custom_call" | custom-call | tf_op jit(solution)/shard_map/fetch/pallas_call | solution.py:51
  18.4 0.9 %collective-permute-start.2 = (bf16[72,896]{1,0:T(8,128)(2,1)S(1)}, bf16[72,896]{1,0:T(8,128)(2,1)S(1)}, u32[]{:S(2)}, u32[]{:S(2)}) collective-permute-start(bf16[72,896]{1,0:T(8,128)(2,1)S(1)} %after.10.refs_0_), channel_id=1, source_target_pairs={{0,2},{2,0},{1,3},{3,1},{4,6},{6,4},{5,7},{7,5},{8,10},{10,8},{9,1... | collective-permute-start | bytes 387080 | tf_op jit(solution)/shard_map/rows1_tp/ppermute | solution.py:32
  20.6 0.9 %collective-permute-start.8 = (bf16[72,896]{1,0:T(8,128)(2,1)S(1)}, bf16[72,896]{1,0:T(8,128)(2,1)S(1)}, u32[]{:S(2)}, u32[]{:S(2)}) collective-permute-start(bf16[72,896]{1,0:T(8,128)(2,1)S(1)} %after.15.refs_0_), channel_id=1, source_target_pairs={{0,2},{2,0},{1,3},{3,1},{4,6},{6,4},{5,7},{7,5},{8,10},{10,8},{9,1... | collective-permute-start | bytes 387080 | tf_op jit(solution)/shard_map/rows2_tp/ppermute | solution.py:32
  21.7 1.3 %back.3 = (bf16[72,896]{1,0:T(8,128)(2,1)S(1)}, bf16[72,896]{1,0:T(8,128)(2,1)S(1)}, bf16[72,896]{1,0:T(8,128)(2,1)S(1)}, bf16[72,896]{1,0:T(8,128)(2,1)S(1)}) custom-call(f32[144,512]{1,0:T(8,128)S(1)} %get-tuple-element.42.sum_ref.earlier_ref, f32[144,512]{1,0:T(8,128)S(1)} %collective-permute-done.5.other_ref, ...), custom_call_target="tpu_custom_call" | custom-call | tf_op jit(solution)/shard_map/back/pallas_call | solution.py:51
  23.0 1.4 %collective-permute-start.14 = (bf16[72,896]{1,0:T(8,128)(2,1)S(1)}, bf16[72,896]{1,0:T(8,128)(2,1)S(1)}, u32[]{:S(2)}, u32[]{:S(2)}) collective-permute-start(bf16[72,896]{1,0:T(8,128)(2,1)S(1)} %get-tuple-element.61), channel_id=1, source_target_pairs={{0,2},{2,0},{1,3},{3,1},{4,6},{6,4},{5,7},{7,5},{8,10},{10,8},{9,1... | collective-permute-start | bytes 387080 | tf_op jit(solution)/shard_map/back3_tp/ppermute | solution.py:32
  25.1 1.3 %collective-permute-done.8.value_ref = bf16[72,896]{1,0:T(8,128)(2,1)S(1)} collective-permute-done((bf16[72,896]{1,0:T(8,128)(2,1)S(1)}, bf16[72,896]{1,0:T(8,128)(2,1)S(1)}, u32[]{:S(2)}, u32[]{:S(2)}) %collective-permute-start.8) | collective-permute-done | bytes 129056 | tf_op jit(solution)/shard_map/rows2_tp/ppermute | solution.py:32
  27.1 1.4 %collective-permute-start.16 = (bf16[72,896]{1,0:T(8,128)(2,1)S(1)}, bf16[72,896]{1,0:T(8,128)(2,1)S(1)}, u32[]{:S(2)}, u32[]{:S(2)}) collective-permute-start(bf16[72,896]{1,0:T(8,128)(2,1)S(1)} %after.19), channel_id=1, source_target_pairs={{0,2},{2,0},{1,3},{3,1},{4,6},{6,4},{5,7},{7,5},{8,10},{10,8},{9,1... | collective-permute-start | bytes 387080 | tf_op jit(solution)/shard_map/back0_tp/ppermute | solution.py:32
  28.9 2.5 %collective-permute-start.15 = (bf16[72,896]{1,0:T(8,128)(2,1)S(1)}, bf16[72,896]{1,0:T(8,128)(2,1)S(1)}, u32[]{:S(2)}, u32[]{:S(2)}) collective-permute-start(bf16[72,896]{1,0:T(8,128)(2,1)S(1)} %add_convert_fusion), channel_id=1, source_target_pairs={{0,12},{4,8},{8,4},{12,0},{1,13},{5,9},{9,5},{13,1},{2,14},{6,10},... | collective-permute-start | bytes 387080 | tf_op jit(solution)/shard_map/back3_ep/ppermute | solution.py:32
  31.5 1.2 %back.4 = (bf16[72,896]{1,0:T(8,128)(2,1)S(1)}, bf16[72,896]{1,0:T(8,128)(2,1)S(1)}) custom-call(f32[72,512]{1,0:T(8,128)S(1)} %get-tuple-element.55.sum_ref.earlier_ref, f32[88,512]{1,0:T(8,128)S(1)} %collective-permute-done.9.other_ref, f32[4,72,512]{2,1,0:T(8,128)S(1)} %get-tuple-element.44.up_by_ref, f32[4,72,512]{2,1,0:T(8,128)S(1)} %get-tuple-element.45.gate_by_ref, ...), custom_call_target="tpu_custom_call" | custom-call | tf_op jit(solution)/shard_map/back/pallas_call | solution.py:51
  32.7 1.5 %collective-permute-start.12 = (bf16[72,896]{1,0:T(8,128)(2,1)S(1)}, bf16[72,896]{1,0:T(8,128)(2,1)S(1)}, u32[]{:S(2)}, u32[]{:S(2)}) collective-permute-start(bf16[72,896]{1,0:T(8,128)(2,1)S(1)} %get-tuple-element.60), channel_id=1, source_target_pairs={{0,2},{2,0},{1,3},{3,1},{4,6},{6,4},{5,7},{7,5},{8,10},{10,8},{9,1... | collective-permute-start | bytes 387080 | tf_op jit(solution)/shard_map/back2_tp/ppermute | solution.py:32
  34.2 1.2 %back.5 = (bf16[72,896]{1,0:T(8,128)(2,1)S(1)}, bf16[72,896]{1,0:T(8,128)(2,1)S(1)}) custom-call(f32[72,512]{1,0:T(8,128)S(1)} %get-tuple-element.49.earlier_ref.refs_4_.sum_ref, bf16[72,512]{1,0:T(8,128)(2,1)S(1)} %after.18.other_ref, f32[4,72,512]{2,1,0:T(8,128)S(1)} %get-tuple-element.44.up_by_ref, f32[4,72,512]{2,1,0:T(8,128)S(1)} %get-tuple-element.45.gate_by_ref, ...), custom_call_target="tpu_custom_call" | custom-call | tf_op jit(solution)/shard_map/back/pallas_call | solution.py:51
  36.1 2.0 %collective-permute-done.12 = bf16[72,896]{1,0:T(8,128)(2,1)S(1)} collective-permute-done((bf16[72,896]{1,0:T(8,128)(2,1)S(1)}, bf16[72,896]{1,0:T(8,128)(2,1)S(1)}, u32[]{:S(2)}, u32[]{:S(2)}) %collective-permute-start.12) | collective-permute-done | bytes 129056 | tf_op jit(solution)/shard_map/back2_tp/ppermute | solution.py:32
  38.1 1.7 %collective-permute-start.13 = (bf16[72,896]{1,0:T(8,128)(2,1)S(1)}, bf16[72,896]{1,0:T(8,128)(2,1)S(1)}, u32[]{:S(2)}, u32[]{:S(2)}) collective-permute-start(bf16[72,896]{1,0:T(8,128)(2,1)S(1)} %add_convert_fusion.1), channel_id=1, source_target_pairs={{0,8},{4,12},{8,0},{12,4},{1,9},{5,13},{9,1},{13,5},{2,10},{6,14},... | collective-permute-start | bytes 387080 | tf_op jit(solution)/shard_map/back2_ep/ppermute | solution.py:32
  39.7 0.9 %collective-permute-done.10 = bf16[72,896]{1,0:T(8,128)(2,1)S(1)} collective-permute-done((bf16[72,896]{1,0:T(8,128)(2,1)S(1)}, bf16[72,896]{1,0:T(8,128)(2,1)S(1)}, u32[]{:S(2)}, u32[]{:S(2)}) %collective-permute-start.10) | collective-permute-done | bytes 129056 | tf_op jit(solution)/shard_map/back1_tp/ppermute | solution.py:32
  42.3 3.6 %collective-permute-done.13.refs_1_ = bf16[72,896]{1,0:T(8,128)(2,1)S(1)} collective-permute-done((bf16[72,896]{1,0:T(8,128)(2,1)S(1)}, bf16[72,896]{1,0:T(8,128)(2,1)S(1)}, u32[]{:S(2)}, u32[]{:S(2)}) %collective-permute-start.13) | collective-permute-done | bytes 129056 | tf_op jit(solution)/shard_map/back2_ep/ppermute | solution.py:32
  46.0 1.3 %collective-permute-done.11.refs_0_ = bf16[72,896]{1,0:T(8,128)(2,1)S(1)} collective-permute-done((bf16[72,896]{1,0:T(8,128)(2,1)S(1)}, bf16[72,896]{1,0:T(8,128)(2,1)S(1)}, u32[]{:S(2)}, u32[]{:S(2)}) %collective-permute-start.11) | collective-permute-done | bytes 129056 | tf_op jit(solution)/shard_map/back1_ep/ppermute | solution.py:32
  47.3 1.2 %unpack_latest.1 = bf16[128,1792]{1,0:T(8,128)(2,1)} custom-call(bf16[2,4,72,128]{3,2,1,0:T(8,128)(2,1)S(1)} %get-tuple-element.33.place_ref.earlier_ref, bf16[72,896]{1,0:T(8,128)(2,1)S(1)} %collective-permute-done.11.refs_0_, bf16[72,896]{1,0:T(8,128)(2,1)S(1)} %collective-permute-done.13.refs_1_, bf16[128,1792]{1,0:T(8,128)(2,1)S(1)} %unpack.1.refs_2_), custom_call_target="tpu_custom_call" | custom-call | tf_op jit(solution)/shard_map/unpack_latest/pallas_call | solution.py:51
  (42 shorter events, 5.7 us)
Async XLA Ops:
  2.2 8.7 %collective-permute-start.1 = (bf16[72,896]{1,0:T(8,128)(2,1)S(1)}, bf16[72,896]{1,0:T(8,128)(2,1)S(1)}, u32[]{:S(2)}, u32[]{:S(2)}) collective-permute-start(bf16[72,896]{1,0:T(8,128)(2,1)S(1)} %get-tuple-element.38.earlier_ref), channel_id=1, source_target_pairs={{0,12},{4,8},{8,4},{12,0},{1,13},{5,9},{9,5},{13,1},{2,14},{6,10},... | collective-permute-start | bytes 387080 | tf_op jit(solution)/shard_map/rows3_ep/ppermute | solution.py:32
  8.5 10.8 %collective-permute-start.4 = (bf16[120,896]{1,0:T(8,128)(2,1)S(1)}, bf16[120,896]{1,0:T(8,128)(2,1)S(1)}, u32[]{:S(2)}, u32[]{:S(2)}) collective-permute-start(bf16[120,896]{1,0:T(8,128)(2,1)S(1)} %get-tuple-element.41), channel_id=1, source_target_pairs={{0,2},{2,0},{1,3},{3,1},{4,6},{6,4},{5,7},{7,5},{8,10},{10,8},{9,1... | collective-permute-start | bytes 645128 | tf_op jit(solution)/shard_map/rows0_tp/ppermute | solution.py:32
  10.0 8.3 %collective-permute-start = (bf16[72,896]{1,0:T(8,128)(2,1)S(1)}, bf16[72,896]{1,0:T(8,128)(2,1)S(1)}, u32[]{:S(2)}, u32[]{:S(2)}) collective-permute-start(bf16[72,896]{1,0:T(8,128)(2,1)S(1)} %get-tuple-element.37), channel_id=1, source_target_pairs={{0,4},{4,0},{8,12},{12,8},{1,5},{5,1},{9,13},{13,9},{2,6},{6,2},{1... | collective-permute-start | bytes 387080 | tf_op jit(solution)/shard_map/rows1_ep/ppermute | solution.py:32
  10.9 8.4 %collective-permute-start.3 = (bf16[72,896]{1,0:T(8,128)(2,1)S(1)}, bf16[72,896]{1,0:T(8,128)(2,1)S(1)}, u32[]{:S(2)}, u32[]{:S(2)}) collective-permute-start(bf16[72,896]{1,0:T(8,128)(2,1)S(1)} %collective-permute-done.1.refs_6_.refs_0_.earlier_ref), channel_id=1, source_target_pairs={{0,2},{2,0},{1,3},{3,1},{4,6},{6,4},{5,7},{7,5},{8,10},{10,8},{9,1... | collective-permute-start | bytes 387080 | tf_op jit(solution)/shard_map/rows3_tp/ppermute | solution.py:32
  13.4 7.2 %collective-permute-start.7 = (bf16[72,896]{1,0:T(8,128)(2,1)S(1)}, bf16[72,896]{1,0:T(8,128)(2,1)S(1)}, u32[]{:S(2)}, u32[]{:S(2)}) collective-permute-start(bf16[72,896]{1,0:T(8,128)(2,1)S(1)} %after.13), channel_id=1, source_target_pairs={{0,8},{4,12},{8,0},{12,4},{1,9},{5,13},{9,1},{13,5},{2,10},{6,14},... | collective-permute-start | bytes 387080 | tf_op jit(solution)/shard_map/rows2_ep/ppermute | solution.py:32
  18.4 6.0 %collective-permute-start.2 = (bf16[72,896]{1,0:T(8,128)(2,1)S(1)}, bf16[72,896]{1,0:T(8,128)(2,1)S(1)}, u32[]{:S(2)}, u32[]{:S(2)}) collective-permute-start(bf16[72,896]{1,0:T(8,128)(2,1)S(1)} %after.10.refs_0_), channel_id=1, source_target_pairs={{0,2},{2,0},{1,3},{3,1},{4,6},{6,4},{5,7},{7,5},{8,10},{10,8},{9,1... | collective-permute-start | bytes 387080 | tf_op jit(solution)/shard_map/rows1_tp/ppermute | solution.py:32
  20.0 1.7 %collective-permute-start.5 = (f32[144,512]{1,0:T(8,128)S(1)}, f32[144,512]{1,0:T(8,128)S(1)}, u32[]{:S(2)}, u32[]{:S(2)}) collective-permute-start(f32[144,512]{1,0:T(8,128)S(1)} %get-tuple-element.43), channel_id=1, source_target_pairs={{0,1},{1,0},{2,3},{3,2},{4,5},{5,4},{6,7},{7,6},{8,9},{9,8},{10,11... | collective-permute-start | bytes 884744 | tf_op jit(solution)/shard_map/hidden3_sub/ppermute | solution.py:32
  20.6 5.7 %collective-permute-start.8 = (bf16[72,896]{1,0:T(8,128)(2,1)S(1)}, bf16[72,896]{1,0:T(8,128)(2,1)S(1)}, u32[]{:S(2)}, u32[]{:S(2)}) collective-permute-start(bf16[72,896]{1,0:T(8,128)(2,1)S(1)} %after.15.refs_0_), channel_id=1, source_target_pairs={{0,2},{2,0},{1,3},{3,1},{4,6},{6,4},{5,7},{7,5},{8,10},{10,8},{9,1... | collective-permute-start | bytes 387080 | tf_op jit(solution)/shard_map/rows2_tp/ppermute | solution.py:32
  23.0 5.9 %collective-permute-start.14 = (bf16[72,896]{1,0:T(8,128)(2,1)S(1)}, bf16[72,896]{1,0:T(8,128)(2,1)S(1)}, u32[]{:S(2)}, u32[]{:S(2)}) collective-permute-start(bf16[72,896]{1,0:T(8,128)(2,1)S(1)} %get-tuple-element.61), channel_id=1, source_target_pairs={{0,2},{2,0},{1,3},{3,1},{4,6},{6,4},{5,7},{7,5},{8,10},{10,8},{9,1... | collective-permute-start | bytes 387080 | tf_op jit(solution)/shard_map/back3_tp/ppermute | solution.py:32
  27.0 4.4 %collective-permute-start.9 = (f32[88,512]{1,0:T(8,128)S(1)}, f32[88,512]{1,0:T(8,128)S(1)}, u32[]{:S(2)}, u32[]{:S(2)}) collective-permute-start(f32[88,512]{1,0:T(8,128)S(1)} %get-tuple-element.56), channel_id=1, source_target_pairs={{0,1},{1,0},{2,3},{3,2},{4,5},{5,4},{6,7},{7,6},{8,9},{9,8},{10,11... | collective-permute-start | bytes 540680 | tf_op jit(solution)/shard_map/hidden2_sub/ppermute | solution.py:32
  27.1 14.8 %collective-permute-start.16 = (bf16[72,896]{1,0:T(8,128)(2,1)S(1)}, bf16[72,896]{1,0:T(8,128)(2,1)S(1)}, u32[]{:S(2)}, u32[]{:S(2)}) collective-permute-start(bf16[72,896]{1,0:T(8,128)(2,1)S(1)} %after.19), channel_id=1, source_target_pairs={{0,2},{2,0},{1,3},{3,1},{4,6},{6,4},{5,7},{7,5},{8,10},{10,8},{9,1... | collective-permute-start | bytes 387080 | tf_op jit(solution)/shard_map/back0_tp/ppermute | solution.py:32
  28.5 5.7 %collective-permute-start.6 = (bf16[72,512]{1,0:T(8,128)(2,1)S(1)}, bf16[72,512]{1,0:T(8,128)(2,1)S(1)}, u32[]{:S(2)}, u32[]{:S(2)}) collective-permute-start(bf16[72,512]{1,0:T(8,128)(2,1)S(1)} %get-tuple-element.50), channel_id=1, source_target_pairs={{0,1},{1,0},{2,3},{3,2},{4,5},{5,4},{6,7},{7,6},{8,9},{9,8},{10,11... | collective-permute-start | bytes 221192 | tf_op jit(solution)/shard_map/hidden1_sub/ppermute | solution.py:32
  28.9 12.9 %collective-permute-start.15 = (bf16[72,896]{1,0:T(8,128)(2,1)S(1)}, bf16[72,896]{1,0:T(8,128)(2,1)S(1)}, u32[]{:S(2)}, u32[]{:S(2)}) collective-permute-start(bf16[72,896]{1,0:T(8,128)(2,1)S(1)} %add_convert_fusion), channel_id=1, source_target_pairs={{0,12},{4,8},{8,4},{12,0},{1,13},{5,9},{9,5},{13,1},{2,14},{6,10},... | collective-permute-start | bytes 387080 | tf_op jit(solution)/shard_map/back3_ep/ppermute | solution.py:32
  32.7 5.4 %collective-permute-start.12 = (bf16[72,896]{1,0:T(8,128)(2,1)S(1)}, bf16[72,896]{1,0:T(8,128)(2,1)S(1)}, u32[]{:S(2)}, u32[]{:S(2)}) collective-permute-start(bf16[72,896]{1,0:T(8,128)(2,1)S(1)} %get-tuple-element.60), channel_id=1, source_target_pairs={{0,2},{2,0},{1,3},{3,1},{4,6},{6,4},{5,7},{7,5},{8,10},{10,8},{9,1... | collective-permute-start | bytes 387080 | tf_op jit(solution)/shard_map/back2_tp/ppermute | solution.py:32
  35.4 5.2 %collective-permute-start.10 = (bf16[72,896]{1,0:T(8,128)(2,1)S(1)}, bf16[72,896]{1,0:T(8,128)(2,1)S(1)}, u32[]{:S(2)}, u32[]{:S(2)}) collective-permute-start(bf16[72,896]{1,0:T(8,128)(2,1)S(1)} %get-tuple-element.59), channel_id=1, source_target_pairs={{0,2},{2,0},{1,3},{3,1},{4,6},{6,4},{5,7},{7,5},{8,10},{10,8},{9,1... | collective-permute-start | bytes 387080 | tf_op jit(solution)/shard_map/back1_tp/ppermute | solution.py:32
  38.1 7.9 %collective-permute-start.13 = (bf16[72,896]{1,0:T(8,128)(2,1)S(1)}, bf16[72,896]{1,0:T(8,128)(2,1)S(1)}, u32[]{:S(2)}, u32[]{:S(2)}) collective-permute-start(bf16[72,896]{1,0:T(8,128)(2,1)S(1)} %add_convert_fusion.1), channel_id=1, source_target_pairs={{0,8},{4,12},{8,0},{12,4},{1,9},{5,13},{9,1},{13,5},{2,10},{6,14},... | collective-permute-start | bytes 387080 | tf_op jit(solution)/shard_map/back2_ep/ppermute | solution.py:32
  40.7 6.6 %collective-permute-start.11 = (bf16[72,896]{1,0:T(8,128)(2,1)S(1)}, bf16[72,896]{1,0:T(8,128)(2,1)S(1)}, u32[]{:S(2)}, u32[]{:S(2)}) collective-permute-start(bf16[72,896]{1,0:T(8,128)(2,1)S(1)} %add_convert_fusion.2), channel_id=1, source_target_pairs={{0,4},{4,0},{8,12},{12,8},{1,5},{5,1},{9,13},{13,9},{2,6},{6,2},{1... | collective-permute-start | bytes 387080 | tf_op jit(solution)/shard_map/back1_ep/ppermute | solution.py:32

commit v17 on v9

--- a/solution.py
+++ b/solution.py
@@ -35,7 +35,7 @@
     return pltpu.VMEM(array.shape, array.dtype)
 
 
-def call(kernel, outs, *args, cost=0, name=None, specs=None, scratch=(), earlier=()):
+def call(kernel, outs, *args, cost=0, name=None, specs=None, outs_in=VMEM, scratch=(), earlier=()):
     specs = (specs or [VMEM] * len(args)) + [ANY] * len(earlier)
     if earlier:
         taken, body = len(args), kernel
@@ -47,7 +47,7 @@
         kernel,
         out_shape=outs,
         in_specs=specs,
-        out_specs=[VMEM] * len(outs),
+        out_specs=[outs_in] * len(outs),
         scratch_shapes=scratch,
         compiler_params=pltpu.CompilerParams(vmem_limit_bytes=VMEM_LIMIT),
         cost_estimate=pl.CostEstimate(flops=cost, bytes_accessed=0, transcendentals=0),
@@ -135,9 +135,33 @@
         copy.wait()
 
 
-def fetch_kernel(*refs):
-    count = len(refs) // 2
-    for copy in fetch(refs[:count], refs[count : 2 * count], refs[-1]):
+def by_xor(value, most, narrow, lane):
+    step = 1
+    while step < narrow:
+        pieces = [value[i * most : (i + step) * most] for i in range(0, narrow, step)]
+        turned = [pieces[i ^ 1] for i in range(len(pieces))]
+        value = jnp.where((lane & step) != 0, jnp.concatenate(turned, axis=0), value)
+        step *= 2
+    return value
+
+
+def fetch_kernel(most, *refs):
+    pre_ref, sems = refs[-2:]
+    wide = pre_ref.shape[1]
+    narrow = pre_ref.shape[2] // most
+    count = (len(refs) - 3) // 2
+    given, (up_ref, gate_ref, *held) = refs[:count], refs[count:-2]
+    copies = fetch(given, [pre_ref] + held, sems)
+    me, lane = lax.axis_index("ep"), lax.axis_index("tp")
+    copies[0].wait()
+    for k in range(wide):
+        gate_pre, up_pre = [
+            by_xor(pre_ref[i, me ^ k].astype(jnp.float32), most, narrow, lane) for i in range(2)
+        ]
+        sig = 1.0 / (1.0 + jnp.exp(-gate_pre))
+        up_ref[k] = gate_pre * sig
+        gate_ref[k] = up_pre * sig * (1.0 + gate_pre * (1.0 - sig))
+    for copy in copies[1:]:
         copy.wait()
 
 
@@ -160,30 +184,14 @@
     sent_ref[:count, :] = total.astype(jnp.bfloat16)
 
 
-def by_xor(value, most, narrow, lane):
-    step = 1
-    while step < narrow:
-        pieces = [value[i * most : (i + step) * most] for i in range(0, narrow, step)]
-        turned = [pieces[i ^ 1] for i in range(len(pieces))]
-        value = jnp.where((lane & step) != 0, jnp.concatenate(turned, axis=0), value)
-        step *= 2
-    return value
-
-
-def back_kernel(most, narrow, group, sum_ref, other_ref, pre_ref, gate_ref, up_ref, *outs):
+def back_kernel(most, group, sum_ref, other_ref, up_by_ref, gate_by_ref, gate_ref, up_ref, *outs):
     half = gate_ref.shape[0] // 2
-    me, lane = lax.axis_index("ep"), lax.axis_index("tp")
     hidden = sum_ref[...] + other_ref[: sum_ref.shape[0], :].astype(jnp.float32)
-    gate_pre, up_pre = [
-        jnp.concatenate(
-            [by_xor(pre_ref[i, me ^ k].astype(jnp.float32), most, narrow, lane) for k in group],
-            axis=0,
-        )
-        for i in range(2)
+    up_by, gate_by = [
+        jnp.concatenate([by_ref[k] for k in group], axis=0) for by_ref in (up_by_ref, gate_by_ref)
     ]
-    sig = 1.0 / (1.0 + jnp.exp(-gate_pre))
-    up_grad = (hidden * gate_pre * sig).astype(jnp.bfloat16)
-    gate_grad = (hidden * up_pre * sig * (1.0 + gate_pre * (1.0 - sig))).astype(jnp.bfloat16)
+    up_grad = (hidden * up_by).astype(jnp.bfloat16)
+    gate_grad = (hidden * gate_by).astype(jnp.bfloat16)
     low = dot(gate_grad, gate_ref[:half], NT) + dot(up_grad, up_ref[:half], NT)
     high = dot(gate_grad, gate_ref[half:], NT) + dot(up_grad, up_ref[half:], NT)
     for i, out in enumerate(outs):
@@ -196,10 +204,13 @@
 
 
 def unpack_kernel(distances, started, place_ref, *refs):
+    if started:
+        refs, held_ref, sems = refs[:-2], refs[-2], refs[-1]
     blocks, others, out_ref = refs[: len(distances)], refs[len(distances) : -1], refs[-1]
     if started:
         others, so_far_ref = others[:-1], others[-1]
     half = out_ref.shape[1] // 2
+    copies = []
     for side in range(2):
         columns = slice(side * half, (side + 1) * half)
         total = so_far_ref[:, columns].astype(jnp.float32) if started else 0.0
@@ -211,7 +222,18 @@
                     rows += other_ref[...].astype(jnp.float32)
                 rows = rows.astype(jnp.bfloat16)
             total = total + dot(place_ref[side, k], rows, TN)
-        out_ref[:, columns] = total.astype(jnp.bfloat16)
+        if started:
+            held_ref[side] = total.astype(jnp.bfloat16)
+            copies.append(
+                pltpu.make_async_copy(
+                    held_ref.at[side], out_ref.at[:, pl.ds(side * half, half)], sems.at[side]
+                )
+            )
+            copies[-1].start()
+        else:
+            out_ref[:, columns] = total.astype(jnp.bfloat16)
+    for copy in copies:
+        copy.wait()
 
 
 def groups_of(wide):
@@ -282,19 +304,20 @@
             if len(groups) > 1 and k == groups[1][0]:
                 arrived[k] = after(arrived[k], packed[first], 1 << 31)
     fetched = [
+        pre_acts.reshape(2, wide, narrow * most, hidden_width),
         w_down[0],
-        pre_acts.reshape(2, wide, narrow * most, hidden_width),
         w_gate[0],
         w_up[0],
         latent,
         latent_gain.reshape(1, -1),
     ]
-    down, pre, gate, up, latent, latent_gain = call(
-        fetch_kernel,
-        [like(array) for array in fetched],
+    factors = pltpu.VMEM((wide, narrow * most, hidden_width), f32)
+    up_by, gate_by, down, gate, up, latent, latent_gain = call(
+        functools.partial(fetch_kernel, most),
+        [factors, factors] + [like(array) for array in fetched[1:]],
         *pinned(*fetched),
         specs=[HBM] * len(fetched),
-        scratch=[pltpu.SemaphoreType.DMA((len(fetched),))],
+        scratch=[like(fetched[0]), pltpu.SemaphoreType.DMA((len(fetched),))],
         earlier=[arrived[first]],
         name="fetch",
     )
@@ -353,11 +376,12 @@
         if moved is not None:
             received = after(received, moved)
         products = call(
-            functools.partial(back_kernel, most, narrow, group),
+            functools.partial(back_kernel, most, group),
             [block] * (len(group) * narrow),
             summed,
             received,
-            pre,
+            up_by,
+            gate_by,
             gate,
             up,
             name="back",
@@ -396,6 +420,8 @@
             place,
             *[returned[k] for k in latest],
             grad_input,
+            outs_in=ANY,
+            scratch=[pltpu.VMEM((2, tokens, half), bf16), pltpu.SemaphoreType.DMA((2,))],
             name="unpack_latest",
         )
     return (grad_input, d_latent)

time: 48 us -> 48 us (level)
  transfers between devices with their start and end apart: 17 -> 17, of which waited for: 7 -> 7; matrix products, arithmetic and copies ran while one was open for 2% -> 2% of each run, Pallas kernels for 16% -> 15%
where the time goes in v17:
time: 48 us; the launch traced here: 47.9 us
  starting transfers between devices  25.7 us (54%)
  Pallas kernels  10.7 us (22%)
  waiting for transfers between devices  9.63 us (20%)
  other arithmetic  1 us (2%)
  between operations  0.79 us (2%)
    ppermute x17, starting transfers between devices, swap(): return lax.ppermute(value, axis, [(i, i ^ step) for i in range(count)])  25.7 us
    pallas_call x8, Pallas kernels, call(): pl.pallas_call(kernel, out_shape=outs, in_specs=specs, out_specs=[outs_in...  10.7 us
    ppermute x17, waiting for transfers between devices, swap(): return lax.ppermute(value, axis, [(i, i ^ step) for i in range(count)])  9.63 us
  transfers between devices with their start and end apart: 17, of which 7 were waited for; matrix products, arithmetic and copies ran while one was open for 2% of the time, Pallas kernels for 15%

profile of v17, /device:TPU:0, one launch (start us, length us, event | category | flops | bytes accessed | tf_op | source)
XLA Modules:
  0.0 47.9 jit_solution(419340929154938028)
XLA Ops:
  0.6 2.3 %pack.1 = (bf16[72,896]{1,0:T(8,128)(2,1)S(1)}, bf16[72,896]{1,0:T(8,128)(2,1)S(1)}, bf16[72,896]{1,0:T(8,128)(2,1)S(1)}, bf16[72,896]{1,0:T(8,128)(2,1)S(1)}, b...) custom-call(s32[1,128]{1,0:T(1,128)} %bitcast.36, f32[1,128]{1,0:T(1,128)} %bitcast.37, ...), custom_call_target="tpu_custom_call" | custom-call | tf_op jit(solution)/shard_map/pack/pallas_call | solution.py:46
  3.0 3.1 %collective-permute-start.4 = (bf16[72,896]{1,0:T(8,128)(2,1)S(1)}, bf16[72,896]{1,0:T(8,128)(2,1)S(1)}, u32[]{:S(2)}, u32[]{:S(2)}) collective-permute-start(bf16[72,896]{1,0:T(8,128)(2,1)S(1)} %get-tuple-element.30), channel_id=1, source_target_pairs={{0,4},{4,0},{8,12},{12,8},{1,5},{5,1},{9,13},{13,9},{2,6},{6,2},{1... | collective-permute-start | bytes 387080 | tf_op jit(solution)/shard_map/rows1_ep/ppermute | solution.py:27
  6.1 2.5 %collective-permute-start = (bf16[72,896]{1,0:T(8,128)(2,1)S(1)}, bf16[72,896]{1,0:T(8,128)(2,1)S(1)}, u32[]{:S(2)}, u32[]{:S(2)}) collective-permute-start(bf16[72,896]{1,0:T(8,128)(2,1)S(1)} %get-tuple-element.29.earlier_ref), channel_id=1, source_target_pairs={{0,12},{4,8},{8,4},{12,0},{1,13},{5,9},{9,5},{13,1},{2,14},{6,10},... | collective-permute-start | bytes 387080 | tf_op jit(solution)/shard_map/rows3_ep/ppermute | solution.py:27
  8.5 1.5 %collective-permute-start.6 = (bf16[72,896]{1,0:T(8,128)(2,1)S(1)}, bf16[72,896]{1,0:T(8,128)(2,1)S(1)}, u32[]{:S(2)}, u32[]{:S(2)}) collective-permute-start(bf16[72,896]{1,0:T(8,128)(2,1)S(1)} %get-tuple-element.31.refs_4_), channel_id=1, source_target_pairs={{0,2},{2,0},{1,3},{3,1},{4,6},{6,4},{5,7},{7,5},{8,10},{10,8},{9,1... | collective-permute-start | bytes 387080 | tf_op jit(solution)/shard_map/rows0_tp/ppermute | solution.py:27
  10.0 1.1 %collective-permute-start.5 = (bf16[72,896]{1,0:T(8,128)(2,1)S(1)}, bf16[72,896]{1,0:T(8,128)(2,1)S(1)}, u32[]{:S(2)}, u32[]{:S(2)}) collective-permute-start(bf16[72,896]{1,0:T(8,128)(2,1)S(1)} %collective-permute-done.4.refs_2_), channel_id=1, source_target_pairs={{0,2},{2,0},{1,3},{3,1},{4,6},{6,4},{5,7},{7,5},{8,10},{10,8},{9,1... | collective-permute-start | bytes 387080 | tf_op jit(solution)/shard_map/rows1_tp/ppermute | solution.py:27
  11.2 0.9 %collective-permute-start.8 = (bf16[128,256]{1,0:T(8,128)(2,1)S(1)}, bf16[128,256]{1,0:T(8,128)(2,1)S(1)}, u32[]{:S(2)}, u32[]{:S(2)}) collective-permute-start(bf16[128,256]{1,0:T(8,128)(2,1)S(1)} %slice_bitcast_fusion), channel_id=1, source_target_pairs={{0,2},{2,0},{1,3},{3,1},{4,6},{6,4},{5,7},{7,5},{8,10},{10,8},{9,1... | collective-permute-start | bytes 196616 | tf_op jit(solution)/shard_map/latent_tp/ppermute | solution.py:27
  12.1 2.5 %collective-permute-done.earlier_ref.refs_6_.refs_0_ = bf16[72,896]{1,0:T(8,128)(2,1)S(1)} collective-permute-done((bf16[72,896]{1,0:T(8,128)(2,1)S(1)}, bf16[72,896]{1,0:T(8,128)(2,1)S(1)}, u32[]{:S(2)}, u32[]{:S(2)}) %collective-permute-start) | collective-permute-done | bytes 129056 | tf_op jit(solution)/shard_map/rows3_ep/ppermute | solution.py:27
  14.6 1.8 %collective-permute-start.1 = (bf16[72,896]{1,0:T(8,128)(2,1)S(1)}, bf16[72,896]{1,0:T(8,128)(2,1)S(1)}, u32[]{:S(2)}, u32[]{:S(2)}) collective-permute-start(bf16[72,896]{1,0:T(8,128)(2,1)S(1)} %after.8), channel_id=1, source_target_pairs={{0,8},{4,12},{8,0},{12,4},{1,9},{5,13},{9,1},{13,5},{2,10},{6,14},... | collective-permute-start | bytes 387080 | tf_op jit(solution)/shard_map/rows2_ep/ppermute | solution.py:27
  16.3 1.5 %collective-permute-start.3 = (bf16[72,896]{1,0:T(8,128)(2,1)S(1)}, bf16[72,896]{1,0:T(8,128)(2,1)S(1)}, u32[]{:S(2)}, u32[]{:S(2)}) collective-permute-start(bf16[72,896]{1,0:T(8,128)(2,1)S(1)} %collective-permute-done.earlier_ref.refs_6_.refs_0_), channel_id=1, source_target_pairs={{0,2},{2,0},{1,3},{3,1},{4,6},{6,4},{5,7},{7,5},{8,10},{10,8},{9,1... | collective-permute-start | bytes 387080 | tf_op jit(solution)/shard_map/rows3_tp/ppermute | solution.py:27
  17.8 2.9 %fetch.1 = (f32[4,72,512]{2,1,0:T(8,128)S(1)}, f32[4,72,512]{2,1,0:T(8,128)S(1)}, bf16[512,1792]{1,0:T(8,128)(2,1)S(1)}, bf16[1792,512]{1,0:T(8,128)(2,1)S(1)}, ...) custom-call(bf16[2,4,72,512]{3,2,1,0:T(8,128)(2,1)} %bitcast.28, ...), custom_call_target="tpu_custom_call" | custom-call | tf_op jit(solution)/shard_map/fetch/pallas_call | solution.py:46
  22.1 1.6 %collective-permute-start.2 = (bf16[72,896]{1,0:T(8,128)(2,1)S(1)}, bf16[72,896]{1,0:T(8,128)(2,1)S(1)}, u32[]{:S(2)}, u32[]{:S(2)}) collective-permute-start(bf16[72,896]{1,0:T(8,128)(2,1)S(1)} %after.9.refs_0_), channel_id=1, source_target_pairs={{0,2},{2,0},{1,3},{3,1},{4,6},{6,4},{5,7},{7,5},{8,10},{10,8},{9,1... | collective-permute-start | bytes 387080 | tf_op jit(solution)/shard_map/rows2_tp/ppermute | solution.py:27
  23.7 1.3 %back.2 = (bf16[72,896]{1,0:T(8,128)(2,1)S(1)}, bf16[72,896]{1,0:T(8,128)(2,1)S(1)}, bf16[72,896]{1,0:T(8,128)(2,1)S(1)}, bf16[72,896]{1,0:T(8,128)(2,1)S(1)}, b...) custom-call(f32[216,512]{1,0:T(8,128)S(1)} %get-tuple-element.33.sum_ref.earlier_ref, ...), custom_call_target="tpu_custom_call" | custom-call | tf_op jit(solution)/shard_map/back/pallas_call | solution.py:46
  25.0 1.4 %collective-permute-start.10 = (bf16[72,896]{1,0:T(8,128)(2,1)S(1)}, bf16[72,896]{1,0:T(8,128)(2,1)S(1)}, u32[]{:S(2)}, u32[]{:S(2)}) collective-permute-start(bf16[72,896]{1,0:T(8,128)(2,1)S(1)} %get-tuple-element.45), channel_id=1, source_target_pairs={{0,2},{2,0},{1,3},{3,1},{4,6},{6,4},{5,7},{7,5},{8,10},{10,8},{9,1... | collective-permute-start | bytes 387080 | tf_op jit(solution)/shard_map/back3_tp/ppermute | solution.py:27
  26.6 1.5 %collective-permute-done.2.value_ref = bf16[72,896]{1,0:T(8,128)(2,1)S(1)} collective-permute-done((bf16[72,896]{1,0:T(8,128)(2,1)S(1)}, bf16[72,896]{1,0:T(8,128)(2,1)S(1)}, u32[]{:S(2)}, u32[]{:S(2)}) %collective-permute-start.2) | collective-permute-done | bytes 129056 | tf_op jit(solution)/shard_map/rows2_tp/ppermute | solution.py:27
  28.9 1.7 %collective-permute-start.14 = (bf16[72,896]{1,0:T(8,128)(2,1)S(1)}, bf16[72,896]{1,0:T(8,128)(2,1)S(1)}, u32[]{:S(2)}, u32[]{:S(2)}) collective-permute-start(bf16[72,896]{1,0:T(8,128)(2,1)S(1)} %after.14), channel_id=1, source_target_pairs={{0,2},{2,0},{1,3},{3,1},{4,6},{6,4},{5,7},{7,5},{8,10},{10,8},{9,1... | collective-permute-start | bytes 387080 | tf_op jit(solution)/shard_map/back1_tp/ppermute | solution.py:27
  30.8 2.0 %collective-permute-start.13 = (bf16[72,896]{1,0:T(8,128)(2,1)S(1)}, bf16[72,896]{1,0:T(8,128)(2,1)S(1)}, u32[]{:S(2)}, u32[]{:S(2)}) collective-permute-start(bf16[72,896]{1,0:T(8,128)(2,1)S(1)} %add_convert_fusion.2.earlier_ref), channel_id=1, source_target_pairs={{0,12},{4,8},{8,4},{12,0},{1,13},{5,9},{9,5},{13,1},{2,14},{6,10},... | collective-permute-start | bytes 387080 | tf_op jit(solution)/shard_map/back3_ep/ppermute | solution.py:27
  32.8 1.2 %back.3 = (bf16[72,896]{1,0:T(8,128)(2,1)S(1)}, bf16[72,896]{1,0:T(8,128)(2,1)S(1)}) custom-call(f32[72,512]{1,0:T(8,128)S(1)} %get-tuple-element.43.sum_ref.earlier_ref, bf16[88,512]{1,0:T(8,128)(2,1)S(1)} %after.13.other_ref, f32[4,72,512]{2,1,0:T(8,128)S(1)} %get-tuple-element.35.up_by_ref, f32[4,72,512]{2,1,0:T(8,128)S(1)} %get-tuple-element.36.gate_by_ref, ...), custom_call_target="tpu_custom_call" | custom-call | tf_op jit(solution)/shard_map/back/pallas_call | solution.py:46
  34.0 1.4 %collective-permute-start.11 = (bf16[72,896]{1,0:T(8,128)(2,1)S(1)}, bf16[72,896]{1,0:T(8,128)(2,1)S(1)}, u32[]{:S(2)}, u32[]{:S(2)}) collective-permute-start(bf16[72,896]{1,0:T(8,128)(2,1)S(1)} %get-tuple-element.47), channel_id=1, source_target_pairs={{0,2},{2,0},{1,3},{3,1},{4,6},{6,4},{5,7},{7,5},{8,10},{10,8},{9,1... | collective-permute-start | bytes 387080 | tf_op jit(solution)/shard_map/back2_tp/ppermute | solution.py:27
  35.5 1.7 %collective-permute-start.15 = (bf16[72,896]{1,0:T(8,128)(2,1)S(1)}, bf16[72,896]{1,0:T(8,128)(2,1)S(1)}, u32[]{:S(2)}, u32[]{:S(2)}) collective-permute-start(bf16[72,896]{1,0:T(8,128)(2,1)S(1)} %add_convert_fusion), channel_id=1, source_target_pairs={{0,4},{4,0},{8,12},{12,8},{1,5},{5,1},{9,13},{13,9},{2,6},{6,2},{1... | collective-permute-start | bytes 387080 | tf_op jit(solution)/shard_map/back1_ep/ppermute | solution.py:27
  37.2 1.8 %collective-permute-done.11 = bf16[72,896]{1,0:T(8,128)(2,1)S(1)} collective-permute-done((bf16[72,896]{1,0:T(8,128)(2,1)S(1)}, bf16[72,896]{1,0:T(8,128)(2,1)S(1)}, u32[]{:S(2)}, u32[]{:S(2)}) %collective-permute-start.11) | collective-permute-done | bytes 129056 | tf_op jit(solution)/shard_map/back2_tp/ppermute | solution.py:27
  39.0 2.0 %collective-permute-start.12 = (bf16[72,896]{1,0:T(8,128)(2,1)S(1)}, bf16[72,896]{1,0:T(8,128)(2,1)S(1)}, u32[]{:S(2)}, u32[]{:S(2)}) collective-permute-start(bf16[72,896]{1,0:T(8,128)(2,1)S(1)} %add_convert_fusion.1.earlier_ref), channel_id=1, source_target_pairs={{0,8},{4,12},{8,0},{12,4},{1,9},{5,13},{9,1},{13,5},{2,10},{6,14},... | collective-permute-start | bytes 387080 | tf_op jit(solution)/shard_map/back2_ep/ppermute | solution.py:27
  41.1 1.4 %collective-permute-start.16 = (bf16[72,896]{1,0:T(8,128)(2,1)S(1)}, bf16[72,896]{1,0:T(8,128)(2,1)S(1)}, u32[]{:S(2)}, u32[]{:S(2)}) collective-permute-start(bf16[72,896]{1,0:T(8,128)(2,1)S(1)} %after.15), channel_id=1, source_target_pairs={{0,2},{2,0},{1,3},{3,1},{4,6},{6,4},{5,7},{7,5},{8,10},{10,8},{9,1... | collective-permute-start | bytes 387080 | tf_op jit(solution)/shard_map/back0_tp/ppermute | solution.py:27
  43.2 2.8 %collective-permute-done.16.refs_3_ = bf16[72,896]{1,0:T(8,128)(2,1)S(1)} collective-permute-done((bf16[72,896]{1,0:T(8,128)(2,1)S(1)}, bf16[72,896]{1,0:T(8,128)(2,1)S(1)}, u32[]{:S(2)}, u32[]{:S(2)}) %collective-permute-start.16) | collective-permute-done | bytes 129056 | tf_op jit(solution)/shard_map/back0_tp/ppermute | solution.py:27
  46.8 1.0 %unpack_latest.1 = bf16[128,1792]{1,0:T(8,128)(2,1)} custom-call(bf16[2,4,72,128]{3,2,1,0:T(8,128)(2,1)S(1)} %get-tuple-element.27.place_ref, bf16[72,896]{1,0:T(8,128)(2,1)S(1)} %collective-permute-done.12.refs_0_, bf16[128,1792]{1,0:T(8,128)(2,1)S(1)} %unpack.1.refs_1_), custom_call_target="tpu_custom_call" | custom-call | tf_op jit(solution)/shard_map/unpack_latest/pallas_call | solution.py:46
  (37 shorter events, 4.2 us)
Async XLA Ops:
  3.0 7.1 %collective-permute-start.4 = (bf16[72,896]{1,0:T(8,128)(2,1)S(1)}, bf16[72,896]{1,0:T(8,128)(2,1)S(1)}, u32[]{:S(2)}, u32[]{:S(2)}) collective-permute-start(bf16[72,896]{1,0:T(8,128)(2,1)S(1)} %get-tuple-element.30), channel_id=1, source_target_pairs={{0,4},{4,0},{8,12},{12,8},{1,5},{5,1},{9,13},{13,9},{2,6},{6,2},{1... | collective-permute-start | bytes 387080 | tf_op jit(solution)/shard_map/rows1_ep/ppermute | solution.py:27
  6.1 8.5 %collective-permute-start = (bf16[72,896]{1,0:T(8,128)(2,1)S(1)}, bf16[72,896]{1,0:T(8,128)(2,1)S(1)}, u32[]{:S(2)}, u32[]{:S(2)}) collective-permute-start(bf16[72,896]{1,0:T(8,128)(2,1)S(1)} %get-tuple-element.29.earlier_ref), channel_id=1, source_target_pairs={{0,12},{4,8},{8,4},{12,0},{1,13},{5,9},{9,5},{13,1},{2,14},{6,10},... | collective-permute-start | bytes 387080 | tf_op jit(solution)/shard_map/rows3_ep/ppermute | solution.py:27
  8.5 12.2 %collective-permute-start.6 = (bf16[72,896]{1,0:T(8,128)(2,1)S(1)}, bf16[72,896]{1,0:T(8,128)(2,1)S(1)}, u32[]{:S(2)}, u32[]{:S(2)}) collective-permute-start(bf16[72,896]{1,0:T(8,128)(2,1)S(1)} %get-tuple-element.31.refs_4_), channel_id=1, source_target_pairs={{0,2},{2,0},{1,3},{3,1},{4,6},{6,4},{5,7},{7,5},{8,10},{10,8},{9,1... | collective-permute-start | bytes 387080 | tf_op jit(solution)/shard_map/rows0_tp/ppermute | solution.py:27
  10.0 10.7 %collective-permute-start.5 = (bf16[72,896]{1,0:T(8,128)(2,1)S(1)}, bf16[72,896]{1,0:T(8,128)(2,1)S(1)}, u32[]{:S(2)}, u32[]{:S(2)}) collective-permute-start(bf16[72,896]{1,0:T(8,128)(2,1)S(1)} %collective-permute-done.4.refs_2_), channel_id=1, source_target_pairs={{0,2},{2,0},{1,3},{3,1},{4,6},{6,4},{5,7},{7,5},{8,10},{10,8},{9,1... | collective-permute-start | bytes 387080 | tf_op jit(solution)/shard_map/rows1_tp/ppermute | solution.py:27
  11.2 12.5 %collective-permute-start.8 = (bf16[128,256]{1,0:T(8,128)(2,1)S(1)}, bf16[128,256]{1,0:T(8,128)(2,1)S(1)}, u32[]{:S(2)}, u32[]{:S(2)}) collective-permute-start(bf16[128,256]{1,0:T(8,128)(2,1)S(1)} %slice_bitcast_fusion), channel_id=1, source_target_pairs={{0,2},{2,0},{1,3},{3,1},{4,6},{6,4},{5,7},{7,5},{8,10},{10,8},{9,1... | collective-permute-start | bytes 196616 | tf_op jit(solution)/shard_map/latent_tp/ppermute | solution.py:27
  14.6 7.5 %collective-permute-start.1 = (bf16[72,896]{1,0:T(8,128)(2,1)S(1)}, bf16[72,896]{1,0:T(8,128)(2,1)S(1)}, u32[]{:S(2)}, u32[]{:S(2)}) collective-permute-start(bf16[72,896]{1,0:T(8,128)(2,1)S(1)} %after.8), channel_id=1, source_target_pairs={{0,8},{4,12},{8,0},{12,4},{1,9},{5,13},{9,1},{13,5},{2,10},{6,14},... | collective-permute-start | bytes 387080 | tf_op jit(solution)/shard_map/rows2_ep/ppermute | solution.py:27
  16.3 4.9 %collective-permute-start.3 = (bf16[72,896]{1,0:T(8,128)(2,1)S(1)}, bf16[72,896]{1,0:T(8,128)(2,1)S(1)}, u32[]{:S(2)}, u32[]{:S(2)}) collective-permute-start(bf16[72,896]{1,0:T(8,128)(2,1)S(1)} %collective-permute-done.earlier_ref.refs_6_.refs_0_), channel_id=1, source_target_pairs={{0,2},{2,0},{1,3},{3,1},{4,6},{6,4},{5,7},{7,5},{8,10},{10,8},{9,1... | collective-permute-start | bytes 387080 | tf_op jit(solution)/shard_map/rows3_tp/ppermute | solution.py:27
  22.0 1.7 %collective-permute-start.7 = (bf16[216,512]{1,0:T(8,128)(2,1)S(1)}, bf16[216,512]{1,0:T(8,128)(2,1)S(1)}, u32[]{:S(2)}, u32[]{:S(2)}) collective-permute-start(bf16[216,512]{1,0:T(8,128)(2,1)S(1)} %get-tuple-element.34), channel_id=1, source_target_pairs={{0,1},{1,0},{2,3},{3,2},{4,5},{5,4},{6,7},{7,6},{8,9},{9,8},{10,11... | collective-permute-start | bytes 663560 | tf_op jit(solution)/shard_map/hidden3_sub/ppermute | solution.py:27
  22.1 5.9 %collective-permute-start.2 = (bf16[72,896]{1,0:T(8,128)(2,1)S(1)}, bf16[72,896]{1,0:T(8,128)(2,1)S(1)}, u32[]{:S(2)}, u32[]{:S(2)}) collective-permute-start(bf16[72,896]{1,0:T(8,128)(2,1)S(1)} %after.9.refs_0_), channel_id=1, source_target_pairs={{0,2},{2,0},{1,3},{3,1},{4,6},{6,4},{5,7},{7,5},{8,10},{10,8},{9,1... | collective-permute-start | bytes 387080 | tf_op jit(solution)/shard_map/rows2_tp/ppermute | solution.py:27
  25.0 5.7 %collective-permute-start.10 = (bf16[72,896]{1,0:T(8,128)(2,1)S(1)}, bf16[72,896]{1,0:T(8,128)(2,1)S(1)}, u32[]{:S(2)}, u32[]{:S(2)}) collective-permute-start(bf16[72,896]{1,0:T(8,128)(2,1)S(1)} %get-tuple-element.45), channel_id=1, source_target_pairs={{0,2},{2,0},{1,3},{3,1},{4,6},{6,4},{5,7},{7,5},{8,10},{10,8},{9,1... | collective-permute-start | bytes 387080 | tf_op jit(solution)/shard_map/back3_tp/ppermute | solution.py:27
  28.8 4.0 %collective-permute-start.9 = (bf16[88,512]{1,0:T(8,128)(2,1)S(1)}, bf16[88,512]{1,0:T(8,128)(2,1)S(1)}, u32[]{:S(2)}, u32[]{:S(2)}) collective-permute-start(bf16[88,512]{1,0:T(8,128)(2,1)S(1)} %get-tuple-element.44), channel_id=1, source_target_pairs={{0,1},{1,0},{2,3},{3,2},{4,5},{5,4},{6,7},{7,6},{8,9},{9,8},{10,11... | collective-permute-start | bytes 270344 | tf_op jit(solution)/shard_map/hidden2_sub/ppermute | solution.py:27
  28.9 6.6 %collective-permute-start.14 = (bf16[72,896]{1,0:T(8,128)(2,1)S(1)}, bf16[72,896]{1,0:T(8,128)(2,1)S(1)}, u32[]{:S(2)}, u32[]{:S(2)}) collective-permute-start(bf16[72,896]{1,0:T(8,128)(2,1)S(1)} %after.14), channel_id=1, source_target_pairs={{0,2},{2,0},{1,3},{3,1},{4,6},{6,4},{5,7},{7,5},{8,10},{10,8},{9,1... | collective-permute-start | bytes 387080 | tf_op jit(solution)/shard_map/back1_tp/ppermute | solution.py:27
  30.8 12.4 %collective-permute-start.13 = (bf16[72,896]{1,0:T(8,128)(2,1)S(1)}, bf16[72,896]{1,0:T(8,128)(2,1)S(1)}, u32[]{:S(2)}, u32[]{:S(2)}) collective-permute-start(bf16[72,896]{1,0:T(8,128)(2,1)S(1)} %add_convert_fusion.2.earlier_ref), channel_id=1, source_target_pairs={{0,12},{4,8},{8,4},{12,0},{1,13},{5,9},{9,5},{13,1},{2,14},{6,10},... | collective-permute-start | bytes 387080 | tf_op jit(solution)/shard_map/back3_ep/ppermute | solution.py:27
  34.0 5.0 %collective-permute-start.11 = (bf16[72,896]{1,0:T(8,128)(2,1)S(1)}, bf16[72,896]{1,0:T(8,128)(2,1)S(1)}, u32[]{:S(2)}, u32[]{:S(2)}) collective-permute-start(bf16[72,896]{1,0:T(8,128)(2,1)S(1)} %get-tuple-element.47), channel_id=1, source_target_pairs={{0,2},{2,0},{1,3},{3,1},{4,6},{6,4},{5,7},{7,5},{8,10},{10,8},{9,1... | collective-permute-start | bytes 387080 | tf_op jit(solution)/shard_map/back2_tp/ppermute | solution.py:27
  35.5 7.8 %collective-permute-start.15 = (bf16[72,896]{1,0:T(8,128)(2,1)S(1)}, bf16[72,896]{1,0:T(8,128)(2,1)S(1)}, u32[]{:S(2)}, u32[]{:S(2)}) collective-permute-start(bf16[72,896]{1,0:T(8,128)(2,1)S(1)} %add_convert_fusion), channel_id=1, source_target_pairs={{0,4},{4,0},{8,12},{12,8},{1,5},{5,1},{9,13},{13,9},{2,6},{6,2},{1... | collective-permute-start | bytes 387080 | tf_op jit(solution)/shard_map/back1_ep/ppermute | solution.py:27
  39.0 7.8 %collective-permute-start.12 = (bf16[72,896]{1,0:T(8,128)(2,1)S(1)}, bf16[72,896]{1,0:T(8,128)(2,1)S(1)}, u32[]{:S(2)}, u32[]{:S(2)}) collective-permute-start(bf16[72,896]{1,0:T(8,128)(2,1)S(1)} %add_convert_fusion.1.earlier_ref), channel_id=1, source_target_pairs={{0,8},{4,12},{8,0},{12,4},{1,9},{5,13},{9,1},{13,5},{2,10},{6,14},... | collective-permute-start | bytes 387080 | tf_op jit(solution)/shard_map/back2_ep/ppermute | solution.py:27
  41.1 4.9 %collective-permute-start.16 = (bf16[72,896]{1,0:T(8,128)(2,1)S(1)}, bf16[72,896]{1,0:T(8,128)(2,1)S(1)}, u32[]{:S(2)}, u32[]{:S(2)}) collective-permute-start(bf16[72,896]{1,0:T(8,128)(2,1)S(1)} %after.15), channel_id=1, source_target_pairs={{0,2},{2,0},{1,3},{3,1},{4,6},{6,4},{5,7},{7,5},{8,10},{10,8},{9,1... | collective-permute-start | bytes 387080 | tf_op jit(solution)/shard_map/back0_tp/ppermute | solution.py:27

commit v18 on v17

--- a/solution.py
+++ b/solution.py
@@ -14,6 +14,7 @@
 ANY = pl.BlockSpec(memory_space=pl.ANY)
 HBM = pl.BlockSpec(memory_space=pltpu.HBM)
 EXTRA = 16
+LEADING = 2
 VMEM_LIMIT = 20 * 1024 * 1024
 
 
@@ -94,19 +95,13 @@
     return copies
 
 
-def pack_kernel(most, order, *refs):
-    given, partial_ref, refs = refs[:4], refs[4], refs[5:]
-    blocks, (place_ref, share_ref), refs = refs[: len(order)], refs[len(order) :][:2], refs[-6:]
-    held, sems, share_sems = refs[:4], refs[4], refs[5]
-    lane, count = lax.axis_index("tp"), partial_ref.shape[0]
+def pack_kernel(most, order, leading, *refs):
+    given, refs = refs[:4], refs[4:]
+    blocks, (place_ref, *held), (ids_ref, sems) = refs[:leading], refs[leading:-2], refs[-2:]
+    held = [ids_ref] + held
     copies = fetch(given, held, sems)
-    shares = fetch(
-        [partial_ref.at[lane ^ j] for j in range(count)],
-        [share_ref.at[j] for j in range(count)],
-        share_sems,
-    )
     copies[0].wait()
-    ids_ref, weights_ref, scales_ref, grad_ref = held
+    weights_ref, scales_ref, grad_ref = held[1:]
     tokens, rows = grad_ref.shape[0], blocks[0].shape[0]
     me = lax.axis_index("ep")
     ids = ids_ref[...]
@@ -130,6 +125,19 @@
     for copy in copies[1:]:
         copy.wait()
     for block_ref, (low, high) in zip(blocks, found):
+        fill(block_ref, most, low, high, weights_ref, scales_ref, grad_ref)
+
+
+def pack_more_kernel(most, order, place_ref, weights_ref, scales_ref, grad_ref, partial_ref, *refs):
+    blocks, (share_ref, sems) = refs[:-2], refs[-2:]
+    lane, count = lax.axis_index("tp"), partial_ref.shape[0]
+    shares = fetch(
+        [partial_ref.at[lane ^ j] for j in range(count)],
+        [share_ref.at[j] for j in range(count)],
+        sems,
+    )
+    for block_ref, k in zip(blocks, order):
+        low, high = place_ref[0, k] != 0, place_ref[1, k] != 0
         fill(block_ref, most, low, high, weights_ref, scales_ref, grad_ref)
     for copy in shares:
         copy.wait()
@@ -267,29 +275,38 @@
     groups = groups_of(wide)
     order = [k for group in groups for k in group]
     partials = latent_partials.reshape(narrow, tokens, latent.shape[1])
-    packed = call(
-        functools.partial(pack_kernel, most, order),
-        [block] * wide + [pltpu.VMEM((2, wide, rows, tokens), bf16), like(partials)],
+    *leading, place, weights, scales, grads = call(
+        functools.partial(pack_kernel, most, order, LEADING),
+        [block] * LEADING
+        + [
+            pltpu.VMEM((2, wide, rows, tokens), bf16),
+            pltpu.VMEM((1, tokens), f32),
+            pltpu.VMEM((grad_scales.shape[1], tokens), f32),
+            pltpu.VMEM((tokens, width), bf16),
+        ],
         *pinned(
             expert_ids.reshape(1, tokens),
             route_weights.reshape(1, tokens),
             grad_scales.T,
             grad_values,
-            partials,
         ),
-        specs=[HBM] * 5,
-        scratch=[
-            pltpu.VMEM((1, tokens), jnp.int32),
-            pltpu.VMEM((1, tokens), f32),
-            pltpu.VMEM((grad_scales.shape[1], tokens), f32),
-            pltpu.VMEM((tokens, width), bf16),
-            pltpu.SemaphoreType.DMA((4,)),
-            pltpu.SemaphoreType.DMA((narrow,)),
-        ],
+        specs=[HBM] * 4,
+        scratch=[pltpu.VMEM((1, tokens), jnp.int32), pltpu.SemaphoreType.DMA((4,))],
         name="pack",
     )
-    place, shares = packed[wide:]
-    packed = dict(zip(order, packed))
+    *packed, shares = call(
+        functools.partial(pack_more_kernel, most, order[LEADING:]),
+        [block] * (wide - LEADING) + [like(partials)],
+        place,
+        weights,
+        scales,
+        grads,
+        *pinned(partials),
+        specs=[VMEM] * 4 + [HBM],
+        scratch=[pltpu.SemaphoreType.DMA((narrow,))],
+        name="pack_more",
+    )
+    packed = dict(zip(order, leading + packed))
 
     def across(k, rows_of_k):
         return [rows_of_k] + [swap(rows_of_k, "tp", j, f"rows{k}") for j in range(1, narrow)]
@@ -350,7 +367,7 @@
         extra = group is groups[-1]
         if extra:
             if received is not None:
-                latent_parts[-1] = after(latent_parts[-1], summed, 1 << 30)
+                latent_parts[-1] = after(latent_parts[-1], summed, 1 << 28)
             own_grad = sum(part.astype(f32) for part in latent_parts)
             gained = own_grad * latent_gain
             row_sums = jnp.stack(

time: 48 us -> 47.6 us (level)
  waiting for transfers between devices: 9.63 us -> 8.41 us
  Pallas kernels: 10.7 us -> 11.6 us
    ppermute x17, waiting for transfers between devices: 9.63 us -> 8.41 us  [swap(): return lax.ppermute(value, axis, [(i, i ^ step) for i in range(count)])]
    pallas_call x8 -> x9, Pallas kernels: 10.7 us -> 11.5 us  [call(): pl.pallas_call(kernel, out_shape=outs, in_specs=specs, out_specs=[outs_in...]
  transfers between devices with their start and end apart: 17 -> 17, of which waited for: 7 -> 7; matrix products, arithmetic and copies ran while one was open for 2% -> 2% of each run, Pallas kernels for 15% -> 18%
where the time goes in v18:
time: 47.6 us; the launch traced here: 47.4 us
  starting transfers between devices  25.7 us (54%)
  Pallas kernels  11.6 us (24%)
  waiting for transfers between devices  8.41 us (18%)
  other arithmetic  1 us (2%)
  between operations  0.8 us (2%)
    ppermute x17, starting transfers between devices, swap(): return lax.ppermute(value, axis, [(i, i ^ step) for i in range(count)])  25.7 us
    pallas_call x9, Pallas kernels, call(): pl.pallas_call(kernel, out_shape=outs, in_specs=specs, out_specs=[outs_in...  11.5 us
    ppermute x17, waiting for transfers between devices, swap(): return lax.ppermute(value, axis, [(i, i ^ step) for i in range(count)])  8.41 us
  transfers between devices with their start and end apart: 17, of which 7 were waited for; matrix products, arithmetic and copies ran while one was open for 2% of the time, Pallas kernels for 18%

profile of v18, /device:TPU:0, one launch (start us, length us, event | category | flops | bytes accessed | tf_op | source)
XLA Modules:
  0.0 47.4 jit_solution(16401554270779865853)
XLA Ops:
  0.6 1.9 %pack.1 = (bf16[72,896]{1,0:T(8,128)(2,1)S(1)}, bf16[72,896]{1,0:T(8,128)(2,1)S(1)}, bf16[2,4,72,128]{3,2,1,0:T(8,128)(2,1)S(1)}, f32[1,128]{1,0:T(1,128)S(1)}, ...) custom-call(s32[1,128]{1,0:T(1,128)} %bitcast.36, f32[1,128]{1,0:T(1,128)} %bitcast.37, f32[14,128]{1,0:T(8,128)} %bitcast.30, ...), custom_call_target="tpu_custom_call" | custom-call | tf_op jit(solution)/shard_map/pack/pallas_call | solution.py:47
  2.5 3.1 %collective-permute-start.4 = (bf16[72,896]{1,0:T(8,128)(2,1)S(1)}, bf16[72,896]{1,0:T(8,128)(2,1)S(1)}, u32[]{:S(2)}, u32[]{:S(2)}) collective-permute-start(bf16[72,896]{1,0:T(8,128)(2,1)S(1)} %get-tuple-element.36), channel_id=1, source_target_pairs={{0,4},{4,0},{8,12},{12,8},{1,5},{5,1},{9,13},{13,9},{2,6},{6,2},{1... | collective-permute-start | bytes 387080 | tf_op jit(solution)/shard_map/rows1_ep/ppermute | solution.py:28
  5.6 2.5 %collective-permute-start = (bf16[72,896]{1,0:T(8,128)(2,1)S(1)}, bf16[72,896]{1,0:T(8,128)(2,1)S(1)}, u32[]{:S(2)}, u32[]{:S(2)}) collective-permute-start(bf16[72,896]{1,0:T(8,128)(2,1)S(1)} %get-tuple-element.35.earlier_ref), channel_id=1, source_target_pairs={{0,12},{4,8},{8,4},{12,0},{1,13},{5,9},{9,5},{13,1},{2,14},{6,10},... | collective-permute-start | bytes 387080 | tf_op jit(solution)/shard_map/rows3_ep/ppermute | solution.py:28
  8.1 1.2 %pack_more.1 = (bf16[72,896]{1,0:T(8,128)(2,1)S(1)}, bf16[72,896]{1,0:T(8,128)(2,1)S(1)}, bf16[2,128,256]{2,1,0:T(8,128)(2,1)S(1)}) custom-call(bf16[2,4,72,128]{3,2,1,0:T(8,128)(2,1)S(1)} %get-tuple-element.30.place_ref, f32[1,128]{1,0:T(1,128)S(1)} %get-tuple-element.31.weights_ref, f32[14,128]{1,0:T(8,128)S(1)} %get-tuple-element.32.scales_ref, ...), custom_call_target="tpu_custom_call" | custom-call | tf_op jit(solution)/shard_map/pack_more/pallas_call | solution.py:47
  9.4 1.6 %collective-permute-start.6 = (bf16[72,896]{1,0:T(8,128)(2,1)S(1)}, bf16[72,896]{1,0:T(8,128)(2,1)S(1)}, u32[]{:S(2)}, u32[]{:S(2)}) collective-permute-start(bf16[72,896]{1,0:T(8,128)(2,1)S(1)} %get-tuple-element.37.refs_4_), channel_id=1, source_target_pairs={{0,2},{2,0},{1,3},{3,1},{4,6},{6,4},{5,7},{7,5},{8,10},{10,8},{9,1... | collective-permute-start | bytes 387080 | tf_op jit(solution)/shard_map/rows0_tp/ppermute | solution.py:28
  11.5 1.5 %collective-permute-start.8 = (bf16[128,256]{1,0:T(8,128)(2,1)S(1)}, bf16[128,256]{1,0:T(8,128)(2,1)S(1)}, u32[]{:S(2)}, u32[]{:S(2)}) collective-permute-start(bf16[128,256]{1,0:T(8,128)(2,1)S(1)} %slice_bitcast_fusion), channel_id=1, source_target_pairs={{0,2},{2,0},{1,3},{3,1},{4,6},{6,4},{5,7},{7,5},{8,10},{10,8},{9,1... | collective-permute-start | bytes 196616 | tf_op jit(solution)/shard_map/latent_tp/ppermute | solution.py:28
  12.9 1.2 %collective-permute-done.earlier_ref.refs_6_.refs_0_ = bf16[72,896]{1,0:T(8,128)(2,1)S(1)} collective-permute-done((bf16[72,896]{1,0:T(8,128)(2,1)S(1)}, bf16[72,896]{1,0:T(8,128)(2,1)S(1)}, u32[]{:S(2)}, u32[]{:S(2)}) %collective-permute-start) | collective-permute-done | bytes 129056 | tf_op jit(solution)/shard_map/rows3_ep/ppermute | solution.py:28
  14.1 1.8 %collective-permute-start.1 = (bf16[72,896]{1,0:T(8,128)(2,1)S(1)}, bf16[72,896]{1,0:T(8,128)(2,1)S(1)}, u32[]{:S(2)}, u32[]{:S(2)}) collective-permute-start(bf16[72,896]{1,0:T(8,128)(2,1)S(1)} %after.8), channel_id=1, source_target_pairs={{0,8},{4,12},{8,0},{12,4},{1,9},{5,13},{9,1},{13,5},{2,10},{6,14},... | collective-permute-start | bytes 387080 | tf_op jit(solution)/shard_map/rows2_ep/ppermute | solution.py:28
  15.9 1.5 %collective-permute-start.3 = (bf16[72,896]{1,0:T(8,128)(2,1)S(1)}, bf16[72,896]{1,0:T(8,128)(2,1)S(1)}, u32[]{:S(2)}, u32[]{:S(2)}) collective-permute-start(bf16[72,896]{1,0:T(8,128)(2,1)S(1)} %collective-permute-done.earlier_ref.refs_6_.refs_0_), channel_id=1, source_target_pairs={{0,2},{2,0},{1,3},{3,1},{4,6},{6,4},{5,7},{7,5},{8,10},{10,8},{9,1... | collective-permute-start | bytes 387080 | tf_op jit(solution)/shard_map/rows3_tp/ppermute | solution.py:28
  17.4 2.9 %fetch.1 = (f32[4,72,512]{2,1,0:T(8,128)S(1)}, f32[4,72,512]{2,1,0:T(8,128)S(1)}, bf16[512,1792]{1,0:T(8,128)(2,1)S(1)}, bf16[1792,512]{1,0:T(8,128)(2,1)S(1)}, ...) custom-call(bf16[2,4,72,512]{3,2,1,0:T(8,128)(2,1)} %bitcast.28, ...), custom_call_target="tpu_custom_call" | custom-call | tf_op jit(solution)/shard_map/fetch/pallas_call | solution.py:47
  21.9 1.6 %collective-permute-start.2 = (bf16[72,896]{1,0:T(8,128)(2,1)S(1)}, bf16[72,896]{1,0:T(8,128)(2,1)S(1)}, u32[]{:S(2)}, u32[]{:S(2)}) collective-permute-start(bf16[72,896]{1,0:T(8,128)(2,1)S(1)} %after.9.refs_0_), channel_id=1, source_target_pairs={{0,2},{2,0},{1,3},{3,1},{4,6},{6,4},{5,7},{7,5},{8,10},{10,8},{9,1... | collective-permute-start | bytes 387080 | tf_op jit(solution)/shard_map/rows2_tp/ppermute | solution.py:28
  23.4 1.3 %back.2 = (bf16[72,896]{1,0:T(8,128)(2,1)S(1)}, bf16[72,896]{1,0:T(8,128)(2,1)S(1)}, bf16[72,896]{1,0:T(8,128)(2,1)S(1)}, bf16[72,896]{1,0:T(8,128)(2,1)S(1)}, b...) custom-call(f32[216,512]{1,0:T(8,128)S(1)} %get-tuple-element.39.sum_ref.earlier_ref, ...), custom_call_target="tpu_custom_call" | custom-call | tf_op jit(solution)/shard_map/back/pallas_call | solution.py:47
  24.7 1.4 %collective-permute-start.10 = (bf16[72,896]{1,0:T(8,128)(2,1)S(1)}, bf16[72,896]{1,0:T(8,128)(2,1)S(1)}, u32[]{:S(2)}, u32[]{:S(2)}) collective-permute-start(bf16[72,896]{1,0:T(8,128)(2,1)S(1)} %get-tuple-element.51), channel_id=1, source_target_pairs={{0,2},{2,0},{1,3},{3,1},{4,6},{6,4},{5,7},{7,5},{8,10},{10,8},{9,1... | collective-permute-start | bytes 387080 | tf_op jit(solution)/shard_map/back3_tp/ppermute | solution.py:28
  26.3 1.5 %collective-permute-done.2.value_ref = bf16[72,896]{1,0:T(8,128)(2,1)S(1)} collective-permute-done((bf16[72,896]{1,0:T(8,128)(2,1)S(1)}, bf16[72,896]{1,0:T(8,128)(2,1)S(1)}, u32[]{:S(2)}, u32[]{:S(2)}) %collective-permute-start.2) | collective-permute-done | bytes 129056 | tf_op jit(solution)/shard_map/rows2_tp/ppermute | solution.py:28
  28.6 1.7 %collective-permute-start.14 = (bf16[72,896]{1,0:T(8,128)(2,1)S(1)}, bf16[72,896]{1,0:T(8,128)(2,1)S(1)}, u32[]{:S(2)}, u32[]{:S(2)}) collective-permute-start(bf16[72,896]{1,0:T(8,128)(2,1)S(1)} %after.14), channel_id=1, source_target_pairs={{0,2},{2,0},{1,3},{3,1},{4,6},{6,4},{5,7},{7,5},{8,10},{10,8},{9,1... | collective-permute-start | bytes 387080 | tf_op jit(solution)/shard_map/back1_tp/ppermute | solution.py:28
  30.5 1.8 %collective-permute-start.13 = (bf16[72,896]{1,0:T(8,128)(2,1)S(1)}, bf16[72,896]{1,0:T(8,128)(2,1)S(1)}, u32[]{:S(2)}, u32[]{:S(2)}) collective-permute-start(bf16[72,896]{1,0:T(8,128)(2,1)S(1)} %add_convert_fusion.2.earlier_ref), channel_id=1, source_target_pairs={{0,12},{4,8},{8,4},{12,0},{1,13},{5,9},{9,5},{13,1},{2,14},{6,10},... | collective-permute-start | bytes 387080 | tf_op jit(solution)/shard_map/back3_ep/ppermute | solution.py:28
  32.3 1.2 %back.3 = (bf16[72,896]{1,0:T(8,128)(2,1)S(1)}, bf16[72,896]{1,0:T(8,128)(2,1)S(1)}) custom-call(f32[72,512]{1,0:T(8,128)S(1)} %get-tuple-element.49.sum_ref.earlier_ref, bf16[88,512]{1,0:T(8,128)(2,1)S(1)} %after.13.other_ref, f32[4,72,512]{2,1,0:T(8,128)S(1)} %get-tuple-element.41.up_by_ref, f32[4,72,512]{2,1,0:T(8,128)S(1)} %get-tuple-element.42.gate_by_ref, ...), custom_call_target="tpu_custom_call" | custom-call | tf_op jit(solution)/shard_map/back/pallas_call | solution.py:47
  33.6 1.5 %collective-permute-start.11 = (bf16[72,896]{1,0:T(8,128)(2,1)S(1)}, bf16[72,896]{1,0:T(8,128)(2,1)S(1)}, u32[]{:S(2)}, u32[]{:S(2)}) collective-permute-start(bf16[72,896]{1,0:T(8,128)(2,1)S(1)} %get-tuple-element.53), channel_id=1, source_target_pairs={{0,2},{2,0},{1,3},{3,1},{4,6},{6,4},{5,7},{7,5},{8,10},{10,8},{9,1... | collective-permute-start | bytes 387080 | tf_op jit(solution)/shard_map/back2_tp/ppermute | solution.py:28
  35.1 1.7 %collective-permute-start.15 = (bf16[72,896]{1,0:T(8,128)(2,1)S(1)}, bf16[72,896]{1,0:T(8,128)(2,1)S(1)}, u32[]{:S(2)}, u32[]{:S(2)}) collective-permute-start(bf16[72,896]{1,0:T(8,128)(2,1)S(1)} %add_convert_fusion), channel_id=1, source_target_pairs={{0,4},{4,0},{8,12},{12,8},{1,5},{5,1},{9,13},{13,9},{2,6},{6,2},{1... | collective-permute-start | bytes 387080 | tf_op jit(solution)/shard_map/back1_ep/ppermute | solution.py:28
  36.8 1.8 %collective-permute-done.11 = bf16[72,896]{1,0:T(8,128)(2,1)S(1)} collective-permute-done((bf16[72,896]{1,0:T(8,128)(2,1)S(1)}, bf16[72,896]{1,0:T(8,128)(2,1)S(1)}, u32[]{:S(2)}, u32[]{:S(2)}) %collective-permute-start.11) | collective-permute-done | bytes 129056 | tf_op jit(solution)/shard_map/back2_tp/ppermute | solution.py:28
  38.6 2.0 %collective-permute-start.12 = (bf16[72,896]{1,0:T(8,128)(2,1)S(1)}, bf16[72,896]{1,0:T(8,128)(2,1)S(1)}, u32[]{:S(2)}, u32[]{:S(2)}) collective-permute-start(bf16[72,896]{1,0:T(8,128)(2,1)S(1)} %add_convert_fusion.1.earlier_ref), channel_id=1, source_target_pairs={{0,8},{4,12},{8,0},{12,4},{1,9},{5,13},{9,1},{13,5},{2,10},{6,14},... | collective-permute-start | bytes 387080 | tf_op jit(solution)/shard_map/back2_ep/ppermute | solution.py:28
  40.7 1.4 %collective-permute-start.16 = (bf16[72,896]{1,0:T(8,128)(2,1)S(1)}, bf16[72,896]{1,0:T(8,128)(2,1)S(1)}, u32[]{:S(2)}, u32[]{:S(2)}) collective-permute-start(bf16[72,896]{1,0:T(8,128)(2,1)S(1)} %after.15), channel_id=1, source_target_pairs={{0,2},{2,0},{1,3},{3,1},{4,6},{6,4},{5,7},{7,5},{8,10},{10,8},{9,1... | collective-permute-start | bytes 387080 | tf_op jit(solution)/shard_map/back0_tp/ppermute | solution.py:28
  42.8 2.8 %collective-permute-done.16.refs_3_ = bf16[72,896]{1,0:T(8,128)(2,1)S(1)} collective-permute-done((bf16[72,896]{1,0:T(8,128)(2,1)S(1)}, bf16[72,896]{1,0:T(8,128)(2,1)S(1)}, u32[]{:S(2)}, u32[]{:S(2)}) %collective-permute-start.16) | collective-permute-done | bytes 129056 | tf_op jit(solution)/shard_map/back0_tp/ppermute | solution.py:28
  46.4 1.0 %unpack_latest.1 = bf16[128,1792]{1,0:T(8,128)(2,1)} custom-call(bf16[2,4,72,128]{3,2,1,0:T(8,128)(2,1)S(1)} %get-tuple-element.30.place_ref, bf16[72,896]{1,0:T(8,128)(2,1)S(1)} %collective-permute-done.12.refs_0_, bf16[128,1792]{1,0:T(8,128)(2,1)S(1)} %unpack.1.refs_1_), custom_call_target="tpu_custom_call" | custom-call | tf_op jit(solution)/shard_map/unpack_latest/pallas_call | solution.py:47
  (38 shorter events, 4.8 us)
Async XLA Ops:
  2.5 8.4 %collective-permute-start.4 = (bf16[72,896]{1,0:T(8,128)(2,1)S(1)}, bf16[72,896]{1,0:T(8,128)(2,1)S(1)}, u32[]{:S(2)}, u32[]{:S(2)}) collective-permute-start(bf16[72,896]{1,0:T(8,128)(2,1)S(1)} %get-tuple-element.36), channel_id=1, source_target_pairs={{0,4},{4,0},{8,12},{12,8},{1,5},{5,1},{9,13},{13,9},{2,6},{6,2},{1... | collective-permute-start | bytes 387080 | tf_op jit(solution)/shard_map/rows1_ep/ppermute | solution.py:28
  5.6 8.5 %collective-permute-start = (bf16[72,896]{1,0:T(8,128)(2,1)S(1)}, bf16[72,896]{1,0:T(8,128)(2,1)S(1)}, u32[]{:S(2)}, u32[]{:S(2)}) collective-permute-start(bf16[72,896]{1,0:T(8,128)(2,1)S(1)} %get-tuple-element.35.earlier_ref), channel_id=1, source_target_pairs={{0,12},{4,8},{8,4},{12,0},{1,13},{5,9},{9,5},{13,1},{2,14},{6,10},... | collective-permute-start | bytes 387080 | tf_op jit(solution)/shard_map/rows3_ep/ppermute | solution.py:28
  9.4 10.9 %collective-permute-start.6 = (bf16[72,896]{1,0:T(8,128)(2,1)S(1)}, bf16[72,896]{1,0:T(8,128)(2,1)S(1)}, u32[]{:S(2)}, u32[]{:S(2)}) collective-permute-start(bf16[72,896]{1,0:T(8,128)(2,1)S(1)} %get-tuple-element.37.refs_4_), channel_id=1, source_target_pairs={{0,2},{2,0},{1,3},{3,1},{4,6},{6,4},{5,7},{7,5},{8,10},{10,8},{9,1... | collective-permute-start | bytes 387080 | tf_op jit(solution)/shard_map/rows0_tp/ppermute | solution.py:28
  10.9 9.3 %collective-permute-start.5 = (bf16[72,896]{1,0:T(8,128)(2,1)S(1)}, bf16[72,896]{1,0:T(8,128)(2,1)S(1)}, u32[]{:S(2)}, u32[]{:S(2)}) collective-permute-start(bf16[72,896]{1,0:T(8,128)(2,1)S(1)} %collective-permute-done.4.refs_2_), channel_id=1, source_target_pairs={{0,2},{2,0},{1,3},{3,1},{4,6},{6,4},{5,7},{7,5},{8,10},{10,8},{9,1... | collective-permute-start | bytes 387080 | tf_op jit(solution)/shard_map/rows1_tp/ppermute | solution.py:28
  11.5 12.0 %collective-permute-start.8 = (bf16[128,256]{1,0:T(8,128)(2,1)S(1)}, bf16[128,256]{1,0:T(8,128)(2,1)S(1)}, u32[]{:S(2)}, u32[]{:S(2)}) collective-permute-start(bf16[128,256]{1,0:T(8,128)(2,1)S(1)} %slice_bitcast_fusion), channel_id=1, source_target_pairs={{0,2},{2,0},{1,3},{3,1},{4,6},{6,4},{5,7},{7,5},{8,10},{10,8},{9,1... | collective-permute-start | bytes 196616 | tf_op jit(solution)/shard_map/latent_tp/ppermute | solution.py:28
  14.1 7.7 %collective-permute-start.1 = (bf16[72,896]{1,0:T(8,128)(2,1)S(1)}, bf16[72,896]{1,0:T(8,128)(2,1)S(1)}, u32[]{:S(2)}, u32[]{:S(2)}) collective-permute-start(bf16[72,896]{1,0:T(8,128)(2,1)S(1)} %after.8), channel_id=1, source_target_pairs={{0,8},{4,12},{8,0},{12,4},{1,9},{5,13},{9,1},{13,5},{2,10},{6,14},... | collective-permute-start | bytes 387080 | tf_op jit(solution)/shard_map/rows2_ep/ppermute | solution.py:28
  15.9 5.1 %collective-permute-start.3 = (bf16[72,896]{1,0:T(8,128)(2,1)S(1)}, bf16[72,896]{1,0:T(8,128)(2,1)S(1)}, u32[]{:S(2)}, u32[]{:S(2)}) collective-permute-start(bf16[72,896]{1,0:T(8,128)(2,1)S(1)} %collective-permute-done.earlier_ref.refs_6_.refs_0_), channel_id=1, source_target_pairs={{0,2},{2,0},{1,3},{3,1},{4,6},{6,4},{5,7},{7,5},{8,10},{10,8},{9,1... | collective-permute-start | bytes 387080 | tf_op jit(solution)/shard_map/rows3_tp/ppermute | solution.py:28
  21.8 1.7 %collective-permute-start.7 = (bf16[216,512]{1,0:T(8,128)(2,1)S(1)}, bf16[216,512]{1,0:T(8,128)(2,1)S(1)}, u32[]{:S(2)}, u32[]{:S(2)}) collective-permute-start(bf16[216,512]{1,0:T(8,128)(2,1)S(1)} %get-tuple-element.40), channel_id=1, source_target_pairs={{0,1},{1,0},{2,3},{3,2},{4,5},{5,4},{6,7},{7,6},{8,9},{9,8},{10,11... | collective-permute-start | bytes 663560 | tf_op jit(solution)/shard_map/hidden3_sub/ppermute | solution.py:28
  21.9 5.9 %collective-permute-start.2 = (bf16[72,896]{1,0:T(8,128)(2,1)S(1)}, bf16[72,896]{1,0:T(8,128)(2,1)S(1)}, u32[]{:S(2)}, u32[]{:S(2)}) collective-permute-start(bf16[72,896]{1,0:T(8,128)(2,1)S(1)} %after.9.refs_0_), channel_id=1, source_target_pairs={{0,2},{2,0},{1,3},{3,1},{4,6},{6,4},{5,7},{7,5},{8,10},{10,8},{9,1... | collective-permute-start | bytes 387080 | tf_op jit(solution)/shard_map/rows2_tp/ppermute | solution.py:28
  24.7 5.7 %collective-permute-start.10 = (bf16[72,896]{1,0:T(8,128)(2,1)S(1)}, bf16[72,896]{1,0:T(8,128)(2,1)S(1)}, u32[]{:S(2)}, u32[]{:S(2)}) collective-permute-start(bf16[72,896]{1,0:T(8,128)(2,1)S(1)} %get-tuple-element.51), channel_id=1, source_target_pairs={{0,2},{2,0},{1,3},{3,1},{4,6},{6,4},{5,7},{7,5},{8,10},{10,8},{9,1... | collective-permute-start | bytes 387080 | tf_op jit(solution)/shard_map/back3_tp/ppermute | solution.py:28
  28.5 3.9 %collective-permute-start.9 = (bf16[88,512]{1,0:T(8,128)(2,1)S(1)}, bf16[88,512]{1,0:T(8,128)(2,1)S(1)}, u32[]{:S(2)}, u32[]{:S(2)}) collective-permute-start(bf16[88,512]{1,0:T(8,128)(2,1)S(1)} %get-tuple-element.50), channel_id=1, source_target_pairs={{0,1},{1,0},{2,3},{3,2},{4,5},{5,4},{6,7},{7,6},{8,9},{9,8},{10,11... | collective-permute-start | bytes 270344 | tf_op jit(solution)/shard_map/hidden2_sub/ppermute | solution.py:28
  28.6 6.5 %collective-permute-start.14 = (bf16[72,896]{1,0:T(8,128)(2,1)S(1)}, bf16[72,896]{1,0:T(8,128)(2,1)S(1)}, u32[]{:S(2)}, u32[]{:S(2)}) collective-permute-start(bf16[72,896]{1,0:T(8,128)(2,1)S(1)} %after.14), channel_id=1, source_target_pairs={{0,2},{2,0},{1,3},{3,1},{4,6},{6,4},{5,7},{7,5},{8,10},{10,8},{9,1... | collective-permute-start | bytes 387080 | tf_op jit(solution)/shard_map/back1_tp/ppermute | solution.py:28
  30.5 12.3 %collective-permute-start.13 = (bf16[72,896]{1,0:T(8,128)(2,1)S(1)}, bf16[72,896]{1,0:T(8,128)(2,1)S(1)}, u32[]{:S(2)}, u32[]{:S(2)}) collective-permute-start(bf16[72,896]{1,0:T(8,128)(2,1)S(1)} %add_convert_fusion.2.earlier_ref), channel_id=1, source_target_pairs={{0,12},{4,8},{8,4},{12,0},{1,13},{5,9},{9,5},{13,1},{2,14},{6,10},... | collective-permute-start | bytes 387080 | tf_op jit(solution)/shard_map/back3_ep/ppermute | solution.py:28
  33.6 5.0 %collective-permute-start.11 = (bf16[72,896]{1,0:T(8,128)(2,1)S(1)}, bf16[72,896]{1,0:T(8,128)(2,1)S(1)}, u32[]{:S(2)}, u32[]{:S(2)}) collective-permute-start(bf16[72,896]{1,0:T(8,128)(2,1)S(1)} %get-tuple-element.53), channel_id=1, source_target_pairs={{0,2},{2,0},{1,3},{3,1},{4,6},{6,4},{5,7},{7,5},{8,10},{10,8},{9,1... | collective-permute-start | bytes 387080 | tf_op jit(solution)/shard_map/back2_tp/ppermute | solution.py:28
  35.1 7.7 %collective-permute-start.15 = (bf16[72,896]{1,0:T(8,128)(2,1)S(1)}, bf16[72,896]{1,0:T(8,128)(2,1)S(1)}, u32[]{:S(2)}, u32[]{:S(2)}) collective-permute-start(bf16[72,896]{1,0:T(8,128)(2,1)S(1)} %add_convert_fusion), channel_id=1, source_target_pairs={{0,4},{4,0},{8,12},{12,8},{1,5},{5,1},{9,13},{13,9},{2,6},{6,2},{1... | collective-permute-start | bytes 387080 | tf_op jit(solution)/shard_map/back1_ep/ppermute | solution.py:28
  38.6 7.8 %collective-permute-start.12 = (bf16[72,896]{1,0:T(8,128)(2,1)S(1)}, bf16[72,896]{1,0:T(8,128)(2,1)S(1)}, u32[]{:S(2)}, u32[]{:S(2)}) collective-permute-start(bf16[72,896]{1,0:T(8,128)(2,1)S(1)} %add_convert_fusion.1.earlier_ref), channel_id=1, source_target_pairs={{0,8},{4,12},{8,0},{12,4},{1,9},{5,13},{9,1},{13,5},{2,10},{6,14},... | collective-permute-start | bytes 387080 | tf_op jit(solution)/shard_map/back2_ep/ppermute | solution.py:28
  40.7 4.9 %collective-permute-start.16 = (bf16[72,896]{1,0:T(8,128)(2,1)S(1)}, bf16[72,896]{1,0:T(8,128)(2,1)S(1)}, u32[]{:S(2)}, u32[]{:S(2)}) collective-permute-start(bf16[72,896]{1,0:T(8,128)(2,1)S(1)} %after.15), channel_id=1, source_target_pairs={{0,2},{2,0},{1,3},{3,1},{4,6},{6,4},{5,7},{7,5},{8,10},{10,8},{9,1... | collective-permute-start | bytes 387080 | tf_op jit(solution)/shard_map/back0_tp/ppermute | solution.py:28

commit v19 on v18

--- a/solution.py
+++ b/solution.py
@@ -69,20 +69,29 @@
     )(value, earlier)
 
 
-def fill(block_ref, most, low, high, weights_ref, scales_ref, grad_ref):
+def fill(blocks, found, weights_ref, scales_ref, grad_ref):
     half, scale_half = grad_ref.shape[1] // 2, scales_ref.shape[0] // 2
+    low, high = [
+        jnp.concatenate([pair[side].astype(jnp.float32) for pair in found], axis=0)
+        for side in range(2)
+    ]
     placed = jnp.dot(
         low.astype(jnp.bfloat16), grad_ref[:, :half], preferred_element_type=jnp.float32
     )
     placed += jnp.dot(
         high.astype(jnp.bfloat16), grad_ref[:, half:], preferred_element_type=jnp.float32
     )
-    scale = dot(low.astype(jnp.float32), scales_ref[:scale_half], NT, lax.Precision.HIGHEST)
-    scale += dot(high.astype(jnp.float32), scales_ref[scale_half:], NT, lax.Precision.HIGHEST)
-    weight = jnp.sum(jnp.where(low | high, weights_ref[...], 0.0), axis=1, keepdims=True)
-    for b in range(scale_half):
-        part = slice(b * 128, (b + 1) * 128)
-        block_ref[:, part] = (placed[:, part] * scale[:, b : b + 1] * weight).astype(jnp.bfloat16)
+    scale = dot(low, scales_ref[:scale_half], NT, lax.Precision.HIGHEST)
+    scale += dot(high, scales_ref[scale_half:], NT, lax.Precision.HIGHEST)
+    weight = jnp.sum((low + high) * weights_ref[...], axis=1, keepdims=True)
+    rows = blocks[0].shape[0]
+    for at, block_ref in enumerate(blocks):
+        own = slice(at * rows, (at + 1) * rows)
+        for b in range(scale_half):
+            part = slice(b * 128, (b + 1) * 128)
+            block_ref[:, part] = (placed[own, part] * scale[own, b : b + 1] * weight[own]).astype(
+                jnp.bfloat16
+            )
 
 
 def fetch(sources, targets, sems, first=0):
@@ -124,8 +133,7 @@
         place_ref[1, k] = high.astype(jnp.bfloat16)
     for copy in copies[1:]:
         copy.wait()
-    for block_ref, (low, high) in zip(blocks, found):
-        fill(block_ref, most, low, high, weights_ref, scales_ref, grad_ref)
+    fill(blocks, found[: len(blocks)], weights_ref, scales_ref, grad_ref)
 
 
 def pack_more_kernel(most, order, place_ref, weights_ref, scales_ref, grad_ref, partial_ref, *refs):
@@ -136,9 +144,8 @@
         [share_ref.at[j] for j in range(count)],
         sems,
     )
-    for block_ref, k in zip(blocks, order):
-        low, high = place_ref[0, k] != 0, place_ref[1, k] != 0
-        fill(block_ref, most, low, high, weights_ref, scales_ref, grad_ref)
+    found = [(place_ref[0, k], place_ref[1, k]) for k in order]
+    fill(blocks, found, weights_ref, scales_ref, grad_ref)
     for copy in shares:
         copy.wait()
 

time: 47.6 us -> 47.6 us (level)
  transfers between devices with their start and end apart: 17 -> 17, of which waited for: 7 -> 7; matrix products, arithmetic and copies ran while one was open for 2% -> 2% of each run, Pallas kernels for 18% -> 19%
where the time goes in v19:
time: 47.6 us; the launch traced here: 47.4 us
  starting transfers between devices  25.4 us (53%)
  Pallas kernels  11.6 us (24%)
  waiting for transfers between devices  8.56 us (18%)
  other arithmetic  1 us (2%)
  between operations  0.8 us (2%)
    ppermute x17, starting transfers between devices, swap(): return lax.ppermute(value, axis, [(i, i ^ step) for i in range(count)])  25.4 us
    pallas_call x9, Pallas kernels, call(): pl.pallas_call(kernel, out_shape=outs, in_specs=specs, out_specs=[outs_in...  11.6 us
    ppermute x17, waiting for transfers between devices, swap(): return lax.ppermute(value, axis, [(i, i ^ step) for i in range(count)])  8.56 us
  transfers between devices with their start and end apart: 17, of which 7 were waited for; matrix products, arithmetic and copies ran while one was open for 2% of the time, Pallas kernels for 19%

profile of v19, /device:TPU:0, one launch (start us, length us, event | category | flops | bytes accessed | tf_op | source)
XLA Modules:
  0.0 47.4 jit_solution(2904632953010492524)
XLA Ops:
  0.6 1.8 %pack.1 = (bf16[72,896]{1,0:T(8,128)(2,1)S(1)}, bf16[72,896]{1,0:T(8,128)(2,1)S(1)}, bf16[2,4,72,128]{3,2,1,0:T(8,128)(2,1)S(1)}, f32[1,128]{1,0:T(1,128)S(1)}, ...) custom-call(s32[1,128]{1,0:T(1,128)} %bitcast.36, f32[1,128]{1,0:T(1,128)} %bitcast.37, f32[14,128]{1,0:T(8,128)} %bitcast.30, ...), custom_call_target="tpu_custom_call" | custom-call | tf_op jit(solution)/shard_map/pack/pallas_call | solution.py:47
  2.4 3.1 %collective-permute-start.4 = (bf16[72,896]{1,0:T(8,128)(2,1)S(1)}, bf16[72,896]{1,0:T(8,128)(2,1)S(1)}, u32[]{:S(2)}, u32[]{:S(2)}) collective-permute-start(bf16[72,896]{1,0:T(8,128)(2,1)S(1)} %get-tuple-element.36), channel_id=1, source_target_pairs={{0,4},{4,0},{8,12},{12,8},{1,5},{5,1},{9,13},{13,9},{2,6},{6,2},{1... | collective-permute-start | bytes 387080 | tf_op jit(solution)/shard_map/rows1_ep/ppermute | solution.py:28
  5.5 2.5 %collective-permute-start = (bf16[72,896]{1,0:T(8,128)(2,1)S(1)}, bf16[72,896]{1,0:T(8,128)(2,1)S(1)}, u32[]{:S(2)}, u32[]{:S(2)}) collective-permute-start(bf16[72,896]{1,0:T(8,128)(2,1)S(1)} %get-tuple-element.35.earlier_ref), channel_id=1, source_target_pairs={{0,12},{4,8},{8,4},{12,0},{1,13},{5,9},{9,5},{13,1},{2,14},{6,10},... | collective-permute-start | bytes 387080 | tf_op jit(solution)/shard_map/rows3_ep/ppermute | solution.py:28
  8.0 1.4 %pack_more.1 = (bf16[72,896]{1,0:T(8,128)(2,1)S(1)}, bf16[72,896]{1,0:T(8,128)(2,1)S(1)}, bf16[2,128,256]{2,1,0:T(8,128)(2,1)S(1)}) custom-call(bf16[2,4,72,128]{3,2,1,0:T(8,128)(2,1)S(1)} %get-tuple-element.30.place_ref, f32[1,128]{1,0:T(1,128)S(1)} %get-tuple-element.31.weights_ref, f32[14,128]{1,0:T(8,128)S(1)} %get-tuple-element.32.scales_ref, ...), custom_call_target="tpu_custom_call" | custom-call | tf_op jit(solution)/shard_map/pack_more/pallas_call | solution.py:47
  9.4 1.6 %collective-permute-start.6 = (bf16[72,896]{1,0:T(8,128)(2,1)S(1)}, bf16[72,896]{1,0:T(8,128)(2,1)S(1)}, u32[]{:S(2)}, u32[]{:S(2)}) collective-permute-start(bf16[72,896]{1,0:T(8,128)(2,1)S(1)} %get-tuple-element.37.refs_4_), channel_id=1, source_target_pairs={{0,2},{2,0},{1,3},{3,1},{4,6},{6,4},{5,7},{7,5},{8,10},{10,8},{9,1... | collective-permute-start | bytes 387080 | tf_op jit(solution)/shard_map/rows0_tp/ppermute | solution.py:28
  11.5 1.5 %collective-permute-start.8 = (bf16[128,256]{1,0:T(8,128)(2,1)S(1)}, bf16[128,256]{1,0:T(8,128)(2,1)S(1)}, u32[]{:S(2)}, u32[]{:S(2)}) collective-permute-start(bf16[128,256]{1,0:T(8,128)(2,1)S(1)} %slice_bitcast_fusion), channel_id=1, source_target_pairs={{0,2},{2,0},{1,3},{3,1},{4,6},{6,4},{5,7},{7,5},{8,10},{10,8},{9,1... | collective-permute-start | bytes 196616 | tf_op jit(solution)/shard_map/latent_tp/ppermute | solution.py:28
  13.0 1.0 %collective-permute-done.earlier_ref.refs_6_.refs_0_ = bf16[72,896]{1,0:T(8,128)(2,1)S(1)} collective-permute-done((bf16[72,896]{1,0:T(8,128)(2,1)S(1)}, bf16[72,896]{1,0:T(8,128)(2,1)S(1)}, u32[]{:S(2)}, u32[]{:S(2)}) %collective-permute-start) | collective-permute-done | bytes 129056 | tf_op jit(solution)/shard_map/rows3_ep/ppermute | solution.py:28
  14.0 1.8 %collective-permute-start.1 = (bf16[72,896]{1,0:T(8,128)(2,1)S(1)}, bf16[72,896]{1,0:T(8,128)(2,1)S(1)}, u32[]{:S(2)}, u32[]{:S(2)}) collective-permute-start(bf16[72,896]{1,0:T(8,128)(2,1)S(1)} %after.8), channel_id=1, source_target_pairs={{0,8},{4,12},{8,0},{12,4},{1,9},{5,13},{9,1},{13,5},{2,10},{6,14},... | collective-permute-start | bytes 387080 | tf_op jit(solution)/shard_map/rows2_ep/ppermute | solution.py:28
  15.8 1.5 %collective-permute-start.3 = (bf16[72,896]{1,0:T(8,128)(2,1)S(1)}, bf16[72,896]{1,0:T(8,128)(2,1)S(1)}, u32[]{:S(2)}, u32[]{:S(2)}) collective-permute-start(bf16[72,896]{1,0:T(8,128)(2,1)S(1)} %collective-permute-done.earlier_ref.refs_6_.refs_0_), channel_id=1, source_target_pairs={{0,2},{2,0},{1,3},{3,1},{4,6},{6,4},{5,7},{7,5},{8,10},{10,8},{9,1... | collective-permute-start | bytes 387080 | tf_op jit(solution)/shard_map/rows3_tp/ppermute | solution.py:28
  17.3 2.9 %fetch.1 = (f32[4,72,512]{2,1,0:T(8,128)S(1)}, f32[4,72,512]{2,1,0:T(8,128)S(1)}, bf16[512,1792]{1,0:T(8,128)(2,1)S(1)}, bf16[1792,512]{1,0:T(8,128)(2,1)S(1)}, ...) custom-call(bf16[2,4,72,512]{3,2,1,0:T(8,128)(2,1)} %bitcast.28, ...), custom_call_target="tpu_custom_call" | custom-call | tf_op jit(solution)/shard_map/fetch/pallas_call | solution.py:47
  21.9 1.6 %collective-permute-start.2 = (bf16[72,896]{1,0:T(8,128)(2,1)S(1)}, bf16[72,896]{1,0:T(8,128)(2,1)S(1)}, u32[]{:S(2)}, u32[]{:S(2)}) collective-permute-start(bf16[72,896]{1,0:T(8,128)(2,1)S(1)} %after.9.refs_0_), channel_id=1, source_target_pairs={{0,2},{2,0},{1,3},{3,1},{4,6},{6,4},{5,7},{7,5},{8,10},{10,8},{9,1... | collective-permute-start | bytes 387080 | tf_op jit(solution)/shard_map/rows2_tp/ppermute | solution.py:28
  23.5 1.3 %back.2 = (bf16[72,896]{1,0:T(8,128)(2,1)S(1)}, bf16[72,896]{1,0:T(8,128)(2,1)S(1)}, bf16[72,896]{1,0:T(8,128)(2,1)S(1)}, bf16[72,896]{1,0:T(8,128)(2,1)S(1)}, b...) custom-call(f32[216,512]{1,0:T(8,128)S(1)} %get-tuple-element.39.sum_ref.earlier_ref, ...), custom_call_target="tpu_custom_call" | custom-call | tf_op jit(solution)/shard_map/back/pallas_call | solution.py:47
  24.8 1.4 %collective-permute-start.10 = (bf16[72,896]{1,0:T(8,128)(2,1)S(1)}, bf16[72,896]{1,0:T(8,128)(2,1)S(1)}, u32[]{:S(2)}, u32[]{:S(2)}) collective-permute-start(bf16[72,896]{1,0:T(8,128)(2,1)S(1)} %get-tuple-element.51), channel_id=1, source_target_pairs={{0,2},{2,0},{1,3},{3,1},{4,6},{6,4},{5,7},{7,5},{8,10},{10,8},{9,1... | collective-permute-start | bytes 387080 | tf_op jit(solution)/shard_map/back3_tp/ppermute | solution.py:28
  26.4 1.5 %collective-permute-done.2.value_ref = bf16[72,896]{1,0:T(8,128)(2,1)S(1)} collective-permute-done((bf16[72,896]{1,0:T(8,128)(2,1)S(1)}, bf16[72,896]{1,0:T(8,128)(2,1)S(1)}, u32[]{:S(2)}, u32[]{:S(2)}) %collective-permute-start.2) | collective-permute-done | bytes 129056 | tf_op jit(solution)/shard_map/rows2_tp/ppermute | solution.py:28
  28.7 1.7 %collective-permute-start.14 = (bf16[72,896]{1,0:T(8,128)(2,1)S(1)}, bf16[72,896]{1,0:T(8,128)(2,1)S(1)}, u32[]{:S(2)}, u32[]{:S(2)}) collective-permute-start(bf16[72,896]{1,0:T(8,128)(2,1)S(1)} %after.14), channel_id=1, source_target_pairs={{0,2},{2,0},{1,3},{3,1},{4,6},{6,4},{5,7},{7,5},{8,10},{10,8},{9,1... | collective-permute-start | bytes 387080 | tf_op jit(solution)/shard_map/back1_tp/ppermute | solution.py:28
  30.6 1.6 %collective-permute-start.13 = (bf16[72,896]{1,0:T(8,128)(2,1)S(1)}, bf16[72,896]{1,0:T(8,128)(2,1)S(1)}, u32[]{:S(2)}, u32[]{:S(2)}) collective-permute-start(bf16[72,896]{1,0:T(8,128)(2,1)S(1)} %add_convert_fusion.2.earlier_ref), channel_id=1, source_target_pairs={{0,12},{4,8},{8,4},{12,0},{1,13},{5,9},{9,5},{13,1},{2,14},{6,10},... | collective-permute-start | bytes 387080 | tf_op jit(solution)/shard_map/back3_ep/ppermute | solution.py:28
  32.2 1.2 %back.3 = (bf16[72,896]{1,0:T(8,128)(2,1)S(1)}, bf16[72,896]{1,0:T(8,128)(2,1)S(1)}) custom-call(f32[72,512]{1,0:T(8,128)S(1)} %get-tuple-element.49.sum_ref.earlier_ref, bf16[88,512]{1,0:T(8,128)(2,1)S(1)} %after.13.other_ref, f32[4,72,512]{2,1,0:T(8,128)S(1)} %get-tuple-element.41.up_by_ref, f32[4,72,512]{2,1,0:T(8,128)S(1)} %get-tuple-element.42.gate_by_ref, ...), custom_call_target="tpu_custom_call" | custom-call | tf_op jit(solution)/shard_map/back/pallas_call | solution.py:47
  33.5 1.5 %collective-permute-start.11 = (bf16[72,896]{1,0:T(8,128)(2,1)S(1)}, bf16[72,896]{1,0:T(8,128)(2,1)S(1)}, u32[]{:S(2)}, u32[]{:S(2)}) collective-permute-start(bf16[72,896]{1,0:T(8,128)(2,1)S(1)} %get-tuple-element.53), channel_id=1, source_target_pairs={{0,2},{2,0},{1,3},{3,1},{4,6},{6,4},{5,7},{7,5},{8,10},{10,8},{9,1... | collective-permute-start | bytes 387080 | tf_op jit(solution)/shard_map/back2_tp/ppermute | solution.py:28
  35.0 1.6 %collective-permute-start.15 = (bf16[72,896]{1,0:T(8,128)(2,1)S(1)}, bf16[72,896]{1,0:T(8,128)(2,1)S(1)}, u32[]{:S(2)}, u32[]{:S(2)}) collective-permute-start(bf16[72,896]{1,0:T(8,128)(2,1)S(1)} %add_convert_fusion), channel_id=1, source_target_pairs={{0,4},{4,0},{8,12},{12,8},{1,5},{5,1},{9,13},{13,9},{2,6},{6,2},{1... | collective-permute-start | bytes 387080 | tf_op jit(solution)/shard_map/back1_ep/ppermute | solution.py:28
  36.7 1.8 %collective-permute-done.11 = bf16[72,896]{1,0:T(8,128)(2,1)S(1)} collective-permute-done((bf16[72,896]{1,0:T(8,128)(2,1)S(1)}, bf16[72,896]{1,0:T(8,128)(2,1)S(1)}, u32[]{:S(2)}, u32[]{:S(2)}) %collective-permute-start.11) | collective-permute-done | bytes 129056 | tf_op jit(solution)/shard_map/back2_tp/ppermute | solution.py:28
  38.5 2.0 %collective-permute-start.12 = (bf16[72,896]{1,0:T(8,128)(2,1)S(1)}, bf16[72,896]{1,0:T(8,128)(2,1)S(1)}, u32[]{:S(2)}, u32[]{:S(2)}) collective-permute-start(bf16[72,896]{1,0:T(8,128)(2,1)S(1)} %add_convert_fusion.1.earlier_ref), channel_id=1, source_target_pairs={{0,8},{4,12},{8,0},{12,4},{1,9},{5,13},{9,1},{13,5},{2,10},{6,14},... | collective-permute-start | bytes 387080 | tf_op jit(solution)/shard_map/back2_ep/ppermute | solution.py:28
  40.5 1.4 %collective-permute-start.16 = (bf16[72,896]{1,0:T(8,128)(2,1)S(1)}, bf16[72,896]{1,0:T(8,128)(2,1)S(1)}, u32[]{:S(2)}, u32[]{:S(2)}) collective-permute-start(bf16[72,896]{1,0:T(8,128)(2,1)S(1)} %after.15), channel_id=1, source_target_pairs={{0,2},{2,0},{1,3},{3,1},{4,6},{6,4},{5,7},{7,5},{8,10},{10,8},{9,1... | collective-permute-start | bytes 387080 | tf_op jit(solution)/shard_map/back0_tp/ppermute | solution.py:28
  42.7 2.8 %collective-permute-done.16.refs_3_ = bf16[72,896]{1,0:T(8,128)(2,1)S(1)} collective-permute-done((bf16[72,896]{1,0:T(8,128)(2,1)S(1)}, bf16[72,896]{1,0:T(8,128)(2,1)S(1)}, u32[]{:S(2)}, u32[]{:S(2)}) %collective-permute-start.16) | collective-permute-done | bytes 129056 | tf_op jit(solution)/shard_map/back0_tp/ppermute | solution.py:28
  46.3 1.0 %unpack_latest.1 = bf16[128,1792]{1,0:T(8,128)(2,1)} custom-call(bf16[2,4,72,128]{3,2,1,0:T(8,128)(2,1)S(1)} %get-tuple-element.30.place_ref, bf16[72,896]{1,0:T(8,128)(2,1)S(1)} %collective-permute-done.12.refs_0_, bf16[128,1792]{1,0:T(8,128)(2,1)S(1)} %unpack.1.refs_1_), custom_call_target="tpu_custom_call" | custom-call | tf_op jit(solution)/shard_map/unpack_latest/pallas_call | solution.py:47
  (38 shorter events, 5.1 us)
Async XLA Ops:
  2.4 8.6 %collective-permute-start.4 = (bf16[72,896]{1,0:T(8,128)(2,1)S(1)}, bf16[72,896]{1,0:T(8,128)(2,1)S(1)}, u32[]{:S(2)}, u32[]{:S(2)}) collective-permute-start(bf16[72,896]{1,0:T(8,128)(2,1)S(1)} %get-tuple-element.36), channel_id=1, source_target_pairs={{0,4},{4,0},{8,12},{12,8},{1,5},{5,1},{9,13},{13,9},{2,6},{6,2},{1... | collective-permute-start | bytes 387080 | tf_op jit(solution)/shard_map/rows1_ep/ppermute | solution.py:28
  5.5 8.5 %collective-permute-start = (bf16[72,896]{1,0:T(8,128)(2,1)S(1)}, bf16[72,896]{1,0:T(8,128)(2,1)S(1)}, u32[]{:S(2)}, u32[]{:S(2)}) collective-permute-start(bf16[72,896]{1,0:T(8,128)(2,1)S(1)} %get-tuple-element.35.earlier_ref), channel_id=1, source_target_pairs={{0,12},{4,8},{8,4},{12,0},{1,13},{5,9},{9,5},{13,1},{2,14},{6,10},... | collective-permute-start | bytes 387080 | tf_op jit(solution)/shard_map/rows3_ep/ppermute | solution.py:28
  9.4 10.7 %collective-permute-start.6 = (bf16[72,896]{1,0:T(8,128)(2,1)S(1)}, bf16[72,896]{1,0:T(8,128)(2,1)S(1)}, u32[]{:S(2)}, u32[]{:S(2)}) collective-permute-start(bf16[72,896]{1,0:T(8,128)(2,1)S(1)} %get-tuple-element.37.refs_4_), channel_id=1, source_target_pairs={{0,2},{2,0},{1,3},{3,1},{4,6},{6,4},{5,7},{7,5},{8,10},{10,8},{9,1... | collective-permute-start | bytes 387080 | tf_op jit(solution)/shard_map/rows0_tp/ppermute | solution.py:28
  11.0 9.1 %collective-permute-start.5 = (bf16[72,896]{1,0:T(8,128)(2,1)S(1)}, bf16[72,896]{1,0:T(8,128)(2,1)S(1)}, u32[]{:S(2)}, u32[]{:S(2)}) collective-permute-start(bf16[72,896]{1,0:T(8,128)(2,1)S(1)} %collective-permute-done.4.refs_2_), channel_id=1, source_target_pairs={{0,2},{2,0},{1,3},{3,1},{4,6},{6,4},{5,7},{7,5},{8,10},{10,8},{9,1... | collective-permute-start | bytes 387080 | tf_op jit(solution)/shard_map/rows1_tp/ppermute | solution.py:28
  11.5 12.0 %collective-permute-start.8 = (bf16[128,256]{1,0:T(8,128)(2,1)S(1)}, bf16[128,256]{1,0:T(8,128)(2,1)S(1)}, u32[]{:S(2)}, u32[]{:S(2)}) collective-permute-start(bf16[128,256]{1,0:T(8,128)(2,1)S(1)} %slice_bitcast_fusion), channel_id=1, source_target_pairs={{0,2},{2,0},{1,3},{3,1},{4,6},{6,4},{5,7},{7,5},{8,10},{10,8},{9,1... | collective-permute-start | bytes 196616 | tf_op jit(solution)/shard_map/latent_tp/ppermute | solution.py:28
  14.0 7.9 %collective-permute-start.1 = (bf16[72,896]{1,0:T(8,128)(2,1)S(1)}, bf16[72,896]{1,0:T(8,128)(2,1)S(1)}, u32[]{:S(2)}, u32[]{:S(2)}) collective-permute-start(bf16[72,896]{1,0:T(8,128)(2,1)S(1)} %after.8), channel_id=1, source_target_pairs={{0,8},{4,12},{8,0},{12,4},{1,9},{5,13},{9,1},{13,5},{2,10},{6,14},... | collective-permute-start | bytes 387080 | tf_op jit(solution)/shard_map/rows2_ep/ppermute | solution.py:28
  15.8 5.3 %collective-permute-start.3 = (bf16[72,896]{1,0:T(8,128)(2,1)S(1)}, bf16[72,896]{1,0:T(8,128)(2,1)S(1)}, u32[]{:S(2)}, u32[]{:S(2)}) collective-permute-start(bf16[72,896]{1,0:T(8,128)(2,1)S(1)} %collective-permute-done.earlier_ref.refs_6_.refs_0_), channel_id=1, source_target_pairs={{0,2},{2,0},{1,3},{3,1},{4,6},{6,4},{5,7},{7,5},{8,10},{10,8},{9,1... | collective-permute-start | bytes 387080 | tf_op jit(solution)/shard_map/rows3_tp/ppermute | solution.py:28
  21.8 1.7 %collective-permute-start.7 = (bf16[216,512]{1,0:T(8,128)(2,1)S(1)}, bf16[216,512]{1,0:T(8,128)(2,1)S(1)}, u32[]{:S(2)}, u32[]{:S(2)}) collective-permute-start(bf16[216,512]{1,0:T(8,128)(2,1)S(1)} %get-tuple-element.40), channel_id=1, source_target_pairs={{0,1},{1,0},{2,3},{3,2},{4,5},{5,4},{6,7},{7,6},{8,9},{9,8},{10,11... | collective-permute-start | bytes 663560 | tf_op jit(solution)/shard_map/hidden3_sub/ppermute | solution.py:28
  21.9 6.0 %collective-permute-start.2 = (bf16[72,896]{1,0:T(8,128)(2,1)S(1)}, bf16[72,896]{1,0:T(8,128)(2,1)S(1)}, u32[]{:S(2)}, u32[]{:S(2)}) collective-permute-start(bf16[72,896]{1,0:T(8,128)(2,1)S(1)} %after.9.refs_0_), channel_id=1, source_target_pairs={{0,2},{2,0},{1,3},{3,1},{4,6},{6,4},{5,7},{7,5},{8,10},{10,8},{9,1... | collective-permute-start | bytes 387080 | tf_op jit(solution)/shard_map/rows2_tp/ppermute | solution.py:28
  24.8 5.7 %collective-permute-start.10 = (bf16[72,896]{1,0:T(8,128)(2,1)S(1)}, bf16[72,896]{1,0:T(8,128)(2,1)S(1)}, u32[]{:S(2)}, u32[]{:S(2)}) collective-permute-start(bf16[72,896]{1,0:T(8,128)(2,1)S(1)} %get-tuple-element.51), channel_id=1, source_target_pairs={{0,2},{2,0},{1,3},{3,1},{4,6},{6,4},{5,7},{7,5},{8,10},{10,8},{9,1... | collective-permute-start | bytes 387080 | tf_op jit(solution)/shard_map/back3_tp/ppermute | solution.py:28
  28.6 3.7 %collective-permute-start.9 = (bf16[88,512]{1,0:T(8,128)(2,1)S(1)}, bf16[88,512]{1,0:T(8,128)(2,1)S(1)}, u32[]{:S(2)}, u32[]{:S(2)}) collective-permute-start(bf16[88,512]{1,0:T(8,128)(2,1)S(1)} %get-tuple-element.50), channel_id=1, source_target_pairs={{0,1},{1,0},{2,3},{3,2},{4,5},{5,4},{6,7},{7,6},{8,9},{9,8},{10,11... | collective-permute-start | bytes 270344 | tf_op jit(solution)/shard_map/hidden2_sub/ppermute | solution.py:28
  28.7 6.3 %collective-permute-start.14 = (bf16[72,896]{1,0:T(8,128)(2,1)S(1)}, bf16[72,896]{1,0:T(8,128)(2,1)S(1)}, u32[]{:S(2)}, u32[]{:S(2)}) collective-permute-start(bf16[72,896]{1,0:T(8,128)(2,1)S(1)} %after.14), channel_id=1, source_target_pairs={{0,2},{2,0},{1,3},{3,1},{4,6},{6,4},{5,7},{7,5},{8,10},{10,8},{9,1... | collective-permute-start | bytes 387080 | tf_op jit(solution)/shard_map/back1_tp/ppermute | solution.py:28
  30.6 12.1 %collective-permute-start.13 = (bf16[72,896]{1,0:T(8,128)(2,1)S(1)}, bf16[72,896]{1,0:T(8,128)(2,1)S(1)}, u32[]{:S(2)}, u32[]{:S(2)}) collective-permute-start(bf16[72,896]{1,0:T(8,128)(2,1)S(1)} %add_convert_fusion.2.earlier_ref), channel_id=1, source_target_pairs={{0,12},{4,8},{8,4},{12,0},{1,13},{5,9},{9,5},{13,1},{2,14},{6,10},... | collective-permute-start | bytes 387080 | tf_op jit(solution)/shard_map/back3_ep/ppermute | solution.py:28
  33.5 5.0 %collective-permute-start.11 = (bf16[72,896]{1,0:T(8,128)(2,1)S(1)}, bf16[72,896]{1,0:T(8,128)(2,1)S(1)}, u32[]{:S(2)}, u32[]{:S(2)}) collective-permute-start(bf16[72,896]{1,0:T(8,128)(2,1)S(1)} %get-tuple-element.53), channel_id=1, source_target_pairs={{0,2},{2,0},{1,3},{3,1},{4,6},{6,4},{5,7},{7,5},{8,10},{10,8},{9,1... | collective-permute-start | bytes 387080 | tf_op jit(solution)/shard_map/back2_tp/ppermute | solution.py:28
  35.0 7.7 %collective-permute-start.15 = (bf16[72,896]{1,0:T(8,128)(2,1)S(1)}, bf16[72,896]{1,0:T(8,128)(2,1)S(1)}, u32[]{:S(2)}, u32[]{:S(2)}) collective-permute-start(bf16[72,896]{1,0:T(8,128)(2,1)S(1)} %add_convert_fusion), channel_id=1, source_target_pairs={{0,4},{4,0},{8,12},{12,8},{1,5},{5,1},{9,13},{13,9},{2,6},{6,2},{1... | collective-permute-start | bytes 387080 | tf_op jit(solution)/shard_map/back1_ep/ppermute | solution.py:28
  38.5 7.8 %collective-permute-start.12 = (bf16[72,896]{1,0:T(8,128)(2,1)S(1)}, bf16[72,896]{1,0:T(8,128)(2,1)S(1)}, u32[]{:S(2)}, u32[]{:S(2)}) collective-permute-start(bf16[72,896]{1,0:T(8,128)(2,1)S(1)} %add_convert_fusion.1.earlier_ref), channel_id=1, source_target_pairs={{0,8},{4,12},{8,0},{12,4},{1,9},{5,13},{9,1},{13,5},{2,10},{6,14},... | collective-permute-start | bytes 387080 | tf_op jit(solution)/shard_map/back2_ep/ppermute | solution.py:28
  40.5 4.9 %collective-permute-start.16 = (bf16[72,896]{1,0:T(8,128)(2,1)S(1)}, bf16[72,896]{1,0:T(8,128)(2,1)S(1)}, u32[]{:S(2)}, u32[]{:S(2)}) collective-permute-start(bf16[72,896]{1,0:T(8,128)(2,1)S(1)} %after.15), channel_id=1, source_target_pairs={{0,2},{2,0},{1,3},{3,1},{4,6},{6,4},{5,7},{7,5},{8,10},{10,8},{9,1... | collective-permute-start | bytes 387080 | tf_op jit(solution)/shard_map/back0_tp/ppermute | solution.py:28

commit v20 on v19

--- a/solution.py
+++ b/solution.py
@@ -144,8 +144,8 @@
         [share_ref.at[j] for j in range(count)],
         sems,
     )
-    found = [(place_ref[0, k], place_ref[1, k]) for k in order]
-    fill(blocks, found, weights_ref, scales_ref, grad_ref)
+    for block_ref, k in zip(blocks, order):
+        fill([block_ref], [(place_ref[0, k], place_ref[1, k])], weights_ref, scales_ref, grad_ref)
     for copy in shares:
         copy.wait()
 

time: 47.6 us -> 47.5 us (level)
  transfers between devices with their start and end apart: 17 -> 17, of which waited for: 7 -> 7; matrix products, arithmetic and copies ran while one was open for 2% -> 2% of each run, Pallas kernels for 19% -> 18%
where the time goes in v20:
time: 47.5 us; the launch traced here: 47.3 us
  starting transfers between devices  25.6 us (54%)
  Pallas kernels  11.4 us (24%)
  waiting for transfers between devices  8.48 us (18%)
  other arithmetic  1 us (2%)
  between operations  0.8 us (2%)
    ppermute x17, starting transfers between devices, swap(): return lax.ppermute(value, axis, [(i, i ^ step) for i in range(count)])  25.6 us
    pallas_call x9, Pallas kernels, call(): pl.pallas_call(kernel, out_shape=outs, in_specs=specs, out_specs=[outs_in...  11.4 us
    ppermute x17, waiting for transfers between devices, swap(): return lax.ppermute(value, axis, [(i, i ^ step) for i in range(count)])  8.48 us
  transfers between devices with their start and end apart: 17, of which 7 were waited for; matrix products, arithmetic and copies ran while one was open for 2% of the time, Pallas kernels for 18%

profile of v20, /device:TPU:0, one launch (start us, length us, event | category | flops | bytes accessed | tf_op | source)
XLA Modules:
  0.0 47.3 jit_solution(9141496244677324639)
XLA Ops:
  0.6 1.8 %pack.1 = (bf16[72,896]{1,0:T(8,128)(2,1)S(1)}, bf16[72,896]{1,0:T(8,128)(2,1)S(1)}, bf16[2,4,72,128]{3,2,1,0:T(8,128)(2,1)S(1)}, f32[1,128]{1,0:T(1,128)S(1)}, ...) custom-call(s32[1,128]{1,0:T(1,128)} %bitcast.36, f32[1,128]{1,0:T(1,128)} %bitcast.37, f32[14,128]{1,0:T(8,128)} %bitcast.30, ...), custom_call_target="tpu_custom_call" | custom-call | tf_op jit(solution)/shard_map/pack/pallas_call | solution.py:47
  2.4 3.1 %collective-permute-start.4 = (bf16[72,896]{1,0:T(8,128)(2,1)S(1)}, bf16[72,896]{1,0:T(8,128)(2,1)S(1)}, u32[]{:S(2)}, u32[]{:S(2)}) collective-permute-start(bf16[72,896]{1,0:T(8,128)(2,1)S(1)} %get-tuple-element.36), channel_id=1, source_target_pairs={{0,4},{4,0},{8,12},{12,8},{1,5},{5,1},{9,13},{13,9},{2,6},{6,2},{1... | collective-permute-start | bytes 387080 | tf_op jit(solution)/shard_map/rows1_ep/ppermute | solution.py:28
  5.5 2.5 %collective-permute-start = (bf16[72,896]{1,0:T(8,128)(2,1)S(1)}, bf16[72,896]{1,0:T(8,128)(2,1)S(1)}, u32[]{:S(2)}, u32[]{:S(2)}) collective-permute-start(bf16[72,896]{1,0:T(8,128)(2,1)S(1)} %get-tuple-element.35.earlier_ref), channel_id=1, source_target_pairs={{0,12},{4,8},{8,4},{12,0},{1,13},{5,9},{9,5},{13,1},{2,14},{6,10},... | collective-permute-start | bytes 387080 | tf_op jit(solution)/shard_map/rows3_ep/ppermute | solution.py:28
  8.0 1.2 %pack_more.1 = (bf16[72,896]{1,0:T(8,128)(2,1)S(1)}, bf16[72,896]{1,0:T(8,128)(2,1)S(1)}, bf16[2,128,256]{2,1,0:T(8,128)(2,1)S(1)}) custom-call(bf16[2,4,72,128]{3,2,1,0:T(8,128)(2,1)S(1)} %get-tuple-element.30.place_ref, f32[1,128]{1,0:T(1,128)S(1)} %get-tuple-element.31.weights_ref, f32[14,128]{1,0:T(8,128)S(1)} %get-tuple-element.32.scales_ref, ...), custom_call_target="tpu_custom_call" | custom-call | tf_op jit(solution)/shard_map/pack_more/pallas_call | solution.py:47
  9.2 1.6 %collective-permute-start.6 = (bf16[72,896]{1,0:T(8,128)(2,1)S(1)}, bf16[72,896]{1,0:T(8,128)(2,1)S(1)}, u32[]{:S(2)}, u32[]{:S(2)}) collective-permute-start(bf16[72,896]{1,0:T(8,128)(2,1)S(1)} %get-tuple-element.37.refs_4_), channel_id=1, source_target_pairs={{0,2},{2,0},{1,3},{3,1},{4,6},{6,4},{5,7},{7,5},{8,10},{10,8},{9,1... | collective-permute-start | bytes 387080 | tf_op jit(solution)/shard_map/rows0_tp/ppermute | solution.py:28
  11.3 1.5 %collective-permute-start.8 = (bf16[128,256]{1,0:T(8,128)(2,1)S(1)}, bf16[128,256]{1,0:T(8,128)(2,1)S(1)}, u32[]{:S(2)}, u32[]{:S(2)}) collective-permute-start(bf16[128,256]{1,0:T(8,128)(2,1)S(1)} %slice_bitcast_fusion), channel_id=1, source_target_pairs={{0,2},{2,0},{1,3},{3,1},{4,6},{6,4},{5,7},{7,5},{8,10},{10,8},{9,1... | collective-permute-start | bytes 196616 | tf_op jit(solution)/shard_map/latent_tp/ppermute | solution.py:28
  12.8 1.2 %collective-permute-done.earlier_ref.refs_6_.refs_0_ = bf16[72,896]{1,0:T(8,128)(2,1)S(1)} collective-permute-done((bf16[72,896]{1,0:T(8,128)(2,1)S(1)}, bf16[72,896]{1,0:T(8,128)(2,1)S(1)}, u32[]{:S(2)}, u32[]{:S(2)}) %collective-permute-start) | collective-permute-done | bytes 129056 | tf_op jit(solution)/shard_map/rows3_ep/ppermute | solution.py:28
  14.0 1.8 %collective-permute-start.1 = (bf16[72,896]{1,0:T(8,128)(2,1)S(1)}, bf16[72,896]{1,0:T(8,128)(2,1)S(1)}, u32[]{:S(2)}, u32[]{:S(2)}) collective-permute-start(bf16[72,896]{1,0:T(8,128)(2,1)S(1)} %after.8), channel_id=1, source_target_pairs={{0,8},{4,12},{8,0},{12,4},{1,9},{5,13},{9,1},{13,5},{2,10},{6,14},... | collective-permute-start | bytes 387080 | tf_op jit(solution)/shard_map/rows2_ep/ppermute | solution.py:28
  15.8 1.5 %collective-permute-start.3 = (bf16[72,896]{1,0:T(8,128)(2,1)S(1)}, bf16[72,896]{1,0:T(8,128)(2,1)S(1)}, u32[]{:S(2)}, u32[]{:S(2)}) collective-permute-start(bf16[72,896]{1,0:T(8,128)(2,1)S(1)} %collective-permute-done.earlier_ref.refs_6_.refs_0_), channel_id=1, source_target_pairs={{0,2},{2,0},{1,3},{3,1},{4,6},{6,4},{5,7},{7,5},{8,10},{10,8},{9,1... | collective-permute-start | bytes 387080 | tf_op jit(solution)/shard_map/rows3_tp/ppermute | solution.py:28
  17.3 2.9 %fetch.1 = (f32[4,72,512]{2,1,0:T(8,128)S(1)}, f32[4,72,512]{2,1,0:T(8,128)S(1)}, bf16[512,1792]{1,0:T(8,128)(2,1)S(1)}, bf16[1792,512]{1,0:T(8,128)(2,1)S(1)}, ...) custom-call(bf16[2,4,72,512]{3,2,1,0:T(8,128)(2,1)} %bitcast.28, ...), custom_call_target="tpu_custom_call" | custom-call | tf_op jit(solution)/shard_map/fetch/pallas_call | solution.py:47
  21.7 1.6 %collective-permute-start.2 = (bf16[72,896]{1,0:T(8,128)(2,1)S(1)}, bf16[72,896]{1,0:T(8,128)(2,1)S(1)}, u32[]{:S(2)}, u32[]{:S(2)}) collective-permute-start(bf16[72,896]{1,0:T(8,128)(2,1)S(1)} %after.9.refs_0_), channel_id=1, source_target_pairs={{0,2},{2,0},{1,3},{3,1},{4,6},{6,4},{5,7},{7,5},{8,10},{10,8},{9,1... | collective-permute-start | bytes 387080 | tf_op jit(solution)/shard_map/rows2_tp/ppermute | solution.py:28
  23.3 1.3 %back.2 = (bf16[72,896]{1,0:T(8,128)(2,1)S(1)}, bf16[72,896]{1,0:T(8,128)(2,1)S(1)}, bf16[72,896]{1,0:T(8,128)(2,1)S(1)}, bf16[72,896]{1,0:T(8,128)(2,1)S(1)}, b...) custom-call(f32[216,512]{1,0:T(8,128)S(1)} %get-tuple-element.39.sum_ref.earlier_ref, ...), custom_call_target="tpu_custom_call" | custom-call | tf_op jit(solution)/shard_map/back/pallas_call | solution.py:47
  24.6 1.4 %collective-permute-start.10 = (bf16[72,896]{1,0:T(8,128)(2,1)S(1)}, bf16[72,896]{1,0:T(8,128)(2,1)S(1)}, u32[]{:S(2)}, u32[]{:S(2)}) collective-permute-start(bf16[72,896]{1,0:T(8,128)(2,1)S(1)} %get-tuple-element.51), channel_id=1, source_target_pairs={{0,2},{2,0},{1,3},{3,1},{4,6},{6,4},{5,7},{7,5},{8,10},{10,8},{9,1... | collective-permute-start | bytes 387080 | tf_op jit(solution)/shard_map/back3_tp/ppermute | solution.py:28
  26.2 1.5 %collective-permute-done.2.value_ref = bf16[72,896]{1,0:T(8,128)(2,1)S(1)} collective-permute-done((bf16[72,896]{1,0:T(8,128)(2,1)S(1)}, bf16[72,896]{1,0:T(8,128)(2,1)S(1)}, u32[]{:S(2)}, u32[]{:S(2)}) %collective-permute-start.2) | collective-permute-done | bytes 129056 | tf_op jit(solution)/shard_map/rows2_tp/ppermute | solution.py:28
  28.5 1.7 %collective-permute-start.14 = (bf16[72,896]{1,0:T(8,128)(2,1)S(1)}, bf16[72,896]{1,0:T(8,128)(2,1)S(1)}, u32[]{:S(2)}, u32[]{:S(2)}) collective-permute-start(bf16[72,896]{1,0:T(8,128)(2,1)S(1)} %after.14), channel_id=1, source_target_pairs={{0,2},{2,0},{1,3},{3,1},{4,6},{6,4},{5,7},{7,5},{8,10},{10,8},{9,1... | collective-permute-start | bytes 387080 | tf_op jit(solution)/shard_map/back1_tp/ppermute | solution.py:28
  30.4 1.8 %collective-permute-start.13 = (bf16[72,896]{1,0:T(8,128)(2,1)S(1)}, bf16[72,896]{1,0:T(8,128)(2,1)S(1)}, u32[]{:S(2)}, u32[]{:S(2)}) collective-permute-start(bf16[72,896]{1,0:T(8,128)(2,1)S(1)} %add_convert_fusion.2.earlier_ref), channel_id=1, source_target_pairs={{0,12},{4,8},{8,4},{12,0},{1,13},{5,9},{9,5},{13,1},{2,14},{6,10},... | collective-permute-start | bytes 387080 | tf_op jit(solution)/shard_map/back3_ep/ppermute | solution.py:28
  32.2 1.2 %back.3 = (bf16[72,896]{1,0:T(8,128)(2,1)S(1)}, bf16[72,896]{1,0:T(8,128)(2,1)S(1)}) custom-call(f32[72,512]{1,0:T(8,128)S(1)} %get-tuple-element.49.sum_ref.earlier_ref, bf16[88,512]{1,0:T(8,128)(2,1)S(1)} %after.13.other_ref, f32[4,72,512]{2,1,0:T(8,128)S(1)} %get-tuple-element.41.up_by_ref, f32[4,72,512]{2,1,0:T(8,128)S(1)} %get-tuple-element.42.gate_by_ref, ...), custom_call_target="tpu_custom_call" | custom-call | tf_op jit(solution)/shard_map/back/pallas_call | solution.py:47
  33.5 1.4 %collective-permute-start.11 = (bf16[72,896]{1,0:T(8,128)(2,1)S(1)}, bf16[72,896]{1,0:T(8,128)(2,1)S(1)}, u32[]{:S(2)}, u32[]{:S(2)}) collective-permute-start(bf16[72,896]{1,0:T(8,128)(2,1)S(1)} %get-tuple-element.53), channel_id=1, source_target_pairs={{0,2},{2,0},{1,3},{3,1},{4,6},{6,4},{5,7},{7,5},{8,10},{10,8},{9,1... | collective-permute-start | bytes 387080 | tf_op jit(solution)/shard_map/back2_tp/ppermute | solution.py:28
  34.9 1.7 %collective-permute-start.15 = (bf16[72,896]{1,0:T(8,128)(2,1)S(1)}, bf16[72,896]{1,0:T(8,128)(2,1)S(1)}, u32[]{:S(2)}, u32[]{:S(2)}) collective-permute-start(bf16[72,896]{1,0:T(8,128)(2,1)S(1)} %add_convert_fusion), channel_id=1, source_target_pairs={{0,4},{4,0},{8,12},{12,8},{1,5},{5,1},{9,13},{13,9},{2,6},{6,2},{1... | collective-permute-start | bytes 387080 | tf_op jit(solution)/shard_map/back1_ep/ppermute | solution.py:28
  36.7 1.8 %collective-permute-done.11 = bf16[72,896]{1,0:T(8,128)(2,1)S(1)} collective-permute-done((bf16[72,896]{1,0:T(8,128)(2,1)S(1)}, bf16[72,896]{1,0:T(8,128)(2,1)S(1)}, u32[]{:S(2)}, u32[]{:S(2)}) %collective-permute-start.11) | collective-permute-done | bytes 129056 | tf_op jit(solution)/shard_map/back2_tp/ppermute | solution.py:28
  38.5 2.0 %collective-permute-start.12 = (bf16[72,896]{1,0:T(8,128)(2,1)S(1)}, bf16[72,896]{1,0:T(8,128)(2,1)S(1)}, u32[]{:S(2)}, u32[]{:S(2)}) collective-permute-start(bf16[72,896]{1,0:T(8,128)(2,1)S(1)} %add_convert_fusion.1.earlier_ref), channel_id=1, source_target_pairs={{0,8},{4,12},{8,0},{12,4},{1,9},{5,13},{9,1},{13,5},{2,10},{6,14},... | collective-permute-start | bytes 387080 | tf_op jit(solution)/shard_map/back2_ep/ppermute | solution.py:28
  40.5 1.4 %collective-permute-start.16 = (bf16[72,896]{1,0:T(8,128)(2,1)S(1)}, bf16[72,896]{1,0:T(8,128)(2,1)S(1)}, u32[]{:S(2)}, u32[]{:S(2)}) collective-permute-start(bf16[72,896]{1,0:T(8,128)(2,1)S(1)} %after.15), channel_id=1, source_target_pairs={{0,2},{2,0},{1,3},{3,1},{4,6},{6,4},{5,7},{7,5},{8,10},{10,8},{9,1... | collective-permute-start | bytes 387080 | tf_op jit(solution)/shard_map/back0_tp/ppermute | solution.py:28
  42.7 2.8 %collective-permute-done.16.refs_3_ = bf16[72,896]{1,0:T(8,128)(2,1)S(1)} collective-permute-done((bf16[72,896]{1,0:T(8,128)(2,1)S(1)}, bf16[72,896]{1,0:T(8,128)(2,1)S(1)}, u32[]{:S(2)}, u32[]{:S(2)}) %collective-permute-start.16) | collective-permute-done | bytes 129056 | tf_op jit(solution)/shard_map/back0_tp/ppermute | solution.py:28
  46.3 1.0 %unpack_latest.1 = bf16[128,1792]{1,0:T(8,128)(2,1)} custom-call(bf16[2,4,72,128]{3,2,1,0:T(8,128)(2,1)S(1)} %get-tuple-element.30.place_ref, bf16[72,896]{1,0:T(8,128)(2,1)S(1)} %collective-permute-done.12.refs_0_, bf16[128,1792]{1,0:T(8,128)(2,1)S(1)} %unpack.1.refs_1_), custom_call_target="tpu_custom_call" | custom-call | tf_op jit(solution)/shard_map/unpack_latest/pallas_call | solution.py:47
  (38 shorter events, 4.9 us)
Async XLA Ops:
  2.4 8.4 %collective-permute-start.4 = (bf16[72,896]{1,0:T(8,128)(2,1)S(1)}, bf16[72,896]{1,0:T(8,128)(2,1)S(1)}, u32[]{:S(2)}, u32[]{:S(2)}) collective-permute-start(bf16[72,896]{1,0:T(8,128)(2,1)S(1)} %get-tuple-element.36), channel_id=1, source_target_pairs={{0,4},{4,0},{8,12},{12,8},{1,5},{5,1},{9,13},{13,9},{2,6},{6,2},{1... | collective-permute-start | bytes 387080 | tf_op jit(solution)/shard_map/rows1_ep/ppermute | solution.py:28
  5.5 8.5 %collective-permute-start = (bf16[72,896]{1,0:T(8,128)(2,1)S(1)}, bf16[72,896]{1,0:T(8,128)(2,1)S(1)}, u32[]{:S(2)}, u32[]{:S(2)}) collective-permute-start(bf16[72,896]{1,0:T(8,128)(2,1)S(1)} %get-tuple-element.35.earlier_ref), channel_id=1, source_target_pairs={{0,12},{4,8},{8,4},{12,0},{1,13},{5,9},{9,5},{13,1},{2,14},{6,10},... | collective-permute-start | bytes 387080 | tf_op jit(solution)/shard_map/rows3_ep/ppermute | solution.py:28
  9.2 10.9 %collective-permute-start.6 = (bf16[72,896]{1,0:T(8,128)(2,1)S(1)}, bf16[72,896]{1,0:T(8,128)(2,1)S(1)}, u32[]{:S(2)}, u32[]{:S(2)}) collective-permute-start(bf16[72,896]{1,0:T(8,128)(2,1)S(1)} %get-tuple-element.37.refs_4_), channel_id=1, source_target_pairs={{0,2},{2,0},{1,3},{3,1},{4,6},{6,4},{5,7},{7,5},{8,10},{10,8},{9,1... | collective-permute-start | bytes 387080 | tf_op jit(solution)/shard_map/rows0_tp/ppermute | solution.py:28
  10.8 9.4 %collective-permute-start.5 = (bf16[72,896]{1,0:T(8,128)(2,1)S(1)}, bf16[72,896]{1,0:T(8,128)(2,1)S(1)}, u32[]{:S(2)}, u32[]{:S(2)}) collective-permute-start(bf16[72,896]{1,0:T(8,128)(2,1)S(1)} %collective-permute-done.4.refs_2_), channel_id=1, source_target_pairs={{0,2},{2,0},{1,3},{3,1},{4,6},{6,4},{5,7},{7,5},{8,10},{10,8},{9,1... | collective-permute-start | bytes 387080 | tf_op jit(solution)/shard_map/rows1_tp/ppermute | solution.py:28
  11.3 12.0 %collective-permute-start.8 = (bf16[128,256]{1,0:T(8,128)(2,1)S(1)}, bf16[128,256]{1,0:T(8,128)(2,1)S(1)}, u32[]{:S(2)}, u32[]{:S(2)}) collective-permute-start(bf16[128,256]{1,0:T(8,128)(2,1)S(1)} %slice_bitcast_fusion), channel_id=1, source_target_pairs={{0,2},{2,0},{1,3},{3,1},{4,6},{6,4},{5,7},{7,5},{8,10},{10,8},{9,1... | collective-permute-start | bytes 196616 | tf_op jit(solution)/shard_map/latent_tp/ppermute | solution.py:28
  14.0 7.7 %collective-permute-start.1 = (bf16[72,896]{1,0:T(8,128)(2,1)S(1)}, bf16[72,896]{1,0:T(8,128)(2,1)S(1)}, u32[]{:S(2)}, u32[]{:S(2)}) collective-permute-start(bf16[72,896]{1,0:T(8,128)(2,1)S(1)} %after.8), channel_id=1, source_target_pairs={{0,8},{4,12},{8,0},{12,4},{1,9},{5,13},{9,1},{13,5},{2,10},{6,14},... | collective-permute-start | bytes 387080 | tf_op jit(solution)/shard_map/rows2_ep/ppermute | solution.py:28
  15.8 5.1 %collective-permute-start.3 = (bf16[72,896]{1,0:T(8,128)(2,1)S(1)}, bf16[72,896]{1,0:T(8,128)(2,1)S(1)}, u32[]{:S(2)}, u32[]{:S(2)}) collective-permute-start(bf16[72,896]{1,0:T(8,128)(2,1)S(1)} %collective-permute-done.earlier_ref.refs_6_.refs_0_), channel_id=1, source_target_pairs={{0,2},{2,0},{1,3},{3,1},{4,6},{6,4},{5,7},{7,5},{8,10},{10,8},{9,1... | collective-permute-start | bytes 387080 | tf_op jit(solution)/shard_map/rows3_tp/ppermute | solution.py:28
  21.6 1.7 %collective-permute-start.7 = (bf16[216,512]{1,0:T(8,128)(2,1)S(1)}, bf16[216,512]{1,0:T(8,128)(2,1)S(1)}, u32[]{:S(2)}, u32[]{:S(2)}) collective-permute-start(bf16[216,512]{1,0:T(8,128)(2,1)S(1)} %get-tuple-element.40), channel_id=1, source_target_pairs={{0,1},{1,0},{2,3},{3,2},{4,5},{5,4},{6,7},{7,6},{8,9},{9,8},{10,11... | collective-permute-start | bytes 663560 | tf_op jit(solution)/shard_map/hidden3_sub/ppermute | solution.py:28
  21.7 6.0 %collective-permute-start.2 = (bf16[72,896]{1,0:T(8,128)(2,1)S(1)}, bf16[72,896]{1,0:T(8,128)(2,1)S(1)}, u32[]{:S(2)}, u32[]{:S(2)}) collective-permute-start(bf16[72,896]{1,0:T(8,128)(2,1)S(1)} %after.9.refs_0_), channel_id=1, source_target_pairs={{0,2},{2,0},{1,3},{3,1},{4,6},{6,4},{5,7},{7,5},{8,10},{10,8},{9,1... | collective-permute-start | bytes 387080 | tf_op jit(solution)/shard_map/rows2_tp/ppermute | solution.py:28
  24.6 5.7 %collective-permute-start.10 = (bf16[72,896]{1,0:T(8,128)(2,1)S(1)}, bf16[72,896]{1,0:T(8,128)(2,1)S(1)}, u32[]{:S(2)}, u32[]{:S(2)}) collective-permute-start(bf16[72,896]{1,0:T(8,128)(2,1)S(1)} %get-tuple-element.51), channel_id=1, source_target_pairs={{0,2},{2,0},{1,3},{3,1},{4,6},{6,4},{5,7},{7,5},{8,10},{10,8},{9,1... | collective-permute-start | bytes 387080 | tf_op jit(solution)/shard_map/back3_tp/ppermute | solution.py:28
  28.4 3.9 %collective-permute-start.9 = (bf16[88,512]{1,0:T(8,128)(2,1)S(1)}, bf16[88,512]{1,0:T(8,128)(2,1)S(1)}, u32[]{:S(2)}, u32[]{:S(2)}) collective-permute-start(bf16[88,512]{1,0:T(8,128)(2,1)S(1)} %get-tuple-element.50), channel_id=1, source_target_pairs={{0,1},{1,0},{2,3},{3,2},{4,5},{5,4},{6,7},{7,6},{8,9},{9,8},{10,11... | collective-permute-start | bytes 270344 | tf_op jit(solution)/shard_map/hidden2_sub/ppermute | solution.py:28
  28.5 6.4 %collective-permute-start.14 = (bf16[72,896]{1,0:T(8,128)(2,1)S(1)}, bf16[72,896]{1,0:T(8,128)(2,1)S(1)}, u32[]{:S(2)}, u32[]{:S(2)}) collective-permute-start(bf16[72,896]{1,0:T(8,128)(2,1)S(1)} %after.14), channel_id=1, source_target_pairs={{0,2},{2,0},{1,3},{3,1},{4,6},{6,4},{5,7},{7,5},{8,10},{10,8},{9,1... | collective-permute-start | bytes 387080 | tf_op jit(solution)/shard_map/back1_tp/ppermute | solution.py:28
  30.4 12.3 %collective-permute-start.13 = (bf16[72,896]{1,0:T(8,128)(2,1)S(1)}, bf16[72,896]{1,0:T(8,128)(2,1)S(1)}, u32[]{:S(2)}, u32[]{:S(2)}) collective-permute-start(bf16[72,896]{1,0:T(8,128)(2,1)S(1)} %add_convert_fusion.2.earlier_ref), channel_id=1, source_target_pairs={{0,12},{4,8},{8,4},{12,0},{1,13},{5,9},{9,5},{13,1},{2,14},{6,10},... | collective-permute-start | bytes 387080 | tf_op jit(solution)/shard_map/back3_ep/ppermute | solution.py:28
  33.5 5.0 %collective-permute-start.11 = (bf16[72,896]{1,0:T(8,128)(2,1)S(1)}, bf16[72,896]{1,0:T(8,128)(2,1)S(1)}, u32[]{:S(2)}, u32[]{:S(2)}) collective-permute-start(bf16[72,896]{1,0:T(8,128)(2,1)S(1)} %get-tuple-element.53), channel_id=1, source_target_pairs={{0,2},{2,0},{1,3},{3,1},{4,6},{6,4},{5,7},{7,5},{8,10},{10,8},{9,1... | collective-permute-start | bytes 387080 | tf_op jit(solution)/shard_map/back2_tp/ppermute | solution.py:28
  34.9 7.7 %collective-permute-start.15 = (bf16[72,896]{1,0:T(8,128)(2,1)S(1)}, bf16[72,896]{1,0:T(8,128)(2,1)S(1)}, u32[]{:S(2)}, u32[]{:S(2)}) collective-permute-start(bf16[72,896]{1,0:T(8,128)(2,1)S(1)} %add_convert_fusion), channel_id=1, source_target_pairs={{0,4},{4,0},{8,12},{12,8},{1,5},{5,1},{9,13},{13,9},{2,6},{6,2},{1... | collective-permute-start | bytes 387080 | tf_op jit(solution)/shard_map/back1_ep/ppermute | solution.py:28
  38.5 7.8 %collective-permute-start.12 = (bf16[72,896]{1,0:T(8,128)(2,1)S(1)}, bf16[72,896]{1,0:T(8,128)(2,1)S(1)}, u32[]{:S(2)}, u32[]{:S(2)}) collective-permute-start(bf16[72,896]{1,0:T(8,128)(2,1)S(1)} %add_convert_fusion.1.earlier_ref), channel_id=1, source_target_pairs={{0,8},{4,12},{8,0},{12,4},{1,9},{5,13},{9,1},{13,5},{2,10},{6,14},... | collective-permute-start | bytes 387080 | tf_op jit(solution)/shard_map/back2_ep/ppermute | solution.py:28
  40.5 4.9 %collective-permute-start.16 = (bf16[72,896]{1,0:T(8,128)(2,1)S(1)}, bf16[72,896]{1,0:T(8,128)(2,1)S(1)}, u32[]{:S(2)}, u32[]{:S(2)}) collective-permute-start(bf16[72,896]{1,0:T(8,128)(2,1)S(1)} %after.15), channel_id=1, source_target_pairs={{0,2},{2,0},{1,3},{3,1},{4,6},{6,4},{5,7},{7,5},{8,10},{10,8},{9,1... | collective-permute-start | bytes 387080 | tf_op jit(solution)/shard_map/back0_tp/ppermute | solution.py:28

commit v21 on v20

--- a/solution.py
+++ b/solution.py
@@ -83,15 +83,13 @@
     )
     scale = dot(low, scales_ref[:scale_half], NT, lax.Precision.HIGHEST)
     scale += dot(high, scales_ref[scale_half:], NT, lax.Precision.HIGHEST)
-    weight = jnp.sum((low + high) * weights_ref[...], axis=1, keepdims=True)
+    scale = scale * jnp.sum((low + high) * weights_ref[...], axis=1, keepdims=True)
     rows = blocks[0].shape[0]
     for at, block_ref in enumerate(blocks):
         own = slice(at * rows, (at + 1) * rows)
         for b in range(scale_half):
             part = slice(b * 128, (b + 1) * 128)
-            block_ref[:, part] = (placed[own, part] * scale[own, b : b + 1] * weight[own]).astype(
-                jnp.bfloat16
-            )
+            block_ref[:, part] = (placed[own, part] * scale[own, b : b + 1]).astype(jnp.bfloat16)
 
 
 def fetch(sources, targets, sems, first=0):

time: 47.5 us -> 47.5 us (level)
  no operation moved by 1% of the time
where the time goes in v21:
time: 47.5 us; the launch traced here: 47.3 us
  starting transfers between devices  25.6 us (54%)
  Pallas kernels  11.4 us (24%)
  waiting for transfers between devices  8.46 us (18%)
  other arithmetic  1 us (2%)
  between operations  0.8 us (2%)
    ppermute x17, starting transfers between devices, swap(): return lax.ppermute(value, axis, [(i, i ^ step) for i in range(count)])  25.6 us
    pallas_call x9, Pallas kernels, call(): pl.pallas_call(kernel, out_shape=outs, in_specs=specs, out_specs=[outs_in...  11.4 us
    ppermute x17, waiting for transfers between devices, swap(): return lax.ppermute(value, axis, [(i, i ^ step) for i in range(count)])  8.46 us
  transfers between devices with their start and end apart: 17, of which 7 were waited for; matrix products, arithmetic and copies ran while one was open for 2% of the time, Pallas kernels for 18%

profile of v21, /device:TPU:0, one launch (start us, length us, event | category | flops | bytes accessed | tf_op | source)
XLA Modules:
  0.0 47.3 jit_solution(17945203642616970759)
XLA Ops:
  0.6 1.8 %pack.1 = (bf16[72,896]{1,0:T(8,128)(2,1)S(1)}, bf16[72,896]{1,0:T(8,128)(2,1)S(1)}, bf16[2,4,72,128]{3,2,1,0:T(8,128)(2,1)S(1)}, f32[1,128]{1,0:T(1,128)S(1)}, ...) custom-call(s32[1,128]{1,0:T(1,128)} %bitcast.36, f32[1,128]{1,0:T(1,128)} %bitcast.37, f32[14,128]{1,0:T(8,128)} %bitcast.30, ...), custom_call_target="tpu_custom_call" | custom-call | tf_op jit(solution)/shard_map/pack/pallas_call | solution.py:47
  2.4 3.1 %collective-permute-start.4 = (bf16[72,896]{1,0:T(8,128)(2,1)S(1)}, bf16[72,896]{1,0:T(8,128)(2,1)S(1)}, u32[]{:S(2)}, u32[]{:S(2)}) collective-permute-start(bf16[72,896]{1,0:T(8,128)(2,1)S(1)} %get-tuple-element.36), channel_id=1, source_target_pairs={{0,4},{4,0},{8,12},{12,8},{1,5},{5,1},{9,13},{13,9},{2,6},{6,2},{1... | collective-permute-start | bytes 387080 | tf_op jit(solution)/shard_map/rows1_ep/ppermute | solution.py:28
  5.5 2.5 %collective-permute-start = (bf16[72,896]{1,0:T(8,128)(2,1)S(1)}, bf16[72,896]{1,0:T(8,128)(2,1)S(1)}, u32[]{:S(2)}, u32[]{:S(2)}) collective-permute-start(bf16[72,896]{1,0:T(8,128)(2,1)S(1)} %get-tuple-element.35.earlier_ref), channel_id=1, source_target_pairs={{0,12},{4,8},{8,4},{12,0},{1,13},{5,9},{9,5},{13,1},{2,14},{6,10},... | collective-permute-start | bytes 387080 | tf_op jit(solution)/shard_map/rows3_ep/ppermute | solution.py:28
  8.0 1.2 %pack_more.1 = (bf16[72,896]{1,0:T(8,128)(2,1)S(1)}, bf16[72,896]{1,0:T(8,128)(2,1)S(1)}, bf16[2,128,256]{2,1,0:T(8,128)(2,1)S(1)}) custom-call(bf16[2,4,72,128]{3,2,1,0:T(8,128)(2,1)S(1)} %get-tuple-element.30.place_ref, f32[1,128]{1,0:T(1,128)S(1)} %get-tuple-element.31.weights_ref, f32[14,128]{1,0:T(8,128)S(1)} %get-tuple-element.32.scales_ref, ...), custom_call_target="tpu_custom_call" | custom-call | tf_op jit(solution)/shard_map/pack_more/pallas_call | solution.py:47
  9.2 1.6 %collective-permute-start.6 = (bf16[72,896]{1,0:T(8,128)(2,1)S(1)}, bf16[72,896]{1,0:T(8,128)(2,1)S(1)}, u32[]{:S(2)}, u32[]{:S(2)}) collective-permute-start(bf16[72,896]{1,0:T(8,128)(2,1)S(1)} %get-tuple-element.37.refs_4_), channel_id=1, source_target_pairs={{0,2},{2,0},{1,3},{3,1},{4,6},{6,4},{5,7},{7,5},{8,10},{10,8},{9,1... | collective-permute-start | bytes 387080 | tf_op jit(solution)/shard_map/rows0_tp/ppermute | solution.py:28
  11.3 1.5 %collective-permute-start.8 = (bf16[128,256]{1,0:T(8,128)(2,1)S(1)}, bf16[128,256]{1,0:T(8,128)(2,1)S(1)}, u32[]{:S(2)}, u32[]{:S(2)}) collective-permute-start(bf16[128,256]{1,0:T(8,128)(2,1)S(1)} %slice_bitcast_fusion), channel_id=1, source_target_pairs={{0,2},{2,0},{1,3},{3,1},{4,6},{6,4},{5,7},{7,5},{8,10},{10,8},{9,1... | collective-permute-start | bytes 196616 | tf_op jit(solution)/shard_map/latent_tp/ppermute | solution.py:28
  12.8 1.2 %collective-permute-done.earlier_ref.refs_6_.refs_0_ = bf16[72,896]{1,0:T(8,128)(2,1)S(1)} collective-permute-done((bf16[72,896]{1,0:T(8,128)(2,1)S(1)}, bf16[72,896]{1,0:T(8,128)(2,1)S(1)}, u32[]{:S(2)}, u32[]{:S(2)}) %collective-permute-start) | collective-permute-done | bytes 129056 | tf_op jit(solution)/shard_map/rows3_ep/ppermute | solution.py:28
  14.0 1.8 %collective-permute-start.1 = (bf16[72,896]{1,0:T(8,128)(2,1)S(1)}, bf16[72,896]{1,0:T(8,128)(2,1)S(1)}, u32[]{:S(2)}, u32[]{:S(2)}) collective-permute-start(bf16[72,896]{1,0:T(8,128)(2,1)S(1)} %after.8), channel_id=1, source_target_pairs={{0,8},{4,12},{8,0},{12,4},{1,9},{5,13},{9,1},{13,5},{2,10},{6,14},... | collective-permute-start | bytes 387080 | tf_op jit(solution)/shard_map/rows2_ep/ppermute | solution.py:28
  15.8 1.5 %collective-permute-start.3 = (bf16[72,896]{1,0:T(8,128)(2,1)S(1)}, bf16[72,896]{1,0:T(8,128)(2,1)S(1)}, u32[]{:S(2)}, u32[]{:S(2)}) collective-permute-start(bf16[72,896]{1,0:T(8,128)(2,1)S(1)} %collective-permute-done.earlier_ref.refs_6_.refs_0_), channel_id=1, source_target_pairs={{0,2},{2,0},{1,3},{3,1},{4,6},{6,4},{5,7},{7,5},{8,10},{10,8},{9,1... | collective-permute-start | bytes 387080 | tf_op jit(solution)/shard_map/rows3_tp/ppermute | solution.py:28
  17.3 2.9 %fetch.1 = (f32[4,72,512]{2,1,0:T(8,128)S(1)}, f32[4,72,512]{2,1,0:T(8,128)S(1)}, bf16[512,1792]{1,0:T(8,128)(2,1)S(1)}, bf16[1792,512]{1,0:T(8,128)(2,1)S(1)}, ...) custom-call(bf16[2,4,72,512]{3,2,1,0:T(8,128)(2,1)} %bitcast.28, ...), custom_call_target="tpu_custom_call" | custom-call | tf_op jit(solution)/shard_map/fetch/pallas_call | solution.py:47
  21.7 1.6 %collective-permute-start.2 = (bf16[72,896]{1,0:T(8,128)(2,1)S(1)}, bf16[72,896]{1,0:T(8,128)(2,1)S(1)}, u32[]{:S(2)}, u32[]{:S(2)}) collective-permute-start(bf16[72,896]{1,0:T(8,128)(2,1)S(1)} %after.9.refs_0_), channel_id=1, source_target_pairs={{0,2},{2,0},{1,3},{3,1},{4,6},{6,4},{5,7},{7,5},{8,10},{10,8},{9,1... | collective-permute-start | bytes 387080 | tf_op jit(solution)/shard_map/rows2_tp/ppermute | solution.py:28
  23.3 1.3 %back.2 = (bf16[72,896]{1,0:T(8,128)(2,1)S(1)}, bf16[72,896]{1,0:T(8,128)(2,1)S(1)}, bf16[72,896]{1,0:T(8,128)(2,1)S(1)}, bf16[72,896]{1,0:T(8,128)(2,1)S(1)}, b...) custom-call(f32[216,512]{1,0:T(8,128)S(1)} %get-tuple-element.39.sum_ref.earlier_ref, ...), custom_call_target="tpu_custom_call" | custom-call | tf_op jit(solution)/shard_map/back/pallas_call | solution.py:47
  24.6 1.4 %collective-permute-start.10 = (bf16[72,896]{1,0:T(8,128)(2,1)S(1)}, bf16[72,896]{1,0:T(8,128)(2,1)S(1)}, u32[]{:S(2)}, u32[]{:S(2)}) collective-permute-start(bf16[72,896]{1,0:T(8,128)(2,1)S(1)} %get-tuple-element.51), channel_id=1, source_target_pairs={{0,2},{2,0},{1,3},{3,1},{4,6},{6,4},{5,7},{7,5},{8,10},{10,8},{9,1... | collective-permute-start | bytes 387080 | tf_op jit(solution)/shard_map/back3_tp/ppermute | solution.py:28
  26.2 1.5 %collective-permute-done.2.value_ref = bf16[72,896]{1,0:T(8,128)(2,1)S(1)} collective-permute-done((bf16[72,896]{1,0:T(8,128)(2,1)S(1)}, bf16[72,896]{1,0:T(8,128)(2,1)S(1)}, u32[]{:S(2)}, u32[]{:S(2)}) %collective-permute-start.2) | collective-permute-done | bytes 129056 | tf_op jit(solution)/shard_map/rows2_tp/ppermute | solution.py:28
  28.4 1.7 %collective-permute-start.14 = (bf16[72,896]{1,0:T(8,128)(2,1)S(1)}, bf16[72,896]{1,0:T(8,128)(2,1)S(1)}, u32[]{:S(2)}, u32[]{:S(2)}) collective-permute-start(bf16[72,896]{1,0:T(8,128)(2,1)S(1)} %after.14), channel_id=1, source_target_pairs={{0,2},{2,0},{1,3},{3,1},{4,6},{6,4},{5,7},{7,5},{8,10},{10,8},{9,1... | collective-permute-start | bytes 387080 | tf_op jit(solution)/shard_map/back1_tp/ppermute | solution.py:28
  30.4 1.8 %collective-permute-start.13 = (bf16[72,896]{1,0:T(8,128)(2,1)S(1)}, bf16[72,896]{1,0:T(8,128)(2,1)S(1)}, u32[]{:S(2)}, u32[]{:S(2)}) collective-permute-start(bf16[72,896]{1,0:T(8,128)(2,1)S(1)} %add_convert_fusion.2.earlier_ref), channel_id=1, source_target_pairs={{0,12},{4,8},{8,4},{12,0},{1,13},{5,9},{9,5},{13,1},{2,14},{6,10},... | collective-permute-start | bytes 387080 | tf_op jit(solution)/shard_map/back3_ep/ppermute | solution.py:28
  32.2 1.2 %back.3 = (bf16[72,896]{1,0:T(8,128)(2,1)S(1)}, bf16[72,896]{1,0:T(8,128)(2,1)S(1)}) custom-call(f32[72,512]{1,0:T(8,128)S(1)} %get-tuple-element.49.sum_ref.earlier_ref, bf16[88,512]{1,0:T(8,128)(2,1)S(1)} %after.13.other_ref, f32[4,72,512]{2,1,0:T(8,128)S(1)} %get-tuple-element.41.up_by_ref, f32[4,72,512]{2,1,0:T(8,128)S(1)} %get-tuple-element.42.gate_by_ref, ...), custom_call_target="tpu_custom_call" | custom-call | tf_op jit(solution)/shard_map/back/pallas_call | solution.py:47
  33.4 1.4 %collective-permute-start.11 = (bf16[72,896]{1,0:T(8,128)(2,1)S(1)}, bf16[72,896]{1,0:T(8,128)(2,1)S(1)}, u32[]{:S(2)}, u32[]{:S(2)}) collective-permute-start(bf16[72,896]{1,0:T(8,128)(2,1)S(1)} %get-tuple-element.53), channel_id=1, source_target_pairs={{0,2},{2,0},{1,3},{3,1},{4,6},{6,4},{5,7},{7,5},{8,10},{10,8},{9,1... | collective-permute-start | bytes 387080 | tf_op jit(solution)/shard_map/back2_tp/ppermute | solution.py:28
  34.9 1.7 %collective-permute-start.15 = (bf16[72,896]{1,0:T(8,128)(2,1)S(1)}, bf16[72,896]{1,0:T(8,128)(2,1)S(1)}, u32[]{:S(2)}, u32[]{:S(2)}) collective-permute-start(bf16[72,896]{1,0:T(8,128)(2,1)S(1)} %add_convert_fusion), channel_id=1, source_target_pairs={{0,4},{4,0},{8,12},{12,8},{1,5},{5,1},{9,13},{13,9},{2,6},{6,2},{1... | collective-permute-start | bytes 387080 | tf_op jit(solution)/shard_map/back1_ep/ppermute | solution.py:28
  36.6 1.8 %collective-permute-done.11 = bf16[72,896]{1,0:T(8,128)(2,1)S(1)} collective-permute-done((bf16[72,896]{1,0:T(8,128)(2,1)S(1)}, bf16[72,896]{1,0:T(8,128)(2,1)S(1)}, u32[]{:S(2)}, u32[]{:S(2)}) %collective-permute-start.11) | collective-permute-done | bytes 129056 | tf_op jit(solution)/shard_map/back2_tp/ppermute | solution.py:28
  38.5 2.0 %collective-permute-start.12 = (bf16[72,896]{1,0:T(8,128)(2,1)S(1)}, bf16[72,896]{1,0:T(8,128)(2,1)S(1)}, u32[]{:S(2)}, u32[]{:S(2)}) collective-permute-start(bf16[72,896]{1,0:T(8,128)(2,1)S(1)} %add_convert_fusion.1.earlier_ref), channel_id=1, source_target_pairs={{0,8},{4,12},{8,0},{12,4},{1,9},{5,13},{9,1},{13,5},{2,10},{6,14},... | collective-permute-start | bytes 387080 | tf_op jit(solution)/shard_map/back2_ep/ppermute | solution.py:28
  40.5 1.4 %collective-permute-start.16 = (bf16[72,896]{1,0:T(8,128)(2,1)S(1)}, bf16[72,896]{1,0:T(8,128)(2,1)S(1)}, u32[]{:S(2)}, u32[]{:S(2)}) collective-permute-start(bf16[72,896]{1,0:T(8,128)(2,1)S(1)} %after.15), channel_id=1, source_target_pairs={{0,2},{2,0},{1,3},{3,1},{4,6},{6,4},{5,7},{7,5},{8,10},{10,8},{9,1... | collective-permute-start | bytes 387080 | tf_op jit(solution)/shard_map/back0_tp/ppermute | solution.py:28
  42.7 2.8 %collective-permute-done.16.refs_3_ = bf16[72,896]{1,0:T(8,128)(2,1)S(1)} collective-permute-done((bf16[72,896]{1,0:T(8,128)(2,1)S(1)}, bf16[72,896]{1,0:T(8,128)(2,1)S(1)}, u32[]{:S(2)}, u32[]{:S(2)}) %collective-permute-start.16) | collective-permute-done | bytes 129056 | tf_op jit(solution)/shard_map/back0_tp/ppermute | solution.py:28
  46.3 1.0 %unpack_latest.1 = bf16[128,1792]{1,0:T(8,128)(2,1)} custom-call(bf16[2,4,72,128]{3,2,1,0:T(8,128)(2,1)S(1)} %get-tuple-element.30.place_ref, bf16[72,896]{1,0:T(8,128)(2,1)S(1)} %collective-permute-done.12.refs_0_, bf16[128,1792]{1,0:T(8,128)(2,1)S(1)} %unpack.1.refs_1_), custom_call_target="tpu_custom_call" | custom-call | tf_op jit(solution)/shard_map/unpack_latest/pallas_call | solution.py:47
  (38 shorter events, 4.8 us)
Async XLA Ops:
  2.4 8.4 %collective-permute-start.4 = (bf16[72,896]{1,0:T(8,128)(2,1)S(1)}, bf16[72,896]{1,0:T(8,128)(2,1)S(1)}, u32[]{:S(2)}, u32[]{:S(2)}) collective-permute-start(bf16[72,896]{1,0:T(8,128)(2,1)S(1)} %get-tuple-element.36), channel_id=1, source_target_pairs={{0,4},{4,0},{8,12},{12,8},{1,5},{5,1},{9,13},{13,9},{2,6},{6,2},{1... | collective-permute-start | bytes 387080 | tf_op jit(solution)/shard_map/rows1_ep/ppermute | solution.py:28
  5.5 8.5 %collective-permute-start = (bf16[72,896]{1,0:T(8,128)(2,1)S(1)}, bf16[72,896]{1,0:T(8,128)(2,1)S(1)}, u32[]{:S(2)}, u32[]{:S(2)}) collective-permute-start(bf16[72,896]{1,0:T(8,128)(2,1)S(1)} %get-tuple-element.35.earlier_ref), channel_id=1, source_target_pairs={{0,12},{4,8},{8,4},{12,0},{1,13},{5,9},{9,5},{13,1},{2,14},{6,10},... | collective-permute-start | bytes 387080 | tf_op jit(solution)/shard_map/rows3_ep/ppermute | solution.py:28
  9.2 10.9 %collective-permute-start.6 = (bf16[72,896]{1,0:T(8,128)(2,1)S(1)}, bf16[72,896]{1,0:T(8,128)(2,1)S(1)}, u32[]{:S(2)}, u32[]{:S(2)}) collective-permute-start(bf16[72,896]{1,0:T(8,128)(2,1)S(1)} %get-tuple-element.37.refs_4_), channel_id=1, source_target_pairs={{0,2},{2,0},{1,3},{3,1},{4,6},{6,4},{5,7},{7,5},{8,10},{10,8},{9,1... | collective-permute-start | bytes 387080 | tf_op jit(solution)/shard_map/rows0_tp/ppermute | solution.py:28
  10.8 9.3 %collective-permute-start.5 = (bf16[72,896]{1,0:T(8,128)(2,1)S(1)}, bf16[72,896]{1,0:T(8,128)(2,1)S(1)}, u32[]{:S(2)}, u32[]{:S(2)}) collective-permute-start(bf16[72,896]{1,0:T(8,128)(2,1)S(1)} %collective-permute-done.4.refs_2_), channel_id=1, source_target_pairs={{0,2},{2,0},{1,3},{3,1},{4,6},{6,4},{5,7},{7,5},{8,10},{10,8},{9,1... | collective-permute-start | bytes 387080 | tf_op jit(solution)/shard_map/rows1_tp/ppermute | solution.py:28
  11.3 12.0 %collective-permute-start.8 = (bf16[128,256]{1,0:T(8,128)(2,1)S(1)}, bf16[128,256]{1,0:T(8,128)(2,1)S(1)}, u32[]{:S(2)}, u32[]{:S(2)}) collective-permute-start(bf16[128,256]{1,0:T(8,128)(2,1)S(1)} %slice_bitcast_fusion), channel_id=1, source_target_pairs={{0,2},{2,0},{1,3},{3,1},{4,6},{6,4},{5,7},{7,5},{8,10},{10,8},{9,1... | collective-permute-start | bytes 196616 | tf_op jit(solution)/shard_map/latent_tp/ppermute | solution.py:28
  14.0 7.7 %collective-permute-start.1 = (bf16[72,896]{1,0:T(8,128)(2,1)S(1)}, bf16[72,896]{1,0:T(8,128)(2,1)S(1)}, u32[]{:S(2)}, u32[]{:S(2)}) collective-permute-start(bf16[72,896]{1,0:T(8,128)(2,1)S(1)} %after.8), channel_id=1, source_target_pairs={{0,8},{4,12},{8,0},{12,4},{1,9},{5,13},{9,1},{13,5},{2,10},{6,14},... | collective-permute-start | bytes 387080 | tf_op jit(solution)/shard_map/rows2_ep/ppermute | solution.py:28
  15.8 5.1 %collective-permute-start.3 = (bf16[72,896]{1,0:T(8,128)(2,1)S(1)}, bf16[72,896]{1,0:T(8,128)(2,1)S(1)}, u32[]{:S(2)}, u32[]{:S(2)}) collective-permute-start(bf16[72,896]{1,0:T(8,128)(2,1)S(1)} %collective-permute-done.earlier_ref.refs_6_.refs_0_), channel_id=1, source_target_pairs={{0,2},{2,0},{1,3},{3,1},{4,6},{6,4},{5,7},{7,5},{8,10},{10,8},{9,1... | collective-permute-start | bytes 387080 | tf_op jit(solution)/shard_map/rows3_tp/ppermute | solution.py:28
  21.6 1.7 %collective-permute-start.7 = (bf16[216,512]{1,0:T(8,128)(2,1)S(1)}, bf16[216,512]{1,0:T(8,128)(2,1)S(1)}, u32[]{:S(2)}, u32[]{:S(2)}) collective-permute-start(bf16[216,512]{1,0:T(8,128)(2,1)S(1)} %get-tuple-element.40), channel_id=1, source_target_pairs={{0,1},{1,0},{2,3},{3,2},{4,5},{5,4},{6,7},{7,6},{8,9},{9,8},{10,11... | collective-permute-start | bytes 663560 | tf_op jit(solution)/shard_map/hidden3_sub/ppermute | solution.py:28
  21.7 5.9 %collective-permute-start.2 = (bf16[72,896]{1,0:T(8,128)(2,1)S(1)}, bf16[72,896]{1,0:T(8,128)(2,1)S(1)}, u32[]{:S(2)}, u32[]{:S(2)}) collective-permute-start(bf16[72,896]{1,0:T(8,128)(2,1)S(1)} %after.9.refs_0_), channel_id=1, source_target_pairs={{0,2},{2,0},{1,3},{3,1},{4,6},{6,4},{5,7},{7,5},{8,10},{10,8},{9,1... | collective-permute-start | bytes 387080 | tf_op jit(solution)/shard_map/rows2_tp/ppermute | solution.py:28
  24.6 5.7 %collective-permute-start.10 = (bf16[72,896]{1,0:T(8,128)(2,1)S(1)}, bf16[72,896]{1,0:T(8,128)(2,1)S(1)}, u32[]{:S(2)}, u32[]{:S(2)}) collective-permute-start(bf16[72,896]{1,0:T(8,128)(2,1)S(1)} %get-tuple-element.51), channel_id=1, source_target_pairs={{0,2},{2,0},{1,3},{3,1},{4,6},{6,4},{5,7},{7,5},{8,10},{10,8},{9,1... | collective-permute-start | bytes 387080 | tf_op jit(solution)/shard_map/back3_tp/ppermute | solution.py:28
  28.4 3.9 %collective-permute-start.9 = (bf16[88,512]{1,0:T(8,128)(2,1)S(1)}, bf16[88,512]{1,0:T(8,128)(2,1)S(1)}, u32[]{:S(2)}, u32[]{:S(2)}) collective-permute-start(bf16[88,512]{1,0:T(8,128)(2,1)S(1)} %get-tuple-element.50), channel_id=1, source_target_pairs={{0,1},{1,0},{2,3},{3,2},{4,5},{5,4},{6,7},{7,6},{8,9},{9,8},{10,11... | collective-permute-start | bytes 270344 | tf_op jit(solution)/shard_map/hidden2_sub/ppermute | solution.py:28
  28.4 6.4 %collective-permute-start.14 = (bf16[72,896]{1,0:T(8,128)(2,1)S(1)}, bf16[72,896]{1,0:T(8,128)(2,1)S(1)}, u32[]{:S(2)}, u32[]{:S(2)}) collective-permute-start(bf16[72,896]{1,0:T(8,128)(2,1)S(1)} %after.14), channel_id=1, source_target_pairs={{0,2},{2,0},{1,3},{3,1},{4,6},{6,4},{5,7},{7,5},{8,10},{10,8},{9,1... | collective-permute-start | bytes 387080 | tf_op jit(solution)/shard_map/back1_tp/ppermute | solution.py:28
  30.4 12.3 %collective-permute-start.13 = (bf16[72,896]{1,0:T(8,128)(2,1)S(1)}, bf16[72,896]{1,0:T(8,128)(2,1)S(1)}, u32[]{:S(2)}, u32[]{:S(2)}) collective-permute-start(bf16[72,896]{1,0:T(8,128)(2,1)S(1)} %add_convert_fusion.2.earlier_ref), channel_id=1, source_target_pairs={{0,12},{4,8},{8,4},{12,0},{1,13},{5,9},{9,5},{13,1},{2,14},{6,10},... | collective-permute-start | bytes 387080 | tf_op jit(solution)/shard_map/back3_ep/ppermute | solution.py:28
  33.4 5.0 %collective-permute-start.11 = (bf16[72,896]{1,0:T(8,128)(2,1)S(1)}, bf16[72,896]{1,0:T(8,128)(2,1)S(1)}, u32[]{:S(2)}, u32[]{:S(2)}) collective-permute-start(bf16[72,896]{1,0:T(8,128)(2,1)S(1)} %get-tuple-element.53), channel_id=1, source_target_pairs={{0,2},{2,0},{1,3},{3,1},{4,6},{6,4},{5,7},{7,5},{8,10},{10,8},{9,1... | collective-permute-start | bytes 387080 | tf_op jit(solution)/shard_map/back2_tp/ppermute | solution.py:28
  34.9 7.8 %collective-permute-start.15 = (bf16[72,896]{1,0:T(8,128)(2,1)S(1)}, bf16[72,896]{1,0:T(8,128)(2,1)S(1)}, u32[]{:S(2)}, u32[]{:S(2)}) collective-permute-start(bf16[72,896]{1,0:T(8,128)(2,1)S(1)} %add_convert_fusion), channel_id=1, source_target_pairs={{0,4},{4,0},{8,12},{12,8},{1,5},{5,1},{9,13},{13,9},{2,6},{6,2},{1... | collective-permute-start | bytes 387080 | tf_op jit(solution)/shard_map/back1_ep/ppermute | solution.py:28
  38.5 7.8 %collective-permute-start.12 = (bf16[72,896]{1,0:T(8,128)(2,1)S(1)}, bf16[72,896]{1,0:T(8,128)(2,1)S(1)}, u32[]{:S(2)}, u32[]{:S(2)}) collective-permute-start(bf16[72,896]{1,0:T(8,128)(2,1)S(1)} %add_convert_fusion.1.earlier_ref), channel_id=1, source_target_pairs={{0,8},{4,12},{8,0},{12,4},{1,9},{5,13},{9,1},{13,5},{2,10},{6,14},... | collective-permute-start | bytes 387080 | tf_op jit(solution)/shard_map/back2_ep/ppermute | solution.py:28
  40.5 4.9 %collective-permute-start.16 = (bf16[72,896]{1,0:T(8,128)(2,1)S(1)}, bf16[72,896]{1,0:T(8,128)(2,1)S(1)}, u32[]{:S(2)}, u32[]{:S(2)}) collective-permute-start(bf16[72,896]{1,0:T(8,128)(2,1)S(1)} %after.15), channel_id=1, source_target_pairs={{0,2},{2,0},{1,3},{3,1},{4,6},{6,4},{5,7},{7,5},{8,10},{10,8},{9,1... | collective-permute-start | bytes 387080 | tf_op jit(solution)/shard_map/back0_tp/ppermute | solution.py:28
